TPU v7x, 32 devices: a whole 2x2x4 slice. The times are simulated.
32 devices in a mesh: pipe: 4 (over z), dp: 4 (over y, x), tensor: 2 (over core).
Axes of the slice: x: 2, y: 2, z: 4, core: 2. Of those that a mesh axis runs over, the one named last changes fastest.
Arguments:
- queries: bfloat16 [4, 512, 8192], P('pipe', 'dp', 'tensor'), may hold values from -5.5 to 5.5
- cache_keys: bfloat16 [512, 2, 4, 1024], P('dp', 'tensor', 'pipe'), may hold values from -5.5 to 5.5
- cache_values: bfloat16 [512, 2, 4, 1024], P('dp', 'tensor', 'pipe'), may hold values from -40 to 40
- doc_lengths: int32 [4, 6], P('dp'), may hold values from 1 to 64, 128 in all within a row
- row_counts: int32 [4, 4], replicated, may hold values from 24 to 40, as said below
- out_gain: bfloat16 [8192], P('tensor'), may hold values from 0.099609375 to 1.8984375
Outputs:
- regrouped: bfloat16 [4, 512, 8192], P('pipe', 'dp', 'tensor')
Inputs may be any that keep to these rules, and one draw needn't show every extreme that they name: row_counts[i, j] is how many rows data group i sends to data group j; each row and each column of row_counts sums to 128; some entry equals 40 in every draw.
All inputs are finite; a program needn't handle non-finite values.
Results may differ from a plain program's by a relative error of at most 0.0085.
Values may be sent and summed in bfloat16 or wider, within the bound.
No kernel may reach another device: no remote copies, remote signals or barrier semaphores. Data moves between devices by JAX's collectives and lax.ppermute only.
A program may use at most 64 MiB of HBM per device.

v0:
```python
import jax
import jax.numpy as jnp
from jax import lax
from jax.sharding import PartitionSpec as P

HEADS = 64
HEAD_DIM = 128


masked_fill = -1e30
norm_eps = 1e-06


def doc_ids(ends, positions):
    return jnp.sum((positions[:, None] >= ends[None, :]).astype(jnp.int32), axis=1)


def body(queries, cache_keys, cache_values, doc_lengths, row_counts, out_gain):
    query = queries[0]
    seq = query.shape[0]
    local_width = query.shape[1]
    heads_dev = local_width // HEAD_DIM
    width = HEADS * HEAD_DIM
    scale = 1.0 / HEAD_DIM**0.5
    ends = jnp.cumsum(doc_lengths[0])
    positions = jnp.arange(seq, dtype=jnp.int32)
    docs = doc_ids(ends, positions)
    allowed = (docs[:, None] == docs[None, :]) & (positions[None, :] <= positions[:, None])
    all_keys, all_values = (
        lax.all_gather(cache_keys, "pipe", axis=2, tiled=True),
        lax.all_gather(cache_values, "pipe", axis=2, tiled=True),
    )
    query_heads = query.reshape(seq, heads_dev, HEAD_DIM)
    scores = (
        jnp.einsum(
            "qhd,khd->hqk",
            query_heads,
            all_keys.reshape(seq, heads_dev, HEAD_DIM),
            preferred_element_type=jnp.float32,
        )
        * scale
    )
    scores = jnp.where(allowed[None], scores, masked_fill)
    top = jnp.max(scores, axis=2)
    weights = jnp.where(allowed[None], jnp.exp(scores - top[:, :, None]), 0.0)
    total = jnp.sum(weights, axis=2)
    accum = jnp.einsum(
        "hqk,khd->hqd",
        weights.astype(jnp.bfloat16),
        all_values.reshape(seq, heads_dev, HEAD_DIM),
        preferred_element_type=jnp.float32,
    )
    count = query_heads.shape[1]
    attn = (
        (accum / total[:, :, None])
        .transpose(1, 0, 2)
        .reshape(seq, count * HEAD_DIM)
        .astype(jnp.bfloat16)
    )
    wide = attn.astype(jnp.float32)
    squares = jnp.sum(wide * wide, axis=1)
    gain = out_gain.astype(jnp.float32)
    groups = lax.axis_size("dp")
    own_group = lax.axis_index("dp")
    capacity = 5 * seq // (4 * groups)
    outgoing = lax.dynamic_index_in_dim(row_counts, own_group, 0, keepdims=False)
    incoming = lax.dynamic_index_in_dim(row_counts, own_group, 1, keepdims=False)
    send_start = jnp.cumsum(outgoing) - outgoing
    slot_ids = jnp.arange(capacity, dtype=jnp.int32)
    valid = (slot_ids[None, :] < outgoing[:, None]).reshape(-1)
    send_rows = jnp.where(valid, (send_start[:, None] + slot_ids[None, :]).reshape(-1), 0)
    col_end = jnp.cumsum(incoming)
    source = jnp.sum((positions[:, None] >= col_end[None, :]).astype(jnp.int32), axis=1)
    onehot = (source[:, None] == jnp.arange(groups, dtype=jnp.int32)[None, :]).astype(jnp.int32)
    begin_of = jnp.sum(onehot * (col_end - incoming)[None, :], axis=1)
    recv_rows = source * capacity + positions - begin_of
    row_total = lax.psum(squares, "tensor")
    normed = (wide * lax.rsqrt(row_total / width + norm_eps)[:, None] * gain[None, :]).astype(
        jnp.bfloat16
    )
    picked = jnp.take(normed, send_rows, axis=0)
    keep = valid.reshape((valid.shape[0],) + (1,) * (normed.ndim - 1))
    picked = jnp.where(keep, picked, jnp.zeros_like(picked))
    got_rows = lax.all_to_all(
        picked.reshape((groups, capacity) + normed.shape[1:]),
        "dp",
        split_axis=0,
        concat_axis=0,
        tiled=True,
    )
    flat = got_rows.reshape((groups * capacity,) + got_rows.shape[2:])
    result = jnp.take(flat, recv_rows, axis=0)
    return result[None]


def solution(mesh):
    return jax.shard_map(
        body,
        mesh=mesh,
        in_specs=(
            P("pipe", "dp", "tensor"),
            P("dp", "tensor", "pipe", None),
            P("dp", "tensor", "pipe", None),
            P("dp", None),
            P(),
            P("tensor"),
        ),
        out_specs=P("pipe", "dp", "tensor"),
        check_vma=False,
    )
```

profile of v0, /device:TPU:0, one launch (start us, length us, event | category | flops | bytes accessed | tf_op | source)
XLA Modules:
  0.0 109.4 jit_solution(3844878853850302804)
XLA Ops:
  6.5 0.0 copy-start
  6.5 0.0 copy-start.2
  6.5 0.0 copy-start.1
  6.5 0.0 all-gather.3.cloned.1.call-start
  6.5 0.7 all-gather.3.cloned.1.call-update
  7.3 0.0 all-gather.5.cloned.1.call-start
  7.3 0.7 all-gather.5.cloned.1.call-update
  8.0 1.4 %copy.35 = bf16[16,8,32,128]{3,2,1,0:T(8,128)(2,1)S(1)} copy(bf16[16,8,32,128]{3,1,2,0:T(8,128)(2,1)} %bitcast.45) | data formatting | bytes 2097152
  9.5 0.0 copy-done
  9.5 0.0 copy-done.2
  9.5 0.2 reduce-window.25
  9.7 0.0 copy-done.1
  9.7 0.2 reduce-window.24
  9.9 0.1 add_select_fusion
  10.0 0.1 select_n.90
  10.1 0.1 convert_reduce_fusion
  10.1 0.1 iota_compare_fusion.2
  10.2 0.1 fusion.10
  10.3 29.3 %all-gather.3.cloned.1.call-done = bf16[128,1,4,1024]{3,0,1,2:T(8,128)(2,1)} async-done(((bf16[128,1,1,1024]{3,0,1,2:T(8,128)(2,1)}), bf16[128,1,4,1024]{3,0,1,2:T(8,128)(2,1)}) %all-gather.3.cloned.1.call-update) | async-done | bytes 1048592 | tf_op jit(solution)/shard_map/all_gather | solution.py:30
  39.6 1.6 %copy.26 = bf16[128,1,4,1024]{0,3,2,1:T(8,128)(2,1)S(1)} copy(bf16[128,1,4,1024]{3,0,1,2:T(8,128)(2,1)} %all-gather.3.cloned.1.call-done) | data formatting | bytes 2097152 | tf_op jit(solution)/shard_map/all_gather | solution.py:30
  41.2 2.3 %fusion.24 = (f32[32,128]{1,0:T(8,128)S(1)}, bf16[32,128,128]{1,2,0:T(8,128)(2,1)}) fusion(pred[128,128]{0,1:T(8,128)(4,1)S(1)} %fusion.10, bf16[128,32,128]{0,2,1:T(8,128)(2,1)S(1)} %bitcast.48, bf16[128,32,128]{2,1,0:T(8,128)(2,1)S(1)} %bitcast.46), kind=kOutput, calls=%fused_computation.49 | convolution fusion | flops 137363584 | bytes 3178496 | tf_op jit(solution)/shard_map/sub | solution.py:45
  43.5 0.0 copy-start.3
  43.5 25.1 %all-gather.5.cloned.1.call-done = bf16[128,1,4,1024]{3,0,1,2:T(8,128)(2,1)} async-done(((bf16[128,1,1,1024]{3,0,1,2:T(8,128)(2,1)}), bf16[128,1,4,1024]{3,0,1,2:T(8,128)(2,1)}) %all-gather.5.cloned.1.call-update) | async-done | bytes 1048592 | tf_op jit(solution)/shard_map/all_gather | solution.py:31
  68.6 1.6 %copy.30 = bf16[128,1,4,1024]{0,3,2,1:T(8,128)(2,1)S(1)} copy(bf16[128,1,4,1024]{3,0,1,2:T(8,128)(2,1)} %all-gather.5.cloned.1.call-done) | data formatting | bytes 2097152 | tf_op jit(solution)/shard_map/all_gather | solution.py:31
  70.2 0.0 copy-done.3
  70.2 2.0 %multiply_reduce_fusion = (f32[128]{0:T(128)S(1)}, f32[128,32,128]{0,2,1:T(8,128)}) fusion(f32[128,32]{0,1:T(8,128)S(1)} %bitcast.53, bf16[128,32,128]{0,2,1:T(8,128)(2,1)S(1)} %bitcast.47, bf16[32,128,128]{1,2,0:T(8,128)(2,1)S(1)} %copy-done.3), kind=kOutput, calls=%fused_computation.6 | convolution fusion | flops 136839040 | bytes 4211200 | tf_op jit(solution)/shard_map/hqk,khd->hqd/dot_general | solution.py:47
  72.2 1.9 %copy.32 = f32[128,4096]{1,0:T(8,128)S(1)} copy(f32[128,4096]{0,1:T(8,128)} %bitcast.44) | data formatting | bytes 4194304 | tf_op jit(solution)/shard_map/convert_element_type | solution.py:60
  74.2 2.5 %psum.7 = f32[128]{0:T(128)S(1)} all-reduce(f32[128]{0:T(128)S(1)} %get-tuple-element.13), channel_id=1, replica_groups=mesh['pipe'=4,'dp'=4,'tensor'=2] {'tensor'}, use_global_device_ids=true, to_apply=%region_9.10 | all-reduce | flops 128 | bytes 1024 | tf_op jit(solution)/shard_map/psum | solution.py:77
  76.6 0.3 multiply_convert_fusion
  76.9 1.4 %gather_fusion = bf16[160,4096]{1,0:T(8,128)(2,1)S(1)} fusion(bf16[128,4096]{1,0:T(8,128)(2,1)S(1)} %multiply_convert_fusion, s32[1024]{0:T(1024)S(1)} %pad_clamp_fusion.1), kind=kCustom, calls=%fused_computation | custom fusion | bytes 2622080 | tf_op jit(solution)/shard_map/jit(_take)/gather | solution.py:81
  78.3 1.3 %select_select_fusion = bf16[4,40,4096]{2,1,0:T(8,128)(2,1)} fusion(bf16[4,40,4096]{2,1,0:T(8,128)(2,1)S(1)} %bitcast.43, pred[4,40]{1,0:T(4,128)(4,1)S(1)} %get-tuple-element.10, pred[4,40]{1,0:T(4,128)(4,1)S(1)} %get-tuple-element.9), kind=kLoop, calls=%fused_computation.11 | loop fusion | flops 1310720 | bytes 2621760 | tf_op jit(solution)/shard_map/jit(_where)/select_n | solution.py:83
  79.6 3.7 %all-to-all-start = ((bf16[4,40,4096]{2,1,0:T(8,128)(2,1)}), bf16[4,40,4096]{2,1,0:T(8,128)(2,1)S(1)}, u32[]{:S(2)}, u32[]{:S(2)}) async-start(bf16[4,40,4096]{2,1,0:T(8,128)(2,1)} %select_select_fusion), calls=%async_computation | async-start | bytes 2621440 | tf_op jit(solution)/shard_map/all_to_all | solution.py:84
  83.3 0.2 fusion.22
  83.5 0.1 reduce.1
  83.6 0.1 convert_reduce_fusion.1
  83.7 0.1 select_reduce_fusion
  83.8 16.4 %all-to-all-done = bf16[4,40,4096]{2,1,0:T(8,128)(2,1)S(1)} async-done(((bf16[4,40,4096]{2,1,0:T(8,128)(2,1)}), bf16[4,40,4096]{2,1,0:T(8,128)(2,1)S(1)}, u32[]{:S(2)}, u32[]{:S(2)}) %all-to-all-start) | async-done | bytes 1310752 | tf_op jit(solution)/shard_map/all_to_all | solution.py:84
  100.2 1.2 %gather_fusion.1 = bf16[128,4096]{1,0:T(8,128)(2,1)S(1)} fusion(bf16[160,4096]{1,0:T(8,128)(2,1)S(1)} %bitcast.42, s32[1024]{0:T(1024)S(1)} %pad_clamp_fusion), kind=kCustom, calls=%fused_computation.1 | custom fusion | bytes 2097664 | tf_op jit(solution)/shard_map/jit(_take)/gather | solution.py:92
  101.4 1.1 %bitcast_select_fusion = bf16[1,128,4096]{2,1,0:T(8,128)(2,1)} fusion(bf16[128,4096]{1,0:T(8,128)(2,1)S(1)} %gather_fusion.1, pred[128]{0:T(512)(128)(4,1)S(1)} %compare_and_fusion.1), kind=kLoop, calls=%fused_computation.12 | loop fusion | flops 524288 | bytes 2097280 | tf_op jit(solution)/shard_map/jit(_take)/select_n | solution.py:92
  (11 shorter events, 0.1 us)
Async XLA Ops:
  6.5 2.9 %copy-start = (bf16[4096]{0:T(1024)(128)(2,1)S(1)}, bf16[4096]{0:T(1024)(128)(2,1)}, u32[]{:S(2)}) copy-start(bf16[4096]{0:T(1024)(128)(2,1)} %param.11) | copy-start | bytes 24580
  6.5 3.0 %copy-start.2 = (s32[1,6]{1,0:T(1,128)S(1)}, s32[1,6]{1,0:T(1,128)}, u32[]{:S(2)}) copy-start(s32[1,6]{1,0:T(1,128)} %param.9) | copy-start | bytes 76
  6.5 3.1 %copy-start.1 = (s32[4,4]{1,0:T(4,128)S(1)}, s32[4,4]{1,0:T(4,128)}, u32[]{:S(2)}) copy-start(s32[4,4]{1,0:T(4,128)} %param.10) | copy-start | bytes 196
  6.5 33.1 %all-gather.3.cloned.1.call-start = ((), (), s32[]{:S(2)}) async-start(), calls=%async_computation.1 | async-start | bytes 1310720 | tf_op jit(solution)/shard_map/all_gather | solution.py:30
  7.3 61.4 %all-gather.5.cloned.1.call-start = ((), (), s32[]{:S(2)}) async-start(), calls=%async_computation.2 | async-start | bytes 1310720 | tf_op jit(solution)/shard_map/all_gather | solution.py:31
  43.5 26.7 %copy-start.3 = (bf16[32,128,128]{1,2,0:T(8,128)(2,1)S(1)}, bf16[32,128,128]{1,2,0:T(8,128)(2,1)}, u32[]{:S(2)}) copy-start(bf16[32,128,128]{1,2,0:T(8,128)(2,1)} %get-tuple-element.12) | copy-start | bytes 3145732
  79.6 20.6 %all-to-all-start = ((bf16[4,40,4096]{2,1,0:T(8,128)(2,1)}), bf16[4,40,4096]{2,1,0:T(8,128)(2,1)S(1)}, u32[]{:S(2)}, u32[]{:S(2)}) async-start(bf16[4,40,4096]{2,1,0:T(8,128)(2,1)} %select_select_fusion), calls=%async_computation | async-start | bytes 2621440 | tf_op jit(solution)/shard_map/all_to_all | solution.py:84
Sparse Core Ops, SparseCore 0:
  8.9 30.6 all-gather.2
  41.2 27.4 all-gather.4
where the time goes:
time: 110 us; the launch traced here: 109 us
  waiting for transfers between devices  72.2 us (66%)
  between operations  13.5 us (12%)
  local copies, waits for them, and re-layouts  9.42 us (9%)
  matrix products  4.28 us (4%)
  other arithmetic  3.82 us (3%)
  starting transfers between devices  3.69 us (3%)
  blocking collectives  2.47 us (2%)
    all_gather x1, waiting for transfers between devices, body(): lax.all_gather(cache_keys, 'pipe', axis=2, tiled=True)  29.3 us
    all_gather x1, waiting for transfers between devices, body(): lax.all_gather(cache_values, 'pipe', axis=2, tiled=True)  25.1 us
    all_to_all x1, waiting for transfers between devices, body(): lax.all_to_all(picked.reshape((groups, capacity) + normed.shape[1:]), 'dp...  16.4 us
    all_to_all x1, starting transfers between devices, body(): lax.all_to_all(picked.reshape((groups, capacity) + normed.shape[1:]), 'dp...  3.65 us
    psum x1, blocking collectives, body(): row_total = lax.psum(squares, 'tensor')  2.47 us
    sub x1, matrix products, body(): weights = jnp.where(allowed[None], jnp.exp(scores - top[:, :, None]), 0.0)  2.3 us
  transfers between devices with their start and end apart: 3, of which 3 were waited for; matrix products, arithmetic and copies ran while one was open for 6% of the time, Pallas kernels for 0%

commit v1 on v0

v1 whole, which is shorter than its diff:
```python
import functools

import jax
import jax.numpy as jnp
import numpy as np
from jax import lax
from jax.experimental import pallas as pl
from jax.experimental.pallas import tpu as pltpu
from jax.sharding import PartitionSpec as P

HEADS = 64
HEAD_DIM = 128

masked_fill = -1e30
norm_eps = 1e-06

VMEM = pl.BlockSpec(memory_space=pltpu.VMEM)
SMEM = pl.BlockSpec(memory_space=pltpu.SMEM)
SCOPED = 32 * 1024 * 1024


def iota(shape, dim):
    return lax.broadcasted_iota(jnp.int32, shape, dim)


def allowed_mask(docs, seq):
    rows, cols = iota((seq, seq), 0), iota((seq, seq), 1)
    row_doc = jnp.zeros((seq, seq), jnp.int32)
    col_doc = jnp.zeros((seq, seq), jnp.int32)
    end = jnp.int32(0)
    for k in range(docs.shape[1]):
        end = end + docs[0, k]
        row_doc = row_doc + (rows >= end).astype(jnp.int32)
        col_doc = col_doc + (cols >= end).astype(jnp.int32)
    return (row_doc == col_doc) & (cols <= rows)


def partner(own, step, pairwise):
    return jnp.bitwise_xor(own, step) if pairwise else jnp.int32(step)


def send_matrix(counts, own, seq, cap, pairwise):
    groups = counts.shape[0]
    rows, cols = iota((groups * cap, seq), 0), iota((groups * cap, seq), 1)
    target = jnp.full((groups * cap, seq), -1, jnp.int32)
    for i in range(groups):
        to = partner(own, i, pairwise)
        begin = jnp.int32(0)
        for j in range(groups):
            begin = begin + jnp.where(j < to, counts[own, j], 0)
        inside = (rows >= i * cap) & (rows < i * cap + counts[own, to])
        target = jnp.where(inside, rows - i * cap + begin, target)
    return (cols == target).astype(jnp.float32).astype(jnp.bfloat16)


def place_matrices(counts, own, seq, cap, pairwise, parts):
    groups = counts.shape[0]
    per = groups // parts
    matrices = []
    for part in range(parts):
        rows, cols = iota((seq, per * cap), 0), iota((seq, per * cap), 1)
        target = jnp.full((seq, per * cap), -1, jnp.int32)
        for slot in range(per):
            source = partner(own, part * per + slot, pairwise)
            begin = jnp.int32(0)
            for j in range(groups):
                begin = begin + jnp.where(j < source, counts[j, own], 0)
            inside = (cols >= slot * cap) & (cols < slot * cap + counts[source, own])
            target = jnp.where(inside, cols - slot * cap + begin, target)
        matrices.append((rows == target).astype(jnp.float32).astype(jnp.bfloat16))
    return matrices


def attend_kernel(jobs, parts, cap, pairwise, meta, docs, counts, *refs):
    count = 1 + sum(1 for job in jobs if job is None)
    queries, (k_ref, v_ref) = refs[:count], refs[count : count + 2]
    outs, attn = refs[count + 2 : -1], refs[-1]
    seq, block = k_ref.shape
    scale = 1.0 / HEAD_DIM**0.5
    mask = allowed_mask(docs, seq)
    extra = 0
    for n, job in enumerate(jobs):
        if job is None:
            extra += 1
            q_ref, base = queries[extra], None
        else:
            q_ref, base = queries[0], meta[0, job] * block
        for h in range(block // HEAD_DIM):
            cols = slice(h * HEAD_DIM, (h + 1) * HEAD_DIM)
            if base is None:
                q = q_ref[:, cols]
            else:
                q = q_ref[:, pl.ds(pl.multiple_of(base + h * HEAD_DIM, HEAD_DIM), HEAD_DIM)]
            scores = lax.dot_general(
                q, k_ref[:, cols], (((1,), (1,)), ((), ())), preferred_element_type=jnp.float32
            )
            scores = jnp.where(mask, scores * scale, masked_fill)
            top = jnp.max(scores, axis=1, keepdims=True)
            weights = jnp.exp(scores - top)
            total = jnp.sum(weights, axis=1, keepdims=True)
            accum = jnp.dot(
                weights.astype(jnp.bfloat16), v_ref[:, cols], preferred_element_type=jnp.float32
            )
            out_cols = slice(n * block + h * HEAD_DIM, n * block + (h + 1) * HEAD_DIM)
            attn[:, out_cols] = (accum * (1.0 / total)).astype(jnp.bfloat16)
    send = send_matrix(counts, meta[0, 0], seq, cap, pairwise)
    rows = send.shape[0] // parts
    picked = jnp.dot(send, attn[...], preferred_element_type=jnp.float32)
    for part in range(parts):
        outs[part][...] = picked[part * rows : (part + 1) * rows].astype(jnp.bfloat16)


def attend(plan, jobs, meta, docs, counts, queries, k, v):
    seq, block = k.shape
    width = len(jobs) * block
    rows = plan.groups * plan.cap // plan.parts
    return pl.pallas_call(
        functools.partial(attend_kernel, jobs, plan.parts, plan.cap, plan.pairwise),
        out_shape=[jax.ShapeDtypeStruct((rows, width), jnp.bfloat16)] * plan.parts,
        in_specs=[SMEM] * 3 + [VMEM] * (len(queries) + 2),
        out_specs=[VMEM] * plan.parts,
        scratch_shapes=[pltpu.VMEM((seq, width), jnp.bfloat16)],
        compiler_params=pltpu.CompilerParams(vmem_limit_bytes=SCOPED),
        name="attend",
    )(meta, docs, counts, *queries, k, v)


def squares_of(ref):
    seq, width = ref.shape
    total = jnp.zeros((seq, HEAD_DIM), jnp.float32)
    for c in range(width // HEAD_DIM):
        wide = ref[:, c * HEAD_DIM : (c + 1) * HEAD_DIM].astype(jnp.float32)
        total = total + wide * wide
    return total


def place_kernel(parts, cap, pairwise, others, meta, counts, *refs):
    got, rest = refs[:parts], refs[parts:]
    seq = rest[-1].shape[0]
    blocks, outs = rest[:others], rest[others:]
    squares = None
    if others:
        outs, squares = outs[:-1], outs[-1]
    matrices = place_matrices(counts, meta[0, 0], seq, cap, pairwise, parts)
    block = outs[0].shape[1]
    for n, out in enumerate(outs):
        cols = slice(n * block, (n + 1) * block)
        placed = jnp.zeros((seq, block), jnp.float32)
        for part in range(parts):
            placed = placed + jnp.dot(
                matrices[part], got[part][:, cols], preferred_element_type=jnp.float32
            )
        out[...] = placed.astype(jnp.bfloat16)
    if others:
        total = squares_of(outs[0])
        for ref in blocks:
            total = total + squares_of(ref)
        squares[...] = total


def place(plan, count, seq, meta, counts, got, others=()):
    block = got[0].shape[1] // count
    shapes = [jax.ShapeDtypeStruct((seq, block), jnp.bfloat16)] * count
    if others:
        shapes.append(jax.ShapeDtypeStruct((seq, HEAD_DIM), jnp.float32))
    return pl.pallas_call(
        functools.partial(place_kernel, plan.parts, plan.cap, plan.pairwise, len(others)),
        out_shape=shapes,
        in_specs=[SMEM] * 2 + [VMEM] * (len(got) + len(others)),
        out_specs=[VMEM] * len(shapes),
        compiler_params=pltpu.CompilerParams(vmem_limit_bytes=SCOPED),
        name="place",
    )(meta, counts, *got, *others)


def norm_kernel(slots, sums, meta, *refs):
    blocks, refs = refs[: len(slots)], refs[len(slots) :]
    squares, (gain, out) = refs[:sums], refs[sums:]
    width = HEADS * HEAD_DIM
    lanes = squares[0][...]
    for ref in squares[1:]:
        lanes = lanes + ref[...]
    mean = jnp.sum(lanes, axis=1, keepdims=True) / width
    factor = jnp.broadcast_to(lax.rsqrt(mean + norm_eps), lanes.shape)
    for slot, ref in zip(slots, blocks, strict=True):
        block = ref.shape[1]
        for c in range(block // HEAD_DIM):
            cols = slice(c * HEAD_DIM, (c + 1) * HEAD_DIM)
            at = pl.ds(pl.multiple_of(meta[0, slot] * block + c * HEAD_DIM, HEAD_DIM), HEAD_DIM)
            wide = ref[:, cols].astype(jnp.float32)
            out[:, at] = (wide * factor * gain[:, at]).astype(jnp.bfloat16)


def norm(slots, meta, blocks, squares, gain):
    seq = blocks[0].shape[0]
    return pl.pallas_call(
        functools.partial(norm_kernel, slots, len(squares)),
        out_shape=jax.ShapeDtypeStruct((seq, gain.shape[1]), jnp.bfloat16),
        in_specs=[SMEM] + [VMEM] * (len(blocks) + len(squares) + 1),
        out_specs=VMEM,
        compiler_params=pltpu.CompilerParams(vmem_limit_bytes=SCOPED),
        name="norm",
    )(meta, *blocks, *squares, gain)


class Plan:
    def __init__(self, mesh, seq):
        self.pipe, self.groups, self.tensor = (mesh.shape[a] for a in ("pipe", "dp", "tensor"))
        self.cap = 5 * seq // (4 * self.groups)
        self.pairwise = self.groups == 4 and self.cap % 8 == 0
        self.parts = self.groups if self.pairwise else 1
        n = self.pipe
        order = [0] + list(range(1, n, 2)) + [i for i in reversed(range(2, n)) if i % 2 == 0]
        self.ring = [(order[i], order[(i + 1) % n]) for i in range(n)]
        where = {d: i for i, d in enumerate(order)}
        back = [[order[(where[p] - t) % n] for t in range(n)] for p in range(n)]
        self.meta = np.array(
            [[g] + back[p] for p in range(n) for g in range(self.groups)], np.int32
        )

    def regroup(self, parts):
        if not self.pairwise:
            return [lax.all_to_all(parts[0], "dp", split_axis=0, concat_axis=0, tiled=True)]
        got = [parts[0]]
        for step in range(1, self.groups):
            pairs = [(g, g ^ step) for g in range(self.groups)]
            got.append(lax.ppermute(parts[step], "dp", pairs))
        return got


def body(mesh, queries, cache_keys, cache_values, doc_lengths, row_counts, out_gain):
    query = queries[0]
    seq, local_width = query.shape
    plan = Plan(mesh, seq)
    n = plan.pipe
    block = local_width // n
    forward, backward = plan.ring, [(b, a) for a, b in plan.ring]
    own = lax.axis_index("pipe") * plan.groups + lax.axis_index("dp")
    meta = lax.dynamic_slice_in_dim(jnp.asarray(plan.meta), own, 1, 0)
    keys, values = cache_keys.reshape(seq, block), cache_values.reshape(seq, block)
    gain = out_gain.astype(jnp.float32).reshape(1, local_width)
    run = functools.partial(attend, plan)

    ahead = lax.dynamic_slice_in_dim(query, meta[0, n] * block, block, 1)
    lent = lax.ppermute(ahead, "pipe", forward)
    k, v = lax.ppermute(keys, "pipe", forward), lax.ppermute(values, "pipe", forward)
    sent = run((1, None), meta, doc_lengths, row_counts, (query, lent), keys, values)
    mine, borrowed = place(plan, 2, seq, meta, row_counts, plan.regroup(sent))
    returned = lax.ppermute(borrowed, "pipe", backward)
    blocks = [mine]
    for t in range(1, n - 1):
        if t < n - 2:
            k_next, v_next = lax.ppermute(k, "pipe", forward), lax.ppermute(v, "pipe", forward)
        sent = run((1 + t,), meta, doc_lengths, row_counts, (query,), k, v)
        got = plan.regroup(sent)
        if t < n - 2:
            blocks += place(plan, 1, seq, meta, row_counts, got)
            k, v = k_next, v_next
    last, squares = place(plan, 1, seq, meta, row_counts, got, (*blocks, returned))
    if plan.tensor == 2:
        sums = [squares, lax.ppermute(squares, "tensor", [(0, 1), (1, 0)])]
    else:
        sums = [lax.psum(squares, "tensor")]
    slots = tuple(range(1, n + 1))
    return norm(slots, meta, (*blocks, last, returned), sums, gain)[None]


def solution(mesh):
    return jax.shard_map(
        functools.partial(body, mesh),
        mesh=mesh,
        in_specs=(
            P("pipe", "dp", "tensor"),
            P("dp", "tensor", "pipe", None),
            P("dp", "tensor", "pipe", None),
            P("dp", None),
            P(),
            P("tensor"),
        ),
        out_specs=P("pipe", "dp", "tensor"),
        check_vma=False,
    )
```

time: 110 us -> 56.3 us (0.51)
  the two profiles are of different devices: /device:TPU:0 before, /device:TPU:25 now
where the time goes in v1:
time: 56.3 us; the launch traced here: 56.1 us
  starting transfers between devices  20.7 us (37%)
  Pallas kernels  15.8 us (28%)
  waiting for transfers between devices  15.3 us (27%)
  local copies, waits for them, and re-layouts  3.55 us (6%)
  between operations  0.76 us (1%)
    ppermute x1, starting transfers between devices, body(): sums = [squares, lax.ppermute(squares, 'tensor', [(0, 1), (1, 0)])]  11 us
    pallas_call x3, Pallas kernels, attend(): pl.pallas_call(functools.partial(attend_kernel, jobs, plan.parts, plan.ca...  10.4 us
    ppermute x9, starting transfers between devices, regroup(): got.append(lax.ppermute(parts[step], 'dp', pairs))  8.14 us
    ppermute x1, waiting for transfers between devices, body(): lent = lax.ppermute(ahead, 'pipe', forward)  6.54 us
    ppermute x9, waiting for transfers between devices, regroup(): got.append(lax.ppermute(parts[step], 'dp', pairs))  5.37 us
    pallas_call x3, Pallas kernels, place(): pl.pallas_call(functools.partial(place_kernel, plan.parts, plan.cap, plan...  3.36 us
    ppermute x1, waiting for transfers between devices, body(): lax.ppermute(values, 'pipe', forward)  2.51 us
    pallas_call x1, Pallas kernels, norm(): pl.pallas_call(functools.partial(norm_kernel, slots, len(squares)), out_s...  1.96 us
  transfers between devices with their start and end apart: 16, of which 8 were waited for; matrix products, arithmetic and copies ran while one was open for 0% of the time, Pallas kernels for 23%

profile of v1, /device:TPU:25, one launch (start us, length us, event | category | flops | bytes accessed | tf_op | source)
XLA Modules:
  0.0 56.1 jit_solution(8685842347416101839)
XLA Ops:
  0.0 0.7 %constant_dynamic-slice_fusion.meta = s32[1,5]{1,0:T(1,128)S(1)} fusion(s32[16,5]{1,0:T(8,128)} %constant.23.clone, s32[]{:T(128)S(6)} %select_n.6), kind=kLoop, calls=%fused_computation.1 | loop fusion | bytes 44 | tf_op jit(solution)/shard_map/dynamic_slice | solution.py:239
  0.7 0.6 %slice.3 = s32[1,1]{1,0:T(1,128)} slice(s32[1,5]{1,0:T(1,128)S(1)} %constant_dynamic-slice_fusion.meta), slice={[0:1], [4:5]} | slice | bytes 8 | tf_op jit(solution)/shard_map/slice | solution.py:244
  1.9 0.0 copy-start.2
  1.9 0.0 copy-start.3
  2.0 1.0 %dynamic-slice_bitcast_fusion = bf16[128,1024]{1,0:T(8,128)(2,1)S(1)} fusion(bf16[1,128,4096]{2,1,0:T(8,128)(2,1)} %param.7, s32[]{:T(128)S(6)} %select_n.7), kind=kLoop, calls=%fused_computation | loop fusion | bytes 524292 | tf_op jit(solution)/shard_map/dynamic_slice | solution.py:244
  3.0 0.2 collective-permute-start
  3.2 0.0 copy-done.2
  3.2 0.0 copy-start.4
  3.2 0.1 collective-permute-start.4
  3.3 0.0 copy-done.3
  3.3 0.0 copy-start.5
  3.3 1.3 %collective-permute-start.5 = (bf16[128,1024]{1,0:T(8,128)(2,1)S(1)}, bf16[128,1024]{1,0:T(8,128)(2,1)S(1)}, u32[]{:S(2)}, u32[]{:S(2)}) collective-permute-start(bf16[128,1024]{1,0:T(8,128)(2,1)S(1)} %bitcast.13), channel_id=1, source_target_pairs={{0,8},{8,24},{24,16},{16,0},{1,9},{9,25},{25,17},{17,1},{2,10},{10... | collective-permute-start | bytes 786440 | tf_op jit(solution)/shard_map/ppermute | solution.py:246
  4.6 6.5 %collective-permute-done.refs_1_ = bf16[128,1024]{1,0:T(8,128)(2,1)S(1)} collective-permute-done((bf16[128,1024]{1,0:T(8,128)(2,1)S(1)}, bf16[128,1024]{1,0:T(8,128)(2,1)S(1)}, u32[]{:S(2)}, u32[]{:S(2)}) %collective-permute-start) | collective-permute-done | bytes 262176 | tf_op jit(solution)/shard_map/ppermute | solution.py:245
  11.1 0.0 copy-done.4
  11.1 0.0 copy-done.5
  11.1 0.0 copy-start
  11.1 1.2 %copy-done = bf16[1,128,4096]{2,1,0:T(8,128)(2,1)S(1)} copy-done((bf16[1,128,4096]{2,1,0:T(8,128)(2,1)S(1)}, bf16[1,128,4096]{2,1,0:T(8,128)(2,1)}, u32[]{:S(2)}) %copy-start) | copy-done | bytes 1048600
  12.3 0.0 copy-start.1
  12.3 4.8 %attend.3 = (bf16[40,2048]{1,0:T(8,128)(2,1)S(1)}, bf16[40,2048]{1,0:T(8,128)(2,1)S(1)}, bf16[40,2048]{1,0:T(8,128)(2,1)S(1)}, bf16[40,2048]{1,0:T(8,128)(2,1)S(1)}) custom-call(s32[1,5]{1,0:T(1,128)S(1)} %constant_dynamic-slice_fusion.meta, s32[1,6]{1,0:T(1,128)S(1)} %copy-done.5, s32[4,4]{1,0:T(4,128)S(1)} %copy-done.4, bf16[128,4096]{1,0:T(8,128)(2,1)S(1)} %bitcast.8, ...), custom_call_target="tpu_custom_call" | custom-call | tf_op jit(solution)/shard_map/attend/pallas_call | solution.py:117
  17.1 1.3 %collective-permute-start.1 = (bf16[40,2048]{1,0:T(8,128)(2,1)S(1)}, bf16[40,2048]{1,0:T(8,128)(2,1)S(1)}, u32[]{:S(2)}, u32[]{:S(2)}) collective-permute-start(bf16[40,2048]{1,0:T(8,128)(2,1)S(1)} %get-tuple-element.22), channel_id=1, source_target_pairs={{0,2},{2,0},{4,6},{6,4},{1,3},{3,1},{5,7},{7,5},{8,10},{10,8},{12,... | collective-permute-start | bytes 491528 | tf_op jit(solution)/shard_map/ppermute | solution.py:227
  18.4 1.2 %collective-permute-start.2 = (bf16[40,2048]{1,0:T(8,128)(2,1)S(1)}, bf16[40,2048]{1,0:T(8,128)(2,1)S(1)}, u32[]{:S(2)}, u32[]{:S(2)}) collective-permute-start(bf16[40,2048]{1,0:T(8,128)(2,1)S(1)} %get-tuple-element.23), channel_id=1, source_target_pairs={{0,4},{2,6},{4,0},{6,2},{1,5},{3,7},{5,1},{7,3},{8,12},{10,14},{12... | collective-permute-start | bytes 491528 | tf_op jit(solution)/shard_map/ppermute | solution.py:227
  19.6 0.2 collective-permute-start.3
  19.8 0.0 collective-permute-done.4.refs_1_
  19.8 0.0 collective-permute-start.9
  19.8 2.5 %collective-permute-done.5.refs_2_ = bf16[128,1024]{1,0:T(8,128)(2,1)S(1)} collective-permute-done((bf16[128,1024]{1,0:T(8,128)(2,1)S(1)}, bf16[128,1024]{1,0:T(8,128)(2,1)S(1)}, u32[]{:S(2)}, u32[]{:S(2)}) %collective-permute-start.5) | collective-permute-done | bytes 262176 | tf_op jit(solution)/shard_map/ppermute | solution.py:246
  22.3 0.0 collective-permute-start.10
  22.4 0.0 collective-permute-done.1.refs_1_
  22.4 0.8 %collective-permute-done.2.refs_2_ = bf16[40,2048]{1,0:T(8,128)(2,1)S(1)} collective-permute-done((bf16[40,2048]{1,0:T(8,128)(2,1)S(1)}, bf16[40,2048]{1,0:T(8,128)(2,1)S(1)}, u32[]{:S(2)}, u32[]{:S(2)}) %collective-permute-start.2) | collective-permute-done | bytes 163872 | tf_op jit(solution)/shard_map/ppermute | solution.py:227
  23.1 2.6 %collective-permute-done.3.refs_3_ = bf16[40,2048]{1,0:T(8,128)(2,1)S(1)} collective-permute-done((bf16[40,2048]{1,0:T(8,128)(2,1)S(1)}, bf16[40,2048]{1,0:T(8,128)(2,1)S(1)}, u32[]{:S(2)}, u32[]{:S(2)}) %collective-permute-start.3) | collective-permute-done | bytes 163872 | tf_op jit(solution)/shard_map/ppermute | solution.py:227
  25.7 1.2 %place.3 = (bf16[128,1024]{1,0:T(8,128)(2,1)S(1)}, bf16[128,1024]{1,0:T(8,128)(2,1)S(1)}) custom-call(s32[1,5]{1,0:T(1,128)S(1)} %constant_dynamic-slice_fusion.meta, s32[4,4]{1,0:T(4,128)S(1)} %copy-done.4, bf16[40,2048]{1,0:T(8,128)(2,1)S(1)} %get-tuple-element.21.refs_0_, bf16[40,2048]{1,0:T(8,128)(2,1)S(1)} %collective-permute-done.1.refs_1_, ...), custom_call_target="tpu_custom_call" | custom-call | tf_op jit(solution)/shard_map/place/pallas_call | solution.py:166
  27.0 0.1 collective-permute-start.14
  27.1 0.0 copy-done.1
  27.1 2.8 %attend.4 = (bf16[40,1024]{1,0:T(8,128)(2,1)S(1)}, bf16[40,1024]{1,0:T(8,128)(2,1)S(1)}, bf16[40,1024]{1,0:T(8,128)(2,1)S(1)}, bf16[40,1024]{1,0:T(8,128)(2,1)S(1)}) custom-call(s32[1,5]{1,0:T(1,128)S(1)} %constant_dynamic-slice_fusion.meta, s32[1,6]{1,0:T(1,128)S(1)} %copy-done.5, s32[4,4]{1,0:T(4,128)S(1)} %copy-done.4, bf16[128,4096]{1,0:T(8,128)(2,1)S(1)} %bitcast.9, ...), custom_call_target="tpu_custom_call" | custom-call | tf_op jit(solution)/shard_map/attend/pallas_call | solution.py:117
  29.9 0.2 collective-permute-start.6
  30.2 1.2 %collective-permute-start.7 = (bf16[40,1024]{1,0:T(8,128)(2,1)S(1)}, bf16[40,1024]{1,0:T(8,128)(2,1)S(1)}, u32[]{:S(2)}, u32[]{:S(2)}) collective-permute-start(bf16[40,1024]{1,0:T(8,128)(2,1)S(1)} %get-tuple-element.28), channel_id=1, source_target_pairs={{0,4},{2,6},{4,0},{6,2},{1,5},{3,7},{5,1},{7,3},{8,12},{10,14},{12... | collective-permute-start | bytes 245768 | tf_op jit(solution)/shard_map/ppermute | solution.py:227
  31.4 0.0 collective-permute-done.9.refs_1_
  31.4 1.2 %collective-permute-start.8 = (bf16[40,1024]{1,0:T(8,128)(2,1)S(1)}, bf16[40,1024]{1,0:T(8,128)(2,1)S(1)}, u32[]{:S(2)}, u32[]{:S(2)}) collective-permute-start(bf16[40,1024]{1,0:T(8,128)(2,1)S(1)} %get-tuple-element.29), channel_id=1, source_target_pairs={{0,6},{2,4},{4,2},{6,0},{1,7},{3,5},{5,3},{7,1},{8,14},{10,12},{12... | collective-permute-start | bytes 245768 | tf_op jit(solution)/shard_map/ppermute | solution.py:227
  32.6 0.0 collective-permute-done.10.refs_2_
  32.6 2.8 %attend.5 = (bf16[40,1024]{1,0:T(8,128)(2,1)S(1)}, bf16[40,1024]{1,0:T(8,128)(2,1)S(1)}, bf16[40,1024]{1,0:T(8,128)(2,1)S(1)}, bf16[40,1024]{1,0:T(8,128)(2,1)S(1)}) custom-call(s32[1,5]{1,0:T(1,128)S(1)} %constant_dynamic-slice_fusion.meta, s32[1,6]{1,0:T(1,128)S(1)} %copy-done.5, s32[4,4]{1,0:T(4,128)S(1)} %copy-done.4, bf16[128,4096]{1,0:T(8,128)(2,1)S(1)} %bitcast.10, ...), custom_call_target="tpu_custom_call" | custom-call | tf_op jit(solution)/shard_map/attend/pallas_call | solution.py:117
  35.5 0.2 collective-permute-start.11
  35.7 0.0 collective-permute-done.6.refs_1_
  35.7 1.2 %collective-permute-start.12 = (bf16[40,1024]{1,0:T(8,128)(2,1)S(1)}, bf16[40,1024]{1,0:T(8,128)(2,1)S(1)}, u32[]{:S(2)}, u32[]{:S(2)}) collective-permute-start(bf16[40,1024]{1,0:T(8,128)(2,1)S(1)} %get-tuple-element.32), channel_id=1, source_target_pairs={{0,4},{2,6},{4,0},{6,2},{1,5},{3,7},{5,1},{7,3},{8,12},{10,14},{12... | collective-permute-start | bytes 245768 | tf_op jit(solution)/shard_map/ppermute | solution.py:227
  37.0 0.0 collective-permute-done.7.refs_2_
  37.0 1.2 %collective-permute-start.13 = (bf16[40,1024]{1,0:T(8,128)(2,1)S(1)}, bf16[40,1024]{1,0:T(8,128)(2,1)S(1)}, u32[]{:S(2)}, u32[]{:S(2)}) collective-permute-start(bf16[40,1024]{1,0:T(8,128)(2,1)S(1)} %get-tuple-element.33), channel_id=1, source_target_pairs={{0,6},{2,4},{4,2},{6,0},{1,7},{3,5},{5,3},{7,1},{8,14},{10,12},{12... | collective-permute-start | bytes 245768 | tf_op jit(solution)/shard_map/ppermute | solution.py:227
  38.2 0.0 collective-permute-done.8.refs_3_
  38.2 1.0 %place.4.refs_5_.refs_1_ = bf16[128,1024]{1,0:T(8,128)(2,1)S(1)} custom-call(s32[1,5]{1,0:T(1,128)S(1)} %constant_dynamic-slice_fusion.meta, s32[4,4]{1,0:T(4,128)S(1)} %copy-done.4, bf16[40,1024]{1,0:T(8,128)(2,1)S(1)} %get-tuple-element.26.refs_0_, bf16[40,1024]{1,0:T(8,128)(2,1)S(1)} %collective-permute-done.6.refs_1_, ...), custom_call_target="tpu_custom_call" | custom-call | tf_op jit(solution)/shard_map/place/pallas_call | solution.py:166
  39.2 0.5 collective-permute-done.11.refs_1_
  39.7 0.5 collective-permute-done.12.refs_2_
  40.2 1.0 %collective-permute-done.13.refs_3_ = bf16[40,1024]{1,0:T(8,128)(2,1)S(1)} collective-permute-done((bf16[40,1024]{1,0:T(8,128)(2,1)S(1)}, bf16[40,1024]{1,0:T(8,128)(2,1)S(1)}, u32[]{:S(2)}, u32[]{:S(2)}) %collective-permute-start.13) | collective-permute-done | bytes 81952 | tf_op jit(solution)/shard_map/ppermute | solution.py:227
  41.2 0.0 collective-permute-done.14.refs_6_.refs_3_
  41.2 0.0 copy-start.6
  41.2 1.1 %place.5 = (bf16[128,1024]{1,0:T(8,128)(2,1)S(1)}, f32[128,128]{1,0:T(8,128)S(1)}) custom-call(s32[1,5]{1,0:T(1,128)S(1)} %constant_dynamic-slice_fusion.meta, s32[4,4]{1,0:T(4,128)S(1)} %copy-done.4, bf16[40,1024]{1,0:T(8,128)(2,1)S(1)} %get-tuple-element.30.refs_0_, bf16[40,1024]{1,0:T(8,128)(2,1)S(1)} %collective-permute-done.11.refs_1_, ...), custom_call_target="tpu_custom_call" | custom-call | tf_op jit(solution)/shard_map/place/pallas_call | solution.py:166
  42.3 11.0 %collective-permute-start.15 = (f32[128,128]{1,0:T(8,128)S(1)}, f32[128,128]{1,0:T(8,128)S(1)}, u32[]{:S(2)}, u32[]{:S(2)}) collective-permute-start(f32[128,128]{1,0:T(8,128)S(1)} %get-tuple-element.36.refs_4_), channel_id=1, source_target_pairs={{0,1},{1,0},{2,3},{3,2},{4,5},{5,4},{6,7},{7,6},{8,9},{9,8},{10,11... | collective-permute-start | bytes 196616 | tf_op jit(solution)/shard_map/ppermute | solution.py:261
  53.3 0.0 copy-done.6
  53.3 0.9 %collective-permute-done.15.refs_5_ = f32[128,128]{1,0:T(8,128)S(1)} collective-permute-done((f32[128,128]{1,0:T(8,128)S(1)}, f32[128,128]{1,0:T(8,128)S(1)}, u32[]{:S(2)}, u32[]{:S(2)}) %collective-permute-start.15) | collective-permute-done | bytes 65568 | tf_op jit(solution)/shard_map/ppermute | solution.py:261
  54.2 2.0 %norm.1 = bf16[128,4096]{1,0:T(8,128)(2,1)} custom-call(s32[1,5]{1,0:T(1,128)S(1)} %constant_dynamic-slice_fusion.meta, bf16[128,1024]{1,0:T(8,128)(2,1)S(1)} %get-tuple-element.25.refs_4_.refs_0_, bf16[128,1024]{1,0:T(8,128)(2,1)S(1)} %place.4.refs_5_.refs_1_, bf16[128,1024]{1,0:T(8,128)(2,1)S(1)} %get-tuple-element.35.refs_2_, ...), custom_call_target="tpu_custom_call" | custom-call | tf_op jit(solution)/shard_map/norm/pallas_call | solution.py:196
  (1 shorter events, 0.0 us)
Async XLA Ops:
  1.9 1.3 %copy-start.2 = (bf16[128,1,1,1024]{3,0,2,1:T(8,128)(2,1)S(1)}, bf16[128,1,1,1024]{3,0,2,1:T(8,128)(2,1)}, u32[]{:S(2)}) copy-start(bf16[128,1,1,1024]{3,0,2,1:T(8,128)(2,1)} %param.8) | copy-start | bytes 786436
  1.9 1.4 %copy-start.3 = (bf16[128,1,1,1024]{3,0,2,1:T(8,128)(2,1)S(1)}, bf16[128,1,1,1024]{3,0,2,1:T(8,128)(2,1)}, u32[]{:S(2)}) copy-start(bf16[128,1,1,1024]{3,0,2,1:T(8,128)(2,1)} %param.9) | copy-start | bytes 786436
  3.0 8.1 %collective-permute-start = (bf16[128,1024]{1,0:T(8,128)(2,1)S(1)}, bf16[128,1024]{1,0:T(8,128)(2,1)S(1)}, u32[]{:S(2)}, u32[]{:S(2)}) collective-permute-start(bf16[128,1024]{1,0:T(8,128)(2,1)S(1)} %dynamic-slice_bitcast_fusion), channel_id=1, source_target_pairs={{0,8},{8,24},{24,16},{16,0},{1,9},{9,25},{25,17},{17,1},{2,10},{10... | collective-permute-start | bytes 786440 | tf_op jit(solution)/shard_map/ppermute | solution.py:245
  3.2 7.9 %copy-start.4 = (s32[4,4]{1,0:T(4,128)S(1)}, s32[4,4]{1,0:T(4,128)}, u32[]{:S(2)}) copy-start(s32[4,4]{1,0:T(4,128)} %counts.11) | copy-start | bytes 196
  3.2 16.6 %collective-permute-start.4 = (bf16[128,1024]{1,0:T(8,128)(2,1)S(1)}, bf16[128,1024]{1,0:T(8,128)(2,1)S(1)}, u32[]{:S(2)}, u32[]{:S(2)}) collective-permute-start(bf16[128,1024]{1,0:T(8,128)(2,1)S(1)} %bitcast.11), channel_id=1, source_target_pairs={{0,8},{8,24},{24,16},{16,0},{1,9},{9,25},{25,17},{17,1},{2,10},{10... | collective-permute-start | bytes 786440 | tf_op jit(solution)/shard_map/ppermute | solution.py:246
  3.3 7.8 %copy-start.5 = (s32[1,6]{1,0:T(1,128)S(1)}, s32[1,6]{1,0:T(1,128)}, u32[]{:S(2)}) copy-start(s32[1,6]{1,0:T(1,128)} %docs.5) | copy-start | bytes 76
  3.3 19.0 %collective-permute-start.5 = (bf16[128,1024]{1,0:T(8,128)(2,1)S(1)}, bf16[128,1024]{1,0:T(8,128)(2,1)S(1)}, u32[]{:S(2)}, u32[]{:S(2)}) collective-permute-start(bf16[128,1024]{1,0:T(8,128)(2,1)S(1)} %bitcast.13), channel_id=1, source_target_pairs={{0,8},{8,24},{24,16},{16,0},{1,9},{9,25},{25,17},{17,1},{2,10},{10... | collective-permute-start | bytes 786440 | tf_op jit(solution)/shard_map/ppermute | solution.py:246
  11.1 1.2 %copy-start = (bf16[1,128,4096]{2,1,0:T(8,128)(2,1)S(1)}, bf16[1,128,4096]{2,1,0:T(8,128)(2,1)}, u32[]{:S(2)}) copy-start(bf16[1,128,4096]{2,1,0:T(8,128)(2,1)} %param.7) | copy-start | bytes 3145732
  12.3 14.7 %copy-start.1 = (bf16[1,128,4096]{2,1,0:T(8,128)(2,1)S(1)}, bf16[1,128,4096]{2,1,0:T(8,128)(2,1)}, u32[]{:S(2)}) copy-start(bf16[1,128,4096]{2,1,0:T(8,128)(2,1)} %param.7) | copy-start | bytes 3145732
  17.1 5.2 %collective-permute-start.1 = (bf16[40,2048]{1,0:T(8,128)(2,1)S(1)}, bf16[40,2048]{1,0:T(8,128)(2,1)S(1)}, u32[]{:S(2)}, u32[]{:S(2)}) collective-permute-start(bf16[40,2048]{1,0:T(8,128)(2,1)S(1)} %get-tuple-element.22), channel_id=1, source_target_pairs={{0,2},{2,0},{4,6},{6,4},{1,3},{3,1},{5,7},{7,5},{8,10},{10,8},{12,... | collective-permute-start | bytes 491528 | tf_op jit(solution)/shard_map/ppermute | solution.py:227
  18.4 4.7 %collective-permute-start.2 = (bf16[40,2048]{1,0:T(8,128)(2,1)S(1)}, bf16[40,2048]{1,0:T(8,128)(2,1)S(1)}, u32[]{:S(2)}, u32[]{:S(2)}) collective-permute-start(bf16[40,2048]{1,0:T(8,128)(2,1)S(1)} %get-tuple-element.23), channel_id=1, source_target_pairs={{0,4},{2,6},{4,0},{6,2},{1,5},{3,7},{5,1},{7,3},{8,12},{10,14},{12... | collective-permute-start | bytes 491528 | tf_op jit(solution)/shard_map/ppermute | solution.py:227
  19.6 6.1 %collective-permute-start.3 = (bf16[40,2048]{1,0:T(8,128)(2,1)S(1)}, bf16[40,2048]{1,0:T(8,128)(2,1)S(1)}, u32[]{:S(2)}, u32[]{:S(2)}) collective-permute-start(bf16[40,2048]{1,0:T(8,128)(2,1)S(1)} %get-tuple-element.24), channel_id=1, source_target_pairs={{0,6},{2,4},{4,2},{6,0},{1,7},{3,5},{5,3},{7,1},{8,14},{10,12},{12... | collective-permute-start | bytes 491528 | tf_op jit(solution)/shard_map/ppermute | solution.py:227
  19.8 11.6 %collective-permute-start.9 = (bf16[128,1024]{1,0:T(8,128)(2,1)S(1)}, bf16[128,1024]{1,0:T(8,128)(2,1)S(1)}, u32[]{:S(2)}, u32[]{:S(2)}) collective-permute-start(bf16[128,1024]{1,0:T(8,128)(2,1)S(1)} %collective-permute-done.4.refs_1_), channel_id=1, source_target_pairs={{0,8},{8,24},{24,16},{16,0},{1,9},{9,25},{25,17},{17,1},{2,10},{10... | collective-permute-start | bytes 786440 | tf_op jit(solution)/shard_map/ppermute | solution.py:253
  22.3 10.3 %collective-permute-start.10 = (bf16[128,1024]{1,0:T(8,128)(2,1)S(1)}, bf16[128,1024]{1,0:T(8,128)(2,1)S(1)}, u32[]{:S(2)}, u32[]{:S(2)}) collective-permute-start(bf16[128,1024]{1,0:T(8,128)(2,1)S(1)} %collective-permute-done.5.refs_2_), channel_id=1, source_target_pairs={{0,8},{8,24},{24,16},{16,0},{1,9},{9,25},{25,17},{17,1},{2,10},{10... | collective-permute-start | bytes 786440 | tf_op jit(solution)/shard_map/ppermute | solution.py:253
  27.0 14.2 %collective-permute-start.14 = (bf16[128,1024]{1,0:T(8,128)(2,1)S(1)}, bf16[128,1024]{1,0:T(8,128)(2,1)S(1)}, u32[]{:S(2)}, u32[]{:S(2)}) collective-permute-start(bf16[128,1024]{1,0:T(8,128)(2,1)S(1)} %get-tuple-element.34), channel_id=1, source_target_pairs={{8,0},{24,8},{16,24},{0,16},{9,1},{25,9},{17,25},{1,17},{10,2},{26... | collective-permute-start | bytes 786440 | tf_op jit(solution)/shard_map/ppermute | solution.py:249
  29.9 5.8 %collective-permute-start.6 = (bf16[40,1024]{1,0:T(8,128)(2,1)S(1)}, bf16[40,1024]{1,0:T(8,128)(2,1)S(1)}, u32[]{:S(2)}, u32[]{:S(2)}) collective-permute-start(bf16[40,1024]{1,0:T(8,128)(2,1)S(1)} %get-tuple-element.27), channel_id=1, source_target_pairs={{0,2},{2,0},{4,6},{6,4},{1,3},{3,1},{5,7},{7,5},{8,10},{10,8},{12,... | collective-permute-start | bytes 245768 | tf_op jit(solution)/shard_map/ppermute | solution.py:227
  30.2 6.8 %collective-permute-start.7 = (bf16[40,1024]{1,0:T(8,128)(2,1)S(1)}, bf16[40,1024]{1,0:T(8,128)(2,1)S(1)}, u32[]{:S(2)}, u32[]{:S(2)}) collective-permute-start(bf16[40,1024]{1,0:T(8,128)(2,1)S(1)} %get-tuple-element.28), channel_id=1, source_target_pairs={{0,4},{2,6},{4,0},{6,2},{1,5},{3,7},{5,1},{7,3},{8,12},{10,14},{12... | collective-permute-start | bytes 245768 | tf_op jit(solution)/shard_map/ppermute | solution.py:227
  31.4 6.8 %collective-permute-start.8 = (bf16[40,1024]{1,0:T(8,128)(2,1)S(1)}, bf16[40,1024]{1,0:T(8,128)(2,1)S(1)}, u32[]{:S(2)}, u32[]{:S(2)}) collective-permute-start(bf16[40,1024]{1,0:T(8,128)(2,1)S(1)} %get-tuple-element.29), channel_id=1, source_target_pairs={{0,6},{2,4},{4,2},{6,0},{1,7},{3,5},{5,3},{7,1},{8,14},{10,12},{12... | collective-permute-start | bytes 245768 | tf_op jit(solution)/shard_map/ppermute | solution.py:227
  35.5 4.2 %collective-permute-start.11 = (bf16[40,1024]{1,0:T(8,128)(2,1)S(1)}, bf16[40,1024]{1,0:T(8,128)(2,1)S(1)}, u32[]{:S(2)}, u32[]{:S(2)}) collective-permute-start(bf16[40,1024]{1,0:T(8,128)(2,1)S(1)} %get-tuple-element.31), channel_id=1, source_target_pairs={{0,2},{2,0},{4,6},{6,4},{1,3},{3,1},{5,7},{7,5},{8,10},{10,8},{12,... | collective-permute-start | bytes 245768 | tf_op jit(solution)/shard_map/ppermute | solution.py:227
  35.7 4.5 %collective-permute-start.12 = (bf16[40,1024]{1,0:T(8,128)(2,1)S(1)}, bf16[40,1024]{1,0:T(8,128)(2,1)S(1)}, u32[]{:S(2)}, u32[]{:S(2)}) collective-permute-start(bf16[40,1024]{1,0:T(8,128)(2,1)S(1)} %get-tuple-element.32), channel_id=1, source_target_pairs={{0,4},{2,6},{4,0},{6,2},{1,5},{3,7},{5,1},{7,3},{8,12},{10,14},{12... | collective-permute-start | bytes 245768 | tf_op jit(solution)/shard_map/ppermute | solution.py:227
  37.0 4.2 %collective-permute-start.13 = (bf16[40,1024]{1,0:T(8,128)(2,1)S(1)}, bf16[40,1024]{1,0:T(8,128)(2,1)S(1)}, u32[]{:S(2)}, u32[]{:S(2)}) collective-permute-start(bf16[40,1024]{1,0:T(8,128)(2,1)S(1)} %get-tuple-element.33), channel_id=1, source_target_pairs={{0,6},{2,4},{4,2},{6,0},{1,7},{3,5},{5,3},{7,1},{8,14},{10,12},{12... | collective-permute-start | bytes 245768 | tf_op jit(solution)/shard_map/ppermute | solution.py:227
  41.2 12.1 %copy-start.6 = (bf16[4096]{0:T(1024)(128)(2,1)S(1)}, bf16[4096]{0:T(1024)(128)(2,1)}, u32[]{:S(2)}) copy-start(bf16[4096]{0:T(1024)(128)(2,1)} %param.12) | copy-start | bytes 24580
  42.3 11.9 %collective-permute-start.15 = (f32[128,128]{1,0:T(8,128)S(1)}, f32[128,128]{1,0:T(8,128)S(1)}, u32[]{:S(2)}, u32[]{:S(2)}) collective-permute-start(f32[128,128]{1,0:T(8,128)S(1)} %get-tuple-element.36.refs_4_), channel_id=1, source_target_pairs={{0,1},{1,0},{2,3},{3,2},{4,5},{5,4},{6,7},{7,6},{8,9},{9,8},{10,11... | collective-permute-start | bytes 196616 | tf_op jit(solution)/shard_map/ppermute | solution.py:261

commit v2 on v0

v2 whole, which is shorter than its diff:
```python
import functools

import jax
import jax.numpy as jnp
from jax import lax
from jax.experimental import pallas as pl
from jax.experimental.pallas import tpu as pltpu
from jax.sharding import PartitionSpec as P

HEADS = 64
HEAD_DIM = 128

masked_fill = -1e30
norm_eps = 1e-06
log2_e = 1.4426950408889634

VMEM = pl.BlockSpec(memory_space=pltpu.VMEM)
SMEM = pl.BlockSpec(memory_space=pltpu.SMEM)
ANY = pl.BlockSpec(memory_space=pl.ANY)
PARAMS = pltpu.CompilerParams(vmem_limit_bytes=32 * 1024 * 1024)


def iota(shape, dim):
    return lax.broadcasted_iota(jnp.int32, shape, dim)


def pick(index, table):
    value = jnp.int32(table[0])
    for i, entry in enumerate(table[1:], 1):
        value = jnp.where(index == i, jnp.int32(entry), value)
    return value


def one_hot(condition):
    return condition.astype(jnp.float32).astype(jnp.bfloat16)


class Plan:
    def __init__(self, mesh, seq, local_width):
        self.pipe, self.groups, self.tensor = (mesh.shape[a] for a in ("pipe", "dp", "tensor"))
        self.seq, self.block = seq, local_width // self.pipe
        self.cap = 5 * seq // (4 * self.groups)
        self.pairwise = self.groups == 4 and self.cap % 8 == 0
        self.parts = self.groups if self.pairwise else 1
        self.rows = self.groups * self.cap // self.parts
        n = self.pipe
        order = [0] + list(range(1, n, 2)) + [i for i in reversed(range(2, n)) if i % 2 == 0]
        self.ring = [(order[i], order[(i + 1) % n]) for i in range(n)]
        where = {d: i for i, d in enumerate(order)}
        self.behind = [[order[(where[p] - t) % n] for p in range(n)] for t in range(n)]

    def partner(self, own, step):
        return jnp.bitwise_xor(own, step) if self.pairwise else jnp.int32(step)

    def regroup(self, parts):
        if not self.pairwise:
            return [lax.all_to_all(parts[0], "dp", split_axis=0, concat_axis=0, tiled=True)]
        got = [parts[0]] + [None] * (self.groups - 1)
        for step in reversed(range(1, self.groups)):
            pairs = [(g, g ^ step) for g in range(self.groups)]
            got[step] = lax.ppermute(parts[step], "dp", pairs)
        return got


def split_kernel(plan, query, *refs):
    outs, sems = refs[:-1], refs[-1]
    place = lax.axis_index("pipe")
    copies = []
    for t, out in enumerate(outs):
        begin = pl.multiple_of(pick(place, plan.behind[t]) * plan.block, plan.block)
        copies.append(
            pltpu.make_async_copy(query.at[:, pl.ds(begin, plan.block)], out, sems.at[t])
        )
        copies[-1].start()
    for copy in copies:
        copy.wait()


def split(plan, query):
    shape = jax.ShapeDtypeStruct((plan.seq, plan.block), query.dtype)
    return pl.pallas_call(
        functools.partial(split_kernel, plan),
        out_shape=[shape] * (plan.pipe - 1),
        in_specs=[ANY],
        out_specs=[VMEM] * (plan.pipe - 1),
        scratch_shapes=[pltpu.SemaphoreType.DMA((plan.pipe - 1,))],
        compiler_params=PARAMS,
        name="split",
    )(query)


def tables_kernel(plan, docs, counts, bias, send, *places):
    seq, cap, groups = plan.seq, plan.cap, plan.groups
    own = lax.axis_index("dp")
    rows, cols = iota((seq, seq), 0), iota((seq, seq), 1)
    row_doc = jnp.zeros((seq, seq), jnp.int32)
    col_doc = jnp.zeros((seq, seq), jnp.int32)
    end = jnp.int32(0)
    for k in range(docs.shape[1]):
        end = end + docs[0, k]
        row_doc = row_doc + (rows >= end).astype(jnp.int32)
        col_doc = col_doc + (cols >= end).astype(jnp.int32)
    bias[...] = jnp.where((row_doc == col_doc) & (rows <= cols), 0.0, masked_fill)
    rows, cols = iota((groups * cap, seq), 0), iota((groups * cap, seq), 1)
    target = jnp.full((groups * cap, seq), -1, jnp.int32)
    for i in range(groups):
        to = plan.partner(own, i)
        begin = jnp.int32(0)
        for j in range(groups):
            begin = begin + jnp.where(j < to, counts[own, j], 0)
        inside = (rows >= i * cap) & (rows < i * cap + counts[own, to])
        target = jnp.where(inside, rows - i * cap + begin, target)
    send[...] = one_hot(cols == target)
    per = groups // plan.parts
    for part, out in enumerate(places):
        rows, cols = iota(out.shape, 0), iota(out.shape, 1)
        target = jnp.full(out.shape, -1, jnp.int32)
        for slot in range(per):
            source = plan.partner(own, part * per + slot)
            begin = jnp.int32(0)
            for j in range(groups):
                begin = begin + jnp.where(j < source, counts[j, own], 0)
            inside = (cols >= slot * cap) & (cols < slot * cap + counts[source, own])
            target = jnp.where(inside, cols - slot * cap + begin, target)
        out[...] = one_hot(rows == target)


def tables(plan, docs, counts):
    shapes = [
        jax.ShapeDtypeStruct((plan.seq, plan.seq), jnp.float32),
        jax.ShapeDtypeStruct((plan.groups * plan.cap, plan.seq), jnp.bfloat16),
    ] + [jax.ShapeDtypeStruct((plan.seq, plan.rows), jnp.bfloat16)] * plan.parts
    bias, send, *places = pl.pallas_call(
        functools.partial(tables_kernel, plan),
        out_shape=shapes,
        in_specs=[SMEM] * 2,
        out_specs=[VMEM] * len(shapes),
        compiler_params=PARAMS,
        name="tables",
    )(docs, counts)
    return bias, send, places


def attend_kernel(plan, jobs, *refs):
    queries, (k_ref, v_ref, bias, send) = refs[:jobs], refs[jobs : jobs + 4]
    outs, attn = refs[jobs + 4 : -1], refs[-1]
    block = plan.block
    heads = [slice(h * HEAD_DIM, (h + 1) * HEAD_DIM) for h in range(block // HEAD_DIM)]
    scale = log2_e / HEAD_DIM**0.5
    for n, q_ref in enumerate(queries):
        scores = [
            lax.dot_general(
                k_ref[:, cols],
                q_ref[:, cols],
                (((1,), (1,)), ((), ())),
                preferred_element_type=jnp.float32,
            )
            for cols in heads
        ]
        weights, totals = [], []
        for score in scores:
            score = score * scale + bias[...]
            weight = jnp.exp2(score - jnp.max(score, axis=0, keepdims=True))
            totals.append(jnp.sum(weight, axis=0, keepdims=True))
            weights.append(weight.astype(jnp.bfloat16))
        for cols, weight, total in zip(heads, weights, totals, strict=True):
            accum = lax.dot_general(
                v_ref[:, cols],
                weight,
                (((0,), (0,)), ((), ())),
                preferred_element_type=jnp.float32,
            )
            rows = slice(n * block + cols.start, n * block + cols.stop)
            attn[rows, :] = (accum * (1.0 / total)).astype(jnp.bfloat16)
    picked = lax.dot_general(
        send[...], attn[...], (((1,), (1,)), ((), ())), preferred_element_type=jnp.float32
    )
    for part, out in enumerate(outs):
        out[...] = picked[part * plan.rows : (part + 1) * plan.rows].astype(jnp.bfloat16)


def attend(plan, queries, k, v, bias, send):
    width = len(queries) * plan.block
    return pl.pallas_call(
        functools.partial(attend_kernel, plan, len(queries)),
        out_shape=[jax.ShapeDtypeStruct((plan.rows, width), jnp.bfloat16)] * plan.parts,
        in_specs=[VMEM] * (len(queries) + 4),
        out_specs=[VMEM] * plan.parts,
        scratch_shapes=[pltpu.VMEM((width, plan.seq), jnp.bfloat16)],
        compiler_params=PARAMS,
        name="attend",
    )(*queries, k, v, bias, send)


def squares_of(ref):
    total = None
    for c in range(0, ref.shape[1], HEAD_DIM):
        wide = ref[:, c : c + HEAD_DIM].astype(jnp.float32)
        total = wide * wide if total is None else total + wide * wide
    return total


def place_kernel(plan, extra, sums, *refs):
    parts = plan.parts
    got, matrices, refs = refs[:parts], refs[parts : 2 * parts], refs[2 * parts :]
    blocks, earlier = refs[:extra], refs[extra : extra + sums]
    outs, squares = refs[extra + sums : -1], refs[-1]
    total = None
    for ref in blocks:
        more = squares_of(ref)
        total = more if total is None else total + more
    for ref in earlier:
        total = ref[...] if total is None else total + ref[...]
    for n, out in enumerate(outs):
        cols = slice(n * plan.block, (n + 1) * plan.block)
        placed = None
        for matrix, ref in zip(matrices, got, strict=True):
            more = jnp.dot(matrix[...], ref[:, cols], preferred_element_type=jnp.float32)
            placed = more if placed is None else placed + more
        out[...] = placed.astype(jnp.bfloat16)
        if n == 0:
            for c in range(0, plan.block, HEAD_DIM):
                wide = placed[:, c : c + HEAD_DIM]
                total = wide * wide if total is None else total + wide * wide
    squares[...] = total


def place(plan, got, matrices, blocks=(), sums=()):
    count = got[0].shape[1] // plan.block
    shapes = [jax.ShapeDtypeStruct((plan.seq, plan.block), jnp.bfloat16)] * count
    shapes.append(jax.ShapeDtypeStruct((plan.seq, HEAD_DIM), jnp.float32))
    args = (*got, *matrices, *blocks, *sums)
    return pl.pallas_call(
        functools.partial(place_kernel, plan, len(blocks), len(sums)),
        out_shape=shapes,
        in_specs=[VMEM] * len(args),
        out_specs=[VMEM] * len(shapes),
        compiler_params=PARAMS,
        name="place",
    )(*args)


def norm_kernel(plan, sums, *refs):
    blocks, refs = refs[: plan.pipe], refs[plan.pipe :]
    squares, (gain, out, held, sems) = refs[:sums], refs[sums:]
    width = HEADS * HEAD_DIM
    lanes = squares[0][...]
    for ref in squares[1:]:
        lanes = lanes + ref[...]
    mean = jnp.sum(lanes, axis=1, keepdims=True) / width
    factor = jnp.broadcast_to(lax.rsqrt(mean + norm_eps), lanes.shape)
    device = lax.axis_index("pipe")
    copies = []
    for t, ref in enumerate(blocks):
        begin = pl.multiple_of(pick(device, plan.behind[t]) * plan.block, plan.block)
        for c in range(0, plan.block, HEAD_DIM):
            cols = slice(c, c + HEAD_DIM)
            at = pl.ds(pl.multiple_of(begin + c, HEAD_DIM), HEAD_DIM)
            wide = ref[:, cols].astype(jnp.float32)
            held[t, :, cols] = (wide * factor * gain[:, at]).astype(jnp.bfloat16)
        copies.append(
            pltpu.make_async_copy(held.at[t], out.at[:, pl.ds(begin, plan.block)], sems.at[t])
        )
        copies[-1].start()
    for copy in copies:
        copy.wait()


def norm(plan, blocks, squares, gain):
    n = plan.pipe
    return pl.pallas_call(
        functools.partial(norm_kernel, plan, len(squares)),
        out_shape=jax.ShapeDtypeStruct((plan.seq, n * plan.block), jnp.bfloat16),
        in_specs=[VMEM] * (n + len(squares) + 1),
        out_specs=ANY,
        scratch_shapes=[
            pltpu.VMEM((n, plan.seq, plan.block), jnp.bfloat16),
            pltpu.SemaphoreType.DMA((n,)),
        ],
        compiler_params=PARAMS,
        name="norm",
    )(*blocks, *squares, gain)


def body(mesh, queries, cache_keys, cache_values, doc_lengths, row_counts, out_gain):
    query = queries[0]
    seq, local_width = query.shape
    plan = Plan(mesh, seq, local_width)
    n = plan.pipe
    forward, backward = plan.ring, [(b, a) for a, b in plan.ring]
    keys = cache_keys.reshape(seq, plan.block)
    values = cache_values.reshape(seq, plan.block)
    gain = out_gain.astype(jnp.float32).reshape(1, local_width)

    asked = split(plan, query)
    begin = pick(lax.axis_index("pipe"), plan.behind[n - 1]) * plan.block
    ahead = lax.dynamic_slice_in_dim(query, begin, plan.block, 1)
    bias, send, places = tables(plan, doc_lengths, row_counts)
    lent = lax.ppermute(ahead, "pipe", forward)
    k, v = lax.ppermute(keys, "pipe", forward), lax.ppermute(values, "pipe", forward)
    sent = attend(plan, (asked[0], lent), keys, values, bias, send)
    mine, borrowed, squares = place(plan, plan.regroup(sent), places)
    returned = lax.ppermute(borrowed, "pipe", backward)
    blocks = [mine]
    for t in range(1, n - 1):
        last = t == n - 2
        if not last:
            k_next, v_next = lax.ppermute(k, "pipe", forward), lax.ppermute(v, "pipe", forward)
        got = plan.regroup(attend(plan, (asked[t],), k, v, bias, send))
        placed, squares = place(plan, got, places, (returned,) if last else (), (squares,))
        blocks.append(placed)
        if not last:
            k, v = k_next, v_next
    if plan.tensor == 2:
        sums = [squares, lax.ppermute(squares, "tensor", [(0, 1), (1, 0)])]
    else:
        sums = [lax.psum(squares, "tensor")]
    return norm(plan, (*blocks, returned), sums, gain)[None]


def solution(mesh):
    return jax.shard_map(
        functools.partial(body, mesh),
        mesh=mesh,
        in_specs=(
            P("pipe", "dp", "tensor"),
            P("dp", "tensor", "pipe", None),
            P("dp", "tensor", "pipe", None),
            P("dp", None),
            P(),
            P("tensor"),
        ),
        out_specs=P("pipe", "dp", "tensor"),
        check_vma=False,
    )
```

time: 110 us -> 50.8 us (0.46)
  the two profiles are of different devices: /device:TPU:0 before, /device:TPU:25 now
where the time goes in v2:
time: 50.8 us; the launch traced here: 50.6 us
  starting transfers between devices  21.2 us (42%)
  waiting for transfers between devices  20.4 us (40%)
  Pallas kernels  6.05 us (12%)
  local copies, waits for them, and re-layouts  2.85 us (6%)
    ppermute x9, starting transfers between devices, regroup(): got[step] = lax.ppermute(parts[step], 'dp', pairs)  9.39 us
    ppermute x1, starting transfers between devices, body(): sums = [squares, lax.ppermute(squares, 'tensor', [(0, 1), (1, 0)])]  7.77 us
    ppermute x1, waiting for transfers between devices, body(): lax.ppermute(keys, 'pipe', forward)  5.61 us
    ppermute x1, waiting for transfers between devices, body(): lax.ppermute(k, 'pipe', forward)  4.61 us
    ppermute x1, waiting for transfers between devices, body(): lent = lax.ppermute(ahead, 'pipe', forward)  3.95 us
    ppermute x9, waiting for transfers between devices, regroup(): got[step] = lax.ppermute(parts[step], 'dp', pairs)  3.59 us
    pallas_call x3, Pallas kernels, attend(): pl.pallas_call(functools.partial(attend_kernel, plan, len(queries)), out_...  2.59 us
    ppermute x1, starting transfers between devices, body(): returned = lax.ppermute(borrowed, 'pipe', backward)  2.41 us
  transfers between devices with their start and end apart: 16, of which 8 were waited for; matrix products, arithmetic and copies ran while one was open for 0% of the time, Pallas kernels for 9%

profile of v2, /device:TPU:25, one launch (start us, length us, event | category | flops | bytes accessed | tf_op | source)
XLA Modules:
  0.0 50.6 jit_solution(5970926455020681220)
XLA Ops:
  0.0 0.0 copy-start.1
  0.0 0.0 copy-start.2
  0.0 1.0 %dynamic-slice_bitcast_fusion = bf16[128,1024]{1,0:T(8,128)(2,1)S(1)} fusion(bf16[1,128,4096]{2,1,0:T(8,128)(2,1)} %param.6, s32[]{:T(128)S(6)} %select_n.16), kind=kLoop, calls=%fused_computation | loop fusion | bytes 524292 | tf_op jit(solution)/shard_map/dynamic_slice | solution.py:297
  1.0 0.2 collective-permute-start
  1.3 0.0 copy-done.1
  1.3 0.1 collective-permute-start.5
  1.3 0.0 copy-done.2
  1.3 1.3 %collective-permute-start.4 = (bf16[128,1024]{1,0:T(8,128)(2,1)S(1)}, bf16[128,1024]{1,0:T(8,128)(2,1)S(1)}, u32[]{:S(2)}, u32[]{:S(2)}) collective-permute-start(bf16[128,1024]{1,0:T(8,128)(2,1)S(1)} %bitcast.10), channel_id=1, source_target_pairs={{0,8},{8,24},{24,16},{16,0},{1,9},{9,25},{25,17},{17,1},{2,10},{10... | collective-permute-start | bytes 786440 | tf_op jit(solution)/shard_map/ppermute | solution.py:300
  2.6 0.0 copy-start
  2.6 1.2 %copy-done = bf16[1,128,4096]{2,1,0:T(8,128)(2,1)S(1)} copy-done((bf16[1,128,4096]{2,1,0:T(8,128)(2,1)S(1)}, bf16[1,128,4096]{2,1,0:T(8,128)(2,1)}, u32[]{:S(2)}) %copy-start) | copy-done | bytes 1048600
  3.8 0.0 copy-start.3
  3.8 0.0 copy-start.4
  3.8 0.1 split.1
  3.9 0.6 %copy-done.3 = s32[4,4]{1,0:T(4,128)S(1)} copy-done((s32[4,4]{1,0:T(4,128)S(1)}, s32[4,4]{1,0:T(4,128)}, u32[]{:S(2)}) %copy-start.3) | copy-done | bytes 88
  4.5 0.0 copy-done.4
  4.5 0.7 %tables.1 = (f32[128,128]{1,0:T(8,128)S(1)}, bf16[160,128]{1,0:T(8,128)(2,1)S(1)}, bf16[128,40]{1,0:T(8,128)(2,1)S(1)}, bf16[128,40]{1,0:T(8,128)(2,1)S(1)}, bf1...) custom-call(s32[1,6]{1,0:T(1,128)S(1)} %copy-done.4, s32[4,4]{1,0:T(4,128)S(1)} %copy-done.3), custom_call_target="tpu_custom_call" | custom-call | tf_op jit(solution)/shard_map/tables/pallas_call | solution.py:133
  5.2 3.9 %collective-permute-done.refs_1_ = bf16[128,1024]{1,0:T(8,128)(2,1)S(1)} collective-permute-done((bf16[128,1024]{1,0:T(8,128)(2,1)S(1)}, bf16[128,1024]{1,0:T(8,128)(2,1)S(1)}, u32[]{:S(2)}, u32[]{:S(2)}) %collective-permute-start) | collective-permute-done | bytes 262176 | tf_op jit(solution)/shard_map/ppermute | solution.py:299
  9.2 1.1 %attend.3 = (bf16[40,2048]{1,0:T(8,128)(2,1)S(1)}, bf16[40,2048]{1,0:T(8,128)(2,1)S(1)}, bf16[40,2048]{1,0:T(8,128)(2,1)S(1)}, bf16[40,2048]{1,0:T(8,128)(2,1)S(1)}) custom-call(bf16[128,1024]{1,0:T(8,128)(2,1)S(1)} %get-tuple-element.33.refs_0_, bf16[128,1024]{1,0:T(8,128)(2,1)S(1)} %collective-permute-done.refs_1_, bf16[128,1024]{1,0:T(8,128)(2,1)S(1)} %bitcast.11, ...), custom_call_target="tpu_custom_call" | custom-call | tf_op jit(solution)/shard_map/attend/pallas_call | solution.py:184
  10.3 1.3 %collective-permute-start.1 = (bf16[40,2048]{1,0:T(8,128)(2,1)S(1)}, bf16[40,2048]{1,0:T(8,128)(2,1)S(1)}, u32[]{:S(2)}, u32[]{:S(2)}) collective-permute-start(bf16[40,2048]{1,0:T(8,128)(2,1)S(1)} %get-tuple-element.37), channel_id=1, source_target_pairs={{0,2},{2,0},{4,6},{6,4},{1,3},{3,1},{5,7},{7,5},{8,10},{10,8},{12,... | collective-permute-start | bytes 491528 | tf_op jit(solution)/shard_map/ppermute | solution.py:61
  11.6 1.2 %collective-permute-start.2 = (bf16[40,2048]{1,0:T(8,128)(2,1)S(1)}, bf16[40,2048]{1,0:T(8,128)(2,1)S(1)}, u32[]{:S(2)}, u32[]{:S(2)}) collective-permute-start(bf16[40,2048]{1,0:T(8,128)(2,1)S(1)} %get-tuple-element.38), channel_id=1, source_target_pairs={{0,4},{2,6},{4,0},{6,2},{1,5},{3,7},{5,1},{7,3},{8,12},{10,14},{12... | collective-permute-start | bytes 491528 | tf_op jit(solution)/shard_map/ppermute | solution.py:61
  12.8 0.2 collective-permute-start.3
  13.0 1.8 %collective-permute-done.5.refs_2_ = bf16[128,1024]{1,0:T(8,128)(2,1)S(1)} collective-permute-done((bf16[128,1024]{1,0:T(8,128)(2,1)S(1)}, bf16[128,1024]{1,0:T(8,128)(2,1)S(1)}, u32[]{:S(2)}, u32[]{:S(2)}) %collective-permute-start.5) | collective-permute-done | bytes 262176 | tf_op jit(solution)/shard_map/ppermute | solution.py:300
  14.8 0.0 collective-permute-start.10
  14.8 5.6 %collective-permute-done.4.refs_1_ = bf16[128,1024]{1,0:T(8,128)(2,1)S(1)} collective-permute-done((bf16[128,1024]{1,0:T(8,128)(2,1)S(1)}, bf16[128,1024]{1,0:T(8,128)(2,1)S(1)}, u32[]{:S(2)}, u32[]{:S(2)}) %collective-permute-start.4) | collective-permute-done | bytes 262176 | tf_op jit(solution)/shard_map/ppermute | solution.py:300
  20.4 0.0 collective-permute-start.9
  20.4 0.0 collective-permute-done.1.refs_1_
  20.4 0.0 collective-permute-done.2.refs_2_
  20.4 0.0 collective-permute-done.3.refs_3_
  20.4 0.7 %place.3 = (bf16[128,1024]{1,0:T(8,128)(2,1)S(1)}, bf16[128,1024]{1,0:T(8,128)(2,1)S(1)}, f32[128,128]{1,0:T(8,128)S(1)}) custom-call(bf16[40,2048]{1,0:T(8,128)(2,1)S(1)} %get-tuple-element.36.refs_0_, bf16[40,2048]{1,0:T(8,128)(2,1)S(1)} %collective-permute-done.1.refs_1_, bf16[40,2048]{1,0:T(8,128)(2,1)S(1)} %collective-permute-done.2.refs_2_, ...), custom_call_target="tpu_custom_call" | custom-call | tf_op jit(solution)/shard_map/place/pallas_call | solution.py:233
  21.1 2.4 %collective-permute-start.14 = (bf16[128,1024]{1,0:T(8,128)(2,1)S(1)}, bf16[128,1024]{1,0:T(8,128)(2,1)S(1)}, u32[]{:S(2)}, u32[]{:S(2)}) collective-permute-start(bf16[128,1024]{1,0:T(8,128)(2,1)S(1)} %get-tuple-element.57), channel_id=1, source_target_pairs={{8,0},{24,8},{16,24},{0,16},{9,1},{25,9},{17,25},{1,17},{10,2},{26... | collective-permute-start | bytes 786440 | tf_op jit(solution)/shard_map/ppermute | solution.py:303
  23.5 0.7 %attend.4 = (bf16[40,1024]{1,0:T(8,128)(2,1)S(1)}, bf16[40,1024]{1,0:T(8,128)(2,1)S(1)}, bf16[40,1024]{1,0:T(8,128)(2,1)S(1)}, bf16[40,1024]{1,0:T(8,128)(2,1)S(1)}) custom-call(bf16[128,1024]{1,0:T(8,128)(2,1)S(1)} %get-tuple-element.45.refs_0_, bf16[128,1024]{1,0:T(8,128)(2,1)S(1)} %collective-permute-done.4.refs_1_, ...), custom_call_target="tpu_custom_call" | custom-call | tf_op jit(solution)/shard_map/attend/pallas_call | solution.py:184
  24.3 1.3 %collective-permute-start.6 = (bf16[40,1024]{1,0:T(8,128)(2,1)S(1)}, bf16[40,1024]{1,0:T(8,128)(2,1)S(1)}, u32[]{:S(2)}, u32[]{:S(2)}) collective-permute-start(bf16[40,1024]{1,0:T(8,128)(2,1)S(1)} %get-tuple-element.47), channel_id=1, source_target_pairs={{0,2},{2,0},{4,6},{6,4},{1,3},{3,1},{5,7},{7,5},{8,10},{10,8},{12,... | collective-permute-start | bytes 245768 | tf_op jit(solution)/shard_map/ppermute | solution.py:61
  25.5 1.2 %collective-permute-start.7 = (bf16[40,1024]{1,0:T(8,128)(2,1)S(1)}, bf16[40,1024]{1,0:T(8,128)(2,1)S(1)}, u32[]{:S(2)}, u32[]{:S(2)}) collective-permute-start(bf16[40,1024]{1,0:T(8,128)(2,1)S(1)} %get-tuple-element.48), channel_id=1, source_target_pairs={{0,4},{2,6},{4,0},{6,2},{1,5},{3,7},{5,1},{7,3},{8,12},{10,14},{12... | collective-permute-start | bytes 245768 | tf_op jit(solution)/shard_map/ppermute | solution.py:61
  26.8 0.0 collective-permute-done.10.refs_2_
  26.8 1.5 %collective-permute-start.8 = (bf16[40,1024]{1,0:T(8,128)(2,1)S(1)}, bf16[40,1024]{1,0:T(8,128)(2,1)S(1)}, u32[]{:S(2)}, u32[]{:S(2)}) collective-permute-start(bf16[40,1024]{1,0:T(8,128)(2,1)S(1)} %get-tuple-element.49), channel_id=1, source_target_pairs={{0,6},{2,4},{4,2},{6,0},{1,7},{3,5},{5,3},{7,1},{8,14},{10,12},{12... | collective-permute-start | bytes 245768 | tf_op jit(solution)/shard_map/ppermute | solution.py:61
  28.2 4.6 %collective-permute-done.9.refs_1_ = bf16[128,1024]{1,0:T(8,128)(2,1)S(1)} collective-permute-done((bf16[128,1024]{1,0:T(8,128)(2,1)S(1)}, bf16[128,1024]{1,0:T(8,128)(2,1)S(1)}, u32[]{:S(2)}, u32[]{:S(2)}) %collective-permute-start.9) | collective-permute-done | bytes 262176 | tf_op jit(solution)/shard_map/ppermute | solution.py:308
  32.8 0.7 %attend.5 = (bf16[40,1024]{1,0:T(8,128)(2,1)S(1)}, bf16[40,1024]{1,0:T(8,128)(2,1)S(1)}, bf16[40,1024]{1,0:T(8,128)(2,1)S(1)}, bf16[40,1024]{1,0:T(8,128)(2,1)S(1)}) custom-call(bf16[128,1024]{1,0:T(8,128)(2,1)S(1)} %get-tuple-element.52.refs_0_, bf16[128,1024]{1,0:T(8,128)(2,1)S(1)} %collective-permute-done.9.refs_1_, ...), custom_call_target="tpu_custom_call" | custom-call | tf_op jit(solution)/shard_map/attend/pallas_call | solution.py:184
  33.6 1.3 %collective-permute-start.11 = (bf16[40,1024]{1,0:T(8,128)(2,1)S(1)}, bf16[40,1024]{1,0:T(8,128)(2,1)S(1)}, u32[]{:S(2)}, u32[]{:S(2)}) collective-permute-start(bf16[40,1024]{1,0:T(8,128)(2,1)S(1)} %get-tuple-element.54), channel_id=1, source_target_pairs={{0,2},{2,0},{4,6},{6,4},{1,3},{3,1},{5,7},{7,5},{8,10},{10,8},{12,... | collective-permute-start | bytes 245768 | tf_op jit(solution)/shard_map/ppermute | solution.py:61
  34.8 0.0 collective-permute-done.6.refs_1_
  34.8 1.2 %collective-permute-start.12 = (bf16[40,1024]{1,0:T(8,128)(2,1)S(1)}, bf16[40,1024]{1,0:T(8,128)(2,1)S(1)}, u32[]{:S(2)}, u32[]{:S(2)}) collective-permute-start(bf16[40,1024]{1,0:T(8,128)(2,1)S(1)} %get-tuple-element.55), channel_id=1, source_target_pairs={{0,4},{2,6},{4,0},{6,2},{1,5},{3,7},{5,1},{7,3},{8,12},{10,14},{12... | collective-permute-start | bytes 245768 | tf_op jit(solution)/shard_map/ppermute | solution.py:61
  36.1 0.0 collective-permute-done.7.refs_2_
  36.1 0.2 collective-permute-start.13
  36.3 0.0 collective-permute-done.8.refs_3_
  36.3 0.4 place.4
  36.7 0.5 %collective-permute-done.11.refs_1_ = bf16[40,1024]{1,0:T(8,128)(2,1)S(1)} collective-permute-done((bf16[40,1024]{1,0:T(8,128)(2,1)S(1)}, bf16[40,1024]{1,0:T(8,128)(2,1)S(1)}, u32[]{:S(2)}, u32[]{:S(2)}) %collective-permute-start.11) | collective-permute-done | bytes 81952 | tf_op jit(solution)/shard_map/ppermute | solution.py:61
  37.2 1.2 %collective-permute-done.12.refs_2_ = bf16[40,1024]{1,0:T(8,128)(2,1)S(1)} collective-permute-done((bf16[40,1024]{1,0:T(8,128)(2,1)S(1)}, bf16[40,1024]{1,0:T(8,128)(2,1)S(1)}, u32[]{:S(2)}, u32[]{:S(2)}) %collective-permute-start.12) | collective-permute-done | bytes 81952 | tf_op jit(solution)/shard_map/ppermute | solution.py:61
  38.4 1.8 %collective-permute-done.13.refs_3_ = bf16[40,1024]{1,0:T(8,128)(2,1)S(1)} collective-permute-done((bf16[40,1024]{1,0:T(8,128)(2,1)S(1)}, bf16[40,1024]{1,0:T(8,128)(2,1)S(1)}, u32[]{:S(2)}, u32[]{:S(2)}) %collective-permute-start.13) | collective-permute-done | bytes 81952 | tf_op jit(solution)/shard_map/ppermute | solution.py:61
  40.3 0.0 collective-permute-done.14.refs_8_.refs_3_
  40.3 0.0 copy-start.5
  40.3 0.4 place.5
  40.7 7.8 %collective-permute-start.15 = (f32[128,128]{1,0:T(8,128)S(1)}, f32[128,128]{1,0:T(8,128)S(1)}, u32[]{:S(2)}, u32[]{:S(2)}) collective-permute-start(f32[128,128]{1,0:T(8,128)S(1)} %get-tuple-element.60.refs_4_), channel_id=1, source_target_pairs={{0,1},{1,0},{2,3},{3,2},{4,5},{5,4},{6,7},{7,6},{8,9},{9,8},{10,11... | collective-permute-start | bytes 196616 | tf_op jit(solution)/shard_map/ppermute | solution.py:315
  48.5 0.0 copy-done.5
  48.5 0.9 %collective-permute-done.15.refs_5_ = f32[128,128]{1,0:T(8,128)S(1)} collective-permute-done((f32[128,128]{1,0:T(8,128)S(1)}, f32[128,128]{1,0:T(8,128)S(1)}, u32[]{:S(2)}, u32[]{:S(2)}) %collective-permute-start.15) | collective-permute-done | bytes 65568 | tf_op jit(solution)/shard_map/ppermute | solution.py:315
  49.4 1.2 %norm.1 = bf16[128,4096]{1,0:T(8,128)(2,1)} custom-call(bf16[128,1024]{1,0:T(8,128)(2,1)S(1)} %get-tuple-element.44.refs_0_, bf16[128,1024]{1,0:T(8,128)(2,1)S(1)} %get-tuple-element.51.refs_1_, bf16[128,1024]{1,0:T(8,128)(2,1)S(1)} %get-tuple-element.59.refs_2_, bf16[128,1024]{1,0:T(8,128)(2,1)S(1)} %collective-permute-done.14.refs_8_.refs_3_, ...), custom_call_target="tpu_custom_call" | custom-call | tf_op jit(solution)/shard_map/norm/pallas_call | solution.py:271
  (1 shorter events, 0.0 us)
Async XLA Ops:
  0.0 1.3 %copy-start.1 = (bf16[128,1,1,1024]{3,0,2,1:T(8,128)(2,1)S(1)}, bf16[128,1,1,1024]{3,0,2,1:T(8,128)(2,1)}, u32[]{:S(2)}) copy-start(bf16[128,1,1,1024]{3,0,2,1:T(8,128)(2,1)} %param.8) | copy-start | bytes 786436
  0.0 1.3 %copy-start.2 = (bf16[128,1,1,1024]{3,0,2,1:T(8,128)(2,1)S(1)}, bf16[128,1,1,1024]{3,0,2,1:T(8,128)(2,1)}, u32[]{:S(2)}) copy-start(bf16[128,1,1,1024]{3,0,2,1:T(8,128)(2,1)} %param.7) | copy-start | bytes 786436
  1.0 8.1 %collective-permute-start = (bf16[128,1024]{1,0:T(8,128)(2,1)S(1)}, bf16[128,1024]{1,0:T(8,128)(2,1)S(1)}, u32[]{:S(2)}, u32[]{:S(2)}) collective-permute-start(bf16[128,1024]{1,0:T(8,128)(2,1)S(1)} %dynamic-slice_bitcast_fusion), channel_id=1, source_target_pairs={{0,8},{8,24},{24,16},{16,0},{1,9},{9,25},{25,17},{17,1},{2,10},{10... | collective-permute-start | bytes 786440 | tf_op jit(solution)/shard_map/ppermute | solution.py:299
  1.3 13.5 %collective-permute-start.5 = (bf16[128,1024]{1,0:T(8,128)(2,1)S(1)}, bf16[128,1024]{1,0:T(8,128)(2,1)S(1)}, u32[]{:S(2)}, u32[]{:S(2)}) collective-permute-start(bf16[128,1024]{1,0:T(8,128)(2,1)S(1)} %bitcast.8), channel_id=1, source_target_pairs={{0,8},{8,24},{24,16},{16,0},{1,9},{9,25},{25,17},{17,1},{2,10},{10... | collective-permute-start | bytes 786440 | tf_op jit(solution)/shard_map/ppermute | solution.py:300
  1.3 19.1 %collective-permute-start.4 = (bf16[128,1024]{1,0:T(8,128)(2,1)S(1)}, bf16[128,1024]{1,0:T(8,128)(2,1)S(1)}, u32[]{:S(2)}, u32[]{:S(2)}) collective-permute-start(bf16[128,1024]{1,0:T(8,128)(2,1)S(1)} %bitcast.10), channel_id=1, source_target_pairs={{0,8},{8,24},{24,16},{16,0},{1,9},{9,25},{25,17},{17,1},{2,10},{10... | collective-permute-start | bytes 786440 | tf_op jit(solution)/shard_map/ppermute | solution.py:300
  2.6 1.2 %copy-start = (bf16[1,128,4096]{2,1,0:T(8,128)(2,1)S(1)}, bf16[1,128,4096]{2,1,0:T(8,128)(2,1)}, u32[]{:S(2)}) copy-start(bf16[1,128,4096]{2,1,0:T(8,128)(2,1)} %param.6) | copy-start | bytes 3145732
  3.8 0.7 %copy-start.3 = (s32[4,4]{1,0:T(4,128)S(1)}, s32[4,4]{1,0:T(4,128)}, u32[]{:S(2)}) copy-start(s32[4,4]{1,0:T(4,128)} %counts.1) | copy-start | bytes 196
  3.8 0.7 %copy-start.4 = (s32[1,6]{1,0:T(1,128)S(1)}, s32[1,6]{1,0:T(1,128)}, u32[]{:S(2)}) copy-start(s32[1,6]{1,0:T(1,128)} %docs.1) | copy-start | bytes 76
  10.3 10.1 %collective-permute-start.1 = (bf16[40,2048]{1,0:T(8,128)(2,1)S(1)}, bf16[40,2048]{1,0:T(8,128)(2,1)S(1)}, u32[]{:S(2)}, u32[]{:S(2)}) collective-permute-start(bf16[40,2048]{1,0:T(8,128)(2,1)S(1)} %get-tuple-element.37), channel_id=1, source_target_pairs={{0,2},{2,0},{4,6},{6,4},{1,3},{3,1},{5,7},{7,5},{8,10},{10,8},{12,... | collective-permute-start | bytes 491528 | tf_op jit(solution)/shard_map/ppermute | solution.py:61
  11.6 8.8 %collective-permute-start.2 = (bf16[40,2048]{1,0:T(8,128)(2,1)S(1)}, bf16[40,2048]{1,0:T(8,128)(2,1)S(1)}, u32[]{:S(2)}, u32[]{:S(2)}) collective-permute-start(bf16[40,2048]{1,0:T(8,128)(2,1)S(1)} %get-tuple-element.38), channel_id=1, source_target_pairs={{0,4},{2,6},{4,0},{6,2},{1,5},{3,7},{5,1},{7,3},{8,12},{10,14},{12... | collective-permute-start | bytes 491528 | tf_op jit(solution)/shard_map/ppermute | solution.py:61
  12.8 7.6 %collective-permute-start.3 = (bf16[40,2048]{1,0:T(8,128)(2,1)S(1)}, bf16[40,2048]{1,0:T(8,128)(2,1)S(1)}, u32[]{:S(2)}, u32[]{:S(2)}) collective-permute-start(bf16[40,2048]{1,0:T(8,128)(2,1)S(1)} %get-tuple-element.39), channel_id=1, source_target_pairs={{0,6},{2,4},{4,2},{6,0},{1,7},{3,5},{5,3},{7,1},{8,14},{10,12},{12... | collective-permute-start | bytes 491528 | tf_op jit(solution)/shard_map/ppermute | solution.py:61
  14.8 12.0 %collective-permute-start.10 = (bf16[128,1024]{1,0:T(8,128)(2,1)S(1)}, bf16[128,1024]{1,0:T(8,128)(2,1)S(1)}, u32[]{:S(2)}, u32[]{:S(2)}) collective-permute-start(bf16[128,1024]{1,0:T(8,128)(2,1)S(1)} %collective-permute-done.5.refs_2_), channel_id=1, source_target_pairs={{0,8},{8,24},{24,16},{16,0},{1,9},{9,25},{25,17},{17,1},{2,10},{10... | collective-permute-start | bytes 786440 | tf_op jit(solution)/shard_map/ppermute | solution.py:308
  20.4 12.4 %collective-permute-start.9 = (bf16[128,1024]{1,0:T(8,128)(2,1)S(1)}, bf16[128,1024]{1,0:T(8,128)(2,1)S(1)}, u32[]{:S(2)}, u32[]{:S(2)}) collective-permute-start(bf16[128,1024]{1,0:T(8,128)(2,1)S(1)} %collective-permute-done.4.refs_1_), channel_id=1, source_target_pairs={{0,8},{8,24},{24,16},{16,0},{1,9},{9,25},{25,17},{17,1},{2,10},{10... | collective-permute-start | bytes 786440 | tf_op jit(solution)/shard_map/ppermute | solution.py:308
  21.1 19.2 %collective-permute-start.14 = (bf16[128,1024]{1,0:T(8,128)(2,1)S(1)}, bf16[128,1024]{1,0:T(8,128)(2,1)S(1)}, u32[]{:S(2)}, u32[]{:S(2)}) collective-permute-start(bf16[128,1024]{1,0:T(8,128)(2,1)S(1)} %get-tuple-element.57), channel_id=1, source_target_pairs={{8,0},{24,8},{16,24},{0,16},{9,1},{25,9},{17,25},{1,17},{10,2},{26... | collective-permute-start | bytes 786440 | tf_op jit(solution)/shard_map/ppermute | solution.py:303
  24.3 10.6 %collective-permute-start.6 = (bf16[40,1024]{1,0:T(8,128)(2,1)S(1)}, bf16[40,1024]{1,0:T(8,128)(2,1)S(1)}, u32[]{:S(2)}, u32[]{:S(2)}) collective-permute-start(bf16[40,1024]{1,0:T(8,128)(2,1)S(1)} %get-tuple-element.47), channel_id=1, source_target_pairs={{0,2},{2,0},{4,6},{6,4},{1,3},{3,1},{5,7},{7,5},{8,10},{10,8},{12,... | collective-permute-start | bytes 245768 | tf_op jit(solution)/shard_map/ppermute | solution.py:61
  25.5 10.6 %collective-permute-start.7 = (bf16[40,1024]{1,0:T(8,128)(2,1)S(1)}, bf16[40,1024]{1,0:T(8,128)(2,1)S(1)}, u32[]{:S(2)}, u32[]{:S(2)}) collective-permute-start(bf16[40,1024]{1,0:T(8,128)(2,1)S(1)} %get-tuple-element.48), channel_id=1, source_target_pairs={{0,4},{2,6},{4,0},{6,2},{1,5},{3,7},{5,1},{7,3},{8,12},{10,14},{12... | collective-permute-start | bytes 245768 | tf_op jit(solution)/shard_map/ppermute | solution.py:61
  26.8 9.5 %collective-permute-start.8 = (bf16[40,1024]{1,0:T(8,128)(2,1)S(1)}, bf16[40,1024]{1,0:T(8,128)(2,1)S(1)}, u32[]{:S(2)}, u32[]{:S(2)}) collective-permute-start(bf16[40,1024]{1,0:T(8,128)(2,1)S(1)} %get-tuple-element.49), channel_id=1, source_target_pairs={{0,6},{2,4},{4,2},{6,0},{1,7},{3,5},{5,3},{7,1},{8,14},{10,12},{12... | collective-permute-start | bytes 245768 | tf_op jit(solution)/shard_map/ppermute | solution.py:61
  33.6 3.7 %collective-permute-start.11 = (bf16[40,1024]{1,0:T(8,128)(2,1)S(1)}, bf16[40,1024]{1,0:T(8,128)(2,1)S(1)}, u32[]{:S(2)}, u32[]{:S(2)}) collective-permute-start(bf16[40,1024]{1,0:T(8,128)(2,1)S(1)} %get-tuple-element.54), channel_id=1, source_target_pairs={{0,2},{2,0},{4,6},{6,4},{1,3},{3,1},{5,7},{7,5},{8,10},{10,8},{12,... | collective-permute-start | bytes 245768 | tf_op jit(solution)/shard_map/ppermute | solution.py:61
  34.8 3.6 %collective-permute-start.12 = (bf16[40,1024]{1,0:T(8,128)(2,1)S(1)}, bf16[40,1024]{1,0:T(8,128)(2,1)S(1)}, u32[]{:S(2)}, u32[]{:S(2)}) collective-permute-start(bf16[40,1024]{1,0:T(8,128)(2,1)S(1)} %get-tuple-element.55), channel_id=1, source_target_pairs={{0,4},{2,6},{4,0},{6,2},{1,5},{3,7},{5,1},{7,3},{8,12},{10,14},{12... | collective-permute-start | bytes 245768 | tf_op jit(solution)/shard_map/ppermute | solution.py:61
  36.1 4.2 %collective-permute-start.13 = (bf16[40,1024]{1,0:T(8,128)(2,1)S(1)}, bf16[40,1024]{1,0:T(8,128)(2,1)S(1)}, u32[]{:S(2)}, u32[]{:S(2)}) collective-permute-start(bf16[40,1024]{1,0:T(8,128)(2,1)S(1)} %get-tuple-element.56), channel_id=1, source_target_pairs={{0,6},{2,4},{4,2},{6,0},{1,7},{3,5},{5,3},{7,1},{8,14},{10,12},{12... | collective-permute-start | bytes 245768 | tf_op jit(solution)/shard_map/ppermute | solution.py:61
  40.3 8.2 %copy-start.5 = (bf16[4096]{0:T(1024)(128)(2,1)S(1)}, bf16[4096]{0:T(1024)(128)(2,1)}, u32[]{:S(2)}) copy-start(bf16[4096]{0:T(1024)(128)(2,1)} %param.11) | copy-start | bytes 24580
  40.7 8.7 %collective-permute-start.15 = (f32[128,128]{1,0:T(8,128)S(1)}, f32[128,128]{1,0:T(8,128)S(1)}, u32[]{:S(2)}, u32[]{:S(2)}) collective-permute-start(f32[128,128]{1,0:T(8,128)S(1)} %get-tuple-element.60.refs_4_), channel_id=1, source_target_pairs={{0,1},{1,0},{2,3},{3,2},{4,5},{5,4},{6,7},{7,6},{8,9},{9,8},{10,11... | collective-permute-start | bytes 196616 | tf_op jit(solution)/shard_map/ppermute | solution.py:315

commit v3 on v2

v3 whole, which is shorter than its diff:
```python
import functools

import jax
import jax.numpy as jnp
from jax import lax
from jax.experimental import pallas as pl
from jax.experimental.pallas import tpu as pltpu
from jax.sharding import PartitionSpec as P

HEADS = 64
HEAD_DIM = 128

masked_fill = -1e30
norm_eps = 1e-06
log2_e = 1.4426950408889634

VMEM = pl.BlockSpec(memory_space=pltpu.VMEM)
SMEM = pl.BlockSpec(memory_space=pltpu.SMEM)
ANY = pl.BlockSpec(memory_space=pl.ANY)
COST = pl.CostEstimate(flops=1, bytes_accessed=1, transcendentals=0)
PARAMS = pltpu.CompilerParams(vmem_limit_bytes=32 * 1024 * 1024)


def iota(shape, dim):
    return lax.broadcasted_iota(jnp.int32, shape, dim)


def pick(index, table):
    value = jnp.int32(table[0])
    for i, entry in enumerate(table[1:], 1):
        value = jnp.where(index == i, jnp.int32(entry), value)
    return value


def one_hot(condition):
    return condition.astype(jnp.float32).astype(jnp.bfloat16)


class Plan:
    def __init__(self, mesh, seq, local_width):
        self.pipe, self.groups, self.tensor = (mesh.shape[a] for a in ("pipe", "dp", "tensor"))
        self.seq, self.block = seq, local_width // self.pipe
        self.cap = 5 * seq // (4 * self.groups)
        self.pairwise = self.groups == 4 and self.cap % 8 == 0
        self.parts = self.groups if self.pairwise else 1
        self.rows = self.groups * self.cap // self.parts
        self.steps = [0, 3, 1, 2] if self.pairwise else list(range(self.groups))
        n = self.pipe
        order = [0] + list(range(1, n, 2)) + [i for i in reversed(range(2, n)) if i % 2 == 0]
        self.ring = [(order[i], order[(i + 1) % n]) for i in range(n)]
        where = {d: i for i, d in enumerate(order)}
        self.behind = [[order[(where[p] - t) % n] for p in range(n)] for t in range(n)]

    def partner(self, own, i):
        step = jnp.int32(self.steps[i])
        return jnp.bitwise_xor(own, step) if self.pairwise else step

    def regroup(self, parts):
        if not self.pairwise:
            return [lax.all_to_all(parts[0], "dp", split_axis=0, concat_axis=0, tiled=True)]
        got = [parts[0]]
        for step, part in zip(self.steps[1:], parts[1:], strict=True):
            got.append(lax.ppermute(part, "dp", [(g, g ^ step) for g in range(self.groups)]))
        return got


def split_kernel(plan, query, *refs):
    outs, sems = refs[:-1], refs[-1]
    place = lax.axis_index("pipe")
    copies = []
    for t, out in enumerate(outs):
        begin = pl.multiple_of(pick(place, plan.behind[t]) * plan.block, plan.block)
        copies.append(
            pltpu.make_async_copy(query.at[:, pl.ds(begin, plan.block)], out, sems.at[t])
        )
        copies[-1].start()
    for copy in copies:
        copy.wait()


def split(plan, query):
    shape = jax.ShapeDtypeStruct((plan.seq, plan.block), query.dtype)
    return pl.pallas_call(
        functools.partial(split_kernel, plan),
        out_shape=[shape] * (plan.pipe - 1),
        in_specs=[ANY],
        out_specs=[VMEM] * (plan.pipe - 1),
        scratch_shapes=[pltpu.SemaphoreType.DMA((plan.pipe - 1,))],
        compiler_params=PARAMS,
        cost_estimate=COST,
        name="split",
    )(query)


def tables_kernel(plan, docs, counts, bias, send, *places):
    seq, cap, groups = plan.seq, plan.cap, plan.groups
    own = lax.axis_index("dp")
    rows, cols = iota((seq, seq), 0), iota((seq, seq), 1)
    row_doc = jnp.zeros((seq, seq), jnp.int32)
    col_doc = jnp.zeros((seq, seq), jnp.int32)
    end = jnp.int32(0)
    for k in range(docs.shape[1]):
        end = end + docs[0, k]
        row_doc = row_doc + (rows >= end).astype(jnp.int32)
        col_doc = col_doc + (cols >= end).astype(jnp.int32)
    bias[...] = jnp.where((row_doc == col_doc) & (rows <= cols), 0.0, masked_fill)
    rows, cols = iota((groups * cap, seq), 0), iota((groups * cap, seq), 1)
    target = jnp.full((groups * cap, seq), -1, jnp.int32)
    for i in range(groups):
        to = plan.partner(own, i)
        begin = jnp.int32(0)
        for j in range(groups):
            begin = begin + jnp.where(j < to, counts[own, j], 0)
        inside = (rows >= i * cap) & (rows < i * cap + counts[own, to])
        target = jnp.where(inside, rows - i * cap + begin, target)
    send[...] = one_hot(cols == target)
    per = groups // plan.parts
    for part, out in enumerate(places):
        rows, cols = iota(out.shape, 0), iota(out.shape, 1)
        target = jnp.full(out.shape, -1, jnp.int32)
        for slot in range(per):
            source = plan.partner(own, part * per + slot)
            begin = jnp.int32(0)
            for j in range(groups):
                begin = begin + jnp.where(j < source, counts[j, own], 0)
            inside = (cols >= slot * cap) & (cols < slot * cap + counts[source, own])
            target = jnp.where(inside, cols - slot * cap + begin, target)
        out[...] = one_hot(rows == target)


def tables(plan, docs, counts):
    shapes = [
        jax.ShapeDtypeStruct((plan.seq, plan.seq), jnp.float32),
        jax.ShapeDtypeStruct((plan.groups * plan.cap, plan.seq), jnp.bfloat16),
    ] + [jax.ShapeDtypeStruct((plan.seq, plan.rows), jnp.bfloat16)] * plan.parts
    bias, send, *places = pl.pallas_call(
        functools.partial(tables_kernel, plan),
        out_shape=shapes,
        in_specs=[SMEM] * 2,
        out_specs=[VMEM] * len(shapes),
        compiler_params=PARAMS,
        cost_estimate=COST,
        name="tables",
    )(docs, counts)
    return bias, send, places


def attend_kernel(plan, jobs, *refs):
    count = len(jobs)
    operands, (bias, send) = refs[: 3 * count], refs[3 * count : 3 * count + 2]
    outs, attn = refs[-1 - plan.parts : -1], refs[-1]
    scale = log2_e / HEAD_DIM**0.5
    base = 0
    for n, (q_from, k_from, v_from, width) in enumerate(jobs):
        q_ref, k_ref, v_ref = operands[3 * n : 3 * n + 3]
        heads = range(0, width, HEAD_DIM)
        scores = [
            lax.dot_general(
                k_ref[:, k_from + h : k_from + h + HEAD_DIM],
                q_ref[:, q_from + h : q_from + h + HEAD_DIM],
                (((1,), (1,)), ((), ())),
                preferred_element_type=jnp.float32,
            )
            for h in heads
        ]
        weights, totals = [], []
        for score in scores:
            score = score * scale + bias[...]
            weight = jnp.exp2(score - jnp.max(score, axis=0, keepdims=True))
            totals.append(jnp.sum(weight, axis=0, keepdims=True))
            weights.append(weight.astype(jnp.bfloat16))
        for h, weight, total in zip(heads, weights, totals, strict=True):
            accum = lax.dot_general(
                v_ref[:, v_from + h : v_from + h + HEAD_DIM],
                weight,
                (((0,), (0,)), ((), ())),
                preferred_element_type=jnp.float32,
            )
            rows = slice(base + h, base + h + HEAD_DIM)
            attn[rows, :] = (accum * (1.0 / total)).astype(jnp.bfloat16)
        base += width
    picked = lax.dot_general(
        send[...], attn[...], (((1,), (1,)), ((), ())), preferred_element_type=jnp.float32
    )
    for part, out in enumerate(outs):
        out[...] = picked[part * plan.rows : (part + 1) * plan.rows].astype(jnp.bfloat16)


def attend(plan, jobs, bias, send, after=None):
    operands = [ref for job in jobs for ref in job[:3]]
    spans = tuple(job[3:] for job in jobs)
    width = sum(span[-1] for span in spans)
    order = () if after is None else (after,)
    return pl.pallas_call(
        functools.partial(attend_kernel, plan, spans),
        out_shape=[jax.ShapeDtypeStruct((plan.rows, width), jnp.bfloat16)] * plan.parts,
        in_specs=[VMEM] * (len(operands) + 2) + [ANY] * len(order),
        out_specs=[VMEM] * plan.parts,
        scratch_shapes=[pltpu.VMEM((width, plan.seq), jnp.bfloat16)],
        compiler_params=PARAMS,
        cost_estimate=COST,
        name="attend",
    )(*operands, bias, send, *order)


def pack_kernel(k_ref, v_ref, first, second):
    half = k_ref.shape[1] // 2
    first[:, :half] = k_ref[:, :half]
    first[:, half:] = v_ref[:, :half]
    second[:, :half] = k_ref[:, half:]
    second[:, half:] = v_ref[:, half:]


def pack(k, v):
    return pl.pallas_call(
        pack_kernel,
        out_shape=[jax.ShapeDtypeStruct(k.shape, k.dtype)] * 2,
        in_specs=[VMEM] * 2,
        out_specs=[VMEM] * 2,
        compiler_params=PARAMS,
        cost_estimate=COST,
        name="pack",
    )(k, v)


def squares_of(ref):
    total = None
    for c in range(0, ref.shape[1], HEAD_DIM):
        wide = ref[:, c : c + HEAD_DIM].astype(jnp.float32)
        total = wide * wide if total is None else total + wide * wide
    return total


def place_kernel(plan, widths, summed, extra, sums, *refs):
    parts = plan.parts
    got, matrices, refs = refs[:parts], refs[parts : 2 * parts], refs[2 * parts :]
    blocks, earlier = refs[:extra], refs[extra : extra + sums]
    outs = refs[extra + sums :]
    totals = [squares_of(ref) for ref in blocks] + [ref[...] for ref in earlier]
    base = 0
    for n, (width, out) in enumerate(zip(widths, outs, strict=False)):
        placed = None
        for matrix, ref in zip(matrices, got, strict=True):
            more = jnp.dot(
                matrix[...], ref[:, base : base + width], preferred_element_type=jnp.float32
            )
            placed = more if placed is None else placed + more
        out[...] = placed.astype(jnp.bfloat16)
        if n < summed:
            for c in range(0, width, HEAD_DIM):
                totals.append(placed[:, c : c + HEAD_DIM] * placed[:, c : c + HEAD_DIM])
        base += width
    if summed:
        total = totals[0]
        for more in totals[1:]:
            total = total + more
        outs[-1][...] = total


def place(plan, got, matrices, widths, summed=1, blocks=(), sums=()):
    shapes = [jax.ShapeDtypeStruct((plan.seq, width), jnp.bfloat16) for width in widths]
    if summed:
        shapes.append(jax.ShapeDtypeStruct((plan.seq, HEAD_DIM), jnp.float32))
    args = (*got, *matrices, *blocks, *sums)
    return pl.pallas_call(
        functools.partial(place_kernel, plan, widths, summed, len(blocks), len(sums)),
        out_shape=shapes,
        in_specs=[VMEM] * len(args),
        out_specs=[VMEM] * len(shapes),
        compiler_params=PARAMS,
        cost_estimate=COST,
        name="place",
    )(*args)


def norm_kernel(plan, spots, sums, *refs):
    count = len(spots)
    pieces, refs = refs[:count], refs[count:]
    squares, (gain, out, held, sems) = refs[:sums], refs[sums:]
    width = HEADS * HEAD_DIM
    lanes = squares[0][...]
    for ref in squares[1:]:
        lanes = lanes + ref[...]
    mean = jnp.sum(lanes, axis=1, keepdims=True) / width
    factor = jnp.broadcast_to(lax.rsqrt(mean + norm_eps), lanes.shape)
    device = lax.axis_index("pipe")
    copies = []
    for i, ((t, offset), ref) in enumerate(zip(spots, pieces, strict=True)):
        begin = pick(device, plan.behind[t]) * plan.block + offset
        size = ref.shape[1]
        for c in range(0, size, HEAD_DIM):
            at = pl.ds(pl.multiple_of(begin + c, HEAD_DIM), HEAD_DIM)
            wide = ref[:, c : c + HEAD_DIM].astype(jnp.float32)
            spot = slice(t * plan.block + offset + c, t * plan.block + offset + c + HEAD_DIM)
            held[:, spot] = (wide * factor * gain[:, at]).astype(jnp.bfloat16)
        spot = pl.ds(t * plan.block + offset, size)
        at = pl.ds(pl.multiple_of(begin, HEAD_DIM), size)
        copies.append(pltpu.make_async_copy(held.at[:, spot], out.at[:, at], sems.at[i]))
        copies[-1].start()
    for copy in copies:
        copy.wait()


def norm(plan, pieces, squares, gain):
    arrays, spots = [piece[0] for piece in pieces], tuple(piece[1:] for piece in pieces)
    return pl.pallas_call(
        functools.partial(norm_kernel, plan, spots, len(squares)),
        out_shape=jax.ShapeDtypeStruct((plan.seq, plan.pipe * plan.block), jnp.bfloat16),
        in_specs=[VMEM] * (len(arrays) + len(squares) + 1),
        out_specs=ANY,
        scratch_shapes=[
            pltpu.VMEM((plan.seq, plan.pipe * plan.block), jnp.bfloat16),
            pltpu.SemaphoreType.DMA((len(arrays),)),
        ],
        compiler_params=PARAMS,
        cost_estimate=COST,
        name="norm",
    )(*arrays, *squares, gain)


def body(mesh, queries, cache_keys, cache_values, doc_lengths, row_counts, out_gain):
    query = queries[0]
    seq, local_width = query.shape
    plan = Plan(mesh, seq, local_width)
    n, block, half = plan.pipe, plan.block, plan.block // 2
    forward, backward = plan.ring, [(b, a) for a, b in plan.ring]
    keys, values = cache_keys.reshape(seq, block), cache_values.reshape(seq, block)
    gain = out_gain.astype(jnp.float32).reshape(1, local_width)

    begin = pick(lax.axis_index("pipe"), plan.behind[n - 1]) * block
    ahead = lax.dynamic_slice_in_dim(query, begin, block, 1)
    ahead, values_out = lax.optimization_barrier((ahead, values))
    pairs = [(keys, values)]
    k, v = lax.ppermute(keys, "pipe", forward), lax.ppermute(values_out, "pipe", forward)
    lent = lax.ppermute(ahead, "pipe", forward)
    for _ in range(n - 3):
        pairs.append((k, v))
        k, v = lax.ppermute(k, "pipe", forward), lax.ppermute(v, "pipe", forward)
    pairs.append((k, v))

    asked = split(plan, query)
    bias, send, places = tables(plan, doc_lengths, row_counts)
    run = functools.partial(attend, plan, bias=bias, send=send)
    jobs = [(asked[t], *pairs[t], 0, 0, 0, block) for t in range(n - 1)]
    got = [plan.regroup(run([jobs[0], (lent, keys, values, 0, 0, 0, block)]))]
    got += [plan.regroup(run([job])) for job in jobs[1:]]
    mine, borrowed, total = place(plan, got[0], places, (block, block), summed=1)
    borrowed, _ = lax.optimization_barrier((borrowed, pairs[-1][0]))
    returned = lax.ppermute(borrowed, "pipe", backward)

    pieces = [(mine, 0, 0), (returned, n - 1, 0)]
    for t, parts in enumerate(got[1:], 1):
        last = t == n - 2
        placed, total = place(
            plan, parts, places, (block,), blocks=(returned,) if last else (), sums=(total,)
        )
        pieces.append((placed, t, 0))
    if plan.tensor == 2:
        sums = (total, lax.ppermute(total, "tensor", [(0, 1), (1, 0)]))
    else:
        sums = (lax.psum(total, "tensor"),)
    return norm(plan, pieces, sums, gain)[None]


def solution(mesh):
    return jax.shard_map(
        functools.partial(body, mesh),
        mesh=mesh,
        in_specs=(
            P("pipe", "dp", "tensor"),
            P("dp", "tensor", "pipe", None),
            P("dp", "tensor", "pipe", None),
            P("dp", None),
            P(),
            P("tensor"),
        ),
        out_specs=P("pipe", "dp", "tensor"),
        check_vma=False,
    )
```

time: 50.8 us -> 49 us (0.965)
  the two profiles are of different devices: /device:TPU:25 before, /device:TPU:27 now
where the time goes in v3:
time: 49 us; the launch traced here: 48.8 us
  waiting for transfers between devices  22.3 us (46%)
  starting transfers between devices  17.5 us (36%)
  Pallas kernels  6.06 us (12%)
  local copies, waits for them, and re-layouts  2.83 us (6%)
    ppermute x9, starting transfers between devices, regroup(): lax.ppermute(part, 'dp', [(g, g ^ step) for g in range(self.groups)])  8.14 us
    ppermute x1, starting transfers between devices, body(): sums = (total, lax.ppermute(total, 'tensor', [(0, 1), (1, 0)]))  7.79 us
    ppermute x9, waiting for transfers between devices, regroup(): lax.ppermute(part, 'dp', [(g, g ^ step) for g in range(self.groups)])  5.71 us
    ppermute x1, waiting for transfers between devices, body(): lax.ppermute(keys, 'pipe', forward)  5.69 us
    ppermute x2, waiting for transfers between devices, body(): k, v = (lax.ppermute(k, 'pipe', forward), lax.ppermute(v, 'pipe', forward))  5.2 us
    ppermute x1, waiting for transfers between devices, body(): lent = lax.ppermute(ahead, 'pipe', forward)  3.02 us
    pallas_call x3, Pallas kernels, attend(): pl.pallas_call(functools.partial(attend_kernel, plan, spans), out_shape=[...  2.6 us
    unnamed x12, local copies, waits for them, and re-layouts  1.82 us
  transfers between devices with their start and end apart: 16, of which 11 were waited for; matrix products, arithmetic and copies ran while one was open for 2% of the time, Pallas kernels for 9%

profile of v3, /device:TPU:27, one launch (start us, length us, event | category | flops | bytes accessed | tf_op | source)
XLA Modules:
  0.0 48.8 jit_solution(4913981566356525221)
XLA Ops:
  0.0 0.2 collective-permute-start.4
  0.2 0.0 copy-start.2
  0.2 1.0 %dynamic-slice_bitcast_fusion = bf16[128,1024]{1,0:T(8,128)(2,1)S(1)} fusion(bf16[1,128,4096]{2,1,0:T(8,128)(2,1)} %param.6, s32[]{:T(128)S(6)} %select_n.16), kind=kLoop, calls=%fused_computation | loop fusion | bytes 524292 | tf_op jit(solution)/shard_map/dynamic_slice | solution.py:331
  1.2 0.1 collective-permute-start
  1.3 0.0 copy-done.2
  1.3 1.3 %collective-permute-start.7 = (bf16[128,1024]{1,0:T(8,128)(2,1)S(1)}, bf16[128,1024]{1,0:T(8,128)(2,1)S(1)}, u32[]{:S(2)}, u32[]{:S(2)}) collective-permute-start(bf16[128,1024]{1,0:T(8,128)(2,1)S(1)} %bitcast.11), channel_id=1, source_target_pairs={{0,8},{8,24},{24,16},{16,0},{1,9},{9,25},{25,17},{17,1},{2,10},{10... | collective-permute-start | bytes 786440 | tf_op jit(solution)/shard_map/ppermute | solution.py:334
  2.6 5.7 %collective-permute-done.4.refs_1_ = bf16[128,1024]{1,0:T(8,128)(2,1)S(1)} collective-permute-done((bf16[128,1024]{1,0:T(8,128)(2,1)}, bf16[128,1024]{1,0:T(8,128)(2,1)S(1)}, u32[]{:S(2)}, u32[]{:S(2)}) %collective-permute-start.4) | collective-permute-done | bytes 262176 | tf_op jit(solution)/shard_map/ppermute | solution.py:334
  8.3 0.0 collective-permute-start.5
  8.3 0.0 copy-start
  8.3 1.2 %copy-done = bf16[1,128,4096]{2,1,0:T(8,128)(2,1)S(1)} copy-done((bf16[1,128,4096]{2,1,0:T(8,128)(2,1)S(1)}, bf16[1,128,4096]{2,1,0:T(8,128)(2,1)}, u32[]{:S(2)}) %copy-start) | copy-done | bytes 1048600
  9.5 0.0 copy-start.3
  9.5 0.0 copy-start.4
  9.5 0.0 copy-start.1
  9.5 0.1 split.1
  9.6 0.6 %copy-done.3 = s32[4,4]{1,0:T(4,128)S(1)} copy-done((s32[4,4]{1,0:T(4,128)S(1)}, s32[4,4]{1,0:T(4,128)}, u32[]{:S(2)}) %copy-start.3) | copy-done | bytes 88
  10.2 0.0 copy-done.4
  10.2 0.7 %tables.1 = (f32[128,128]{1,0:T(8,128)S(1)}, bf16[160,128]{1,0:T(8,128)(2,1)S(1)}, bf16[128,40]{1,0:T(8,128)(2,1)S(1)}, bf16[128,40]{1,0:T(8,128)(2,1)S(1)}, bf1...) custom-call(s32[1,6]{1,0:T(1,128)S(1)} %copy-done.4, s32[4,4]{1,0:T(4,128)S(1)} %copy-done.3), custom_call_target="tpu_custom_call" | custom-call | flops 1 | bytes 1 | tf_op jit(solution)/shard_map/tables/pallas_call | solution.py:136
  10.9 3.0 %collective-permute-done.refs_3_ = bf16[128,1024]{1,0:T(8,128)(2,1)S(1)} collective-permute-done((bf16[128,1024]{1,0:T(8,128)(2,1)S(1)}, bf16[128,1024]{1,0:T(8,128)(2,1)S(1)}, u32[]{:S(2)}, u32[]{:S(2)}) %collective-permute-start) | collective-permute-done | bytes 262176 | tf_op jit(solution)/shard_map/ppermute | solution.py:335
  13.9 0.0 copy-done.1
  13.9 1.1 %attend.3 = (bf16[40,2048]{1,0:T(8,128)(2,1)S(1)}, bf16[40,2048]{1,0:T(8,128)(2,1)S(1)}, bf16[40,2048]{1,0:T(8,128)(2,1)S(1)}, bf16[40,2048]{1,0:T(8,128)(2,1)S(1)}) custom-call(bf16[128,1024]{1,0:T(8,128)(2,1)S(1)} %get-tuple-element.36.refs_0_, bf16[128,1024]{1,0:T(8,128)(2,1)S(1)} %bitcast.9, bf16[128,1024]{1,0:T(8,128)(2,1)S(1)} %bitcast.12, ...), custom_call_target="tpu_custom_call" | custom-call | flops 1 | bytes 1 | tf_op jit(solution)/shard_map/attend/pallas_call | solution.py:194
  15.0 1.3 %collective-permute-start.1 = (bf16[40,2048]{1,0:T(8,128)(2,1)S(1)}, bf16[40,2048]{1,0:T(8,128)(2,1)S(1)}, u32[]{:S(2)}, u32[]{:S(2)}) collective-permute-start(bf16[40,2048]{1,0:T(8,128)(2,1)S(1)} %get-tuple-element.41), channel_id=1, source_target_pairs={{0,6},{2,4},{4,2},{6,0},{1,7},{3,5},{5,3},{7,1},{8,14},{10,12},{12... | collective-permute-start | bytes 491528 | tf_op jit(solution)/shard_map/ppermute | solution.py:63
  16.3 1.2 %collective-permute-start.2 = (bf16[40,2048]{1,0:T(8,128)(2,1)S(1)}, bf16[40,2048]{1,0:T(8,128)(2,1)S(1)}, u32[]{:S(2)}, u32[]{:S(2)}) collective-permute-start(bf16[40,2048]{1,0:T(8,128)(2,1)S(1)} %get-tuple-element.42), channel_id=1, source_target_pairs={{0,2},{2,0},{4,6},{6,4},{1,3},{3,1},{5,7},{7,5},{8,10},{10,8},{12,... | collective-permute-start | bytes 491528 | tf_op jit(solution)/shard_map/ppermute | solution.py:63
  17.5 0.2 collective-permute-start.3
  17.8 1.8 %collective-permute-done.7.refs_2_ = bf16[128,1024]{1,0:T(8,128)(2,1)S(1)} collective-permute-done((bf16[128,1024]{1,0:T(8,128)(2,1)S(1)}, bf16[128,1024]{1,0:T(8,128)(2,1)S(1)}, u32[]{:S(2)}, u32[]{:S(2)}) %collective-permute-start.7) | collective-permute-done | bytes 262176 | tf_op jit(solution)/shard_map/ppermute | solution.py:334
  19.5 0.0 collective-permute-start.11
  19.5 1.0 %collective-permute-done.1.refs_1_ = bf16[40,2048]{1,0:T(8,128)(2,1)S(1)} collective-permute-done((bf16[40,2048]{1,0:T(8,128)(2,1)S(1)}, bf16[40,2048]{1,0:T(8,128)(2,1)S(1)}, u32[]{:S(2)}, u32[]{:S(2)}) %collective-permute-start.1) | collective-permute-done | bytes 163872 | tf_op jit(solution)/shard_map/ppermute | solution.py:63
  20.5 2.1 %collective-permute-done.2.refs_2_ = bf16[40,2048]{1,0:T(8,128)(2,1)S(1)} collective-permute-done((bf16[40,2048]{1,0:T(8,128)(2,1)S(1)}, bf16[40,2048]{1,0:T(8,128)(2,1)S(1)}, u32[]{:S(2)}, u32[]{:S(2)}) %collective-permute-start.2) | collective-permute-done | bytes 163872 | tf_op jit(solution)/shard_map/ppermute | solution.py:63
  22.6 0.0 collective-permute-done.3.refs_3_
  22.6 0.7 %place.3 = (bf16[128,1024]{1,0:T(8,128)(2,1)S(1)}, bf16[128,1024]{1,0:T(8,128)(2,1)S(1)}, f32[128,128]{1,0:T(8,128)S(1)}) custom-call(bf16[40,2048]{1,0:T(8,128)(2,1)S(1)} %get-tuple-element.40.refs_0_, bf16[40,2048]{1,0:T(8,128)(2,1)S(1)} %collective-permute-done.1.refs_1_, bf16[40,2048]{1,0:T(8,128)(2,1)S(1)} %collective-permute-done.2.refs_2_, ...), custom_call_target="tpu_custom_call" | custom-call | flops 1 | bytes 1 | tf_op jit(solution)/shard_map/place/pallas_call | solution.py:265
  23.3 1.9 %collective-permute-done.5.refs_1_ = bf16[128,1024]{1,0:T(8,128)(2,1)S(1)} collective-permute-done((bf16[128,1024]{1,0:T(8,128)(2,1)S(1)}, bf16[128,1024]{1,0:T(8,128)(2,1)S(1)}, u32[]{:S(2)}, u32[]{:S(2)}) %collective-permute-start.5) | collective-permute-done | bytes 262176 | tf_op jit(solution)/shard_map/ppermute | solution.py:338
  25.1 0.0 collective-permute-start.6
  25.1 0.7 %attend.4 = (bf16[40,1024]{1,0:T(8,128)(2,1)S(1)}, bf16[40,1024]{1,0:T(8,128)(2,1)S(1)}, bf16[40,1024]{1,0:T(8,128)(2,1)S(1)}, bf16[40,1024]{1,0:T(8,128)(2,1)S(1)}) custom-call(bf16[128,1024]{1,0:T(8,128)(2,1)S(1)} %get-tuple-element.51.refs_0_, bf16[128,1024]{1,0:T(8,128)(2,1)S(1)} %collective-permute-done.4.refs_1_, ...), custom_call_target="tpu_custom_call" | custom-call | flops 1 | bytes 1 | tf_op jit(solution)/shard_map/attend/pallas_call | solution.py:194
  25.9 1.3 %collective-permute-start.10 = (bf16[40,1024]{1,0:T(8,128)(2,1)S(1)}, bf16[40,1024]{1,0:T(8,128)(2,1)S(1)}, u32[]{:S(2)}, u32[]{:S(2)}) collective-permute-start(bf16[40,1024]{1,0:T(8,128)(2,1)S(1)} %get-tuple-element.56), channel_id=1, source_target_pairs={{0,4},{2,6},{4,0},{6,2},{1,5},{3,7},{5,1},{7,3},{8,12},{10,14},{12... | collective-permute-start | bytes 245768 | tf_op jit(solution)/shard_map/ppermute | solution.py:63
  27.2 0.2 collective-permute-start.8
  27.4 1.2 %collective-permute-start.9 = (bf16[40,1024]{1,0:T(8,128)(2,1)S(1)}, bf16[40,1024]{1,0:T(8,128)(2,1)S(1)}, u32[]{:S(2)}, u32[]{:S(2)}) collective-permute-start(bf16[40,1024]{1,0:T(8,128)(2,1)S(1)} %get-tuple-element.55), channel_id=1, source_target_pairs={{0,2},{2,0},{4,6},{6,4},{1,3},{3,1},{5,7},{7,5},{8,10},{10,8},{12,... | collective-permute-start | bytes 245768 | tf_op jit(solution)/shard_map/ppermute | solution.py:63
  28.6 3.3 %collective-permute-done.11.refs_2_ = bf16[128,1024]{1,0:T(8,128)(2,1)S(1)} collective-permute-done((bf16[128,1024]{1,0:T(8,128)(2,1)S(1)}, bf16[128,1024]{1,0:T(8,128)(2,1)S(1)}, u32[]{:S(2)}, u32[]{:S(2)}) %collective-permute-start.11) | collective-permute-done | bytes 262176 | tf_op jit(solution)/shard_map/ppermute | solution.py:338
  31.9 0.7 %attend.5 = (bf16[40,1024]{1,0:T(8,128)(2,1)S(1)}, bf16[40,1024]{1,0:T(8,128)(2,1)S(1)}, bf16[40,1024]{1,0:T(8,128)(2,1)S(1)}, bf16[40,1024]{1,0:T(8,128)(2,1)S(1)}) custom-call(bf16[128,1024]{1,0:T(8,128)(2,1)S(1)} %get-tuple-element.59.refs_0_, bf16[128,1024]{1,0:T(8,128)(2,1)S(1)} %collective-permute-done.5.refs_1_, ...), custom_call_target="tpu_custom_call" | custom-call | flops 1 | bytes 1 | tf_op jit(solution)/shard_map/attend/pallas_call | solution.py:194
  32.7 1.3 %collective-permute-start.12 = (bf16[40,1024]{1,0:T(8,128)(2,1)S(1)}, bf16[40,1024]{1,0:T(8,128)(2,1)S(1)}, u32[]{:S(2)}, u32[]{:S(2)}) collective-permute-start(bf16[40,1024]{1,0:T(8,128)(2,1)S(1)} %get-tuple-element.61), channel_id=1, source_target_pairs={{0,6},{2,4},{4,2},{6,0},{1,7},{3,5},{5,3},{7,1},{8,14},{10,12},{12... | collective-permute-start | bytes 245768 | tf_op jit(solution)/shard_map/ppermute | solution.py:63
  34.0 0.0 collective-permute-done.10.refs_3_
  34.0 1.2 %collective-permute-start.13 = (bf16[40,1024]{1,0:T(8,128)(2,1)S(1)}, bf16[40,1024]{1,0:T(8,128)(2,1)S(1)}, u32[]{:S(2)}, u32[]{:S(2)}) collective-permute-start(bf16[40,1024]{1,0:T(8,128)(2,1)S(1)} %get-tuple-element.62), channel_id=1, source_target_pairs={{0,2},{2,0},{4,6},{6,4},{1,3},{3,1},{5,7},{7,5},{8,10},{10,8},{12,... | collective-permute-start | bytes 245768 | tf_op jit(solution)/shard_map/ppermute | solution.py:63
  35.2 0.0 collective-permute-done.8.refs_1_
  35.2 0.2 collective-permute-start.14
  35.4 0.0 collective-permute-done.9.refs_2_
  35.4 0.4 place.4
  35.8 1.4 %collective-permute-done.12.refs_1_ = bf16[40,1024]{1,0:T(8,128)(2,1)S(1)} collective-permute-done((bf16[40,1024]{1,0:T(8,128)(2,1)S(1)}, bf16[40,1024]{1,0:T(8,128)(2,1)S(1)}, u32[]{:S(2)}, u32[]{:S(2)}) %collective-permute-start.12) | collective-permute-done | bytes 81952 | tf_op jit(solution)/shard_map/ppermute | solution.py:63
  37.2 0.6 %collective-permute-done.13.refs_2_ = bf16[40,1024]{1,0:T(8,128)(2,1)S(1)} collective-permute-done((bf16[40,1024]{1,0:T(8,128)(2,1)S(1)}, bf16[40,1024]{1,0:T(8,128)(2,1)S(1)}, u32[]{:S(2)}, u32[]{:S(2)}) %collective-permute-start.13) | collective-permute-done | bytes 81952 | tf_op jit(solution)/shard_map/ppermute | solution.py:63
  37.9 0.6 %collective-permute-done.14.refs_3_ = bf16[40,1024]{1,0:T(8,128)(2,1)S(1)} collective-permute-done((bf16[40,1024]{1,0:T(8,128)(2,1)S(1)}, bf16[40,1024]{1,0:T(8,128)(2,1)S(1)}, u32[]{:S(2)}, u32[]{:S(2)}) %collective-permute-start.14) | collective-permute-done | bytes 81952 | tf_op jit(solution)/shard_map/ppermute | solution.py:63
  38.5 0.0 collective-permute-done.6.refs_8_.refs_1_
  38.5 0.0 copy-start.5
  38.5 0.4 place.5
  38.9 7.8 %collective-permute-start.15 = (f32[128,128]{1,0:T(8,128)S(1)}, f32[128,128]{1,0:T(8,128)S(1)}, u32[]{:S(2)}, u32[]{:S(2)}) collective-permute-start(f32[128,128]{1,0:T(8,128)S(1)} %get-tuple-element.66.refs_4_), channel_id=1, source_target_pairs={{0,1},{1,0},{2,3},{3,2},{4,5},{5,4},{6,7},{7,6},{8,9},{9,8},{10,11... | collective-permute-start | bytes 196616 | tf_op jit(solution)/shard_map/ppermute | solution.py:359
  46.7 0.0 copy-done.5
  46.7 0.9 %collective-permute-done.15.refs_5_ = f32[128,128]{1,0:T(8,128)S(1)} collective-permute-done((f32[128,128]{1,0:T(8,128)S(1)}, f32[128,128]{1,0:T(8,128)S(1)}, u32[]{:S(2)}, u32[]{:S(2)}) %collective-permute-start.15) | collective-permute-done | bytes 65568 | tf_op jit(solution)/shard_map/ppermute | solution.py:359
  47.6 1.2 %norm.1 = bf16[128,4096]{1,0:T(8,128)(2,1)} custom-call(bf16[128,1024]{1,0:T(8,128)(2,1)S(1)} %get-tuple-element.48.refs_0_, bf16[128,1024]{1,0:T(8,128)(2,1)S(1)} %collective-permute-done.6.refs_8_.refs_1_, bf16[128,1024]{1,0:T(8,128)(2,1)S(1)} %get-tuple-element.58.refs_2_, bf16[128,1024]{1,0:T(8,128)(2,1)S(1)} %get-tuple-element.65.refs_3_, ...), custom_call_target="tpu_custom_call" | custom-call | flops 1 | bytes 1 | tf_op jit(solution)/shard_map/norm/pallas_call | solution.py:306
  (1 shorter events, 0.0 us)
Async XLA Ops:
  0.0 8.3 %collective-permute-start.4 = (bf16[128,1024]{1,0:T(8,128)(2,1)}, bf16[128,1024]{1,0:T(8,128)(2,1)S(1)}, u32[]{:S(2)}, u32[]{:S(2)}) collective-permute-start(bf16[128,1024]{1,0:T(8,128)(2,1)} %bitcast.8), channel_id=1, source_target_pairs={{0,8},{8,24},{24,16},{16,0},{1,9},{9,25},{25,17},{17,1},{2,10},{10... | collective-permute-start | bytes 786440 | tf_op jit(solution)/shard_map/ppermute | solution.py:334
  0.2 1.1 %copy-start.2 = (bf16[128,1,1,1024]{3,0,2,1:T(8,128)(2,1)S(1)}, bf16[128,1,1,1024]{3,0,2,1:T(8,128)(2,1)}, u32[]{:S(2)}) copy-start(bf16[128,1,1,1024]{3,0,2,1:T(8,128)(2,1)} %param.8) | copy-start | bytes 786436
  1.2 12.7 %collective-permute-start = (bf16[128,1024]{1,0:T(8,128)(2,1)S(1)}, bf16[128,1024]{1,0:T(8,128)(2,1)S(1)}, u32[]{:S(2)}, u32[]{:S(2)}) collective-permute-start(bf16[128,1024]{1,0:T(8,128)(2,1)S(1)} %dynamic-slice_bitcast_fusion), channel_id=1, source_target_pairs={{0,8},{8,24},{24,16},{16,0},{1,9},{9,25},{25,17},{17,1},{2,10},{10... | collective-permute-start | bytes 786440 | tf_op jit(solution)/shard_map/ppermute | solution.py:335
  1.3 18.2 %collective-permute-start.7 = (bf16[128,1024]{1,0:T(8,128)(2,1)S(1)}, bf16[128,1024]{1,0:T(8,128)(2,1)S(1)}, u32[]{:S(2)}, u32[]{:S(2)}) collective-permute-start(bf16[128,1024]{1,0:T(8,128)(2,1)S(1)} %bitcast.11), channel_id=1, source_target_pairs={{0,8},{8,24},{24,16},{16,0},{1,9},{9,25},{25,17},{17,1},{2,10},{10... | collective-permute-start | bytes 786440 | tf_op jit(solution)/shard_map/ppermute | solution.py:334
  8.3 16.9 %collective-permute-start.5 = (bf16[128,1024]{1,0:T(8,128)(2,1)S(1)}, bf16[128,1024]{1,0:T(8,128)(2,1)S(1)}, u32[]{:S(2)}, u32[]{:S(2)}) collective-permute-start(bf16[128,1024]{1,0:T(8,128)(2,1)S(1)} %collective-permute-done.4.refs_1_), channel_id=1, source_target_pairs={{0,8},{8,24},{24,16},{16,0},{1,9},{9,25},{25,17},{17,1},{2,10},{10... | collective-permute-start | bytes 786440 | tf_op jit(solution)/shard_map/ppermute | solution.py:338
  8.3 1.2 %copy-start = (bf16[1,128,4096]{2,1,0:T(8,128)(2,1)S(1)}, bf16[1,128,4096]{2,1,0:T(8,128)(2,1)}, u32[]{:S(2)}) copy-start(bf16[1,128,4096]{2,1,0:T(8,128)(2,1)} %param.6) | copy-start | bytes 3145732
  9.5 0.7 %copy-start.3 = (s32[4,4]{1,0:T(4,128)S(1)}, s32[4,4]{1,0:T(4,128)}, u32[]{:S(2)}) copy-start(s32[4,4]{1,0:T(4,128)} %counts.1) | copy-start | bytes 196
  9.5 0.7 %copy-start.4 = (s32[1,6]{1,0:T(1,128)S(1)}, s32[1,6]{1,0:T(1,128)}, u32[]{:S(2)}) copy-start(s32[1,6]{1,0:T(1,128)} %docs.1) | copy-start | bytes 76
  9.5 4.4 %copy-start.1 = (bf16[128,1,1,1024]{3,0,2,1:T(8,128)(2,1)S(1)}, bf16[128,1,1,1024]{3,0,2,1:T(8,128)(2,1)}, u32[]{:S(2)}) copy-start(bf16[128,1,1,1024]{3,0,2,1:T(8,128)(2,1)} %param.7) | copy-start | bytes 786436
  15.0 5.4 %collective-permute-start.1 = (bf16[40,2048]{1,0:T(8,128)(2,1)S(1)}, bf16[40,2048]{1,0:T(8,128)(2,1)S(1)}, u32[]{:S(2)}, u32[]{:S(2)}) collective-permute-start(bf16[40,2048]{1,0:T(8,128)(2,1)S(1)} %get-tuple-element.41), channel_id=1, source_target_pairs={{0,6},{2,4},{4,2},{6,0},{1,7},{3,5},{5,3},{7,1},{8,14},{10,12},{12... | collective-permute-start | bytes 491528 | tf_op jit(solution)/shard_map/ppermute | solution.py:63
  16.3 6.3 %collective-permute-start.2 = (bf16[40,2048]{1,0:T(8,128)(2,1)S(1)}, bf16[40,2048]{1,0:T(8,128)(2,1)S(1)}, u32[]{:S(2)}, u32[]{:S(2)}) collective-permute-start(bf16[40,2048]{1,0:T(8,128)(2,1)S(1)} %get-tuple-element.42), channel_id=1, source_target_pairs={{0,2},{2,0},{4,6},{6,4},{1,3},{3,1},{5,7},{7,5},{8,10},{10,8},{12,... | collective-permute-start | bytes 491528 | tf_op jit(solution)/shard_map/ppermute | solution.py:63
  17.5 5.0 %collective-permute-start.3 = (bf16[40,2048]{1,0:T(8,128)(2,1)S(1)}, bf16[40,2048]{1,0:T(8,128)(2,1)S(1)}, u32[]{:S(2)}, u32[]{:S(2)}) collective-permute-start(bf16[40,2048]{1,0:T(8,128)(2,1)S(1)} %get-tuple-element.43), channel_id=1, source_target_pairs={{0,4},{2,6},{4,0},{6,2},{1,5},{3,7},{5,1},{7,3},{8,12},{10,14},{12... | collective-permute-start | bytes 491528 | tf_op jit(solution)/shard_map/ppermute | solution.py:63
  19.5 12.4 %collective-permute-start.11 = (bf16[128,1024]{1,0:T(8,128)(2,1)S(1)}, bf16[128,1024]{1,0:T(8,128)(2,1)S(1)}, u32[]{:S(2)}, u32[]{:S(2)}) collective-permute-start(bf16[128,1024]{1,0:T(8,128)(2,1)S(1)} %collective-permute-done.7.refs_2_), channel_id=1, source_target_pairs={{0,8},{8,24},{24,16},{16,0},{1,9},{9,25},{25,17},{17,1},{2,10},{10... | collective-permute-start | bytes 786440 | tf_op jit(solution)/shard_map/ppermute | solution.py:338
  25.1 13.3 %collective-permute-start.6 = (bf16[128,1024]{1,0:T(8,128)(2,1)S(1)}, bf16[128,1024]{1,0:T(8,128)(2,1)S(1)}, u32[]{:S(2)}, u32[]{:S(2)}) collective-permute-start(bf16[128,1024]{1,0:T(8,128)(2,1)S(1)} %get-tuple-element.50), channel_id=1, source_target_pairs={{8,0},{24,8},{16,24},{0,16},{9,1},{25,9},{17,25},{1,17},{10,2},{26... | collective-permute-start | bytes 786440 | tf_op jit(solution)/shard_map/ppermute | solution.py:349
  25.9 8.1 %collective-permute-start.10 = (bf16[40,1024]{1,0:T(8,128)(2,1)S(1)}, bf16[40,1024]{1,0:T(8,128)(2,1)S(1)}, u32[]{:S(2)}, u32[]{:S(2)}) collective-permute-start(bf16[40,1024]{1,0:T(8,128)(2,1)S(1)} %get-tuple-element.56), channel_id=1, source_target_pairs={{0,4},{2,6},{4,0},{6,2},{1,5},{3,7},{5,1},{7,3},{8,12},{10,14},{12... | collective-permute-start | bytes 245768 | tf_op jit(solution)/shard_map/ppermute | solution.py:63
  27.2 8.0 %collective-permute-start.8 = (bf16[40,1024]{1,0:T(8,128)(2,1)S(1)}, bf16[40,1024]{1,0:T(8,128)(2,1)S(1)}, u32[]{:S(2)}, u32[]{:S(2)}) collective-permute-start(bf16[40,1024]{1,0:T(8,128)(2,1)S(1)} %get-tuple-element.54), channel_id=1, source_target_pairs={{0,6},{2,4},{4,2},{6,0},{1,7},{3,5},{5,3},{7,1},{8,14},{10,12},{12... | collective-permute-start | bytes 245768 | tf_op jit(solution)/shard_map/ppermute | solution.py:63
  27.4 8.0 %collective-permute-start.9 = (bf16[40,1024]{1,0:T(8,128)(2,1)S(1)}, bf16[40,1024]{1,0:T(8,128)(2,1)S(1)}, u32[]{:S(2)}, u32[]{:S(2)}) collective-permute-start(bf16[40,1024]{1,0:T(8,128)(2,1)S(1)} %get-tuple-element.55), channel_id=1, source_target_pairs={{0,2},{2,0},{4,6},{6,4},{1,3},{3,1},{5,7},{7,5},{8,10},{10,8},{12,... | collective-permute-start | bytes 245768 | tf_op jit(solution)/shard_map/ppermute | solution.py:63
  32.7 4.6 %collective-permute-start.12 = (bf16[40,1024]{1,0:T(8,128)(2,1)S(1)}, bf16[40,1024]{1,0:T(8,128)(2,1)S(1)}, u32[]{:S(2)}, u32[]{:S(2)}) collective-permute-start(bf16[40,1024]{1,0:T(8,128)(2,1)S(1)} %get-tuple-element.61), channel_id=1, source_target_pairs={{0,6},{2,4},{4,2},{6,0},{1,7},{3,5},{5,3},{7,1},{8,14},{10,12},{12... | collective-permute-start | bytes 245768 | tf_op jit(solution)/shard_map/ppermute | solution.py:63
  34.0 3.9 %collective-permute-start.13 = (bf16[40,1024]{1,0:T(8,128)(2,1)S(1)}, bf16[40,1024]{1,0:T(8,128)(2,1)S(1)}, u32[]{:S(2)}, u32[]{:S(2)}) collective-permute-start(bf16[40,1024]{1,0:T(8,128)(2,1)S(1)} %get-tuple-element.62), channel_id=1, source_target_pairs={{0,2},{2,0},{4,6},{6,4},{1,3},{3,1},{5,7},{7,5},{8,10},{10,8},{12,... | collective-permute-start | bytes 245768 | tf_op jit(solution)/shard_map/ppermute | solution.py:63
  35.2 3.3 %collective-permute-start.14 = (bf16[40,1024]{1,0:T(8,128)(2,1)S(1)}, bf16[40,1024]{1,0:T(8,128)(2,1)S(1)}, u32[]{:S(2)}, u32[]{:S(2)}) collective-permute-start(bf16[40,1024]{1,0:T(8,128)(2,1)S(1)} %get-tuple-element.63), channel_id=1, source_target_pairs={{0,4},{2,6},{4,0},{6,2},{1,5},{3,7},{5,1},{7,3},{8,12},{10,14},{12... | collective-permute-start | bytes 245768 | tf_op jit(solution)/shard_map/ppermute | solution.py:63
  38.5 8.2 %copy-start.5 = (bf16[4096]{0:T(1024)(128)(2,1)S(1)}, bf16[4096]{0:T(1024)(128)(2,1)}, u32[]{:S(2)}) copy-start(bf16[4096]{0:T(1024)(128)(2,1)} %param.11) | copy-start | bytes 24580
  38.9 8.7 %collective-permute-start.15 = (f32[128,128]{1,0:T(8,128)S(1)}, f32[128,128]{1,0:T(8,128)S(1)}, u32[]{:S(2)}, u32[]{:S(2)}) collective-permute-start(f32[128,128]{1,0:T(8,128)S(1)} %get-tuple-element.66.refs_4_), channel_id=1, source_target_pairs={{0,1},{1,0},{2,3},{3,2},{4,5},{5,4},{6,7},{7,6},{8,9},{9,8},{10,11... | collective-permute-start | bytes 196616 | tf_op jit(solution)/shard_map/ppermute | solution.py:359

commit v4 on v3

--- a/solution.py
+++ b/solution.py
@@ -329,14 +329,10 @@
 
     begin = pick(lax.axis_index("pipe"), plan.behind[n - 1]) * block
     ahead = lax.dynamic_slice_in_dim(query, begin, block, 1)
-    ahead, values_out = lax.optimization_barrier((ahead, values))
+    lent = lax.ppermute(ahead, "pipe", forward)
     pairs = [(keys, values)]
-    k, v = lax.ppermute(keys, "pipe", forward), lax.ppermute(values_out, "pipe", forward)
-    lent = lax.ppermute(ahead, "pipe", forward)
-    for _ in range(n - 3):
-        pairs.append((k, v))
-        k, v = lax.ppermute(k, "pipe", forward), lax.ppermute(v, "pipe", forward)
-    pairs.append((k, v))
+    for _ in range(n - 2):
+        pairs.append(tuple(lax.ppermute(x, "pipe", forward) for x in pairs[-1]))
 
     asked = split(plan, query)
     bias, send, places = tables(plan, doc_lengths, row_counts)
@@ -345,16 +341,14 @@
     got = [plan.regroup(run([jobs[0], (lent, keys, values, 0, 0, 0, block)]))]
     got += [plan.regroup(run([job])) for job in jobs[1:]]
     mine, borrowed, total = place(plan, got[0], places, (block, block), summed=1)
-    borrowed, _ = lax.optimization_barrier((borrowed, pairs[-1][0]))
+    pieces = [(mine, 0, 0)]
+    for t, parts in enumerate(got[1:-1], 1):
+        placed, total = place(plan, parts, places, (block,), sums=(total,))
+        pieces.append((placed, t, 0))
+    borrowed, total, *_ = lax.optimization_barrier((borrowed, total, *pairs[-1]))
     returned = lax.ppermute(borrowed, "pipe", backward)
-
-    pieces = [(mine, 0, 0), (returned, n - 1, 0)]
-    for t, parts in enumerate(got[1:], 1):
-        last = t == n - 2
-        placed, total = place(
-            plan, parts, places, (block,), blocks=(returned,) if last else (), sums=(total,)
-        )
-        pieces.append((placed, t, 0))
+    placed, total = place(plan, got[-1], places, (block,), blocks=(returned,), sums=(total,))
+    pieces += [(placed, n - 2, 0), (returned, n - 1, 0)]
     if plan.tensor == 2:
         sums = (total, lax.ppermute(total, "tensor", [(0, 1), (1, 0)]))
     else:

time: 49 us -> 52.8 us (1.078)
  the two profiles are of different devices: /device:TPU:27 before, /device:TPU:0 now
where the time goes in v4:
time: 52.8 us; the launch traced here: 52.6 us
  starting transfers between devices  22.4 us (42%)
  waiting for transfers between devices  21 us (40%)
  Pallas kernels  6.1 us (12%)
  local copies, waits for them, and re-layouts  2.95 us (6%)
    ppermute x9, starting transfers between devices, regroup(): lax.ppermute(part, 'dp', [(g, g ^ step) for g in range(self.groups)])  11.6 us
    ppermute x4, starting transfers between devices, body(): pairs.append(tuple((lax.ppermute(x, 'pipe', forward) for x in pairs[-1])))  10.1 us
    ppermute x9, waiting for transfers between devices, regroup(): lax.ppermute(part, 'dp', [(g, g ^ step) for g in range(self.groups)])  10 us
    ppermute x4, waiting for transfers between devices, body(): pairs.append(tuple((lax.ppermute(x, 'pipe', forward) for x in pairs[-1])))  9.92 us
    pallas_call x3, Pallas kernels, attend(): pl.pallas_call(functools.partial(attend_kernel, plan, spans), out_shape=[...  2.61 us
    unnamed x12, local copies, waits for them, and re-layouts  1.98 us
    pallas_call x3, Pallas kernels, place(): pl.pallas_call(functools.partial(place_kernel, plan, widths, summed, len(...  1.52 us
    pallas_call x1, Pallas kernels, norm(): pl.pallas_call(functools.partial(norm_kernel, plan, spots, len(squares)),...  1.18 us
  transfers between devices with their start and end apart: 16, of which 8 were waited for; matrix products, arithmetic and copies ran while one was open for 2% of the time, Pallas kernels for 9%

profile of v4, /device:TPU:0, one launch (start us, length us, event | category | flops | bytes accessed | tf_op | source)
XLA Modules:
  0.0 52.6 jit_solution(439018714194139292)
XLA Ops:
  0.0 3.0 %collective-permute-start.4 = (bf16[128,1024]{1,0:T(8,128)(2,1)}, bf16[128,1024]{1,0:T(8,128)(2,1)S(1)}, u32[]{:S(2)}, u32[]{:S(2)}) collective-permute-start(bf16[128,1024]{1,0:T(8,128)(2,1)} %bitcast.8), channel_id=1, source_target_pairs={{0,8},{8,24},{24,16},{16,0},{1,9},{9,25},{25,17},{17,1},{2,10},{10... | collective-permute-start | bytes 786440 | tf_op jit(solution)/shard_map/ppermute | solution.py:335
  3.0 2.6 %collective-permute-start.5 = (bf16[128,1024]{1,0:T(8,128)(2,1)}, bf16[128,1024]{1,0:T(8,128)(2,1)S(1)}, u32[]{:S(2)}, u32[]{:S(2)}) collective-permute-start(bf16[128,1024]{1,0:T(8,128)(2,1)} %bitcast.11), channel_id=1, source_target_pairs={{0,8},{8,24},{24,16},{16,0},{1,9},{9,25},{25,17},{17,1},{2,10},{10... | collective-permute-start | bytes 786440 | tf_op jit(solution)/shard_map/ppermute | solution.py:335
  5.6 1.0 %dynamic-slice_bitcast_fusion = bf16[128,1024]{1,0:T(8,128)(2,1)S(1)} fusion(bf16[1,128,4096]{2,1,0:T(8,128)(2,1)} %param.6, s32[]{:T(128)S(6)} %select_n.16), kind=kLoop, calls=%fused_computation | loop fusion | bytes 524292 | tf_op jit(solution)/shard_map/dynamic_slice | solution.py:331
  6.6 0.5 collective-permute-start
  7.1 9.9 %collective-permute-done.5.refs_2_ = bf16[128,1024]{1,0:T(8,128)(2,1)S(1)} collective-permute-done((bf16[128,1024]{1,0:T(8,128)(2,1)}, bf16[128,1024]{1,0:T(8,128)(2,1)S(1)}, u32[]{:S(2)}, u32[]{:S(2)}) %collective-permute-start.5) | collective-permute-done | bytes 262176 | tf_op jit(solution)/shard_map/ppermute | solution.py:335
  17.0 1.3 %collective-permute-start.10 = (bf16[128,1024]{1,0:T(8,128)(2,1)S(1)}, bf16[128,1024]{1,0:T(8,128)(2,1)S(1)}, u32[]{:S(2)}, u32[]{:S(2)}) collective-permute-start(bf16[128,1024]{1,0:T(8,128)(2,1)S(1)} %collective-permute-done.5.refs_2_), channel_id=1, source_target_pairs={{0,8},{8,24},{24,16},{16,0},{1,9},{9,25},{25,17},{17,1},{2,10},{10... | collective-permute-start | bytes 786440 | tf_op jit(solution)/shard_map/ppermute | solution.py:335
  18.3 0.0 collective-permute-done.4.refs_1_
  18.3 3.3 %collective-permute-start.9 = (bf16[128,1024]{1,0:T(8,128)(2,1)S(1)}, bf16[128,1024]{1,0:T(8,128)(2,1)S(1)}, u32[]{:S(2)}, u32[]{:S(2)}) collective-permute-start(bf16[128,1024]{1,0:T(8,128)(2,1)S(1)} %collective-permute-done.4.refs_1_), channel_id=1, source_target_pairs={{0,8},{8,24},{24,16},{16,0},{1,9},{9,25},{25,17},{17,1},{2,10},{10... | collective-permute-start | bytes 786440 | tf_op jit(solution)/shard_map/ppermute | solution.py:335
  21.5 0.0 copy-start
  21.5 1.2 %copy-done = bf16[1,128,4096]{2,1,0:T(8,128)(2,1)S(1)} copy-done((bf16[1,128,4096]{2,1,0:T(8,128)(2,1)S(1)}, bf16[1,128,4096]{2,1,0:T(8,128)(2,1)}, u32[]{:S(2)}) %copy-start) | copy-done | bytes 1048600
  22.8 0.0 copy-start.3
  22.8 0.0 copy-start.4
  22.8 0.0 copy-start.1
  22.8 0.0 copy-start.2
  22.8 0.1 split.1
  22.9 0.6 %copy-done.3 = s32[4,4]{1,0:T(4,128)S(1)} copy-done((s32[4,4]{1,0:T(4,128)S(1)}, s32[4,4]{1,0:T(4,128)}, u32[]{:S(2)}) %copy-start.3) | copy-done | bytes 88
  23.4 0.0 copy-done.4
  23.4 0.7 %tables.1 = (f32[128,128]{1,0:T(8,128)S(1)}, bf16[160,128]{1,0:T(8,128)(2,1)S(1)}, bf16[128,40]{1,0:T(8,128)(2,1)S(1)}, bf16[128,40]{1,0:T(8,128)(2,1)S(1)}, bf1...) custom-call(s32[1,6]{1,0:T(1,128)S(1)} %copy-done.4, s32[4,4]{1,0:T(4,128)S(1)} %copy-done.3), custom_call_target="tpu_custom_call" | custom-call | flops 1 | bytes 1 | tf_op jit(solution)/shard_map/tables/pallas_call | solution.py:136
  24.1 0.0 collective-permute-done.refs_3_
  24.1 0.0 copy-done.1
  24.2 0.0 copy-done.2
  24.2 1.1 %attend.3 = (bf16[40,2048]{1,0:T(8,128)(2,1)S(1)}, bf16[40,2048]{1,0:T(8,128)(2,1)S(1)}, bf16[40,2048]{1,0:T(8,128)(2,1)S(1)}, bf16[40,2048]{1,0:T(8,128)(2,1)S(1)}) custom-call(bf16[128,1024]{1,0:T(8,128)(2,1)S(1)} %get-tuple-element.35.refs_0_, bf16[128,1024]{1,0:T(8,128)(2,1)S(1)} %bitcast.9, bf16[128,1024]{1,0:T(8,128)(2,1)S(1)} %bitcast.12, ...), custom_call_target="tpu_custom_call" | custom-call | flops 1 | bytes 1 | tf_op jit(solution)/shard_map/attend/pallas_call | solution.py:194
  25.3 2.5 %collective-permute-start.1 = (bf16[40,2048]{1,0:T(8,128)(2,1)S(1)}, bf16[40,2048]{1,0:T(8,128)(2,1)S(1)}, u32[]{:S(2)}, u32[]{:S(2)}) collective-permute-start(bf16[40,2048]{1,0:T(8,128)(2,1)S(1)} %get-tuple-element.39), channel_id=1, source_target_pairs={{0,6},{2,4},{4,2},{6,0},{1,7},{3,5},{5,3},{7,1},{8,14},{10,12},{12... | collective-permute-start | bytes 491528 | tf_op jit(solution)/shard_map/ppermute | solution.py:63
  27.8 0.5 %collective-permute-start.2 = (bf16[40,2048]{1,0:T(8,128)(2,1)S(1)}, bf16[40,2048]{1,0:T(8,128)(2,1)S(1)}, u32[]{:S(2)}, u32[]{:S(2)}) collective-permute-start(bf16[40,2048]{1,0:T(8,128)(2,1)S(1)} %get-tuple-element.40), channel_id=1, source_target_pairs={{0,2},{2,0},{4,6},{6,4},{1,3},{3,1},{5,7},{7,5},{8,10},{10,8},{12,... | collective-permute-start | bytes 491528 | tf_op jit(solution)/shard_map/ppermute | solution.py:63
  28.4 0.5 collective-permute-start.3
  28.9 0.7 %attend.4 = (bf16[40,1024]{1,0:T(8,128)(2,1)S(1)}, bf16[40,1024]{1,0:T(8,128)(2,1)S(1)}, bf16[40,1024]{1,0:T(8,128)(2,1)S(1)}, bf16[40,1024]{1,0:T(8,128)(2,1)S(1)}) custom-call(bf16[128,1024]{1,0:T(8,128)(2,1)S(1)} %get-tuple-element.47.refs_0_, bf16[128,1024]{1,0:T(8,128)(2,1)S(1)} %collective-permute-done.4.refs_1_, ...), custom_call_target="tpu_custom_call" | custom-call | flops 1 | bytes 1 | tf_op jit(solution)/shard_map/attend/pallas_call | solution.py:194
  29.6 2.0 %collective-permute-done.1.refs_1_ = bf16[40,2048]{1,0:T(8,128)(2,1)S(1)} collective-permute-done((bf16[40,2048]{1,0:T(8,128)(2,1)S(1)}, bf16[40,2048]{1,0:T(8,128)(2,1)S(1)}, u32[]{:S(2)}, u32[]{:S(2)}) %collective-permute-start.1) | collective-permute-done | bytes 163872 | tf_op jit(solution)/shard_map/ppermute | solution.py:63
  31.6 2.5 %collective-permute-start.6 = (bf16[40,1024]{1,0:T(8,128)(2,1)S(1)}, bf16[40,1024]{1,0:T(8,128)(2,1)S(1)}, u32[]{:S(2)}, u32[]{:S(2)}) collective-permute-start(bf16[40,1024]{1,0:T(8,128)(2,1)S(1)} %get-tuple-element.49), channel_id=1, source_target_pairs={{0,6},{2,4},{4,2},{6,0},{1,7},{3,5},{5,3},{7,1},{8,14},{10,12},{12... | collective-permute-start | bytes 245768 | tf_op jit(solution)/shard_map/ppermute | solution.py:63
  34.2 1.0 %collective-permute-done.2.refs_2_ = bf16[40,2048]{1,0:T(8,128)(2,1)S(1)} collective-permute-done((bf16[40,2048]{1,0:T(8,128)(2,1)S(1)}, bf16[40,2048]{1,0:T(8,128)(2,1)S(1)}, u32[]{:S(2)}, u32[]{:S(2)}) %collective-permute-start.2) | collective-permute-done | bytes 163872 | tf_op jit(solution)/shard_map/ppermute | solution.py:63
  35.2 1.5 %collective-permute-start.7 = (bf16[40,1024]{1,0:T(8,128)(2,1)S(1)}, bf16[40,1024]{1,0:T(8,128)(2,1)S(1)}, u32[]{:S(2)}, u32[]{:S(2)}) collective-permute-start(bf16[40,1024]{1,0:T(8,128)(2,1)S(1)} %get-tuple-element.50), channel_id=1, source_target_pairs={{0,2},{2,0},{4,6},{6,4},{1,3},{3,1},{5,7},{7,5},{8,10},{10,8},{12,... | collective-permute-start | bytes 245768 | tf_op jit(solution)/shard_map/ppermute | solution.py:63
  36.7 0.0 collective-permute-done.3.refs_3_
  36.7 0.5 collective-permute-start.8
  37.2 0.7 %place.3 = (bf16[128,1024]{1,0:T(8,128)(2,1)S(1)}, bf16[128,1024]{1,0:T(8,128)(2,1)S(1)}, f32[128,128]{1,0:T(8,128)S(1)}) custom-call(bf16[40,2048]{1,0:T(8,128)(2,1)S(1)} %get-tuple-element.38.refs_0_, bf16[40,2048]{1,0:T(8,128)(2,1)S(1)} %collective-permute-done.1.refs_1_, bf16[40,2048]{1,0:T(8,128)(2,1)S(1)} %collective-permute-done.2.refs_2_, ...), custom_call_target="tpu_custom_call" | custom-call | flops 1 | bytes 1 | tf_op jit(solution)/shard_map/place/pallas_call | solution.py:265
  37.9 0.0 collective-permute-done.6.refs_1_
  37.9 1.7 %collective-permute-done.7.refs_2_ = bf16[40,1024]{1,0:T(8,128)(2,1)S(1)} collective-permute-done((bf16[40,1024]{1,0:T(8,128)(2,1)S(1)}, bf16[40,1024]{1,0:T(8,128)(2,1)S(1)}, u32[]{:S(2)}, u32[]{:S(2)}) %collective-permute-start.7) | collective-permute-done | bytes 81952 | tf_op jit(solution)/shard_map/ppermute | solution.py:63
  39.6 2.4 %collective-permute-done.8.refs_3_ = bf16[40,1024]{1,0:T(8,128)(2,1)S(1)} collective-permute-done((bf16[40,1024]{1,0:T(8,128)(2,1)S(1)}, bf16[40,1024]{1,0:T(8,128)(2,1)S(1)}, u32[]{:S(2)}, u32[]{:S(2)}) %collective-permute-start.8) | collective-permute-done | bytes 81952 | tf_op jit(solution)/shard_map/ppermute | solution.py:63
  42.0 0.4 place.4
  42.4 0.0 collective-permute-done.10.refs_2_
  42.4 0.0 collective-permute-done.9.refs_1_
  42.4 0.1 collective-permute-start.14
  42.5 0.7 %attend.5 = (bf16[40,1024]{1,0:T(8,128)(2,1)S(1)}, bf16[40,1024]{1,0:T(8,128)(2,1)S(1)}, bf16[40,1024]{1,0:T(8,128)(2,1)S(1)}, bf16[40,1024]{1,0:T(8,128)(2,1)S(1)}) custom-call(bf16[128,1024]{1,0:T(8,128)(2,1)S(1)} %get-tuple-element.54.refs_0_, bf16[128,1024]{1,0:T(8,128)(2,1)S(1)} %collective-permute-done.9.refs_1_, ...), custom_call_target="tpu_custom_call" | custom-call | flops 1 | bytes 1 | tf_op jit(solution)/shard_map/attend/pallas_call | solution.py:194
  43.2 0.9 %collective-permute-start.11 = (bf16[40,1024]{1,0:T(8,128)(2,1)S(1)}, bf16[40,1024]{1,0:T(8,128)(2,1)S(1)}, u32[]{:S(2)}, u32[]{:S(2)}) collective-permute-start(bf16[40,1024]{1,0:T(8,128)(2,1)S(1)} %get-tuple-element.56), channel_id=1, source_target_pairs={{0,6},{2,4},{4,2},{6,0},{1,7},{3,5},{5,3},{7,1},{8,14},{10,12},{12... | collective-permute-start | bytes 245768 | tf_op jit(solution)/shard_map/ppermute | solution.py:63
  44.2 1.1 %collective-permute-start.12 = (bf16[40,1024]{1,0:T(8,128)(2,1)S(1)}, bf16[40,1024]{1,0:T(8,128)(2,1)S(1)}, u32[]{:S(2)}, u32[]{:S(2)}) collective-permute-start(bf16[40,1024]{1,0:T(8,128)(2,1)S(1)} %get-tuple-element.57), channel_id=1, source_target_pairs={{0,2},{2,0},{4,6},{6,4},{1,3},{3,1},{5,7},{7,5},{8,10},{10,8},{12,... | collective-permute-start | bytes 245768 | tf_op jit(solution)/shard_map/ppermute | solution.py:63
  45.2 1.6 %collective-permute-start.13 = (bf16[40,1024]{1,0:T(8,128)(2,1)S(1)}, bf16[40,1024]{1,0:T(8,128)(2,1)S(1)}, u32[]{:S(2)}, u32[]{:S(2)}) collective-permute-start(bf16[40,1024]{1,0:T(8,128)(2,1)S(1)} %get-tuple-element.58), channel_id=1, source_target_pairs={{0,4},{2,6},{4,0},{6,2},{1,5},{3,7},{5,1},{7,3},{8,12},{10,14},{12... | collective-permute-start | bytes 245768 | tf_op jit(solution)/shard_map/ppermute | solution.py:63
  46.8 1.9 %collective-permute-done.11.refs_1_ = bf16[40,1024]{1,0:T(8,128)(2,1)S(1)} collective-permute-done((bf16[40,1024]{1,0:T(8,128)(2,1)S(1)}, bf16[40,1024]{1,0:T(8,128)(2,1)S(1)}, u32[]{:S(2)}, u32[]{:S(2)}) %collective-permute-start.11) | collective-permute-done | bytes 81952 | tf_op jit(solution)/shard_map/ppermute | solution.py:63
  48.6 0.0 collective-permute-done.12.refs_2_
  48.6 1.0 %collective-permute-done.13.refs_3_ = bf16[40,1024]{1,0:T(8,128)(2,1)S(1)} collective-permute-done((bf16[40,1024]{1,0:T(8,128)(2,1)S(1)}, bf16[40,1024]{1,0:T(8,128)(2,1)S(1)}, u32[]{:S(2)}, u32[]{:S(2)}) %collective-permute-start.13) | collective-permute-done | bytes 81952 | tf_op jit(solution)/shard_map/ppermute | solution.py:63
  49.7 0.0 collective-permute-done.14.refs_8_.refs_3_
  49.7 0.0 copy-start.5
  49.7 0.4 place.5
  50.1 0.1 collective-permute-start.15
  50.2 0.2 copy-done.5
  50.4 1.0 %collective-permute-done.15.refs_5_ = f32[128,128]{1,0:T(8,128)S(1)} collective-permute-done((f32[128,128]{1,0:T(8,128)S(1)}, f32[128,128]{1,0:T(8,128)S(1)}, u32[]{:S(2)}, u32[]{:S(2)}) %collective-permute-start.15) | collective-permute-done | bytes 65568 | tf_op jit(solution)/shard_map/ppermute | solution.py:353
  51.4 1.2 %norm.1 = bf16[128,4096]{1,0:T(8,128)(2,1)} custom-call(bf16[128,1024]{1,0:T(8,128)(2,1)S(1)} %get-tuple-element.46.refs_0_, bf16[128,1024]{1,0:T(8,128)(2,1)S(1)} %get-tuple-element.53.refs_1_, bf16[128,1024]{1,0:T(8,128)(2,1)S(1)} %get-tuple-element.63.refs_2_, bf16[128,1024]{1,0:T(8,128)(2,1)S(1)} %collective-permute-done.14.refs_8_.refs_3_, ...), custom_call_target="tpu_custom_call" | custom-call | flops 1 | bytes 1 | tf_op jit(solution)/shard_map/norm/pallas_call | solution.py:306
  (1 shorter events, 0.0 us)
Async XLA Ops:
  0.0 18.3 %collective-permute-start.4 = (bf16[128,1024]{1,0:T(8,128)(2,1)}, bf16[128,1024]{1,0:T(8,128)(2,1)S(1)}, u32[]{:S(2)}, u32[]{:S(2)}) collective-permute-start(bf16[128,1024]{1,0:T(8,128)(2,1)} %bitcast.8), channel_id=1, source_target_pairs={{0,8},{8,24},{24,16},{16,0},{1,9},{9,25},{25,17},{17,1},{2,10},{10... | collective-permute-start | bytes 786440 | tf_op jit(solution)/shard_map/ppermute | solution.py:335
  3.0 14.0 %collective-permute-start.5 = (bf16[128,1024]{1,0:T(8,128)(2,1)}, bf16[128,1024]{1,0:T(8,128)(2,1)S(1)}, u32[]{:S(2)}, u32[]{:S(2)}) collective-permute-start(bf16[128,1024]{1,0:T(8,128)(2,1)} %bitcast.11), channel_id=1, source_target_pairs={{0,8},{8,24},{24,16},{16,0},{1,9},{9,25},{25,17},{17,1},{2,10},{10... | collective-permute-start | bytes 786440 | tf_op jit(solution)/shard_map/ppermute | solution.py:335
  6.6 17.6 %collective-permute-start = (bf16[128,1024]{1,0:T(8,128)(2,1)S(1)}, bf16[128,1024]{1,0:T(8,128)(2,1)S(1)}, u32[]{:S(2)}, u32[]{:S(2)}) collective-permute-start(bf16[128,1024]{1,0:T(8,128)(2,1)S(1)} %dynamic-slice_bitcast_fusion), channel_id=1, source_target_pairs={{0,8},{8,24},{24,16},{16,0},{1,9},{9,25},{25,17},{17,1},{2,10},{10... | collective-permute-start | bytes 786440 | tf_op jit(solution)/shard_map/ppermute | solution.py:332
  17.0 25.4 %collective-permute-start.10 = (bf16[128,1024]{1,0:T(8,128)(2,1)S(1)}, bf16[128,1024]{1,0:T(8,128)(2,1)S(1)}, u32[]{:S(2)}, u32[]{:S(2)}) collective-permute-start(bf16[128,1024]{1,0:T(8,128)(2,1)S(1)} %collective-permute-done.5.refs_2_), channel_id=1, source_target_pairs={{0,8},{8,24},{24,16},{16,0},{1,9},{9,25},{25,17},{17,1},{2,10},{10... | collective-permute-start | bytes 786440 | tf_op jit(solution)/shard_map/ppermute | solution.py:335
  18.3 24.2 %collective-permute-start.9 = (bf16[128,1024]{1,0:T(8,128)(2,1)S(1)}, bf16[128,1024]{1,0:T(8,128)(2,1)S(1)}, u32[]{:S(2)}, u32[]{:S(2)}) collective-permute-start(bf16[128,1024]{1,0:T(8,128)(2,1)S(1)} %collective-permute-done.4.refs_1_), channel_id=1, source_target_pairs={{0,8},{8,24},{24,16},{16,0},{1,9},{9,25},{25,17},{17,1},{2,10},{10... | collective-permute-start | bytes 786440 | tf_op jit(solution)/shard_map/ppermute | solution.py:335
  21.5 1.2 %copy-start = (bf16[1,128,4096]{2,1,0:T(8,128)(2,1)S(1)}, bf16[1,128,4096]{2,1,0:T(8,128)(2,1)}, u32[]{:S(2)}) copy-start(bf16[1,128,4096]{2,1,0:T(8,128)(2,1)} %param.6) | copy-start | bytes 3145732
  22.8 0.7 %copy-start.3 = (s32[4,4]{1,0:T(4,128)S(1)}, s32[4,4]{1,0:T(4,128)}, u32[]{:S(2)}) copy-start(s32[4,4]{1,0:T(4,128)} %counts.1) | copy-start | bytes 196
  22.8 0.7 %copy-start.4 = (s32[1,6]{1,0:T(1,128)S(1)}, s32[1,6]{1,0:T(1,128)}, u32[]{:S(2)}) copy-start(s32[1,6]{1,0:T(1,128)} %docs.1) | copy-start | bytes 76
  22.8 1.4 %copy-start.1 = (bf16[128,1,1,1024]{3,0,2,1:T(8,128)(2,1)S(1)}, bf16[128,1,1,1024]{3,0,2,1:T(8,128)(2,1)}, u32[]{:S(2)}) copy-start(bf16[128,1,1,1024]{3,0,2,1:T(8,128)(2,1)} %param.7) | copy-start | bytes 786436
  22.8 1.4 %copy-start.2 = (bf16[128,1,1,1024]{3,0,2,1:T(8,128)(2,1)S(1)}, bf16[128,1,1,1024]{3,0,2,1:T(8,128)(2,1)}, u32[]{:S(2)}) copy-start(bf16[128,1,1,1024]{3,0,2,1:T(8,128)(2,1)} %param.8) | copy-start | bytes 786436
  25.3 6.3 %collective-permute-start.1 = (bf16[40,2048]{1,0:T(8,128)(2,1)S(1)}, bf16[40,2048]{1,0:T(8,128)(2,1)S(1)}, u32[]{:S(2)}, u32[]{:S(2)}) collective-permute-start(bf16[40,2048]{1,0:T(8,128)(2,1)S(1)} %get-tuple-element.39), channel_id=1, source_target_pairs={{0,6},{2,4},{4,2},{6,0},{1,7},{3,5},{5,3},{7,1},{8,14},{10,12},{12... | collective-permute-start | bytes 491528 | tf_op jit(solution)/shard_map/ppermute | solution.py:63
  27.8 7.3 %collective-permute-start.2 = (bf16[40,2048]{1,0:T(8,128)(2,1)S(1)}, bf16[40,2048]{1,0:T(8,128)(2,1)S(1)}, u32[]{:S(2)}, u32[]{:S(2)}) collective-permute-start(bf16[40,2048]{1,0:T(8,128)(2,1)S(1)} %get-tuple-element.40), channel_id=1, source_target_pairs={{0,2},{2,0},{4,6},{6,4},{1,3},{3,1},{5,7},{7,5},{8,10},{10,8},{12,... | collective-permute-start | bytes 491528 | tf_op jit(solution)/shard_map/ppermute | solution.py:63
  28.4 8.3 %collective-permute-start.3 = (bf16[40,2048]{1,0:T(8,128)(2,1)S(1)}, bf16[40,2048]{1,0:T(8,128)(2,1)S(1)}, u32[]{:S(2)}, u32[]{:S(2)}) collective-permute-start(bf16[40,2048]{1,0:T(8,128)(2,1)S(1)} %get-tuple-element.41), channel_id=1, source_target_pairs={{0,4},{2,6},{4,0},{6,2},{1,5},{3,7},{5,1},{7,3},{8,12},{10,14},{12... | collective-permute-start | bytes 491528 | tf_op jit(solution)/shard_map/ppermute | solution.py:63
  31.6 6.2 %collective-permute-start.6 = (bf16[40,1024]{1,0:T(8,128)(2,1)S(1)}, bf16[40,1024]{1,0:T(8,128)(2,1)S(1)}, u32[]{:S(2)}, u32[]{:S(2)}) collective-permute-start(bf16[40,1024]{1,0:T(8,128)(2,1)S(1)} %get-tuple-element.49), channel_id=1, source_target_pairs={{0,6},{2,4},{4,2},{6,0},{1,7},{3,5},{5,3},{7,1},{8,14},{10,12},{12... | collective-permute-start | bytes 245768 | tf_op jit(solution)/shard_map/ppermute | solution.py:63
  35.2 4.4 %collective-permute-start.7 = (bf16[40,1024]{1,0:T(8,128)(2,1)S(1)}, bf16[40,1024]{1,0:T(8,128)(2,1)S(1)}, u32[]{:S(2)}, u32[]{:S(2)}) collective-permute-start(bf16[40,1024]{1,0:T(8,128)(2,1)S(1)} %get-tuple-element.50), channel_id=1, source_target_pairs={{0,2},{2,0},{4,6},{6,4},{1,3},{3,1},{5,7},{7,5},{8,10},{10,8},{12,... | collective-permute-start | bytes 245768 | tf_op jit(solution)/shard_map/ppermute | solution.py:63
  36.7 5.3 %collective-permute-start.8 = (bf16[40,1024]{1,0:T(8,128)(2,1)S(1)}, bf16[40,1024]{1,0:T(8,128)(2,1)S(1)}, u32[]{:S(2)}, u32[]{:S(2)}) collective-permute-start(bf16[40,1024]{1,0:T(8,128)(2,1)S(1)} %get-tuple-element.51), channel_id=1, source_target_pairs={{0,4},{2,6},{4,0},{6,2},{1,5},{3,7},{5,1},{7,3},{8,12},{10,14},{12... | collective-permute-start | bytes 245768 | tf_op jit(solution)/shard_map/ppermute | solution.py:63
  42.4 7.2 %collective-permute-start.14 = (bf16[128,1024]{1,0:T(8,128)(2,1)S(1)}, bf16[128,1024]{1,0:T(8,128)(2,1)S(1)}, u32[]{:S(2)}, u32[]{:S(2)}) collective-permute-start(bf16[128,1024]{1,0:T(8,128)(2,1)S(1)} %get-tuple-element.61), channel_id=1, source_target_pairs={{8,0},{24,8},{16,24},{0,16},{9,1},{25,9},{17,25},{1,17},{10,2},{26... | collective-permute-start | bytes 786440 | tf_op jit(solution)/shard_map/ppermute | solution.py:349
  43.2 5.4 %collective-permute-start.11 = (bf16[40,1024]{1,0:T(8,128)(2,1)S(1)}, bf16[40,1024]{1,0:T(8,128)(2,1)S(1)}, u32[]{:S(2)}, u32[]{:S(2)}) collective-permute-start(bf16[40,1024]{1,0:T(8,128)(2,1)S(1)} %get-tuple-element.56), channel_id=1, source_target_pairs={{0,6},{2,4},{4,2},{6,0},{1,7},{3,5},{5,3},{7,1},{8,14},{10,12},{12... | collective-permute-start | bytes 245768 | tf_op jit(solution)/shard_map/ppermute | solution.py:63
  44.2 4.5 %collective-permute-start.12 = (bf16[40,1024]{1,0:T(8,128)(2,1)S(1)}, bf16[40,1024]{1,0:T(8,128)(2,1)S(1)}, u32[]{:S(2)}, u32[]{:S(2)}) collective-permute-start(bf16[40,1024]{1,0:T(8,128)(2,1)S(1)} %get-tuple-element.57), channel_id=1, source_target_pairs={{0,2},{2,0},{4,6},{6,4},{1,3},{3,1},{5,7},{7,5},{8,10},{10,8},{12,... | collective-permute-start | bytes 245768 | tf_op jit(solution)/shard_map/ppermute | solution.py:63
  45.2 4.4 %collective-permute-start.13 = (bf16[40,1024]{1,0:T(8,128)(2,1)S(1)}, bf16[40,1024]{1,0:T(8,128)(2,1)S(1)}, u32[]{:S(2)}, u32[]{:S(2)}) collective-permute-start(bf16[40,1024]{1,0:T(8,128)(2,1)S(1)} %get-tuple-element.58), channel_id=1, source_target_pairs={{0,4},{2,6},{4,0},{6,2},{1,5},{3,7},{5,1},{7,3},{8,12},{10,14},{12... | collective-permute-start | bytes 245768 | tf_op jit(solution)/shard_map/ppermute | solution.py:63
  49.7 0.7 %copy-start.5 = (bf16[4096]{0:T(1024)(128)(2,1)S(1)}, bf16[4096]{0:T(1024)(128)(2,1)}, u32[]{:S(2)}) copy-start(bf16[4096]{0:T(1024)(128)(2,1)} %param.11) | copy-start | bytes 24580
  50.1 1.3 %collective-permute-start.15 = (f32[128,128]{1,0:T(8,128)S(1)}, f32[128,128]{1,0:T(8,128)S(1)}, u32[]{:S(2)}, u32[]{:S(2)}) collective-permute-start(f32[128,128]{1,0:T(8,128)S(1)} %get-tuple-element.64.refs_4_), channel_id=1, source_target_pairs={{0,1},{1,0},{2,3},{3,2},{4,5},{5,4},{6,7},{7,6},{8,9},{9,8},{10,11... | collective-permute-start | bytes 196616 | tf_op jit(solution)/shard_map/ppermute | solution.py:353

commit v5 on v4

--- a/solution.py
+++ b/solution.py
@@ -338,16 +338,18 @@
     bias, send, places = tables(plan, doc_lengths, row_counts)
     run = functools.partial(attend, plan, bias=bias, send=send)
     jobs = [(asked[t], *pairs[t], 0, 0, 0, block) for t in range(n - 1)]
-    got = [plan.regroup(run([jobs[0], (lent, keys, values, 0, 0, 0, block)]))]
-    got += [plan.regroup(run([job])) for job in jobs[1:]]
-    mine, borrowed, total = place(plan, got[0], places, (block, block), summed=1)
-    pieces = [(mine, 0, 0)]
-    for t, parts in enumerate(got[1:-1], 1):
-        placed, total = place(plan, parts, places, (block,), sums=(total,))
+    pieces, sums = [], ()
+    for t in range(n - 2):
+        got = plan.regroup(run([jobs[t]]))
+        placed, total = place(plan, got, places, (block,), sums=sums)
         pieces.append((placed, t, 0))
+        sums = (total,)
+    borrowed = plan.regroup(run([(lent, keys, values, 0, 0, 0, block)], after=total))
+    (borrowed,) = place(plan, borrowed, places, (block,), summed=0)
     borrowed, total, *_ = lax.optimization_barrier((borrowed, total, *pairs[-1]))
     returned = lax.ppermute(borrowed, "pipe", backward)
-    placed, total = place(plan, got[-1], places, (block,), blocks=(returned,), sums=(total,))
+    got = plan.regroup(run([jobs[n - 2]]))
+    placed, total = place(plan, got, places, (block,), blocks=(returned,), sums=(total,))
     pieces += [(placed, n - 2, 0), (returned, n - 1, 0)]
     if plan.tensor == 2:
         sums = (total, lax.ppermute(total, "tensor", [(0, 1), (1, 0)]))

time: 52.8 us -> 52.6 us (level); the launches traced: 52.6 us -> 51.8 us
  waiting for transfers between devices: 21 us -> 17.1 us
  starting transfers between devices: 22.4 us -> 25 us
    ppermute x4, waiting for transfers between devices: 9.92 us -> 3.16 us  [body(): pairs.append(tuple((lax.ppermute(x, 'pipe', forward) for x in pairs[-1])))]
    ppermute x9 -> x12, starting transfers between devices: 11.6 us -> 15.2 us  [regroup(): lax.ppermute(part, 'dp', [(g, g ^ step) for g in range(self.groups)])]
    ppermute x4, starting transfers between devices: 10.1 us -> 7.21 us  [body(): pairs.append(tuple((lax.ppermute(x, 'pipe', forward) for x in pairs[-1])))]
    ppermute x9 -> x12, waiting for transfers between devices: 10 us -> 12.9 us  [regroup(): lax.ppermute(part, 'dp', [(g, g ^ step) for g in range(self.groups)])]
    ppermute x1, starting transfers between devices: 0.06 us -> 2.06 us  [body(): returned = lax.ppermute(borrowed, 'pipe', backward)]
    pallas_call x3 -> x4, Pallas kernels: 2.61 us -> 2.92 us  [attend(): pl.pallas_call(functools.partial(attend_kernel, plan, spans), out_shape=[...]
    pallas_call x3 -> x4, Pallas kernels: 1.52 us -> 1.64 us  [place(): pl.pallas_call(functools.partial(place_kernel, plan, widths, summed, len(...]
  transfers between devices with their start and end apart: 16 -> 19, of which waited for: 8 -> 12; matrix products, arithmetic and copies ran while one was open for 2% -> 2% of each run, Pallas kernels for 9% -> 10%
where the time goes in v5:
time: 52.6 us; the launch traced here: 51.8 us
  starting transfers between devices  25 us (48%)
  waiting for transfers between devices  17.1 us (33%)
  Pallas kernels  6.53 us (12%)
  local copies, waits for them, and re-layouts  2.95 us (6%)
    ppermute x12, starting transfers between devices, regroup(): lax.ppermute(part, 'dp', [(g, g ^ step) for g in range(self.groups)])  15.2 us
    ppermute x12, waiting for transfers between devices, regroup(): lax.ppermute(part, 'dp', [(g, g ^ step) for g in range(self.groups)])  12.9 us
    ppermute x4, starting transfers between devices, body(): pairs.append(tuple((lax.ppermute(x, 'pipe', forward) for x in pairs[-1])))  7.21 us
    ppermute x4, waiting for transfers between devices, body(): pairs.append(tuple((lax.ppermute(x, 'pipe', forward) for x in pairs[-1])))  3.16 us
    pallas_call x4, Pallas kernels, attend(): pl.pallas_call(functools.partial(attend_kernel, plan, spans), out_shape=[...  2.92 us
    ppermute x1, starting transfers between devices, body(): returned = lax.ppermute(borrowed, 'pipe', backward)  2.06 us
    unnamed x12, local copies, waits for them, and re-layouts  1.99 us
    pallas_call x4, Pallas kernels, place(): pl.pallas_call(functools.partial(place_kernel, plan, widths, summed, len(...  1.64 us
  transfers between devices with their start and end apart: 19, of which 12 were waited for; matrix products, arithmetic and copies ran while one was open for 2% of the time, Pallas kernels for 10%

profile of v5, /device:TPU:0, one launch (start us, length us, event | category | flops | bytes accessed | tf_op | source)
XLA Modules:
  0.0 51.8 jit_solution(17569340682361941509)
XLA Ops:
  0.0 3.0 %collective-permute-start.3 = (bf16[128,1024]{1,0:T(8,128)(2,1)}, bf16[128,1024]{1,0:T(8,128)(2,1)S(1)}, u32[]{:S(2)}, u32[]{:S(2)}) collective-permute-start(bf16[128,1024]{1,0:T(8,128)(2,1)} %bitcast.8), channel_id=1, source_target_pairs={{0,8},{8,24},{24,16},{16,0},{1,9},{9,25},{25,17},{17,1},{2,10},{10... | collective-permute-start | bytes 786440 | tf_op jit(solution)/shard_map/ppermute | solution.py:335
  3.0 2.6 %collective-permute-start.4 = (bf16[128,1024]{1,0:T(8,128)(2,1)}, bf16[128,1024]{1,0:T(8,128)(2,1)S(1)}, u32[]{:S(2)}, u32[]{:S(2)}) collective-permute-start(bf16[128,1024]{1,0:T(8,128)(2,1)} %bitcast.11), channel_id=1, source_target_pairs={{0,8},{8,24},{24,16},{16,0},{1,9},{9,25},{25,17},{17,1},{2,10},{10... | collective-permute-start | bytes 786440 | tf_op jit(solution)/shard_map/ppermute | solution.py:335
  5.6 1.0 %dynamic-slice_bitcast_fusion = bf16[128,1024]{1,0:T(8,128)(2,1)S(1)} fusion(bf16[1,128,4096]{2,1,0:T(8,128)(2,1)} %param.6, s32[]{:T(128)S(6)} %select_n.16), kind=kLoop, calls=%fused_computation | loop fusion | bytes 524292 | tf_op jit(solution)/shard_map/dynamic_slice | solution.py:331
  6.6 0.5 collective-permute-start.13
  7.1 0.0 copy-start
  7.1 1.2 %copy-done = bf16[1,128,4096]{2,1,0:T(8,128)(2,1)S(1)} copy-done((bf16[1,128,4096]{2,1,0:T(8,128)(2,1)S(1)}, bf16[1,128,4096]{2,1,0:T(8,128)(2,1)}, u32[]{:S(2)}) %copy-start) | copy-done | bytes 1048600
  8.3 0.0 copy-start.3
  8.3 0.0 copy-start.4
  8.3 0.0 copy-start.1
  8.3 0.0 copy-start.2
  8.3 0.1 split.1
  8.4 0.6 %copy-done.3 = s32[4,4]{1,0:T(4,128)S(1)} copy-done((s32[4,4]{1,0:T(4,128)S(1)}, s32[4,4]{1,0:T(4,128)}, u32[]{:S(2)}) %copy-start.3) | copy-done | bytes 88
  9.0 0.0 copy-done.4
  9.0 0.7 %tables.1 = (f32[128,128]{1,0:T(8,128)S(1)}, bf16[160,128]{1,0:T(8,128)(2,1)S(1)}, bf16[128,40]{1,0:T(8,128)(2,1)S(1)}, bf16[128,40]{1,0:T(8,128)(2,1)S(1)}, bf1...) custom-call(s32[1,6]{1,0:T(1,128)S(1)} %copy-done.4, s32[4,4]{1,0:T(4,128)S(1)} %copy-done.3), custom_call_target="tpu_custom_call" | custom-call | flops 1 | bytes 1 | tf_op jit(solution)/shard_map/tables/pallas_call | solution.py:136
  9.7 0.0 copy-done.1
  9.7 0.0 copy-done.2
  9.7 0.7 %attend.4 = (bf16[40,1024]{1,0:T(8,128)(2,1)S(1)}, bf16[40,1024]{1,0:T(8,128)(2,1)S(1)}, bf16[40,1024]{1,0:T(8,128)(2,1)S(1)}, bf16[40,1024]{1,0:T(8,128)(2,1)S(1)}) custom-call(bf16[128,1024]{1,0:T(8,128)(2,1)S(1)} %get-tuple-element.38.refs_0_, bf16[128,1024]{1,0:T(8,128)(2,1)S(1)} %bitcast.9, bf16[128,1024]{1,0:T(8,128)(2,1)S(1)} %bitcast.12, ...), custom_call_target="tpu_custom_call" | custom-call | flops 1 | bytes 1 | tf_op jit(solution)/shard_map/attend/pallas_call | solution.py:194
  10.4 2.5 %collective-permute-start = (bf16[40,1024]{1,0:T(8,128)(2,1)S(1)}, bf16[40,1024]{1,0:T(8,128)(2,1)S(1)}, u32[]{:S(2)}, u32[]{:S(2)}) collective-permute-start(bf16[40,1024]{1,0:T(8,128)(2,1)S(1)} %get-tuple-element.42), channel_id=1, source_target_pairs={{0,6},{2,4},{4,2},{6,0},{1,7},{3,5},{5,3},{7,1},{8,14},{10,12},{12... | collective-permute-start | bytes 245768 | tf_op jit(solution)/shard_map/ppermute | solution.py:63
  13.0 0.5 %collective-permute-start.1 = (bf16[40,1024]{1,0:T(8,128)(2,1)S(1)}, bf16[40,1024]{1,0:T(8,128)(2,1)S(1)}, u32[]{:S(2)}, u32[]{:S(2)}) collective-permute-start(bf16[40,1024]{1,0:T(8,128)(2,1)S(1)} %get-tuple-element.43), channel_id=1, source_target_pairs={{0,2},{2,0},{4,6},{6,4},{1,3},{3,1},{5,7},{7,5},{8,10},{10,8},{12,... | collective-permute-start | bytes 245768 | tf_op jit(solution)/shard_map/ppermute | solution.py:63
  13.5 0.0 collective-permute-done.3.refs_1_
  13.5 0.3 collective-permute-start.8
  13.8 3.2 %collective-permute-done.4.refs_2_ = bf16[128,1024]{1,0:T(8,128)(2,1)S(1)} collective-permute-done((bf16[128,1024]{1,0:T(8,128)(2,1)}, bf16[128,1024]{1,0:T(8,128)(2,1)S(1)}, u32[]{:S(2)}, u32[]{:S(2)}) %collective-permute-start.4) | collective-permute-done | bytes 262176 | tf_op jit(solution)/shard_map/ppermute | solution.py:335
  17.0 1.3 %collective-permute-start.9 = (bf16[128,1024]{1,0:T(8,128)(2,1)S(1)}, bf16[128,1024]{1,0:T(8,128)(2,1)S(1)}, u32[]{:S(2)}, u32[]{:S(2)}) collective-permute-start(bf16[128,1024]{1,0:T(8,128)(2,1)S(1)} %collective-permute-done.4.refs_2_), channel_id=1, source_target_pairs={{0,8},{8,24},{24,16},{16,0},{1,9},{9,25},{25,17},{17,1},{2,10},{10... | collective-permute-start | bytes 786440 | tf_op jit(solution)/shard_map/ppermute | solution.py:335
  18.3 0.7 %attend.5 = (bf16[40,1024]{1,0:T(8,128)(2,1)S(1)}, bf16[40,1024]{1,0:T(8,128)(2,1)S(1)}, bf16[40,1024]{1,0:T(8,128)(2,1)S(1)}, bf16[40,1024]{1,0:T(8,128)(2,1)S(1)}) custom-call(bf16[128,1024]{1,0:T(8,128)(2,1)S(1)} %get-tuple-element.50.refs_0_, bf16[128,1024]{1,0:T(8,128)(2,1)S(1)} %collective-permute-done.3.refs_1_, ...), custom_call_target="tpu_custom_call" | custom-call | flops 1 | bytes 1 | tf_op jit(solution)/shard_map/attend/pallas_call | solution.py:194
  19.0 0.0 collective-permute-done.refs_1_
  19.0 1.6 %collective-permute-start.2 = (bf16[40,1024]{1,0:T(8,128)(2,1)S(1)}, bf16[40,1024]{1,0:T(8,128)(2,1)S(1)}, u32[]{:S(2)}, u32[]{:S(2)}) collective-permute-start(bf16[40,1024]{1,0:T(8,128)(2,1)S(1)} %get-tuple-element.44), channel_id=1, source_target_pairs={{0,4},{2,6},{4,0},{6,2},{1,5},{3,7},{5,1},{7,3},{8,12},{10,14},{12... | collective-permute-start | bytes 245768 | tf_op jit(solution)/shard_map/ppermute | solution.py:63
  20.6 0.0 collective-permute-done.1.refs_2_
  20.6 1.4 %collective-permute-start.5 = (bf16[40,1024]{1,0:T(8,128)(2,1)S(1)}, bf16[40,1024]{1,0:T(8,128)(2,1)S(1)}, u32[]{:S(2)}, u32[]{:S(2)}) collective-permute-start(bf16[40,1024]{1,0:T(8,128)(2,1)S(1)} %get-tuple-element.52), channel_id=1, source_target_pairs={{0,6},{2,4},{4,2},{6,0},{1,7},{3,5},{5,3},{7,1},{8,14},{10,12},{12... | collective-permute-start | bytes 245768 | tf_op jit(solution)/shard_map/ppermute | solution.py:63
  22.0 1.5 %collective-permute-done.2.refs_3_ = bf16[40,1024]{1,0:T(8,128)(2,1)S(1)} collective-permute-done((bf16[40,1024]{1,0:T(8,128)(2,1)S(1)}, bf16[40,1024]{1,0:T(8,128)(2,1)S(1)}, u32[]{:S(2)}, u32[]{:S(2)}) %collective-permute-start.2) | collective-permute-done | bytes 81952 | tf_op jit(solution)/shard_map/ppermute | solution.py:63
  23.5 1.5 %collective-permute-start.6 = (bf16[40,1024]{1,0:T(8,128)(2,1)S(1)}, bf16[40,1024]{1,0:T(8,128)(2,1)S(1)}, u32[]{:S(2)}, u32[]{:S(2)}) collective-permute-start(bf16[40,1024]{1,0:T(8,128)(2,1)S(1)} %get-tuple-element.53), channel_id=1, source_target_pairs={{0,2},{2,0},{4,6},{6,4},{1,3},{3,1},{5,7},{7,5},{8,10},{10,8},{12,... | collective-permute-start | bytes 245768 | tf_op jit(solution)/shard_map/ppermute | solution.py:63
  25.0 1.0 %collective-permute-done.5.refs_1_ = bf16[40,1024]{1,0:T(8,128)(2,1)S(1)} collective-permute-done((bf16[40,1024]{1,0:T(8,128)(2,1)S(1)}, bf16[40,1024]{1,0:T(8,128)(2,1)S(1)}, u32[]{:S(2)}, u32[]{:S(2)}) %collective-permute-start.5) | collective-permute-done | bytes 81952 | tf_op jit(solution)/shard_map/ppermute | solution.py:63
  26.0 0.5 collective-permute-start.7
  26.6 0.4 place.4
  27.0 1.0 %collective-permute-done.6.refs_2_ = bf16[40,1024]{1,0:T(8,128)(2,1)S(1)} collective-permute-done((bf16[40,1024]{1,0:T(8,128)(2,1)S(1)}, bf16[40,1024]{1,0:T(8,128)(2,1)S(1)}, u32[]{:S(2)}, u32[]{:S(2)}) %collective-permute-start.6) | collective-permute-done | bytes 81952 | tf_op jit(solution)/shard_map/ppermute | solution.py:63
  28.0 2.5 %collective-permute-done.7.refs_3_ = bf16[40,1024]{1,0:T(8,128)(2,1)S(1)} collective-permute-done((bf16[40,1024]{1,0:T(8,128)(2,1)S(1)}, bf16[40,1024]{1,0:T(8,128)(2,1)S(1)}, u32[]{:S(2)}, u32[]{:S(2)}) %collective-permute-start.7) | collective-permute-done | bytes 81952 | tf_op jit(solution)/shard_map/ppermute | solution.py:63
  30.5 0.4 place.5
  30.9 0.0 collective-permute-done.13.refs_0_
  30.9 0.7 %attend.7 = (bf16[40,1024]{1,0:T(8,128)(2,1)S(1)}, bf16[40,1024]{1,0:T(8,128)(2,1)S(1)}, bf16[40,1024]{1,0:T(8,128)(2,1)S(1)}, bf16[40,1024]{1,0:T(8,128)(2,1)S(1)}) custom-call(bf16[128,1024]{1,0:T(8,128)(2,1)S(1)} %collective-permute-done.13.refs_0_, bf16[128,1024]{1,0:T(8,128)(2,1)S(1)} %bitcast.10, bf16[128,1024]{1,0:T(8,128)(2,1)S(1)} %bitcast.13, ...), custom_call_target="tpu_custom_call" | custom-call | flops 1 | bytes 1 | tf_op jit(solution)/shard_map/attend/pallas_call | solution.py:194
  31.6 1.5 %collective-permute-start.14 = (bf16[40,1024]{1,0:T(8,128)(2,1)S(1)}, bf16[40,1024]{1,0:T(8,128)(2,1)S(1)}, u32[]{:S(2)}, u32[]{:S(2)}) collective-permute-start(bf16[40,1024]{1,0:T(8,128)(2,1)S(1)} %get-tuple-element.64), channel_id=1, source_target_pairs={{0,6},{2,4},{4,2},{6,0},{1,7},{3,5},{5,3},{7,1},{8,14},{10,12},{12... | collective-permute-start | bytes 245768 | tf_op jit(solution)/shard_map/ppermute | solution.py:63
  33.1 0.5 %collective-permute-start.15 = (bf16[40,1024]{1,0:T(8,128)(2,1)S(1)}, bf16[40,1024]{1,0:T(8,128)(2,1)S(1)}, u32[]{:S(2)}, u32[]{:S(2)}) collective-permute-start(bf16[40,1024]{1,0:T(8,128)(2,1)S(1)} %get-tuple-element.65), channel_id=1, source_target_pairs={{0,2},{2,0},{4,6},{6,4},{1,3},{3,1},{5,7},{7,5},{8,10},{10,8},{12,... | collective-permute-start | bytes 245768 | tf_op jit(solution)/shard_map/ppermute | solution.py:63
  33.7 1.5 %collective-permute-start.16 = (bf16[40,1024]{1,0:T(8,128)(2,1)S(1)}, bf16[40,1024]{1,0:T(8,128)(2,1)S(1)}, u32[]{:S(2)}, u32[]{:S(2)}) collective-permute-start(bf16[40,1024]{1,0:T(8,128)(2,1)S(1)} %get-tuple-element.66), channel_id=1, source_target_pairs={{0,4},{2,6},{4,0},{6,2},{1,5},{3,7},{5,1},{7,3},{8,12},{10,14},{12... | collective-permute-start | bytes 245768 | tf_op jit(solution)/shard_map/ppermute | solution.py:63
  35.2 1.9 %collective-permute-done.14.refs_1_ = bf16[40,1024]{1,0:T(8,128)(2,1)S(1)} collective-permute-done((bf16[40,1024]{1,0:T(8,128)(2,1)S(1)}, bf16[40,1024]{1,0:T(8,128)(2,1)S(1)}, u32[]{:S(2)}, u32[]{:S(2)}) %collective-permute-start.14) | collective-permute-done | bytes 81952 | tf_op jit(solution)/shard_map/ppermute | solution.py:63
  37.1 0.5 %collective-permute-done.15.refs_2_ = bf16[40,1024]{1,0:T(8,128)(2,1)S(1)} collective-permute-done((bf16[40,1024]{1,0:T(8,128)(2,1)S(1)}, bf16[40,1024]{1,0:T(8,128)(2,1)S(1)}, u32[]{:S(2)}, u32[]{:S(2)}) %collective-permute-start.15) | collective-permute-done | bytes 81952 | tf_op jit(solution)/shard_map/ppermute | solution.py:63
  37.6 0.5 %collective-permute-done.16.refs_3_ = bf16[40,1024]{1,0:T(8,128)(2,1)S(1)} collective-permute-done((bf16[40,1024]{1,0:T(8,128)(2,1)S(1)}, bf16[40,1024]{1,0:T(8,128)(2,1)S(1)}, u32[]{:S(2)}, u32[]{:S(2)}) %collective-permute-start.16) | collective-permute-done | bytes 81952 | tf_op jit(solution)/shard_map/ppermute | solution.py:63
  38.1 0.4 place.6
  38.5 0.0 collective-permute-done.8.refs_1_
  38.5 0.0 collective-permute-done.9.refs_2_
  38.6 2.1 %collective-permute-start.17 = (bf16[128,1024]{1,0:T(8,128)(2,1)S(1)}, bf16[128,1024]{1,0:T(8,128)(2,1)S(1)}, u32[]{:S(2)}, u32[]{:S(2)}) collective-permute-start(bf16[128,1024]{1,0:T(8,128)(2,1)S(1)} %place.6), channel_id=1, source_target_pairs={{8,0},{24,8},{16,24},{0,16},{9,1},{25,9},{17,25},{1,17},{10,2},{26... | collective-permute-start | bytes 786440 | tf_op jit(solution)/shard_map/ppermute | solution.py:350
  40.6 0.7 %attend.6 = (bf16[40,1024]{1,0:T(8,128)(2,1)S(1)}, bf16[40,1024]{1,0:T(8,128)(2,1)S(1)}, bf16[40,1024]{1,0:T(8,128)(2,1)S(1)}, bf16[40,1024]{1,0:T(8,128)(2,1)S(1)}) custom-call(bf16[128,1024]{1,0:T(8,128)(2,1)S(1)} %get-tuple-element.57.refs_0_, bf16[128,1024]{1,0:T(8,128)(2,1)S(1)} %collective-permute-done.8.refs_1_, ...), custom_call_target="tpu_custom_call" | custom-call | flops 1 | bytes 1 | tf_op jit(solution)/shard_map/attend/pallas_call | solution.py:194
  41.4 2.5 %collective-permute-start.10 = (bf16[40,1024]{1,0:T(8,128)(2,1)S(1)}, bf16[40,1024]{1,0:T(8,128)(2,1)S(1)}, u32[]{:S(2)}, u32[]{:S(2)}) collective-permute-start(bf16[40,1024]{1,0:T(8,128)(2,1)S(1)} %get-tuple-element.59), channel_id=1, source_target_pairs={{0,6},{2,4},{4,2},{6,0},{1,7},{3,5},{5,3},{7,1},{8,14},{10,12},{12... | collective-permute-start | bytes 245768 | tf_op jit(solution)/shard_map/ppermute | solution.py:63
  43.9 0.5 %collective-permute-start.11 = (bf16[40,1024]{1,0:T(8,128)(2,1)S(1)}, bf16[40,1024]{1,0:T(8,128)(2,1)S(1)}, u32[]{:S(2)}, u32[]{:S(2)}) collective-permute-start(bf16[40,1024]{1,0:T(8,128)(2,1)S(1)} %get-tuple-element.60), channel_id=1, source_target_pairs={{0,2},{2,0},{4,6},{6,4},{1,3},{3,1},{5,7},{7,5},{8,10},{10,8},{12,... | collective-permute-start | bytes 245768 | tf_op jit(solution)/shard_map/ppermute | solution.py:63
  44.4 0.5 collective-permute-start.12
  44.9 1.9 %collective-permute-done.10.refs_1_ = bf16[40,1024]{1,0:T(8,128)(2,1)S(1)} collective-permute-done((bf16[40,1024]{1,0:T(8,128)(2,1)S(1)}, bf16[40,1024]{1,0:T(8,128)(2,1)S(1)}, u32[]{:S(2)}, u32[]{:S(2)}) %collective-permute-start.10) | collective-permute-done | bytes 81952 | tf_op jit(solution)/shard_map/ppermute | solution.py:63
  46.8 1.6 %collective-permute-done.11.refs_2_ = bf16[40,1024]{1,0:T(8,128)(2,1)S(1)} collective-permute-done((bf16[40,1024]{1,0:T(8,128)(2,1)S(1)}, bf16[40,1024]{1,0:T(8,128)(2,1)S(1)}, u32[]{:S(2)}, u32[]{:S(2)}) %collective-permute-start.11) | collective-permute-done | bytes 81952 | tf_op jit(solution)/shard_map/ppermute | solution.py:63
  48.3 0.5 %collective-permute-done.12.refs_3_ = bf16[40,1024]{1,0:T(8,128)(2,1)S(1)} collective-permute-done((bf16[40,1024]{1,0:T(8,128)(2,1)S(1)}, bf16[40,1024]{1,0:T(8,128)(2,1)S(1)}, u32[]{:S(2)}, u32[]{:S(2)}) %collective-permute-start.12) | collective-permute-done | bytes 81952 | tf_op jit(solution)/shard_map/ppermute | solution.py:63
  48.9 0.0 collective-permute-done.17.refs_8_.refs_3_
  48.9 0.0 copy-start.5
  48.9 0.4 place.7
  49.3 0.1 collective-permute-start.18
  49.4 0.2 copy-done.5
  49.6 1.0 %collective-permute-done.18.refs_5_ = f32[128,128]{1,0:T(8,128)S(1)} collective-permute-done((f32[128,128]{1,0:T(8,128)S(1)}, f32[128,128]{1,0:T(8,128)S(1)}, u32[]{:S(2)}, u32[]{:S(2)}) %collective-permute-start.18) | collective-permute-done | bytes 65568 | tf_op jit(solution)/shard_map/ppermute | solution.py:355
  50.6 1.2 %norm.1 = bf16[128,4096]{1,0:T(8,128)(2,1)} custom-call(bf16[128,1024]{1,0:T(8,128)(2,1)S(1)} %get-tuple-element.49.refs_0_, bf16[128,1024]{1,0:T(8,128)(2,1)S(1)} %get-tuple-element.56.refs_1_, bf16[128,1024]{1,0:T(8,128)(2,1)S(1)} %get-tuple-element.69.refs_2_, bf16[128,1024]{1,0:T(8,128)(2,1)S(1)} %collective-permute-done.17.refs_8_.refs_3_, ...), custom_call_target="tpu_custom_call" | custom-call | flops 1 | bytes 1 | tf_op jit(solution)/shard_map/norm/pallas_call | solution.py:306
  (1 shorter events, 0.0 us)
Async XLA Ops:
  0.0 13.5 %collective-permute-start.3 = (bf16[128,1024]{1,0:T(8,128)(2,1)}, bf16[128,1024]{1,0:T(8,128)(2,1)S(1)}, u32[]{:S(2)}, u32[]{:S(2)}) collective-permute-start(bf16[128,1024]{1,0:T(8,128)(2,1)} %bitcast.8), channel_id=1, source_target_pairs={{0,8},{8,24},{24,16},{16,0},{1,9},{9,25},{25,17},{17,1},{2,10},{10... | collective-permute-start | bytes 786440 | tf_op jit(solution)/shard_map/ppermute | solution.py:335
  3.0 14.0 %collective-permute-start.4 = (bf16[128,1024]{1,0:T(8,128)(2,1)}, bf16[128,1024]{1,0:T(8,128)(2,1)S(1)}, u32[]{:S(2)}, u32[]{:S(2)}) collective-permute-start(bf16[128,1024]{1,0:T(8,128)(2,1)} %bitcast.11), channel_id=1, source_target_pairs={{0,8},{8,24},{24,16},{16,0},{1,9},{9,25},{25,17},{17,1},{2,10},{10... | collective-permute-start | bytes 786440 | tf_op jit(solution)/shard_map/ppermute | solution.py:335
  6.6 24.3 %collective-permute-start.13 = (bf16[128,1024]{1,0:T(8,128)(2,1)S(1)}, bf16[128,1024]{1,0:T(8,128)(2,1)S(1)}, u32[]{:S(2)}, u32[]{:S(2)}) collective-permute-start(bf16[128,1024]{1,0:T(8,128)(2,1)S(1)} %dynamic-slice_bitcast_fusion), channel_id=1, source_target_pairs={{0,8},{8,24},{24,16},{16,0},{1,9},{9,25},{25,17},{17,1},{2,10},{10... | collective-permute-start | bytes 786440 | tf_op jit(solution)/shard_map/ppermute | solution.py:332
  7.1 1.2 %copy-start = (bf16[1,128,4096]{2,1,0:T(8,128)(2,1)S(1)}, bf16[1,128,4096]{2,1,0:T(8,128)(2,1)}, u32[]{:S(2)}) copy-start(bf16[1,128,4096]{2,1,0:T(8,128)(2,1)} %param.6) | copy-start | bytes 3145732
  8.3 0.7 %copy-start.3 = (s32[4,4]{1,0:T(4,128)S(1)}, s32[4,4]{1,0:T(4,128)}, u32[]{:S(2)}) copy-start(s32[4,4]{1,0:T(4,128)} %counts.1) | copy-start | bytes 196
  8.3 0.7 %copy-start.4 = (s32[1,6]{1,0:T(1,128)S(1)}, s32[1,6]{1,0:T(1,128)}, u32[]{:S(2)}) copy-start(s32[1,6]{1,0:T(1,128)} %docs.1) | copy-start | bytes 76
  8.3 1.4 %copy-start.1 = (bf16[128,1,1,1024]{3,0,2,1:T(8,128)(2,1)S(1)}, bf16[128,1,1,1024]{3,0,2,1:T(8,128)(2,1)}, u32[]{:S(2)}) copy-start(bf16[128,1,1,1024]{3,0,2,1:T(8,128)(2,1)} %param.7) | copy-start | bytes 786436
  8.3 1.4 %copy-start.2 = (bf16[128,1,1,1024]{3,0,2,1:T(8,128)(2,1)S(1)}, bf16[128,1,1,1024]{3,0,2,1:T(8,128)(2,1)}, u32[]{:S(2)}) copy-start(bf16[128,1,1,1024]{3,0,2,1:T(8,128)(2,1)} %param.8) | copy-start | bytes 786436
  10.4 8.5 %collective-permute-start = (bf16[40,1024]{1,0:T(8,128)(2,1)S(1)}, bf16[40,1024]{1,0:T(8,128)(2,1)S(1)}, u32[]{:S(2)}, u32[]{:S(2)}) collective-permute-start(bf16[40,1024]{1,0:T(8,128)(2,1)S(1)} %get-tuple-element.42), channel_id=1, source_target_pairs={{0,6},{2,4},{4,2},{6,0},{1,7},{3,5},{5,3},{7,1},{8,14},{10,12},{12... | collective-permute-start | bytes 245768 | tf_op jit(solution)/shard_map/ppermute | solution.py:63
  13.0 7.6 %collective-permute-start.1 = (bf16[40,1024]{1,0:T(8,128)(2,1)S(1)}, bf16[40,1024]{1,0:T(8,128)(2,1)S(1)}, u32[]{:S(2)}, u32[]{:S(2)}) collective-permute-start(bf16[40,1024]{1,0:T(8,128)(2,1)S(1)} %get-tuple-element.43), channel_id=1, source_target_pairs={{0,2},{2,0},{4,6},{6,4},{1,3},{3,1},{5,7},{7,5},{8,10},{10,8},{12,... | collective-permute-start | bytes 245768 | tf_op jit(solution)/shard_map/ppermute | solution.py:63
  13.5 25.0 %collective-permute-start.8 = (bf16[128,1024]{1,0:T(8,128)(2,1)S(1)}, bf16[128,1024]{1,0:T(8,128)(2,1)S(1)}, u32[]{:S(2)}, u32[]{:S(2)}) collective-permute-start(bf16[128,1024]{1,0:T(8,128)(2,1)S(1)} %collective-permute-done.3.refs_1_), channel_id=1, source_target_pairs={{0,8},{8,24},{24,16},{16,0},{1,9},{9,25},{25,17},{17,1},{2,10},{10... | collective-permute-start | bytes 786440 | tf_op jit(solution)/shard_map/ppermute | solution.py:335
  17.0 21.6 %collective-permute-start.9 = (bf16[128,1024]{1,0:T(8,128)(2,1)S(1)}, bf16[128,1024]{1,0:T(8,128)(2,1)S(1)}, u32[]{:S(2)}, u32[]{:S(2)}) collective-permute-start(bf16[128,1024]{1,0:T(8,128)(2,1)S(1)} %collective-permute-done.4.refs_2_), channel_id=1, source_target_pairs={{0,8},{8,24},{24,16},{16,0},{1,9},{9,25},{25,17},{17,1},{2,10},{10... | collective-permute-start | bytes 786440 | tf_op jit(solution)/shard_map/ppermute | solution.py:335
  19.0 4.5 %collective-permute-start.2 = (bf16[40,1024]{1,0:T(8,128)(2,1)S(1)}, bf16[40,1024]{1,0:T(8,128)(2,1)S(1)}, u32[]{:S(2)}, u32[]{:S(2)}) collective-permute-start(bf16[40,1024]{1,0:T(8,128)(2,1)S(1)} %get-tuple-element.44), channel_id=1, source_target_pairs={{0,4},{2,6},{4,0},{6,2},{1,5},{3,7},{5,1},{7,3},{8,12},{10,14},{12... | collective-permute-start | bytes 245768 | tf_op jit(solution)/shard_map/ppermute | solution.py:63
  20.6 5.4 %collective-permute-start.5 = (bf16[40,1024]{1,0:T(8,128)(2,1)S(1)}, bf16[40,1024]{1,0:T(8,128)(2,1)S(1)}, u32[]{:S(2)}, u32[]{:S(2)}) collective-permute-start(bf16[40,1024]{1,0:T(8,128)(2,1)S(1)} %get-tuple-element.52), channel_id=1, source_target_pairs={{0,6},{2,4},{4,2},{6,0},{1,7},{3,5},{5,3},{7,1},{8,14},{10,12},{12... | collective-permute-start | bytes 245768 | tf_op jit(solution)/shard_map/ppermute | solution.py:63
  23.5 4.4 %collective-permute-start.6 = (bf16[40,1024]{1,0:T(8,128)(2,1)S(1)}, bf16[40,1024]{1,0:T(8,128)(2,1)S(1)}, u32[]{:S(2)}, u32[]{:S(2)}) collective-permute-start(bf16[40,1024]{1,0:T(8,128)(2,1)S(1)} %get-tuple-element.53), channel_id=1, source_target_pairs={{0,2},{2,0},{4,6},{6,4},{1,3},{3,1},{5,7},{7,5},{8,10},{10,8},{12,... | collective-permute-start | bytes 245768 | tf_op jit(solution)/shard_map/ppermute | solution.py:63
  26.0 4.4 %collective-permute-start.7 = (bf16[40,1024]{1,0:T(8,128)(2,1)S(1)}, bf16[40,1024]{1,0:T(8,128)(2,1)S(1)}, u32[]{:S(2)}, u32[]{:S(2)}) collective-permute-start(bf16[40,1024]{1,0:T(8,128)(2,1)S(1)} %get-tuple-element.54), channel_id=1, source_target_pairs={{0,4},{2,6},{4,0},{6,2},{1,5},{3,7},{5,1},{7,3},{8,12},{10,14},{12... | collective-permute-start | bytes 245768 | tf_op jit(solution)/shard_map/ppermute | solution.py:63
  31.6 5.4 %collective-permute-start.14 = (bf16[40,1024]{1,0:T(8,128)(2,1)S(1)}, bf16[40,1024]{1,0:T(8,128)(2,1)S(1)}, u32[]{:S(2)}, u32[]{:S(2)}) collective-permute-start(bf16[40,1024]{1,0:T(8,128)(2,1)S(1)} %get-tuple-element.64), channel_id=1, source_target_pairs={{0,6},{2,4},{4,2},{6,0},{1,7},{3,5},{5,3},{7,1},{8,14},{10,12},{12... | collective-permute-start | bytes 245768 | tf_op jit(solution)/shard_map/ppermute | solution.py:63
  33.1 4.4 %collective-permute-start.15 = (bf16[40,1024]{1,0:T(8,128)(2,1)S(1)}, bf16[40,1024]{1,0:T(8,128)(2,1)S(1)}, u32[]{:S(2)}, u32[]{:S(2)}) collective-permute-start(bf16[40,1024]{1,0:T(8,128)(2,1)S(1)} %get-tuple-element.65), channel_id=1, source_target_pairs={{0,2},{2,0},{4,6},{6,4},{1,3},{3,1},{5,7},{7,5},{8,10},{10,8},{12,... | collective-permute-start | bytes 245768 | tf_op jit(solution)/shard_map/ppermute | solution.py:63
  33.7 4.4 %collective-permute-start.16 = (bf16[40,1024]{1,0:T(8,128)(2,1)S(1)}, bf16[40,1024]{1,0:T(8,128)(2,1)S(1)}, u32[]{:S(2)}, u32[]{:S(2)}) collective-permute-start(bf16[40,1024]{1,0:T(8,128)(2,1)S(1)} %get-tuple-element.66), channel_id=1, source_target_pairs={{0,4},{2,6},{4,0},{6,2},{1,5},{3,7},{5,1},{7,3},{8,12},{10,14},{12... | collective-permute-start | bytes 245768 | tf_op jit(solution)/shard_map/ppermute | solution.py:63
  38.6 10.3 %collective-permute-start.17 = (bf16[128,1024]{1,0:T(8,128)(2,1)S(1)}, bf16[128,1024]{1,0:T(8,128)(2,1)S(1)}, u32[]{:S(2)}, u32[]{:S(2)}) collective-permute-start(bf16[128,1024]{1,0:T(8,128)(2,1)S(1)} %place.6), channel_id=1, source_target_pairs={{8,0},{24,8},{16,24},{0,16},{9,1},{25,9},{17,25},{1,17},{10,2},{26... | collective-permute-start | bytes 786440 | tf_op jit(solution)/shard_map/ppermute | solution.py:350
  41.4 5.4 %collective-permute-start.10 = (bf16[40,1024]{1,0:T(8,128)(2,1)S(1)}, bf16[40,1024]{1,0:T(8,128)(2,1)S(1)}, u32[]{:S(2)}, u32[]{:S(2)}) collective-permute-start(bf16[40,1024]{1,0:T(8,128)(2,1)S(1)} %get-tuple-element.59), channel_id=1, source_target_pairs={{0,6},{2,4},{4,2},{6,0},{1,7},{3,5},{5,3},{7,1},{8,14},{10,12},{12... | collective-permute-start | bytes 245768 | tf_op jit(solution)/shard_map/ppermute | solution.py:63
  43.9 4.4 %collective-permute-start.11 = (bf16[40,1024]{1,0:T(8,128)(2,1)S(1)}, bf16[40,1024]{1,0:T(8,128)(2,1)S(1)}, u32[]{:S(2)}, u32[]{:S(2)}) collective-permute-start(bf16[40,1024]{1,0:T(8,128)(2,1)S(1)} %get-tuple-element.60), channel_id=1, source_target_pairs={{0,2},{2,0},{4,6},{6,4},{1,3},{3,1},{5,7},{7,5},{8,10},{10,8},{12,... | collective-permute-start | bytes 245768 | tf_op jit(solution)/shard_map/ppermute | solution.py:63
  44.4 4.4 %collective-permute-start.12 = (bf16[40,1024]{1,0:T(8,128)(2,1)S(1)}, bf16[40,1024]{1,0:T(8,128)(2,1)S(1)}, u32[]{:S(2)}, u32[]{:S(2)}) collective-permute-start(bf16[40,1024]{1,0:T(8,128)(2,1)S(1)} %get-tuple-element.61), channel_id=1, source_target_pairs={{0,4},{2,6},{4,0},{6,2},{1,5},{3,7},{5,1},{7,3},{8,12},{10,14},{12... | collective-permute-start | bytes 245768 | tf_op jit(solution)/shard_map/ppermute | solution.py:63
  48.9 0.7 %copy-start.5 = (bf16[4096]{0:T(1024)(128)(2,1)S(1)}, bf16[4096]{0:T(1024)(128)(2,1)}, u32[]{:S(2)}) copy-start(bf16[4096]{0:T(1024)(128)(2,1)} %param.11) | copy-start | bytes 24580
  49.3 1.3 %collective-permute-start.18 = (f32[128,128]{1,0:T(8,128)S(1)}, f32[128,128]{1,0:T(8,128)S(1)}, u32[]{:S(2)}, u32[]{:S(2)}) collective-permute-start(f32[128,128]{1,0:T(8,128)S(1)} %get-tuple-element.70.refs_4_), channel_id=1, source_target_pairs={{0,1},{1,0},{2,3},{3,2},{4,5},{5,4},{6,7},{7,6},{8,9},{9,8},{10,11... | collective-permute-start | bytes 196616 | tf_op jit(solution)/shard_map/ppermute | solution.py:355

commit v6 on v5

--- a/solution.py
+++ b/solution.py
@@ -329,23 +329,27 @@
 
     begin = pick(lax.axis_index("pipe"), plan.behind[n - 1]) * block
     ahead = lax.dynamic_slice_in_dim(query, begin, block, 1)
-    lent = lax.ppermute(ahead, "pipe", forward)
-    pairs = [(keys, values)]
-    for _ in range(n - 2):
-        pairs.append(tuple(lax.ppermute(x, "pipe", forward) for x in pairs[-1]))
-
     asked = split(plan, query)
     bias, send, places = tables(plan, doc_lengths, row_counts)
     run = functools.partial(attend, plan, bias=bias, send=send)
+    lent = lax.ppermute(ahead, "pipe", forward)
+    sent = run([(asked[0], keys, values, 0, 0, 0, block), (lent, keys, values, 0, 0, 0, block)])
+    arrived = plan.regroup(sent)
+    pairs = [(keys, values)]
+    k, v = lax.ppermute(keys, "pipe", forward), lax.ppermute(values, "pipe", forward)
+    for _ in range(n - 3):
+        pairs.append((k, v))
+        k, *_ = lax.optimization_barrier((k, *arrived))
+        k, v = lax.ppermute(k, "pipe", forward), lax.ppermute(v, "pipe", forward)
+    pairs.append((k, v))
     jobs = [(asked[t], *pairs[t], 0, 0, 0, block) for t in range(n - 1)]
-    pieces, sums = [], ()
-    for t in range(n - 2):
+
+    mine, borrowed, total = place(plan, arrived, places, (block, block), summed=1)
+    pieces = [(mine, 0, 0)]
+    for t in range(1, n - 2):
         got = plan.regroup(run([jobs[t]]))
-        placed, total = place(plan, got, places, (block,), sums=sums)
+        placed, total = place(plan, got, places, (block,), sums=(total,))
         pieces.append((placed, t, 0))
-        sums = (total,)
-    borrowed = plan.regroup(run([(lent, keys, values, 0, 0, 0, block)], after=total))
-    (borrowed,) = place(plan, borrowed, places, (block,), summed=0)
     borrowed, total, *_ = lax.optimization_barrier((borrowed, total, *pairs[-1]))
     returned = lax.ppermute(borrowed, "pipe", backward)
     got = plan.regroup(run([jobs[n - 2]]))

time: 52.6 us -> 47 us (0.89); the launches traced: 51.8 us -> 46.8 us
  starting transfers between devices: 25 us -> 20.9 us
    ppermute x12 -> x9, waiting for transfers between devices: 12.9 us -> 7.18 us  [regroup(): lax.ppermute(part, 'dp', [(g, g ^ step) for g in range(self.groups)])]
    ppermute x12 -> x9, starting transfers between devices: 15.2 us -> 10.7 us  [regroup(): lax.ppermute(part, 'dp', [(g, g ^ step) for g in range(self.groups)])]
    ppermute x4, waiting for transfers between devices: 3.16 us -> 5.91 us  [the longest x1 4.46 us: body(): lax.ppermute(keys, 'pipe', forward)]
    ppermute x1, starting transfers between devices: 0.5 us -> 3.08 us  [body(): lent = lax.ppermute(ahead, 'pipe', forward)]
    ppermute x1, waiting for transfers between devices: 0.01 us -> 2.5 us  [body(): lent = lax.ppermute(ahead, 'pipe', forward)]
    ppermute x4, starting transfers between devices: 7.21 us -> 5.4 us  [the longest x1 2.59 us: body(): lax.ppermute(values, 'pipe', forward)]
    pallas_call x4 -> x3, Pallas kernels: 2.92 us -> 2.6 us  [attend(): pl.pallas_call(functools.partial(attend_kernel, plan, spans), out_shape=[...]
    pallas_call x4 -> x3, Pallas kernels: 1.64 us -> 1.51 us  [place(): pl.pallas_call(functools.partial(place_kernel, plan, widths, summed, len(...]
  transfers between devices with their start and end apart: 19 -> 16, of which waited for: 12 -> 11; matrix products, arithmetic and copies ran while one was open for 2% -> 0% of each run, Pallas kernels for 10% -> 10%
where the time goes in v6:
time: 47 us; the launch traced here: 46.8 us
  starting transfers between devices  20.9 us (44%)
  waiting for transfers between devices  16.6 us (35%)
  Pallas kernels  6.06 us (13%)
  local copies, waits for them, and re-layouts  3.04 us (6%)
    ppermute x9, starting transfers between devices, regroup(): lax.ppermute(part, 'dp', [(g, g ^ step) for g in range(self.groups)])  10.7 us
    ppermute x9, waiting for transfers between devices, regroup(): lax.ppermute(part, 'dp', [(g, g ^ step) for g in range(self.groups)])  7.18 us
    ppermute x1, waiting for transfers between devices, body(): lax.ppermute(keys, 'pipe', forward)  4.46 us
    ppermute x1, starting transfers between devices, body(): lent = lax.ppermute(ahead, 'pipe', forward)  3.08 us
    pallas_call x3, Pallas kernels, attend(): pl.pallas_call(functools.partial(attend_kernel, plan, spans), out_shape=[...  2.6 us
    ppermute x1, starting transfers between devices, body(): lax.ppermute(values, 'pipe', forward)  2.59 us
    ppermute x1, waiting for transfers between devices, body(): lent = lax.ppermute(ahead, 'pipe', forward)  2.5 us
    ppermute x2, starting transfers between devices, body(): k, v = (lax.ppermute(k, 'pipe', forward), lax.ppermute(v, 'pipe', forward))  2.36 us
  transfers between devices with their start and end apart: 16, of which 11 were waited for; matrix products, arithmetic and copies ran while one was open for 0% of the time, Pallas kernels for 10%

profile of v6, /device:TPU:0, one launch (start us, length us, event | category | flops | bytes accessed | tf_op | source)
XLA Modules:
  0.0 46.8 jit_solution(56352096286388268)
XLA Ops:
  0.0 0.0 copy-start.1
  0.0 0.0 copy-start.2
  0.0 1.0 %dynamic-slice_bitcast_fusion = bf16[128,1024]{1,0:T(8,128)(2,1)S(1)} fusion(bf16[1,128,4096]{2,1,0:T(8,128)(2,1)} %param.6, s32[]{:T(128)S(6)} %select_n.16), kind=kLoop, calls=%fused_computation | loop fusion | bytes 524292 | tf_op jit(solution)/shard_map/dynamic_slice | solution.py:331
  1.0 3.1 %collective-permute-start = (bf16[128,1024]{1,0:T(8,128)(2,1)S(1)}, bf16[128,1024]{1,0:T(8,128)(2,1)S(1)}, u32[]{:S(2)}, u32[]{:S(2)}) collective-permute-start(bf16[128,1024]{1,0:T(8,128)(2,1)S(1)} %dynamic-slice_bitcast_fusion), channel_id=1, source_target_pairs={{0,8},{8,24},{24,16},{16,0},{1,9},{9,25},{25,17},{17,1},{2,10},{10... | collective-permute-start | bytes 786440 | tf_op jit(solution)/shard_map/ppermute | solution.py:335
  4.1 0.0 copy-done.1
  4.1 2.6 %collective-permute-start.5 = (bf16[128,1024]{1,0:T(8,128)(2,1)S(1)}, bf16[128,1024]{1,0:T(8,128)(2,1)S(1)}, u32[]{:S(2)}, u32[]{:S(2)}) collective-permute-start(bf16[128,1024]{1,0:T(8,128)(2,1)S(1)} %bitcast.8), channel_id=1, source_target_pairs={{0,8},{8,24},{24,16},{16,0},{1,9},{9,25},{25,17},{17,1},{2,10},{10... | collective-permute-start | bytes 786440 | tf_op jit(solution)/shard_map/ppermute | solution.py:339
  6.7 0.0 copy-done.2
  6.7 0.4 collective-permute-start.4
  7.2 0.0 copy-start
  7.2 1.2 %copy-done = bf16[1,128,4096]{2,1,0:T(8,128)(2,1)S(1)} copy-done((bf16[1,128,4096]{2,1,0:T(8,128)(2,1)S(1)}, bf16[1,128,4096]{2,1,0:T(8,128)(2,1)}, u32[]{:S(2)}) %copy-start) | copy-done | bytes 1048600
  8.4 0.0 copy-start.3
  8.4 0.0 copy-start.4
  8.4 0.1 split.1
  8.5 0.6 %copy-done.3 = s32[4,4]{1,0:T(4,128)S(1)} copy-done((s32[4,4]{1,0:T(4,128)S(1)}, s32[4,4]{1,0:T(4,128)}, u32[]{:S(2)}) %copy-start.3) | copy-done | bytes 88
  9.1 0.0 copy-done.4
  9.1 0.7 %tables.1 = (f32[128,128]{1,0:T(8,128)S(1)}, bf16[160,128]{1,0:T(8,128)(2,1)S(1)}, bf16[128,40]{1,0:T(8,128)(2,1)S(1)}, bf16[128,40]{1,0:T(8,128)(2,1)S(1)}, bf1...) custom-call(s32[1,6]{1,0:T(1,128)S(1)} %copy-done.4, s32[4,4]{1,0:T(4,128)S(1)} %copy-done.3), custom_call_target="tpu_custom_call" | custom-call | flops 1 | bytes 1 | tf_op jit(solution)/shard_map/tables/pallas_call | solution.py:136
  9.8 2.5 %collective-permute-done.refs_3_ = bf16[128,1024]{1,0:T(8,128)(2,1)S(1)} collective-permute-done((bf16[128,1024]{1,0:T(8,128)(2,1)S(1)}, bf16[128,1024]{1,0:T(8,128)(2,1)S(1)}, u32[]{:S(2)}, u32[]{:S(2)}) %collective-permute-start) | collective-permute-done | bytes 262176 | tf_op jit(solution)/shard_map/ppermute | solution.py:335
  12.3 1.1 %attend.3 = (bf16[40,2048]{1,0:T(8,128)(2,1)S(1)}, bf16[40,2048]{1,0:T(8,128)(2,1)S(1)}, bf16[40,2048]{1,0:T(8,128)(2,1)S(1)}, bf16[40,2048]{1,0:T(8,128)(2,1)S(1)}) custom-call(bf16[128,1024]{1,0:T(8,128)(2,1)S(1)} %get-tuple-element.36.refs_0_, bf16[128,1024]{1,0:T(8,128)(2,1)S(1)} %bitcast.12, bf16[128,1024]{1,0:T(8,128)(2,1)S(1)} %bitcast.9, ...), custom_call_target="tpu_custom_call" | custom-call | flops 1 | bytes 1 | tf_op jit(solution)/shard_map/attend/pallas_call | solution.py:194
  13.4 2.9 %collective-permute-start.1 = (bf16[40,2048]{1,0:T(8,128)(2,1)S(1)}, bf16[40,2048]{1,0:T(8,128)(2,1)S(1)}, u32[]{:S(2)}, u32[]{:S(2)}) collective-permute-start(bf16[40,2048]{1,0:T(8,128)(2,1)S(1)} %get-tuple-element.40), channel_id=1, source_target_pairs={{0,6},{2,4},{4,2},{6,0},{1,7},{3,5},{5,3},{7,1},{8,14},{10,12},{12... | collective-permute-start | bytes 491528 | tf_op jit(solution)/shard_map/ppermute | solution.py:63
  16.3 0.5 %collective-permute-start.2 = (bf16[40,2048]{1,0:T(8,128)(2,1)S(1)}, bf16[40,2048]{1,0:T(8,128)(2,1)S(1)}, u32[]{:S(2)}, u32[]{:S(2)}) collective-permute-start(bf16[40,2048]{1,0:T(8,128)(2,1)S(1)} %get-tuple-element.41), channel_id=1, source_target_pairs={{0,2},{2,0},{4,6},{6,4},{1,3},{3,1},{5,7},{7,5},{8,10},{10,8},{12,... | collective-permute-start | bytes 491528 | tf_op jit(solution)/shard_map/ppermute | solution.py:63
  16.8 0.1 collective-permute-start.3
  17.0 0.9 %collective-permute-done.5.refs_2_ = bf16[128,1024]{1,0:T(8,128)(2,1)S(1)} collective-permute-done((bf16[128,1024]{1,0:T(8,128)(2,1)S(1)}, bf16[128,1024]{1,0:T(8,128)(2,1)S(1)}, u32[]{:S(2)}, u32[]{:S(2)}) %collective-permute-start.5) | collective-permute-done | bytes 262176 | tf_op jit(solution)/shard_map/ppermute | solution.py:339
  17.9 1.2 %collective-permute-start.10 = (bf16[128,1024]{1,0:T(8,128)(2,1)S(1)}, bf16[128,1024]{1,0:T(8,128)(2,1)S(1)}, u32[]{:S(2)}, u32[]{:S(2)}) collective-permute-start(bf16[128,1024]{1,0:T(8,128)(2,1)S(1)} %collective-permute-done.5.refs_2_), channel_id=1, source_target_pairs={{0,8},{8,24},{24,16},{16,0},{1,9},{9,25},{25,17},{17,1},{2,10},{10... | collective-permute-start | bytes 786440 | tf_op jit(solution)/shard_map/ppermute | solution.py:343
  19.0 4.5 %collective-permute-done.4.refs_1_ = bf16[128,1024]{1,0:T(8,128)(2,1)S(1)} collective-permute-done((bf16[128,1024]{1,0:T(8,128)(2,1)S(1)}, bf16[128,1024]{1,0:T(8,128)(2,1)S(1)}, u32[]{:S(2)}, u32[]{:S(2)}) %collective-permute-start.4) | collective-permute-done | bytes 262176 | tf_op jit(solution)/shard_map/ppermute | solution.py:339
  23.5 0.0 collective-permute-done.1.refs_1_
  23.5 0.0 collective-permute-done.2.refs_2_
  23.5 0.0 collective-permute-done.3.refs_3_
  23.5 1.2 %collective-permute-start.9 = (bf16[128,1024]{1,0:T(8,128)(2,1)S(1)}, bf16[128,1024]{1,0:T(8,128)(2,1)S(1)}, u32[]{:S(2)}, u32[]{:S(2)}) collective-permute-start(bf16[128,1024]{1,0:T(8,128)(2,1)S(1)} %collective-permute-done.4.refs_1_), channel_id=1, source_target_pairs={{0,8},{8,24},{24,16},{16,0},{1,9},{9,25},{25,17},{17,1},{2,10},{10... | collective-permute-start | bytes 786440 | tf_op jit(solution)/shard_map/ppermute | solution.py:343
  24.7 0.7 %attend.4 = (bf16[40,1024]{1,0:T(8,128)(2,1)S(1)}, bf16[40,1024]{1,0:T(8,128)(2,1)S(1)}, bf16[40,1024]{1,0:T(8,128)(2,1)S(1)}, bf16[40,1024]{1,0:T(8,128)(2,1)S(1)}) custom-call(bf16[128,1024]{1,0:T(8,128)(2,1)S(1)} %get-tuple-element.48.refs_0_, bf16[128,1024]{1,0:T(8,128)(2,1)S(1)} %collective-permute-done.4.refs_1_, ...), custom_call_target="tpu_custom_call" | custom-call | flops 1 | bytes 1 | tf_op jit(solution)/shard_map/attend/pallas_call | solution.py:194
  25.4 2.5 %collective-permute-start.6 = (bf16[40,1024]{1,0:T(8,128)(2,1)S(1)}, bf16[40,1024]{1,0:T(8,128)(2,1)S(1)}, u32[]{:S(2)}, u32[]{:S(2)}) collective-permute-start(bf16[40,1024]{1,0:T(8,128)(2,1)S(1)} %get-tuple-element.50), channel_id=1, source_target_pairs={{0,6},{2,4},{4,2},{6,0},{1,7},{3,5},{5,3},{7,1},{8,14},{10,12},{12... | collective-permute-start | bytes 245768 | tf_op jit(solution)/shard_map/ppermute | solution.py:63
  28.0 0.5 %collective-permute-start.7 = (bf16[40,1024]{1,0:T(8,128)(2,1)S(1)}, bf16[40,1024]{1,0:T(8,128)(2,1)S(1)}, u32[]{:S(2)}, u32[]{:S(2)}) collective-permute-start(bf16[40,1024]{1,0:T(8,128)(2,1)S(1)} %get-tuple-element.51), channel_id=1, source_target_pairs={{0,2},{2,0},{4,6},{6,4},{1,3},{3,1},{5,7},{7,5},{8,10},{10,8},{12,... | collective-permute-start | bytes 245768 | tf_op jit(solution)/shard_map/ppermute | solution.py:63
  28.5 0.5 %collective-permute-start.8 = (bf16[40,1024]{1,0:T(8,128)(2,1)S(1)}, bf16[40,1024]{1,0:T(8,128)(2,1)S(1)}, u32[]{:S(2)}, u32[]{:S(2)}) collective-permute-start(bf16[40,1024]{1,0:T(8,128)(2,1)S(1)} %get-tuple-element.52), channel_id=1, source_target_pairs={{0,4},{2,6},{4,0},{6,2},{1,5},{3,7},{5,1},{7,3},{8,12},{10,14},{12... | collective-permute-start | bytes 245768 | tf_op jit(solution)/shard_map/ppermute | solution.py:63
  29.0 0.7 %place.3 = (bf16[128,1024]{1,0:T(8,128)(2,1)S(1)}, bf16[128,1024]{1,0:T(8,128)(2,1)S(1)}, f32[128,128]{1,0:T(8,128)S(1)}) custom-call(bf16[40,2048]{1,0:T(8,128)(2,1)S(1)} %get-tuple-element.39.refs_0_, bf16[40,2048]{1,0:T(8,128)(2,1)S(1)} %collective-permute-done.1.refs_1_, bf16[40,2048]{1,0:T(8,128)(2,1)S(1)} %collective-permute-done.2.refs_2_, ...), custom_call_target="tpu_custom_call" | custom-call | flops 1 | bytes 1 | tf_op jit(solution)/shard_map/place/pallas_call | solution.py:265
  29.7 1.2 %collective-permute-done.6.refs_1_ = bf16[40,1024]{1,0:T(8,128)(2,1)S(1)} collective-permute-done((bf16[40,1024]{1,0:T(8,128)(2,1)S(1)}, bf16[40,1024]{1,0:T(8,128)(2,1)S(1)}, u32[]{:S(2)}, u32[]{:S(2)}) %collective-permute-start.6) | collective-permute-done | bytes 81952 | tf_op jit(solution)/shard_map/ppermute | solution.py:63
  30.9 1.5 %collective-permute-done.7.refs_2_ = bf16[40,1024]{1,0:T(8,128)(2,1)S(1)} collective-permute-done((bf16[40,1024]{1,0:T(8,128)(2,1)S(1)}, bf16[40,1024]{1,0:T(8,128)(2,1)S(1)}, u32[]{:S(2)}, u32[]{:S(2)}) %collective-permute-start.7) | collective-permute-done | bytes 81952 | tf_op jit(solution)/shard_map/ppermute | solution.py:63
  32.4 0.5 %collective-permute-done.8.refs_3_ = bf16[40,1024]{1,0:T(8,128)(2,1)S(1)} collective-permute-done((bf16[40,1024]{1,0:T(8,128)(2,1)S(1)}, bf16[40,1024]{1,0:T(8,128)(2,1)S(1)}, u32[]{:S(2)}, u32[]{:S(2)}) %collective-permute-start.8) | collective-permute-done | bytes 81952 | tf_op jit(solution)/shard_map/ppermute | solution.py:63
  32.9 0.4 place.4
  33.4 0.0 collective-permute-done.10.refs_2_
  33.4 0.5 %collective-permute-done.9.refs_1_ = bf16[128,1024]{1,0:T(8,128)(2,1)S(1)} collective-permute-done((bf16[128,1024]{1,0:T(8,128)(2,1)S(1)}, bf16[128,1024]{1,0:T(8,128)(2,1)S(1)}, u32[]{:S(2)}, u32[]{:S(2)}) %collective-permute-start.9) | collective-permute-done | bytes 262176 | tf_op jit(solution)/shard_map/ppermute | solution.py:343
  33.9 1.7 %collective-permute-start.14 = (bf16[128,1024]{1,0:T(8,128)(2,1)S(1)}, bf16[128,1024]{1,0:T(8,128)(2,1)S(1)}, u32[]{:S(2)}, u32[]{:S(2)}) collective-permute-start(bf16[128,1024]{1,0:T(8,128)(2,1)S(1)} %get-tuple-element.63), channel_id=1, source_target_pairs={{8,0},{24,8},{16,24},{0,16},{9,1},{25,9},{17,25},{1,17},{10,2},{26... | collective-permute-start | bytes 786440 | tf_op jit(solution)/shard_map/ppermute | solution.py:354
  35.6 0.7 %attend.5 = (bf16[40,1024]{1,0:T(8,128)(2,1)S(1)}, bf16[40,1024]{1,0:T(8,128)(2,1)S(1)}, bf16[40,1024]{1,0:T(8,128)(2,1)S(1)}, bf16[40,1024]{1,0:T(8,128)(2,1)S(1)}) custom-call(bf16[128,1024]{1,0:T(8,128)(2,1)S(1)} %get-tuple-element.55.refs_0_, bf16[128,1024]{1,0:T(8,128)(2,1)S(1)} %collective-permute-done.9.refs_1_, ...), custom_call_target="tpu_custom_call" | custom-call | flops 1 | bytes 1 | tf_op jit(solution)/shard_map/attend/pallas_call | solution.py:194
  36.4 2.5 %collective-permute-start.11 = (bf16[40,1024]{1,0:T(8,128)(2,1)S(1)}, bf16[40,1024]{1,0:T(8,128)(2,1)S(1)}, u32[]{:S(2)}, u32[]{:S(2)}) collective-permute-start(bf16[40,1024]{1,0:T(8,128)(2,1)S(1)} %get-tuple-element.58), channel_id=1, source_target_pairs={{0,6},{2,4},{4,2},{6,0},{1,7},{3,5},{5,3},{7,1},{8,14},{10,12},{12... | collective-permute-start | bytes 245768 | tf_op jit(solution)/shard_map/ppermute | solution.py:63
  38.9 0.5 %collective-permute-start.12 = (bf16[40,1024]{1,0:T(8,128)(2,1)S(1)}, bf16[40,1024]{1,0:T(8,128)(2,1)S(1)}, u32[]{:S(2)}, u32[]{:S(2)}) collective-permute-start(bf16[40,1024]{1,0:T(8,128)(2,1)S(1)} %get-tuple-element.59), channel_id=1, source_target_pairs={{0,2},{2,0},{4,6},{6,4},{1,3},{3,1},{5,7},{7,5},{8,10},{10,8},{12,... | collective-permute-start | bytes 245768 | tf_op jit(solution)/shard_map/ppermute | solution.py:63
  39.4 0.5 %collective-permute-start.13 = (bf16[40,1024]{1,0:T(8,128)(2,1)S(1)}, bf16[40,1024]{1,0:T(8,128)(2,1)S(1)}, u32[]{:S(2)}, u32[]{:S(2)}) collective-permute-start(bf16[40,1024]{1,0:T(8,128)(2,1)S(1)} %get-tuple-element.60), channel_id=1, source_target_pairs={{0,4},{2,6},{4,0},{6,2},{1,5},{3,7},{5,1},{7,3},{8,12},{10,14},{12... | collective-permute-start | bytes 245768 | tf_op jit(solution)/shard_map/ppermute | solution.py:63
  39.9 2.0 %collective-permute-done.11.refs_1_ = bf16[40,1024]{1,0:T(8,128)(2,1)S(1)} collective-permute-done((bf16[40,1024]{1,0:T(8,128)(2,1)S(1)}, bf16[40,1024]{1,0:T(8,128)(2,1)S(1)}, u32[]{:S(2)}, u32[]{:S(2)}) %collective-permute-start.11) | collective-permute-done | bytes 81952 | tf_op jit(solution)/shard_map/ppermute | solution.py:63
  41.9 1.4 %collective-permute-done.12.refs_2_ = bf16[40,1024]{1,0:T(8,128)(2,1)S(1)} collective-permute-done((bf16[40,1024]{1,0:T(8,128)(2,1)S(1)}, bf16[40,1024]{1,0:T(8,128)(2,1)S(1)}, u32[]{:S(2)}, u32[]{:S(2)}) %collective-permute-start.12) | collective-permute-done | bytes 81952 | tf_op jit(solution)/shard_map/ppermute | solution.py:63
  43.3 0.5 %collective-permute-done.13.refs_3_ = bf16[40,1024]{1,0:T(8,128)(2,1)S(1)} collective-permute-done((bf16[40,1024]{1,0:T(8,128)(2,1)S(1)}, bf16[40,1024]{1,0:T(8,128)(2,1)S(1)}, u32[]{:S(2)}, u32[]{:S(2)}) %collective-permute-start.13) | collective-permute-done | bytes 81952 | tf_op jit(solution)/shard_map/ppermute | solution.py:63
  43.9 0.0 collective-permute-done.14.refs_8_.refs_3_
  43.9 0.0 copy-start.5
  43.9 0.4 place.5
  44.3 0.1 collective-permute-start.15
  44.4 0.2 copy-done.5
  44.6 1.0 %collective-permute-done.15.refs_5_ = f32[128,128]{1,0:T(8,128)S(1)} collective-permute-done((f32[128,128]{1,0:T(8,128)S(1)}, f32[128,128]{1,0:T(8,128)S(1)}, u32[]{:S(2)}, u32[]{:S(2)}) %collective-permute-start.15) | collective-permute-done | bytes 65568 | tf_op jit(solution)/shard_map/ppermute | solution.py:359
  45.6 1.2 %norm.1 = bf16[128,4096]{1,0:T(8,128)(2,1)} custom-call(bf16[128,1024]{1,0:T(8,128)(2,1)S(1)} %get-tuple-element.47.refs_0_, bf16[128,1024]{1,0:T(8,128)(2,1)S(1)} %get-tuple-element.54.refs_1_, bf16[128,1024]{1,0:T(8,128)(2,1)S(1)} %get-tuple-element.65.refs_2_, bf16[128,1024]{1,0:T(8,128)(2,1)S(1)} %collective-permute-done.14.refs_8_.refs_3_, ...), custom_call_target="tpu_custom_call" | custom-call | flops 1 | bytes 1 | tf_op jit(solution)/shard_map/norm/pallas_call | solution.py:306
  (1 shorter events, 0.0 us)
Async XLA Ops:
  0.0 4.1 %copy-start.1 = (bf16[128,1,1,1024]{3,0,2,1:T(8,128)(2,1)S(1)}, bf16[128,1,1,1024]{3,0,2,1:T(8,128)(2,1)}, u32[]{:S(2)}) copy-start(bf16[128,1,1,1024]{3,0,2,1:T(8,128)(2,1)} %param.8) | copy-start | bytes 786436
  0.0 6.7 %copy-start.2 = (bf16[128,1,1,1024]{3,0,2,1:T(8,128)(2,1)S(1)}, bf16[128,1,1,1024]{3,0,2,1:T(8,128)(2,1)}, u32[]{:S(2)}) copy-start(bf16[128,1,1,1024]{3,0,2,1:T(8,128)(2,1)} %param.7) | copy-start | bytes 786436
  1.0 11.2 %collective-permute-start = (bf16[128,1024]{1,0:T(8,128)(2,1)S(1)}, bf16[128,1024]{1,0:T(8,128)(2,1)S(1)}, u32[]{:S(2)}, u32[]{:S(2)}) collective-permute-start(bf16[128,1024]{1,0:T(8,128)(2,1)S(1)} %dynamic-slice_bitcast_fusion), channel_id=1, source_target_pairs={{0,8},{8,24},{24,16},{16,0},{1,9},{9,25},{25,17},{17,1},{2,10},{10... | collective-permute-start | bytes 786440 | tf_op jit(solution)/shard_map/ppermute | solution.py:335
  4.1 13.8 %collective-permute-start.5 = (bf16[128,1024]{1,0:T(8,128)(2,1)S(1)}, bf16[128,1024]{1,0:T(8,128)(2,1)S(1)}, u32[]{:S(2)}, u32[]{:S(2)}) collective-permute-start(bf16[128,1024]{1,0:T(8,128)(2,1)S(1)} %bitcast.8), channel_id=1, source_target_pairs={{0,8},{8,24},{24,16},{16,0},{1,9},{9,25},{25,17},{17,1},{2,10},{10... | collective-permute-start | bytes 786440 | tf_op jit(solution)/shard_map/ppermute | solution.py:339
  6.7 16.8 %collective-permute-start.4 = (bf16[128,1024]{1,0:T(8,128)(2,1)S(1)}, bf16[128,1024]{1,0:T(8,128)(2,1)S(1)}, u32[]{:S(2)}, u32[]{:S(2)}) collective-permute-start(bf16[128,1024]{1,0:T(8,128)(2,1)S(1)} %bitcast.11), channel_id=1, source_target_pairs={{0,8},{8,24},{24,16},{16,0},{1,9},{9,25},{25,17},{17,1},{2,10},{10... | collective-permute-start | bytes 786440 | tf_op jit(solution)/shard_map/ppermute | solution.py:339
  7.2 1.2 %copy-start = (bf16[1,128,4096]{2,1,0:T(8,128)(2,1)S(1)}, bf16[1,128,4096]{2,1,0:T(8,128)(2,1)}, u32[]{:S(2)}) copy-start(bf16[1,128,4096]{2,1,0:T(8,128)(2,1)} %param.6) | copy-start | bytes 3145732
  8.4 0.7 %copy-start.3 = (s32[4,4]{1,0:T(4,128)S(1)}, s32[4,4]{1,0:T(4,128)}, u32[]{:S(2)}) copy-start(s32[4,4]{1,0:T(4,128)} %counts.1) | copy-start | bytes 196
  8.4 0.7 %copy-start.4 = (s32[1,6]{1,0:T(1,128)S(1)}, s32[1,6]{1,0:T(1,128)}, u32[]{:S(2)}) copy-start(s32[1,6]{1,0:T(1,128)} %docs.1) | copy-start | bytes 76
  13.4 10.1 %collective-permute-start.1 = (bf16[40,2048]{1,0:T(8,128)(2,1)S(1)}, bf16[40,2048]{1,0:T(8,128)(2,1)S(1)}, u32[]{:S(2)}, u32[]{:S(2)}) collective-permute-start(bf16[40,2048]{1,0:T(8,128)(2,1)S(1)} %get-tuple-element.40), channel_id=1, source_target_pairs={{0,6},{2,4},{4,2},{6,0},{1,7},{3,5},{5,3},{7,1},{8,14},{10,12},{12... | collective-permute-start | bytes 491528 | tf_op jit(solution)/shard_map/ppermute | solution.py:63
  16.3 7.2 %collective-permute-start.2 = (bf16[40,2048]{1,0:T(8,128)(2,1)S(1)}, bf16[40,2048]{1,0:T(8,128)(2,1)S(1)}, u32[]{:S(2)}, u32[]{:S(2)}) collective-permute-start(bf16[40,2048]{1,0:T(8,128)(2,1)S(1)} %get-tuple-element.41), channel_id=1, source_target_pairs={{0,2},{2,0},{4,6},{6,4},{1,3},{3,1},{5,7},{7,5},{8,10},{10,8},{12,... | collective-permute-start | bytes 491528 | tf_op jit(solution)/shard_map/ppermute | solution.py:63
  16.8 6.7 %collective-permute-start.3 = (bf16[40,2048]{1,0:T(8,128)(2,1)S(1)}, bf16[40,2048]{1,0:T(8,128)(2,1)S(1)}, u32[]{:S(2)}, u32[]{:S(2)}) collective-permute-start(bf16[40,2048]{1,0:T(8,128)(2,1)S(1)} %get-tuple-element.42), channel_id=1, source_target_pairs={{0,4},{2,6},{4,0},{6,2},{1,5},{3,7},{5,1},{7,3},{8,12},{10,14},{12... | collective-permute-start | bytes 491528 | tf_op jit(solution)/shard_map/ppermute | solution.py:63
  17.9 15.5 %collective-permute-start.10 = (bf16[128,1024]{1,0:T(8,128)(2,1)S(1)}, bf16[128,1024]{1,0:T(8,128)(2,1)S(1)}, u32[]{:S(2)}, u32[]{:S(2)}) collective-permute-start(bf16[128,1024]{1,0:T(8,128)(2,1)S(1)} %collective-permute-done.5.refs_2_), channel_id=1, source_target_pairs={{0,8},{8,24},{24,16},{16,0},{1,9},{9,25},{25,17},{17,1},{2,10},{10... | collective-permute-start | bytes 786440 | tf_op jit(solution)/shard_map/ppermute | solution.py:343
  23.5 10.4 %collective-permute-start.9 = (bf16[128,1024]{1,0:T(8,128)(2,1)S(1)}, bf16[128,1024]{1,0:T(8,128)(2,1)S(1)}, u32[]{:S(2)}, u32[]{:S(2)}) collective-permute-start(bf16[128,1024]{1,0:T(8,128)(2,1)S(1)} %collective-permute-done.4.refs_1_), channel_id=1, source_target_pairs={{0,8},{8,24},{24,16},{16,0},{1,9},{9,25},{25,17},{17,1},{2,10},{10... | collective-permute-start | bytes 786440 | tf_op jit(solution)/shard_map/ppermute | solution.py:343
  25.4 5.4 %collective-permute-start.6 = (bf16[40,1024]{1,0:T(8,128)(2,1)S(1)}, bf16[40,1024]{1,0:T(8,128)(2,1)S(1)}, u32[]{:S(2)}, u32[]{:S(2)}) collective-permute-start(bf16[40,1024]{1,0:T(8,128)(2,1)S(1)} %get-tuple-element.50), channel_id=1, source_target_pairs={{0,6},{2,4},{4,2},{6,0},{1,7},{3,5},{5,3},{7,1},{8,14},{10,12},{12... | collective-permute-start | bytes 245768 | tf_op jit(solution)/shard_map/ppermute | solution.py:63
  28.0 4.4 %collective-permute-start.7 = (bf16[40,1024]{1,0:T(8,128)(2,1)S(1)}, bf16[40,1024]{1,0:T(8,128)(2,1)S(1)}, u32[]{:S(2)}, u32[]{:S(2)}) collective-permute-start(bf16[40,1024]{1,0:T(8,128)(2,1)S(1)} %get-tuple-element.51), channel_id=1, source_target_pairs={{0,2},{2,0},{4,6},{6,4},{1,3},{3,1},{5,7},{7,5},{8,10},{10,8},{12,... | collective-permute-start | bytes 245768 | tf_op jit(solution)/shard_map/ppermute | solution.py:63
  28.5 4.4 %collective-permute-start.8 = (bf16[40,1024]{1,0:T(8,128)(2,1)S(1)}, bf16[40,1024]{1,0:T(8,128)(2,1)S(1)}, u32[]{:S(2)}, u32[]{:S(2)}) collective-permute-start(bf16[40,1024]{1,0:T(8,128)(2,1)S(1)} %get-tuple-element.52), channel_id=1, source_target_pairs={{0,4},{2,6},{4,0},{6,2},{1,5},{3,7},{5,1},{7,3},{8,12},{10,14},{12... | collective-permute-start | bytes 245768 | tf_op jit(solution)/shard_map/ppermute | solution.py:63
  33.9 10.0 %collective-permute-start.14 = (bf16[128,1024]{1,0:T(8,128)(2,1)S(1)}, bf16[128,1024]{1,0:T(8,128)(2,1)S(1)}, u32[]{:S(2)}, u32[]{:S(2)}) collective-permute-start(bf16[128,1024]{1,0:T(8,128)(2,1)S(1)} %get-tuple-element.63), channel_id=1, source_target_pairs={{8,0},{24,8},{16,24},{0,16},{9,1},{25,9},{17,25},{1,17},{10,2},{26... | collective-permute-start | bytes 786440 | tf_op jit(solution)/shard_map/ppermute | solution.py:354
  36.4 5.5 %collective-permute-start.11 = (bf16[40,1024]{1,0:T(8,128)(2,1)S(1)}, bf16[40,1024]{1,0:T(8,128)(2,1)S(1)}, u32[]{:S(2)}, u32[]{:S(2)}) collective-permute-start(bf16[40,1024]{1,0:T(8,128)(2,1)S(1)} %get-tuple-element.58), channel_id=1, source_target_pairs={{0,6},{2,4},{4,2},{6,0},{1,7},{3,5},{5,3},{7,1},{8,14},{10,12},{12... | collective-permute-start | bytes 245768 | tf_op jit(solution)/shard_map/ppermute | solution.py:63
  38.9 4.4 %collective-permute-start.12 = (bf16[40,1024]{1,0:T(8,128)(2,1)S(1)}, bf16[40,1024]{1,0:T(8,128)(2,1)S(1)}, u32[]{:S(2)}, u32[]{:S(2)}) collective-permute-start(bf16[40,1024]{1,0:T(8,128)(2,1)S(1)} %get-tuple-element.59), channel_id=1, source_target_pairs={{0,2},{2,0},{4,6},{6,4},{1,3},{3,1},{5,7},{7,5},{8,10},{10,8},{12,... | collective-permute-start | bytes 245768 | tf_op jit(solution)/shard_map/ppermute | solution.py:63
  39.4 4.4 %collective-permute-start.13 = (bf16[40,1024]{1,0:T(8,128)(2,1)S(1)}, bf16[40,1024]{1,0:T(8,128)(2,1)S(1)}, u32[]{:S(2)}, u32[]{:S(2)}) collective-permute-start(bf16[40,1024]{1,0:T(8,128)(2,1)S(1)} %get-tuple-element.60), channel_id=1, source_target_pairs={{0,4},{2,6},{4,0},{6,2},{1,5},{3,7},{5,1},{7,3},{8,12},{10,14},{12... | collective-permute-start | bytes 245768 | tf_op jit(solution)/shard_map/ppermute | solution.py:63
  43.9 0.7 %copy-start.5 = (bf16[4096]{0:T(1024)(128)(2,1)S(1)}, bf16[4096]{0:T(1024)(128)(2,1)}, u32[]{:S(2)}) copy-start(bf16[4096]{0:T(1024)(128)(2,1)} %param.11) | copy-start | bytes 24580
  44.3 1.3 %collective-permute-start.15 = (f32[128,128]{1,0:T(8,128)S(1)}, f32[128,128]{1,0:T(8,128)S(1)}, u32[]{:S(2)}, u32[]{:S(2)}) collective-permute-start(f32[128,128]{1,0:T(8,128)S(1)} %get-tuple-element.66.refs_4_), channel_id=1, source_target_pairs={{0,1},{1,0},{2,3},{3,2},{4,5},{5,4},{6,7},{7,6},{8,9},{9,8},{10,11... | collective-permute-start | bytes 196616 | tf_op jit(solution)/shard_map/ppermute | solution.py:359

commit v7 on v6

--- a/solution.py
+++ b/solution.py
@@ -145,40 +145,34 @@
     return bias, send, places
 
 
-def attend_kernel(plan, jobs, *refs):
-    count = len(jobs)
-    operands, (bias, send) = refs[: 3 * count], refs[3 * count : 3 * count + 2]
-    outs, attn = refs[-1 - plan.parts : -1], refs[-1]
-    scale = log2_e / HEAD_DIM**0.5
-    base = 0
-    for n, (q_from, k_from, v_from, width) in enumerate(jobs):
-        q_ref, k_ref, v_ref = operands[3 * n : 3 * n + 3]
-        heads = range(0, width, HEAD_DIM)
-        scores = [
-            lax.dot_general(
-                k_ref[:, k_from + h : k_from + h + HEAD_DIM],
-                q_ref[:, q_from + h : q_from + h + HEAD_DIM],
-                (((1,), (1,)), ((), ())),
-                preferred_element_type=jnp.float32,
-            )
-            for h in heads
-        ]
-        weights, totals = [], []
-        for score in scores:
-            score = score * scale + bias[...]
-            weight = jnp.exp2(score - jnp.max(score, axis=0, keepdims=True))
-            totals.append(jnp.sum(weight, axis=0, keepdims=True))
-            weights.append(weight.astype(jnp.bfloat16))
-        for h, weight, total in zip(heads, weights, totals, strict=True):
-            accum = lax.dot_general(
-                v_ref[:, v_from + h : v_from + h + HEAD_DIM],
-                weight,
-                (((0,), (0,)), ((), ())),
-                preferred_element_type=jnp.float32,
-            )
-            rows = slice(base + h, base + h + HEAD_DIM)
-            attn[rows, :] = (accum * (1.0 / total)).astype(jnp.bfloat16)
-        base += width
+def softmax(score, bias):
+    score = score * (log2_e / HEAD_DIM**0.5) + bias
+    weight = jnp.exp2(score - jnp.max(score, axis=0, keepdims=True))
+    return weight.astype(jnp.bfloat16), 1.0 / jnp.sum(weight, axis=0, keepdims=True)
+
+
+def head_columns(plan):
+    return [slice(c, c + HEAD_DIM) for c in range(0, plan.block, HEAD_DIM)]
+
+
+def all_weights(plan, q_ref, k_ref, bias):
+    scores = [
+        lax.dot_general(
+            k_ref[:, cols], q_ref[:, cols], (((1,), (1,)), ((), ())), preferred_element_type=jnp.float32
+        )
+        for cols in head_columns(plan)
+    ]
+    return [softmax(score, bias[...]) for score in scores]
+
+
+def weighted(v_ref, cols, weight, inverse):
+    accum = lax.dot_general(
+        v_ref[:, cols], weight, (((0,), (0,)), ((), ())), preferred_element_type=jnp.float32
+    )
+    return (accum * inverse).astype(jnp.bfloat16)
+
+
+def pick_rows(plan, send, attn, outs):
     picked = lax.dot_general(
         send[...], attn[...], (((1,), (1,)), ((), ())), preferred_element_type=jnp.float32
     )
@@ -186,41 +180,91 @@
         out[...] = picked[part * plan.rows : (part + 1) * plan.rows].astype(jnp.bfloat16)
 
 
-def attend(plan, jobs, bias, send, after=None):
-    operands = [ref for job in jobs for ref in job[:3]]
-    spans = tuple(job[3:] for job in jobs)
-    width = sum(span[-1] for span in spans)
-    order = () if after is None else (after,)
-    return pl.pallas_call(
-        functools.partial(attend_kernel, plan, spans),
+def heads_kernel(plan, q_ref, k_ref, v_ref, bias, _, attn):
+    weights = all_weights(plan, q_ref, k_ref, bias)
+    for cols, (weight, inverse) in zip(head_columns(plan), weights, strict=True):
+        attn[cols, :] = weighted(v_ref, cols, weight, inverse)
+
+
+def heads(plan, query, k, v, bias, after):
+    return pl.pallas_call(
+        functools.partial(heads_kernel, plan),
+        out_shape=jax.ShapeDtypeStruct((plan.block, plan.seq), jnp.bfloat16),
+        in_specs=[VMEM] * 4 + [ANY],
+        out_specs=VMEM,
+        compiler_params=PARAMS,
+        cost_estimate=COST,
+        name="heads",
+    )(query, k, v, bias, after)
+
+
+def attend_kernel(plan, bases, q_ref, k_ref, v_ref, bias, send, *refs):
+    outs, attn = refs[-1 - plan.parts : -1], refs[-1]
+    for i, base in enumerate(refs[:bases]):
+        attn[i * plan.block : (i + 1) * plan.block, :] = base[...]
+    weights = all_weights(plan, q_ref, k_ref, bias)
+    for cols, (weight, inverse) in zip(head_columns(plan), weights, strict=True):
+        rows = slice(bases * plan.block + cols.start, bases * plan.block + cols.stop)
+        attn[rows, :] = weighted(v_ref, cols, weight, inverse)
+    pick_rows(plan, send, attn, outs)
+
+
+def attend(plan, query, k, v, bias, send, bases=(), after=()):
+    width = (len(bases) + 1) * plan.block
+    return pl.pallas_call(
+        functools.partial(attend_kernel, plan, len(bases)),
         out_shape=[jax.ShapeDtypeStruct((plan.rows, width), jnp.bfloat16)] * plan.parts,
-        in_specs=[VMEM] * (len(operands) + 2) + [ANY] * len(order),
+        in_specs=[VMEM] * (5 + len(bases)) + [ANY] * len(after),
         out_specs=[VMEM] * plan.parts,
         scratch_shapes=[pltpu.VMEM((width, plan.seq), jnp.bfloat16)],
         compiler_params=PARAMS,
         cost_estimate=COST,
         name="attend",
-    )(*operands, bias, send, *order)
-
-
-def pack_kernel(k_ref, v_ref, first, second):
-    half = k_ref.shape[1] // 2
-    first[:, :half] = k_ref[:, :half]
-    first[:, half:] = v_ref[:, :half]
-    second[:, :half] = k_ref[:, half:]
-    second[:, half:] = v_ref[:, half:]
-
-
-def pack(k, v):
-    return pl.pallas_call(
-        pack_kernel,
-        out_shape=[jax.ShapeDtypeStruct(k.shape, k.dtype)] * 2,
-        in_specs=[VMEM] * 2,
+    )(query, k, v, bias, send, *bases, *after)
+
+
+def weigh_kernel(plan, q_ref, k_ref, bias, *refs):
+    weights, inverses = refs[-2:]
+    found = all_weights(plan, q_ref, k_ref, bias)
+    for h, (cols, (weight, inverse)) in enumerate(zip(head_columns(plan), found, strict=True)):
+        weights[cols, :] = weight
+        inverses[h : h + 1, :] = inverse
+
+
+def weigh(plan, query, k, bias, after=()):
+    count = plan.block // HEAD_DIM
+    return pl.pallas_call(
+        functools.partial(weigh_kernel, plan),
+        out_shape=[
+            jax.ShapeDtypeStruct((plan.block, plan.seq), jnp.bfloat16),
+            jax.ShapeDtypeStruct((count, plan.seq), jnp.float32),
+        ],
+        in_specs=[VMEM] * 3 + [ANY] * len(after),
         out_specs=[VMEM] * 2,
         compiler_params=PARAMS,
         cost_estimate=COST,
-        name="pack",
-    )(k, v)
+        name="weigh",
+    )(query, k, bias, *after)
+
+
+def finish_kernel(plan, weights, inverses, v_ref, send, *refs):
+    outs, attn = refs[:-1], refs[-1]
+    for h, cols in enumerate(head_columns(plan)):
+        attn[cols, :] = weighted(v_ref, cols, weights[cols, :], inverses[h : h + 1, :])
+    pick_rows(plan, send, attn, outs)
+
+
+def finish(plan, weights, inverses, v, send):
+    return pl.pallas_call(
+        functools.partial(finish_kernel, plan),
+        out_shape=[jax.ShapeDtypeStruct((plan.rows, plan.block), jnp.bfloat16)] * plan.parts,
+        in_specs=[VMEM] * 4,
+        out_specs=[VMEM] * plan.parts,
+        scratch_shapes=[pltpu.VMEM((plan.block, plan.seq), jnp.bfloat16)],
+        compiler_params=PARAMS,
+        cost_estimate=COST,
+        name="finish",
+    )(weights, inverses, v, send)
 
 
 def squares_of(ref):
@@ -331,28 +375,24 @@
     ahead = lax.dynamic_slice_in_dim(query, begin, block, 1)
     asked = split(plan, query)
     bias, send, places = tables(plan, doc_lengths, row_counts)
-    run = functools.partial(attend, plan, bias=bias, send=send)
+    k, v = lax.ppermute(keys, "pipe", forward), lax.ppermute(values, "pipe", forward)
     lent = lax.ppermute(ahead, "pipe", forward)
-    sent = run([(asked[0], keys, values, 0, 0, 0, block), (lent, keys, values, 0, 0, 0, block)])
-    arrived = plan.regroup(sent)
-    pairs = [(keys, values)]
-    k, v = lax.ppermute(keys, "pipe", forward), lax.ppermute(values, "pipe", forward)
-    for _ in range(n - 3):
-        pairs.append((k, v))
-        k, *_ = lax.optimization_barrier((k, *arrived))
-        k, v = lax.ppermute(k, "pipe", forward), lax.ppermute(v, "pipe", forward)
-    pairs.append((k, v))
-    jobs = [(asked[t], *pairs[t], 0, 0, 0, block) for t in range(n - 1)]
-
+    own = heads(plan, asked[0], keys, values, bias, after=bias)
+    arrived = plan.regroup(attend(plan, lent, keys, values, bias, send, bases=(own,)))
     mine, borrowed, total = place(plan, arrived, places, (block, block), summed=1)
     pieces = [(mine, 0, 0)]
     for t in range(1, n - 2):
-        got = plan.regroup(run([jobs[t]]))
+        sent = attend(plan, asked[t], k, v, bias, send)
+        got = plan.regroup(sent)
         placed, total = place(plan, got, places, (block,), sums=(total,))
         pieces.append((placed, t, 0))
-    borrowed, total, *_ = lax.optimization_barrier((borrowed, total, *pairs[-1]))
+        if t == 1:
+            v, *_ = lax.optimization_barrier((v, *arrived))
+        k, v = lax.ppermute(k, "pipe", forward), lax.ppermute(v, "pipe", forward)
+    weights = weigh(plan, asked[n - 2], k, bias, after=())
+    borrowed, *_ = lax.optimization_barrier((borrowed, *weights, v, *got))
     returned = lax.ppermute(borrowed, "pipe", backward)
-    got = plan.regroup(run([jobs[n - 2]]))
+    got = plan.regroup(finish(plan, *weights, v, send))
     placed, total = place(plan, got, places, (block,), blocks=(returned,), sums=(total,))
     pieces += [(placed, n - 2, 0), (returned, n - 1, 0)]
     if plan.tensor == 2:

time: 47 us -> 46.8 us (level)
  waiting for transfers between devices: 16.6 us -> 16.1 us
    ppermute x1, waiting for transfers between devices: 0.91 us -> 4.46 us  [body(): lax.ppermute(values, 'pipe', forward)]
    ppermute x1, waiting for transfers between devices: 4.46 us -> 1.31 us  [body(): lax.ppermute(keys, 'pipe', forward)]
    ppermute x1, starting transfers between devices: 0.45 us -> 2.59 us  [body(): lax.ppermute(keys, 'pipe', forward)]
    ppermute x1, starting transfers between devices: 2.59 us -> 0.45 us  [body(): lax.ppermute(values, 'pipe', forward)]
    ppermute x9, waiting for transfers between devices: 7.18 us -> 6.39 us  [regroup(): lax.ppermute(part, 'dp', [(g, g ^ step) for g in range(self.groups)])]
    ppermute x1, waiting for transfers between devices: 2.5 us -> 1.97 us  [body(): lent = lax.ppermute(ahead, 'pipe', forward)]
    pallas_call x3 -> x5, Pallas kernels: 2.6 us -> 2.82 us  [the longest x2 1.47 us: attend(): pl.pallas_call(functools.partial(attend_kernel, plan, len(bases)), out_sh...]
where the time goes in v7:
time: 46.8 us; the launch traced here: 46.5 us
  starting transfers between devices  20.9 us (45%)
  waiting for transfers between devices  16.1 us (34%)
  Pallas kernels  6.26 us (13%)
  local copies, waits for them, and re-layouts  3.05 us (7%)
    ppermute x9, starting transfers between devices, regroup(): lax.ppermute(part, 'dp', [(g, g ^ step) for g in range(self.groups)])  10.7 us
    ppermute x9, waiting for transfers between devices, regroup(): lax.ppermute(part, 'dp', [(g, g ^ step) for g in range(self.groups)])  6.39 us
    ppermute x1, waiting for transfers between devices, body(): lax.ppermute(values, 'pipe', forward)  4.46 us
    ppermute x1, starting transfers between devices, body(): lent = lax.ppermute(ahead, 'pipe', forward)  3.08 us
    ppermute x1, starting transfers between devices, body(): lax.ppermute(keys, 'pipe', forward)  2.59 us
    ppermute x2, starting transfers between devices, body(): k, v = (lax.ppermute(k, 'pipe', forward), lax.ppermute(v, 'pipe', forward))  2.36 us
    unnamed x12, local copies, waits for them, and re-layouts  2.02 us
    ppermute x1, waiting for transfers between devices, body(): lent = lax.ppermute(ahead, 'pipe', forward)  1.97 us
  transfers between devices with their start and end apart: 16, of which 11 were waited for; matrix products, arithmetic and copies ran while one was open for 0% of the time, Pallas kernels for 10%

profile of v7, /device:TPU:0, one launch (start us, length us, event | category | flops | bytes accessed | tf_op | source)
XLA Modules:
  0.0 46.5 jit_solution(14637768215769923620)
XLA Ops:
  0.0 0.0 copy-start.1
  0.0 0.0 copy-start.2
  0.0 1.0 %dynamic-slice_bitcast_fusion = bf16[128,1024]{1,0:T(8,128)(2,1)S(1)} fusion(bf16[1,128,4096]{2,1,0:T(8,128)(2,1)} %param.6, s32[]{:T(128)S(6)} %select_n.16), kind=kLoop, calls=%fused_computation | loop fusion | bytes 524292 | tf_op jit(solution)/shard_map/dynamic_slice | solution.py:375
  1.0 3.1 %collective-permute-start = (bf16[128,1024]{1,0:T(8,128)(2,1)S(1)}, bf16[128,1024]{1,0:T(8,128)(2,1)S(1)}, u32[]{:S(2)}, u32[]{:S(2)}) collective-permute-start(bf16[128,1024]{1,0:T(8,128)(2,1)S(1)} %dynamic-slice_bitcast_fusion), channel_id=1, source_target_pairs={{0,8},{8,24},{24,16},{16,0},{1,9},{9,25},{25,17},{17,1},{2,10},{10... | collective-permute-start | bytes 786440 | tf_op jit(solution)/shard_map/ppermute | solution.py:379
  4.1 0.0 copy-done.1
  4.1 2.6 %collective-permute-start.4 = (bf16[128,1024]{1,0:T(8,128)(2,1)S(1)}, bf16[128,1024]{1,0:T(8,128)(2,1)S(1)}, u32[]{:S(2)}, u32[]{:S(2)}) collective-permute-start(bf16[128,1024]{1,0:T(8,128)(2,1)S(1)} %bitcast.8), channel_id=1, source_target_pairs={{0,8},{8,24},{24,16},{16,0},{1,9},{9,25},{25,17},{17,1},{2,10},{10... | collective-permute-start | bytes 786440 | tf_op jit(solution)/shard_map/ppermute | solution.py:378
  6.7 0.0 copy-done.2
  6.7 0.4 collective-permute-start.5
  7.2 0.0 copy-start
  7.2 1.2 %copy-done = bf16[1,128,4096]{2,1,0:T(8,128)(2,1)S(1)} copy-done((bf16[1,128,4096]{2,1,0:T(8,128)(2,1)S(1)}, bf16[1,128,4096]{2,1,0:T(8,128)(2,1)}, u32[]{:S(2)}) %copy-start) | copy-done | bytes 1048600
  8.4 0.0 copy-start.3
  8.4 0.0 copy-start.4
  8.4 0.1 split.1
  8.5 0.6 %copy-done.3 = s32[4,4]{1,0:T(4,128)S(1)} copy-done((s32[4,4]{1,0:T(4,128)S(1)}, s32[4,4]{1,0:T(4,128)}, u32[]{:S(2)}) %copy-start.3) | copy-done | bytes 88
  9.1 0.0 copy-done.4
  9.1 0.7 %tables.1 = (f32[128,128]{1,0:T(8,128)S(1)}, bf16[160,128]{1,0:T(8,128)(2,1)S(1)}, bf16[128,40]{1,0:T(8,128)(2,1)S(1)}, bf16[128,40]{1,0:T(8,128)(2,1)S(1)}, bf1...) custom-call(s32[1,6]{1,0:T(1,128)S(1)} %copy-done.4, s32[4,4]{1,0:T(4,128)S(1)} %copy-done.3), custom_call_target="tpu_custom_call" | custom-call | flops 1 | bytes 1 | tf_op jit(solution)/shard_map/tables/pallas_call | solution.py:136
  9.8 0.5 %heads.1.refs_0_ = bf16[1024,128]{1,0:T(8,128)(2,1)S(1)} custom-call(bf16[128,1024]{1,0:T(8,128)(2,1)S(1)} %get-tuple-element.39.q_ref, bf16[128,1024]{1,0:T(8,128)(2,1)S(1)} %bitcast.9, bf16[128,1024]{1,0:T(8,128)(2,1)S(1)} %bitcast.12, f32[128,128]{1,0:T(8,128)S(1)} %get-tuple-element.37.bias._, f32[128,128]{1,0:T(8,128)S(1)} %get-tuple-element.37.bias._), custom_call_target="tpu_custom_call" | custom-call | flops 1 | bytes 1 | tf_op jit(solution)/shard_map/heads/pallas_call | solution.py:190
  10.3 2.0 %collective-permute-done.q_ref = bf16[128,1024]{1,0:T(8,128)(2,1)S(1)} collective-permute-done((bf16[128,1024]{1,0:T(8,128)(2,1)S(1)}, bf16[128,1024]{1,0:T(8,128)(2,1)S(1)}, u32[]{:S(2)}, u32[]{:S(2)}) %collective-permute-start) | collective-permute-done | bytes 262176 | tf_op jit(solution)/shard_map/ppermute | solution.py:379
  12.3 0.7 %attend.2 = (bf16[40,2048]{1,0:T(8,128)(2,1)S(1)}, bf16[40,2048]{1,0:T(8,128)(2,1)S(1)}, bf16[40,2048]{1,0:T(8,128)(2,1)S(1)}, bf16[40,2048]{1,0:T(8,128)(2,1)S(1)}) custom-call(bf16[128,1024]{1,0:T(8,128)(2,1)S(1)} %collective-permute-done.q_ref, bf16[128,1024]{1,0:T(8,128)(2,1)S(1)} %bitcast.10, bf16[128,1024]{1,0:T(8,128)(2,1)S(1)} %bitcast.13, ...), custom_call_target="tpu_custom_call" | custom-call | flops 1 | bytes 1 | tf_op jit(solution)/shard_map/attend/pallas_call | solution.py:214
  13.0 2.9 %collective-permute-start.1 = (bf16[40,2048]{1,0:T(8,128)(2,1)S(1)}, bf16[40,2048]{1,0:T(8,128)(2,1)S(1)}, u32[]{:S(2)}, u32[]{:S(2)}) collective-permute-start(bf16[40,2048]{1,0:T(8,128)(2,1)S(1)} %get-tuple-element.41), channel_id=1, source_target_pairs={{0,6},{2,4},{4,2},{6,0},{1,7},{3,5},{5,3},{7,1},{8,14},{10,12},{12... | collective-permute-start | bytes 491528 | tf_op jit(solution)/shard_map/ppermute | solution.py:63
  15.9 0.5 %collective-permute-start.2 = (bf16[40,2048]{1,0:T(8,128)(2,1)S(1)}, bf16[40,2048]{1,0:T(8,128)(2,1)S(1)}, u32[]{:S(2)}, u32[]{:S(2)}) collective-permute-start(bf16[40,2048]{1,0:T(8,128)(2,1)S(1)} %get-tuple-element.42), channel_id=1, source_target_pairs={{0,2},{2,0},{4,6},{6,4},{1,3},{3,1},{5,7},{7,5},{8,10},{10,8},{12,... | collective-permute-start | bytes 491528 | tf_op jit(solution)/shard_map/ppermute | solution.py:63
  16.4 0.1 collective-permute-start.3
  16.6 1.3 %collective-permute-done.4.k_ref = bf16[128,1024]{1,0:T(8,128)(2,1)S(1)} collective-permute-done((bf16[128,1024]{1,0:T(8,128)(2,1)S(1)}, bf16[128,1024]{1,0:T(8,128)(2,1)S(1)}, u32[]{:S(2)}, u32[]{:S(2)}) %collective-permute-start.4) | collective-permute-done | bytes 262176 | tf_op jit(solution)/shard_map/ppermute | solution.py:378
  17.9 1.2 %collective-permute-start.9 = (bf16[128,1024]{1,0:T(8,128)(2,1)S(1)}, bf16[128,1024]{1,0:T(8,128)(2,1)S(1)}, u32[]{:S(2)}, u32[]{:S(2)}) collective-permute-start(bf16[128,1024]{1,0:T(8,128)(2,1)S(1)} %collective-permute-done.4.k_ref), channel_id=1, source_target_pairs={{0,8},{8,24},{24,16},{16,0},{1,9},{9,25},{25,17},{17,1},{2,10},{10... | collective-permute-start | bytes 786440 | tf_op jit(solution)/shard_map/ppermute | solution.py:391
  19.0 4.5 %collective-permute-done.5.v_ref = bf16[128,1024]{1,0:T(8,128)(2,1)S(1)} collective-permute-done((bf16[128,1024]{1,0:T(8,128)(2,1)S(1)}, bf16[128,1024]{1,0:T(8,128)(2,1)S(1)}, u32[]{:S(2)}, u32[]{:S(2)}) %collective-permute-start.5) | collective-permute-done | bytes 262176 | tf_op jit(solution)/shard_map/ppermute | solution.py:378
  23.5 0.0 collective-permute-done.1.refs_1_
  23.5 0.0 collective-permute-done.2.refs_2_
  23.5 0.0 collective-permute-done.3.refs_3_
  23.5 1.2 %collective-permute-start.10 = (bf16[128,1024]{1,0:T(8,128)(2,1)S(1)}, bf16[128,1024]{1,0:T(8,128)(2,1)S(1)}, u32[]{:S(2)}, u32[]{:S(2)}) collective-permute-start(bf16[128,1024]{1,0:T(8,128)(2,1)S(1)} %collective-permute-done.5.v_ref), channel_id=1, source_target_pairs={{0,8},{8,24},{24,16},{16,0},{1,9},{9,25},{25,17},{17,1},{2,10},{10... | collective-permute-start | bytes 786440 | tf_op jit(solution)/shard_map/ppermute | solution.py:391
  24.7 0.7 %attend.3 = (bf16[40,1024]{1,0:T(8,128)(2,1)S(1)}, bf16[40,1024]{1,0:T(8,128)(2,1)S(1)}, bf16[40,1024]{1,0:T(8,128)(2,1)S(1)}, bf16[40,1024]{1,0:T(8,128)(2,1)S(1)}) custom-call(bf16[128,1024]{1,0:T(8,128)(2,1)S(1)} %get-tuple-element.49.q_ref, bf16[128,1024]{1,0:T(8,128)(2,1)S(1)} %collective-permute-done.4.k_ref, ...), custom_call_target="tpu_custom_call" | custom-call | flops 1 | bytes 1 | tf_op jit(solution)/shard_map/attend/pallas_call | solution.py:214
  25.4 2.5 %collective-permute-start.6 = (bf16[40,1024]{1,0:T(8,128)(2,1)S(1)}, bf16[40,1024]{1,0:T(8,128)(2,1)S(1)}, u32[]{:S(2)}, u32[]{:S(2)}) collective-permute-start(bf16[40,1024]{1,0:T(8,128)(2,1)S(1)} %get-tuple-element.51), channel_id=1, source_target_pairs={{0,6},{2,4},{4,2},{6,0},{1,7},{3,5},{5,3},{7,1},{8,14},{10,12},{12... | collective-permute-start | bytes 245768 | tf_op jit(solution)/shard_map/ppermute | solution.py:63
  28.0 0.5 %collective-permute-start.7 = (bf16[40,1024]{1,0:T(8,128)(2,1)S(1)}, bf16[40,1024]{1,0:T(8,128)(2,1)S(1)}, u32[]{:S(2)}, u32[]{:S(2)}) collective-permute-start(bf16[40,1024]{1,0:T(8,128)(2,1)S(1)} %get-tuple-element.52), channel_id=1, source_target_pairs={{0,2},{2,0},{4,6},{6,4},{1,3},{3,1},{5,7},{7,5},{8,10},{10,8},{12,... | collective-permute-start | bytes 245768 | tf_op jit(solution)/shard_map/ppermute | solution.py:63
  28.5 0.5 %collective-permute-start.8 = (bf16[40,1024]{1,0:T(8,128)(2,1)S(1)}, bf16[40,1024]{1,0:T(8,128)(2,1)S(1)}, u32[]{:S(2)}, u32[]{:S(2)}) collective-permute-start(bf16[40,1024]{1,0:T(8,128)(2,1)S(1)} %get-tuple-element.53), channel_id=1, source_target_pairs={{0,4},{2,6},{4,0},{6,2},{1,5},{3,7},{5,1},{7,3},{8,12},{10,14},{12... | collective-permute-start | bytes 245768 | tf_op jit(solution)/shard_map/ppermute | solution.py:63
  29.0 0.7 %place.3 = (bf16[128,1024]{1,0:T(8,128)(2,1)S(1)}, bf16[128,1024]{1,0:T(8,128)(2,1)S(1)}, f32[128,128]{1,0:T(8,128)S(1)}) custom-call(bf16[40,2048]{1,0:T(8,128)(2,1)S(1)} %get-tuple-element.40.refs_0_, bf16[40,2048]{1,0:T(8,128)(2,1)S(1)} %collective-permute-done.1.refs_1_, bf16[40,2048]{1,0:T(8,128)(2,1)S(1)} %collective-permute-done.2.refs_2_, ...), custom_call_target="tpu_custom_call" | custom-call | flops 1 | bytes 1 | tf_op jit(solution)/shard_map/place/pallas_call | solution.py:309
  29.7 0.0 collective-permute-done.9.k_ref
  29.7 0.4 weigh.1
  30.1 0.8 %collective-permute-done.6.refs_1_ = bf16[40,1024]{1,0:T(8,128)(2,1)S(1)} collective-permute-done((bf16[40,1024]{1,0:T(8,128)(2,1)S(1)}, bf16[40,1024]{1,0:T(8,128)(2,1)S(1)}, u32[]{:S(2)}, u32[]{:S(2)}) %collective-permute-start.6) | collective-permute-done | bytes 81952 | tf_op jit(solution)/shard_map/ppermute | solution.py:63
  30.9 1.5 %collective-permute-done.7.refs_2_ = bf16[40,1024]{1,0:T(8,128)(2,1)S(1)} collective-permute-done((bf16[40,1024]{1,0:T(8,128)(2,1)S(1)}, bf16[40,1024]{1,0:T(8,128)(2,1)S(1)}, u32[]{:S(2)}, u32[]{:S(2)}) %collective-permute-start.7) | collective-permute-done | bytes 81952 | tf_op jit(solution)/shard_map/ppermute | solution.py:63
  32.4 0.5 %collective-permute-done.8.refs_3_ = bf16[40,1024]{1,0:T(8,128)(2,1)S(1)} collective-permute-done((bf16[40,1024]{1,0:T(8,128)(2,1)S(1)}, bf16[40,1024]{1,0:T(8,128)(2,1)S(1)}, u32[]{:S(2)}, u32[]{:S(2)}) %collective-permute-start.8) | collective-permute-done | bytes 81952 | tf_op jit(solution)/shard_map/ppermute | solution.py:63
  32.9 1.0 %collective-permute-done.10.v_ref = bf16[128,1024]{1,0:T(8,128)(2,1)S(1)} collective-permute-done((bf16[128,1024]{1,0:T(8,128)(2,1)S(1)}, bf16[128,1024]{1,0:T(8,128)(2,1)S(1)}, u32[]{:S(2)}, u32[]{:S(2)}) %collective-permute-start.10) | collective-permute-done | bytes 262176 | tf_op jit(solution)/shard_map/ppermute | solution.py:391
  33.9 1.7 %collective-permute-start.14 = (bf16[128,1024]{1,0:T(8,128)(2,1)S(1)}, bf16[128,1024]{1,0:T(8,128)(2,1)S(1)}, u32[]{:S(2)}, u32[]{:S(2)}) collective-permute-start(bf16[128,1024]{1,0:T(8,128)(2,1)S(1)} %get-tuple-element.65), channel_id=1, source_target_pairs={{8,0},{24,8},{16,24},{0,16},{9,1},{25,9},{17,25},{1,17},{10,2},{26... | collective-permute-start | bytes 786440 | tf_op jit(solution)/shard_map/ppermute | solution.py:394
  35.6 0.5 finish.1
  36.1 2.5 %collective-permute-start.11 = (bf16[40,1024]{1,0:T(8,128)(2,1)S(1)}, bf16[40,1024]{1,0:T(8,128)(2,1)S(1)}, u32[]{:S(2)}, u32[]{:S(2)}) collective-permute-start(bf16[40,1024]{1,0:T(8,128)(2,1)S(1)} %get-tuple-element.61), channel_id=1, source_target_pairs={{0,6},{2,4},{4,2},{6,0},{1,7},{3,5},{5,3},{7,1},{8,14},{10,12},{12... | collective-permute-start | bytes 245768 | tf_op jit(solution)/shard_map/ppermute | solution.py:63
  38.6 0.5 %collective-permute-start.12 = (bf16[40,1024]{1,0:T(8,128)(2,1)S(1)}, bf16[40,1024]{1,0:T(8,128)(2,1)S(1)}, u32[]{:S(2)}, u32[]{:S(2)}) collective-permute-start(bf16[40,1024]{1,0:T(8,128)(2,1)S(1)} %get-tuple-element.62), channel_id=1, source_target_pairs={{0,2},{2,0},{4,6},{6,4},{1,3},{3,1},{5,7},{7,5},{8,10},{10,8},{12,... | collective-permute-start | bytes 245768 | tf_op jit(solution)/shard_map/ppermute | solution.py:63
  39.2 0.5 %collective-permute-start.13 = (bf16[40,1024]{1,0:T(8,128)(2,1)S(1)}, bf16[40,1024]{1,0:T(8,128)(2,1)S(1)}, u32[]{:S(2)}, u32[]{:S(2)}) collective-permute-start(bf16[40,1024]{1,0:T(8,128)(2,1)S(1)} %get-tuple-element.63), channel_id=1, source_target_pairs={{0,4},{2,6},{4,0},{6,2},{1,5},{3,7},{5,1},{7,3},{8,12},{10,14},{12... | collective-permute-start | bytes 245768 | tf_op jit(solution)/shard_map/ppermute | solution.py:63
  39.7 0.4 place.4
  40.1 1.5 %collective-permute-done.11.refs_1_ = bf16[40,1024]{1,0:T(8,128)(2,1)S(1)} collective-permute-done((bf16[40,1024]{1,0:T(8,128)(2,1)S(1)}, bf16[40,1024]{1,0:T(8,128)(2,1)S(1)}, u32[]{:S(2)}, u32[]{:S(2)}) %collective-permute-start.11) | collective-permute-done | bytes 81952 | tf_op jit(solution)/shard_map/ppermute | solution.py:63
  41.6 1.4 %collective-permute-done.12.refs_2_ = bf16[40,1024]{1,0:T(8,128)(2,1)S(1)} collective-permute-done((bf16[40,1024]{1,0:T(8,128)(2,1)S(1)}, bf16[40,1024]{1,0:T(8,128)(2,1)S(1)}, u32[]{:S(2)}, u32[]{:S(2)}) %collective-permute-start.12) | collective-permute-done | bytes 81952 | tf_op jit(solution)/shard_map/ppermute | solution.py:63
  43.1 0.5 %collective-permute-done.13.refs_3_ = bf16[40,1024]{1,0:T(8,128)(2,1)S(1)} collective-permute-done((bf16[40,1024]{1,0:T(8,128)(2,1)S(1)}, bf16[40,1024]{1,0:T(8,128)(2,1)S(1)}, u32[]{:S(2)}, u32[]{:S(2)}) %collective-permute-start.13) | collective-permute-done | bytes 81952 | tf_op jit(solution)/shard_map/ppermute | solution.py:63
  43.6 0.0 collective-permute-done.14.refs_8_.refs_3_
  43.6 0.0 copy-start.5
  43.6 0.4 place.5
  44.0 0.1 collective-permute-start.15
  44.1 0.2 copy-done.5
  44.3 1.0 %collective-permute-done.15.refs_5_ = f32[128,128]{1,0:T(8,128)S(1)} collective-permute-done((f32[128,128]{1,0:T(8,128)S(1)}, f32[128,128]{1,0:T(8,128)S(1)}, u32[]{:S(2)}, u32[]{:S(2)}) %collective-permute-start.15) | collective-permute-done | bytes 65568 | tf_op jit(solution)/shard_map/ppermute | solution.py:399
  45.3 1.2 %norm.1 = bf16[128,4096]{1,0:T(8,128)(2,1)} custom-call(bf16[128,1024]{1,0:T(8,128)(2,1)S(1)} %get-tuple-element.48.refs_0_, bf16[128,1024]{1,0:T(8,128)(2,1)S(1)} %get-tuple-element.55.refs_1_, bf16[128,1024]{1,0:T(8,128)(2,1)S(1)} %get-tuple-element.67.refs_2_, bf16[128,1024]{1,0:T(8,128)(2,1)S(1)} %collective-permute-done.14.refs_8_.refs_3_, ...), custom_call_target="tpu_custom_call" | custom-call | flops 1 | bytes 1 | tf_op jit(solution)/shard_map/norm/pallas_call | solution.py:350
  (1 shorter events, 0.0 us)
Async XLA Ops:
  0.0 4.1 %copy-start.1 = (bf16[128,1,1,1024]{3,0,2,1:T(8,128)(2,1)S(1)}, bf16[128,1,1,1024]{3,0,2,1:T(8,128)(2,1)}, u32[]{:S(2)}) copy-start(bf16[128,1,1,1024]{3,0,2,1:T(8,128)(2,1)} %param.7) | copy-start | bytes 786436
  0.0 6.7 %copy-start.2 = (bf16[128,1,1,1024]{3,0,2,1:T(8,128)(2,1)S(1)}, bf16[128,1,1,1024]{3,0,2,1:T(8,128)(2,1)}, u32[]{:S(2)}) copy-start(bf16[128,1,1,1024]{3,0,2,1:T(8,128)(2,1)} %param.8) | copy-start | bytes 786436
  1.0 11.2 %collective-permute-start = (bf16[128,1024]{1,0:T(8,128)(2,1)S(1)}, bf16[128,1024]{1,0:T(8,128)(2,1)S(1)}, u32[]{:S(2)}, u32[]{:S(2)}) collective-permute-start(bf16[128,1024]{1,0:T(8,128)(2,1)S(1)} %dynamic-slice_bitcast_fusion), channel_id=1, source_target_pairs={{0,8},{8,24},{24,16},{16,0},{1,9},{9,25},{25,17},{17,1},{2,10},{10... | collective-permute-start | bytes 786440 | tf_op jit(solution)/shard_map/ppermute | solution.py:379
  4.1 13.8 %collective-permute-start.4 = (bf16[128,1024]{1,0:T(8,128)(2,1)S(1)}, bf16[128,1024]{1,0:T(8,128)(2,1)S(1)}, u32[]{:S(2)}, u32[]{:S(2)}) collective-permute-start(bf16[128,1024]{1,0:T(8,128)(2,1)S(1)} %bitcast.8), channel_id=1, source_target_pairs={{0,8},{8,24},{24,16},{16,0},{1,9},{9,25},{25,17},{17,1},{2,10},{10... | collective-permute-start | bytes 786440 | tf_op jit(solution)/shard_map/ppermute | solution.py:378
  6.7 16.8 %collective-permute-start.5 = (bf16[128,1024]{1,0:T(8,128)(2,1)S(1)}, bf16[128,1024]{1,0:T(8,128)(2,1)S(1)}, u32[]{:S(2)}, u32[]{:S(2)}) collective-permute-start(bf16[128,1024]{1,0:T(8,128)(2,1)S(1)} %bitcast.11), channel_id=1, source_target_pairs={{0,8},{8,24},{24,16},{16,0},{1,9},{9,25},{25,17},{17,1},{2,10},{10... | collective-permute-start | bytes 786440 | tf_op jit(solution)/shard_map/ppermute | solution.py:378
  7.2 1.2 %copy-start = (bf16[1,128,4096]{2,1,0:T(8,128)(2,1)S(1)}, bf16[1,128,4096]{2,1,0:T(8,128)(2,1)}, u32[]{:S(2)}) copy-start(bf16[1,128,4096]{2,1,0:T(8,128)(2,1)} %param.6) | copy-start | bytes 3145732
  8.4 0.7 %copy-start.3 = (s32[4,4]{1,0:T(4,128)S(1)}, s32[4,4]{1,0:T(4,128)}, u32[]{:S(2)}) copy-start(s32[4,4]{1,0:T(4,128)} %counts.1) | copy-start | bytes 196
  8.4 0.7 %copy-start.4 = (s32[1,6]{1,0:T(1,128)S(1)}, s32[1,6]{1,0:T(1,128)}, u32[]{:S(2)}) copy-start(s32[1,6]{1,0:T(1,128)} %docs.1) | copy-start | bytes 76
  13.0 10.5 %collective-permute-start.1 = (bf16[40,2048]{1,0:T(8,128)(2,1)S(1)}, bf16[40,2048]{1,0:T(8,128)(2,1)S(1)}, u32[]{:S(2)}, u32[]{:S(2)}) collective-permute-start(bf16[40,2048]{1,0:T(8,128)(2,1)S(1)} %get-tuple-element.41), channel_id=1, source_target_pairs={{0,6},{2,4},{4,2},{6,0},{1,7},{3,5},{5,3},{7,1},{8,14},{10,12},{12... | collective-permute-start | bytes 491528 | tf_op jit(solution)/shard_map/ppermute | solution.py:63
  15.9 7.6 %collective-permute-start.2 = (bf16[40,2048]{1,0:T(8,128)(2,1)S(1)}, bf16[40,2048]{1,0:T(8,128)(2,1)S(1)}, u32[]{:S(2)}, u32[]{:S(2)}) collective-permute-start(bf16[40,2048]{1,0:T(8,128)(2,1)S(1)} %get-tuple-element.42), channel_id=1, source_target_pairs={{0,2},{2,0},{4,6},{6,4},{1,3},{3,1},{5,7},{7,5},{8,10},{10,8},{12,... | collective-permute-start | bytes 491528 | tf_op jit(solution)/shard_map/ppermute | solution.py:63
  16.4 7.1 %collective-permute-start.3 = (bf16[40,2048]{1,0:T(8,128)(2,1)S(1)}, bf16[40,2048]{1,0:T(8,128)(2,1)S(1)}, u32[]{:S(2)}, u32[]{:S(2)}) collective-permute-start(bf16[40,2048]{1,0:T(8,128)(2,1)S(1)} %get-tuple-element.43), channel_id=1, source_target_pairs={{0,4},{2,6},{4,0},{6,2},{1,5},{3,7},{5,1},{7,3},{8,12},{10,14},{12... | collective-permute-start | bytes 491528 | tf_op jit(solution)/shard_map/ppermute | solution.py:63
  17.9 11.8 %collective-permute-start.9 = (bf16[128,1024]{1,0:T(8,128)(2,1)S(1)}, bf16[128,1024]{1,0:T(8,128)(2,1)S(1)}, u32[]{:S(2)}, u32[]{:S(2)}) collective-permute-start(bf16[128,1024]{1,0:T(8,128)(2,1)S(1)} %collective-permute-done.4.k_ref), channel_id=1, source_target_pairs={{0,8},{8,24},{24,16},{16,0},{1,9},{9,25},{25,17},{17,1},{2,10},{10... | collective-permute-start | bytes 786440 | tf_op jit(solution)/shard_map/ppermute | solution.py:391
  23.5 10.4 %collective-permute-start.10 = (bf16[128,1024]{1,0:T(8,128)(2,1)S(1)}, bf16[128,1024]{1,0:T(8,128)(2,1)S(1)}, u32[]{:S(2)}, u32[]{:S(2)}) collective-permute-start(bf16[128,1024]{1,0:T(8,128)(2,1)S(1)} %collective-permute-done.5.v_ref), channel_id=1, source_target_pairs={{0,8},{8,24},{24,16},{16,0},{1,9},{9,25},{25,17},{17,1},{2,10},{10... | collective-permute-start | bytes 786440 | tf_op jit(solution)/shard_map/ppermute | solution.py:391
  25.4 5.4 %collective-permute-start.6 = (bf16[40,1024]{1,0:T(8,128)(2,1)S(1)}, bf16[40,1024]{1,0:T(8,128)(2,1)S(1)}, u32[]{:S(2)}, u32[]{:S(2)}) collective-permute-start(bf16[40,1024]{1,0:T(8,128)(2,1)S(1)} %get-tuple-element.51), channel_id=1, source_target_pairs={{0,6},{2,4},{4,2},{6,0},{1,7},{3,5},{5,3},{7,1},{8,14},{10,12},{12... | collective-permute-start | bytes 245768 | tf_op jit(solution)/shard_map/ppermute | solution.py:63
  28.0 4.4 %collective-permute-start.7 = (bf16[40,1024]{1,0:T(8,128)(2,1)S(1)}, bf16[40,1024]{1,0:T(8,128)(2,1)S(1)}, u32[]{:S(2)}, u32[]{:S(2)}) collective-permute-start(bf16[40,1024]{1,0:T(8,128)(2,1)S(1)} %get-tuple-element.52), channel_id=1, source_target_pairs={{0,2},{2,0},{4,6},{6,4},{1,3},{3,1},{5,7},{7,5},{8,10},{10,8},{12,... | collective-permute-start | bytes 245768 | tf_op jit(solution)/shard_map/ppermute | solution.py:63
  28.5 4.4 %collective-permute-start.8 = (bf16[40,1024]{1,0:T(8,128)(2,1)S(1)}, bf16[40,1024]{1,0:T(8,128)(2,1)S(1)}, u32[]{:S(2)}, u32[]{:S(2)}) collective-permute-start(bf16[40,1024]{1,0:T(8,128)(2,1)S(1)} %get-tuple-element.53), channel_id=1, source_target_pairs={{0,4},{2,6},{4,0},{6,2},{1,5},{3,7},{5,1},{7,3},{8,12},{10,14},{12... | collective-permute-start | bytes 245768 | tf_op jit(solution)/shard_map/ppermute | solution.py:63
  33.9 9.7 %collective-permute-start.14 = (bf16[128,1024]{1,0:T(8,128)(2,1)S(1)}, bf16[128,1024]{1,0:T(8,128)(2,1)S(1)}, u32[]{:S(2)}, u32[]{:S(2)}) collective-permute-start(bf16[128,1024]{1,0:T(8,128)(2,1)S(1)} %get-tuple-element.65), channel_id=1, source_target_pairs={{8,0},{24,8},{16,24},{0,16},{9,1},{25,9},{17,25},{1,17},{10,2},{26... | collective-permute-start | bytes 786440 | tf_op jit(solution)/shard_map/ppermute | solution.py:394
  36.1 5.5 %collective-permute-start.11 = (bf16[40,1024]{1,0:T(8,128)(2,1)S(1)}, bf16[40,1024]{1,0:T(8,128)(2,1)S(1)}, u32[]{:S(2)}, u32[]{:S(2)}) collective-permute-start(bf16[40,1024]{1,0:T(8,128)(2,1)S(1)} %get-tuple-element.61), channel_id=1, source_target_pairs={{0,6},{2,4},{4,2},{6,0},{1,7},{3,5},{5,3},{7,1},{8,14},{10,12},{12... | collective-permute-start | bytes 245768 | tf_op jit(solution)/shard_map/ppermute | solution.py:63
  38.6 4.4 %collective-permute-start.12 = (bf16[40,1024]{1,0:T(8,128)(2,1)S(1)}, bf16[40,1024]{1,0:T(8,128)(2,1)S(1)}, u32[]{:S(2)}, u32[]{:S(2)}) collective-permute-start(bf16[40,1024]{1,0:T(8,128)(2,1)S(1)} %get-tuple-element.62), channel_id=1, source_target_pairs={{0,2},{2,0},{4,6},{6,4},{1,3},{3,1},{5,7},{7,5},{8,10},{10,8},{12,... | collective-permute-start | bytes 245768 | tf_op jit(solution)/shard_map/ppermute | solution.py:63
  39.2 4.4 %collective-permute-start.13 = (bf16[40,1024]{1,0:T(8,128)(2,1)S(1)}, bf16[40,1024]{1,0:T(8,128)(2,1)S(1)}, u32[]{:S(2)}, u32[]{:S(2)}) collective-permute-start(bf16[40,1024]{1,0:T(8,128)(2,1)S(1)} %get-tuple-element.63), channel_id=1, source_target_pairs={{0,4},{2,6},{4,0},{6,2},{1,5},{3,7},{5,1},{7,3},{8,12},{10,14},{12... | collective-permute-start | bytes 245768 | tf_op jit(solution)/shard_map/ppermute | solution.py:63
  43.6 0.7 %copy-start.5 = (bf16[4096]{0:T(1024)(128)(2,1)S(1)}, bf16[4096]{0:T(1024)(128)(2,1)}, u32[]{:S(2)}) copy-start(bf16[4096]{0:T(1024)(128)(2,1)} %param.11) | copy-start | bytes 24580
  44.0 1.3 %collective-permute-start.15 = (f32[128,128]{1,0:T(8,128)S(1)}, f32[128,128]{1,0:T(8,128)S(1)}, u32[]{:S(2)}, u32[]{:S(2)}) collective-permute-start(f32[128,128]{1,0:T(8,128)S(1)} %get-tuple-element.68.refs_4_), channel_id=1, source_target_pairs={{0,1},{1,0},{2,3},{3,2},{4,5},{5,4},{6,7},{7,6},{8,9},{9,8},{10,11... | collective-permute-start | bytes 196616 | tf_op jit(solution)/shard_map/ppermute | solution.py:399

commit v8 on v7

--- a/solution.py
+++ b/solution.py
@@ -248,23 +248,23 @@
 
 
 def finish_kernel(plan, weights, inverses, v_ref, send, *refs):
-    outs, attn = refs[:-1], refs[-1]
+    outs, attn = refs[-1 - plan.parts : -1], refs[-1]
     for h, cols in enumerate(head_columns(plan)):
         attn[cols, :] = weighted(v_ref, cols, weights[cols, :], inverses[h : h + 1, :])
     pick_rows(plan, send, attn, outs)
 
 
-def finish(plan, weights, inverses, v, send):
+def finish(plan, weights, inverses, v, send, after=()):
     return pl.pallas_call(
         functools.partial(finish_kernel, plan),
         out_shape=[jax.ShapeDtypeStruct((plan.rows, plan.block), jnp.bfloat16)] * plan.parts,
-        in_specs=[VMEM] * 4,
+        in_specs=[VMEM] * 4 + [ANY] * len(after),
         out_specs=[VMEM] * plan.parts,
         scratch_shapes=[pltpu.VMEM((plan.block, plan.seq), jnp.bfloat16)],
         compiler_params=PARAMS,
         cost_estimate=COST,
         name="finish",
-    )(weights, inverses, v, send)
+    )(weights, inverses, v, send, *after)
 
 
 def squares_of(ref):
@@ -382,17 +382,21 @@
     mine, borrowed, total = place(plan, arrived, places, (block, block), summed=1)
     pieces = [(mine, 0, 0)]
     for t in range(1, n - 2):
-        sent = attend(plan, asked[t], k, v, bias, send)
+        sent = attend(plan, asked[t], k, v, bias, send, after=arrived[1:2] or arrived)
         got = plan.regroup(sent)
         placed, total = place(plan, got, places, (block,), sums=(total,))
         pieces.append((placed, t, 0))
         if t == 1:
-            v, *_ = lax.optimization_barrier((v, *arrived))
+            pass
         k, v = lax.ppermute(k, "pipe", forward), lax.ppermute(v, "pipe", forward)
-    weights = weigh(plan, asked[n - 2], k, bias, after=())
-    borrowed, *_ = lax.optimization_barrier((borrowed, *weights, v, *got))
+    weights = weigh(plan, asked[n - 2], k, bias, after=(borrowed,))
+    if plan.tensor == 2:
+        met = lax.ppermute(weights[1], "tensor", [(0, 1), (1, 0)])
+    else:
+        met = weights[1]
+    borrowed, *_ = lax.optimization_barrier((borrowed, met, *got))
     returned = lax.ppermute(borrowed, "pipe", backward)
-    got = plan.regroup(finish(plan, *weights, v, send))
+    got = plan.regroup(finish(plan, *weights, v, send, after=(met,)))
     placed, total = place(plan, got, places, (block,), blocks=(returned,), sums=(total,))
     pieces += [(placed, n - 2, 0), (returned, n - 1, 0)]
     if plan.tensor == 2:

time: 46.8 us -> 44.8 us (0.957)
  waiting for transfers between devices: 16.1 us -> 14.3 us
    ppermute x1, waiting for transfers between devices: 4.46 us -> 1.31 us  [body(): lax.ppermute(values, 'pipe', forward)]
    ppermute x1, waiting for transfers between devices: 1.31 us -> 4.24 us  [body(): lax.ppermute(keys, 'pipe', forward)]
    ppermute x2, waiting for transfers between devices: 0.97 us -> 0.01 us  [body(): k, v = (lax.ppermute(k, 'pipe', forward), lax.ppermute(v, 'pipe', forward))]
    ppermute x1, waiting for transfers between devices: 1.97 us -> 1.22 us  [body(): lent = lax.ppermute(ahead, 'pipe', forward)]
  transfers between devices with their start and end apart: 16 -> 17, of which waited for: 11 -> 11; matrix products, arithmetic and copies ran while one was open for 0% -> 2% of each run, Pallas kernels for 10% -> 11%
where the time goes in v8:
time: 44.8 us; the launch traced here: 44.6 us
  starting transfers between devices  20.8 us (46%)
  waiting for transfers between devices  14.3 us (32%)
  Pallas kernels  6.28 us (14%)
  local copies, waits for them, and re-layouts  3.02 us (7%)
    ppermute x9, starting transfers between devices, regroup(): lax.ppermute(part, 'dp', [(g, g ^ step) for g in range(self.groups)])  10.7 us
    ppermute x9, waiting for transfers between devices, regroup(): lax.ppermute(part, 'dp', [(g, g ^ step) for g in range(self.groups)])  6.46 us
    ppermute x1, waiting for transfers between devices, body(): lax.ppermute(keys, 'pipe', forward)  4.24 us
    ppermute x1, starting transfers between devices, body(): lax.ppermute(keys, 'pipe', forward)  3.02 us
    ppermute x1, starting transfers between devices, body(): lent = lax.ppermute(ahead, 'pipe', forward)  2.64 us
    ppermute x2, starting transfers between devices, body(): k, v = (lax.ppermute(k, 'pipe', forward), lax.ppermute(v, 'pipe', forward))  2.42 us
    unnamed x12, local copies, waits for them, and re-layouts  2.01 us
    pallas_call x3, Pallas kernels, place(): pl.pallas_call(functools.partial(place_kernel, plan, widths, summed, len(...  1.51 us
  transfers between devices with their start and end apart: 17, of which 11 were waited for; matrix products, arithmetic and copies ran while one was open for 2% of the time, Pallas kernels for 11%

profile of v8, /device:TPU:0, one launch (start us, length us, event | category | flops | bytes accessed | tf_op | source)
XLA Modules:
  0.0 44.6 jit_solution(7634793413007892625)
XLA Ops:
  0.0 3.0 %collective-permute-start.4 = (bf16[128,1024]{1,0:T(8,128)(2,1)}, bf16[128,1024]{1,0:T(8,128)(2,1)S(1)}, u32[]{:S(2)}, u32[]{:S(2)}) collective-permute-start(bf16[128,1024]{1,0:T(8,128)(2,1)} %bitcast.8), channel_id=1, source_target_pairs={{0,8},{8,24},{24,16},{16,0},{1,9},{9,25},{25,17},{17,1},{2,10},{10... | collective-permute-start | bytes 786440 | tf_op jit(solution)/shard_map/ppermute | solution.py:378
  3.0 0.0 copy-start.2
  3.0 1.0 %dynamic-slice_bitcast_fusion = bf16[128,1024]{1,0:T(8,128)(2,1)S(1)} fusion(bf16[1,128,4096]{2,1,0:T(8,128)(2,1)} %param.6, s32[]{:T(128)S(6)} %select_n.16), kind=kLoop, calls=%fused_computation | loop fusion | bytes 524292 | tf_op jit(solution)/shard_map/dynamic_slice | solution.py:375
  4.0 2.6 %collective-permute-start = (bf16[128,1024]{1,0:T(8,128)(2,1)S(1)}, bf16[128,1024]{1,0:T(8,128)(2,1)S(1)}, u32[]{:S(2)}, u32[]{:S(2)}) collective-permute-start(bf16[128,1024]{1,0:T(8,128)(2,1)S(1)} %dynamic-slice_bitcast_fusion), channel_id=1, source_target_pairs={{0,8},{8,24},{24,16},{16,0},{1,9},{9,25},{25,17},{17,1},{2,10},{10... | collective-permute-start | bytes 786440 | tf_op jit(solution)/shard_map/ppermute | solution.py:379
  6.7 0.0 copy-done.2
  6.7 0.4 %collective-permute-start.5 = (bf16[128,1024]{1,0:T(8,128)(2,1)S(1)}, bf16[128,1024]{1,0:T(8,128)(2,1)S(1)}, u32[]{:S(2)}, u32[]{:S(2)}) collective-permute-start(bf16[128,1024]{1,0:T(8,128)(2,1)S(1)} %bitcast.11), channel_id=1, source_target_pairs={{0,8},{8,24},{24,16},{16,0},{1,9},{9,25},{25,17},{17,1},{2,10},{10... | collective-permute-start | bytes 786440 | tf_op jit(solution)/shard_map/ppermute | solution.py:378
  7.1 4.2 %collective-permute-done.4.k_ref = bf16[128,1024]{1,0:T(8,128)(2,1)S(1)} collective-permute-done((bf16[128,1024]{1,0:T(8,128)(2,1)}, bf16[128,1024]{1,0:T(8,128)(2,1)S(1)}, u32[]{:S(2)}, u32[]{:S(2)}) %collective-permute-start.4) | collective-permute-done | bytes 262176 | tf_op jit(solution)/shard_map/ppermute | solution.py:378
  11.4 1.3 %collective-permute-start.9 = (bf16[128,1024]{1,0:T(8,128)(2,1)S(1)}, bf16[128,1024]{1,0:T(8,128)(2,1)S(1)}, u32[]{:S(2)}, u32[]{:S(2)}) collective-permute-start(bf16[128,1024]{1,0:T(8,128)(2,1)S(1)} %collective-permute-done.4.k_ref), channel_id=1, source_target_pairs={{0,8},{8,24},{24,16},{16,0},{1,9},{9,25},{25,17},{17,1},{2,10},{10... | collective-permute-start | bytes 786440 | tf_op jit(solution)/shard_map/ppermute | solution.py:391
  12.6 0.0 copy-start
  12.6 1.2 %copy-done = bf16[1,128,4096]{2,1,0:T(8,128)(2,1)S(1)} copy-done((bf16[1,128,4096]{2,1,0:T(8,128)(2,1)S(1)}, bf16[1,128,4096]{2,1,0:T(8,128)(2,1)}, u32[]{:S(2)}) %copy-start) | copy-done | bytes 1048600
  13.9 0.0 copy-start.3
  13.9 0.0 copy-start.4
  13.9 0.0 copy-start.1
  13.9 0.1 split.1
  14.0 0.6 %copy-done.3 = s32[4,4]{1,0:T(4,128)S(1)} copy-done((s32[4,4]{1,0:T(4,128)S(1)}, s32[4,4]{1,0:T(4,128)}, u32[]{:S(2)}) %copy-start.3) | copy-done | bytes 88
  14.5 0.0 copy-done.4
  14.6 0.7 %tables.1 = (f32[128,128]{1,0:T(8,128)S(1)}, bf16[160,128]{1,0:T(8,128)(2,1)S(1)}, bf16[128,40]{1,0:T(8,128)(2,1)S(1)}, bf16[128,40]{1,0:T(8,128)(2,1)S(1)}, bf1...) custom-call(s32[1,6]{1,0:T(1,128)S(1)} %copy-done.4, s32[4,4]{1,0:T(4,128)S(1)} %copy-done.3), custom_call_target="tpu_custom_call" | custom-call | flops 1 | bytes 1 | tf_op jit(solution)/shard_map/tables/pallas_call | solution.py:136
  15.2 0.0 copy-done.1
  15.2 0.5 %heads.1.refs_0_ = bf16[1024,128]{1,0:T(8,128)(2,1)S(1)} custom-call(bf16[128,1024]{1,0:T(8,128)(2,1)S(1)} %get-tuple-element.38.q_ref, bf16[128,1024]{1,0:T(8,128)(2,1)S(1)} %bitcast.9, bf16[128,1024]{1,0:T(8,128)(2,1)S(1)} %bitcast.12, f32[128,128]{1,0:T(8,128)S(1)} %get-tuple-element.36.bias._, f32[128,128]{1,0:T(8,128)S(1)} %get-tuple-element.36.bias._), custom_call_target="tpu_custom_call" | custom-call | flops 1 | bytes 1 | tf_op jit(solution)/shard_map/heads/pallas_call | solution.py:190
  15.8 1.2 %collective-permute-done.q_ref = bf16[128,1024]{1,0:T(8,128)(2,1)S(1)} collective-permute-done((bf16[128,1024]{1,0:T(8,128)(2,1)S(1)}, bf16[128,1024]{1,0:T(8,128)(2,1)S(1)}, u32[]{:S(2)}, u32[]{:S(2)}) %collective-permute-start) | collective-permute-done | bytes 262176 | tf_op jit(solution)/shard_map/ppermute | solution.py:379
  17.0 0.7 %attend.2 = (bf16[40,2048]{1,0:T(8,128)(2,1)S(1)}, bf16[40,2048]{1,0:T(8,128)(2,1)S(1)}, bf16[40,2048]{1,0:T(8,128)(2,1)S(1)}, bf16[40,2048]{1,0:T(8,128)(2,1)S(1)}) custom-call(bf16[128,1024]{1,0:T(8,128)(2,1)S(1)} %collective-permute-done.q_ref, bf16[128,1024]{1,0:T(8,128)(2,1)S(1)} %bitcast.10, bf16[128,1024]{1,0:T(8,128)(2,1)S(1)} %bitcast.13, ...), custom_call_target="tpu_custom_call" | custom-call | flops 1 | bytes 1 | tf_op jit(solution)/shard_map/attend/pallas_call | solution.py:214
  17.7 2.9 %collective-permute-start.1 = (bf16[40,2048]{1,0:T(8,128)(2,1)S(1)}, bf16[40,2048]{1,0:T(8,128)(2,1)S(1)}, u32[]{:S(2)}, u32[]{:S(2)}) collective-permute-start(bf16[40,2048]{1,0:T(8,128)(2,1)S(1)} %get-tuple-element.40), channel_id=1, source_target_pairs={{0,6},{2,4},{4,2},{6,0},{1,7},{3,5},{5,3},{7,1},{8,14},{10,12},{12... | collective-permute-start | bytes 491528 | tf_op jit(solution)/shard_map/ppermute | solution.py:63
  20.6 0.5 %collective-permute-start.2 = (bf16[40,2048]{1,0:T(8,128)(2,1)S(1)}, bf16[40,2048]{1,0:T(8,128)(2,1)S(1)}, u32[]{:S(2)}, u32[]{:S(2)}) collective-permute-start(bf16[40,2048]{1,0:T(8,128)(2,1)S(1)} %get-tuple-element.41), channel_id=1, source_target_pairs={{0,2},{2,0},{4,6},{6,4},{1,3},{3,1},{5,7},{7,5},{8,10},{10,8},{12,... | collective-permute-start | bytes 491528 | tf_op jit(solution)/shard_map/ppermute | solution.py:63
  21.2 0.1 collective-permute-start.3
  21.3 1.3 %collective-permute-done.5.v_ref = bf16[128,1024]{1,0:T(8,128)(2,1)S(1)} collective-permute-done((bf16[128,1024]{1,0:T(8,128)(2,1)S(1)}, bf16[128,1024]{1,0:T(8,128)(2,1)S(1)}, u32[]{:S(2)}, u32[]{:S(2)}) %collective-permute-start.5) | collective-permute-done | bytes 262176 | tf_op jit(solution)/shard_map/ppermute | solution.py:378
  22.6 1.2 %collective-permute-start.10 = (bf16[128,1024]{1,0:T(8,128)(2,1)S(1)}, bf16[128,1024]{1,0:T(8,128)(2,1)S(1)}, u32[]{:S(2)}, u32[]{:S(2)}) collective-permute-start(bf16[128,1024]{1,0:T(8,128)(2,1)S(1)} %collective-permute-done.5.v_ref), channel_id=1, source_target_pairs={{0,8},{8,24},{24,16},{16,0},{1,9},{9,25},{25,17},{17,1},{2,10},{10... | collective-permute-start | bytes 786440 | tf_op jit(solution)/shard_map/ppermute | solution.py:391
  23.8 1.3 %collective-permute-done.1.refs_1_.refs_0_ = bf16[40,2048]{1,0:T(8,128)(2,1)S(1)} collective-permute-done((bf16[40,2048]{1,0:T(8,128)(2,1)S(1)}, bf16[40,2048]{1,0:T(8,128)(2,1)S(1)}, u32[]{:S(2)}, u32[]{:S(2)}) %collective-permute-start.1) | collective-permute-done | bytes 163872 | tf_op jit(solution)/shard_map/ppermute | solution.py:63
  25.0 0.7 %attend.3 = (bf16[40,1024]{1,0:T(8,128)(2,1)S(1)}, bf16[40,1024]{1,0:T(8,128)(2,1)S(1)}, bf16[40,1024]{1,0:T(8,128)(2,1)S(1)}, bf16[40,1024]{1,0:T(8,128)(2,1)S(1)}) custom-call(bf16[128,1024]{1,0:T(8,128)(2,1)S(1)} %get-tuple-element.48.q_ref, bf16[128,1024]{1,0:T(8,128)(2,1)S(1)} %collective-permute-done.4.k_ref, ...), custom_call_target="tpu_custom_call" | custom-call | flops 1 | bytes 1 | tf_op jit(solution)/shard_map/attend/pallas_call | solution.py:214
  25.8 2.3 %collective-permute-start.6 = (bf16[40,1024]{1,0:T(8,128)(2,1)S(1)}, bf16[40,1024]{1,0:T(8,128)(2,1)S(1)}, u32[]{:S(2)}, u32[]{:S(2)}) collective-permute-start(bf16[40,1024]{1,0:T(8,128)(2,1)S(1)} %get-tuple-element.50), channel_id=1, source_target_pairs={{0,6},{2,4},{4,2},{6,0},{1,7},{3,5},{5,3},{7,1},{8,14},{10,12},{12... | collective-permute-start | bytes 245768 | tf_op jit(solution)/shard_map/ppermute | solution.py:63
  28.1 0.0 collective-permute-done.2.refs_2_
  28.1 0.7 %collective-permute-start.7 = (bf16[40,1024]{1,0:T(8,128)(2,1)S(1)}, bf16[40,1024]{1,0:T(8,128)(2,1)S(1)}, u32[]{:S(2)}, u32[]{:S(2)}) collective-permute-start(bf16[40,1024]{1,0:T(8,128)(2,1)S(1)} %get-tuple-element.51), channel_id=1, source_target_pairs={{0,2},{2,0},{4,6},{6,4},{1,3},{3,1},{5,7},{7,5},{8,10},{10,8},{12,... | collective-permute-start | bytes 245768 | tf_op jit(solution)/shard_map/ppermute | solution.py:63
  28.9 0.0 collective-permute-done.3.refs_3_
  28.9 0.5 %collective-permute-start.8 = (bf16[40,1024]{1,0:T(8,128)(2,1)S(1)}, bf16[40,1024]{1,0:T(8,128)(2,1)S(1)}, u32[]{:S(2)}, u32[]{:S(2)}) collective-permute-start(bf16[40,1024]{1,0:T(8,128)(2,1)S(1)} %get-tuple-element.52), channel_id=1, source_target_pairs={{0,4},{2,6},{4,0},{6,2},{1,5},{3,7},{5,1},{7,3},{8,12},{10,14},{12... | collective-permute-start | bytes 245768 | tf_op jit(solution)/shard_map/ppermute | solution.py:63
  29.4 0.7 %place.3 = (bf16[128,1024]{1,0:T(8,128)(2,1)S(1)}, bf16[128,1024]{1,0:T(8,128)(2,1)S(1)}, f32[128,128]{1,0:T(8,128)S(1)}) custom-call(bf16[40,2048]{1,0:T(8,128)(2,1)S(1)} %get-tuple-element.39.refs_0_, bf16[40,2048]{1,0:T(8,128)(2,1)S(1)} %collective-permute-done.1.refs_1_.refs_0_, bf16[40,2048]{1,0:T(8,128)(2,1)S(1)} %collective-permute-done.2.refs_2_, ...), custom_call_target="tpu_custom_call" | custom-call | flops 1 | bytes 1 | tf_op jit(solution)/shard_map/place/pallas_call | solution.py:309
  30.0 0.0 collective-permute-done.9.k_ref
  30.1 0.4 weigh.1
  30.4 0.1 collective-permute-start.11
  30.5 0.7 %collective-permute-done.6.refs_1_ = bf16[40,1024]{1,0:T(8,128)(2,1)S(1)} collective-permute-done((bf16[40,1024]{1,0:T(8,128)(2,1)S(1)}, bf16[40,1024]{1,0:T(8,128)(2,1)S(1)}, u32[]{:S(2)}, u32[]{:S(2)}) %collective-permute-start.6) | collective-permute-done | bytes 81952 | tf_op jit(solution)/shard_map/ppermute | solution.py:63
  31.2 1.4 %collective-permute-done.7.refs_2_ = bf16[40,1024]{1,0:T(8,128)(2,1)S(1)} collective-permute-done((bf16[40,1024]{1,0:T(8,128)(2,1)S(1)}, bf16[40,1024]{1,0:T(8,128)(2,1)S(1)}, u32[]{:S(2)}, u32[]{:S(2)}) %collective-permute-start.7) | collective-permute-done | bytes 81952 | tf_op jit(solution)/shard_map/ppermute | solution.py:63
  32.6 0.7 %collective-permute-done.8.refs_3_ = bf16[40,1024]{1,0:T(8,128)(2,1)S(1)} collective-permute-done((bf16[40,1024]{1,0:T(8,128)(2,1)S(1)}, bf16[40,1024]{1,0:T(8,128)(2,1)S(1)}, u32[]{:S(2)}, u32[]{:S(2)}) %collective-permute-start.8) | collective-permute-done | bytes 81952 | tf_op jit(solution)/shard_map/ppermute | solution.py:63
  33.3 0.0 collective-permute-done.11.refs_0_
  33.3 1.5 %collective-permute-start.15 = (bf16[128,1024]{1,0:T(8,128)(2,1)S(1)}, bf16[128,1024]{1,0:T(8,128)(2,1)S(1)}, u32[]{:S(2)}, u32[]{:S(2)}) collective-permute-start(bf16[128,1024]{1,0:T(8,128)(2,1)S(1)} %get-tuple-element.63.refs_0_), channel_id=1, source_target_pairs={{8,0},{24,8},{16,24},{0,16},{9,1},{25,9},{17,25},{1,17},{10,2},{26... | collective-permute-start | bytes 786440 | tf_op jit(solution)/shard_map/ppermute | solution.py:398
  34.8 0.0 collective-permute-done.10.v_ref
  34.8 0.5 %finish.1 = (bf16[40,1024]{1,0:T(8,128)(2,1)S(1)}, bf16[40,1024]{1,0:T(8,128)(2,1)S(1)}, bf16[40,1024]{1,0:T(8,128)(2,1)S(1)}, bf16[40,1024]{1,0:T(8,128)(2,1)S(1)}) custom-call(bf16[1024,128]{1,0:T(8,128)(2,1)S(1)} %get-tuple-element.57.weights, f32[8,128]{1,0:T(8,128)S(1)} %get-tuple-element.58.inverses, ...), custom_call_target="tpu_custom_call" | custom-call | flops 1 | bytes 1 | tf_op jit(solution)/shard_map/finish/pallas_call | solution.py:258
  35.3 1.4 %collective-permute-start.12 = (bf16[40,1024]{1,0:T(8,128)(2,1)S(1)}, bf16[40,1024]{1,0:T(8,128)(2,1)S(1)}, u32[]{:S(2)}, u32[]{:S(2)}) collective-permute-start(bf16[40,1024]{1,0:T(8,128)(2,1)S(1)} %get-tuple-element.60), channel_id=1, source_target_pairs={{0,6},{2,4},{4,2},{6,0},{1,7},{3,5},{5,3},{7,1},{8,14},{10,12},{12... | collective-permute-start | bytes 245768 | tf_op jit(solution)/shard_map/ppermute | solution.py:63
  36.7 0.5 %collective-permute-start.13 = (bf16[40,1024]{1,0:T(8,128)(2,1)S(1)}, bf16[40,1024]{1,0:T(8,128)(2,1)S(1)}, u32[]{:S(2)}, u32[]{:S(2)}) collective-permute-start(bf16[40,1024]{1,0:T(8,128)(2,1)S(1)} %get-tuple-element.61), channel_id=1, source_target_pairs={{0,2},{2,0},{4,6},{6,4},{1,3},{3,1},{5,7},{7,5},{8,10},{10,8},{12,... | collective-permute-start | bytes 245768 | tf_op jit(solution)/shard_map/ppermute | solution.py:63
  37.2 1.6 %collective-permute-start.14 = (bf16[40,1024]{1,0:T(8,128)(2,1)S(1)}, bf16[40,1024]{1,0:T(8,128)(2,1)S(1)}, u32[]{:S(2)}, u32[]{:S(2)}) collective-permute-start(bf16[40,1024]{1,0:T(8,128)(2,1)S(1)} %get-tuple-element.62), channel_id=1, source_target_pairs={{0,4},{2,6},{4,0},{6,2},{1,5},{3,7},{5,1},{7,3},{8,12},{10,14},{12... | collective-permute-start | bytes 245768 | tf_op jit(solution)/shard_map/ppermute | solution.py:63
  38.8 0.4 place.4
  39.2 1.4 %collective-permute-done.12.refs_1_ = bf16[40,1024]{1,0:T(8,128)(2,1)S(1)} collective-permute-done((bf16[40,1024]{1,0:T(8,128)(2,1)S(1)}, bf16[40,1024]{1,0:T(8,128)(2,1)S(1)}, u32[]{:S(2)}, u32[]{:S(2)}) %collective-permute-start.12) | collective-permute-done | bytes 81952 | tf_op jit(solution)/shard_map/ppermute | solution.py:63
  40.7 0.4 collective-permute-done.13.refs_2_
  41.1 0.5 %collective-permute-done.14.refs_3_ = bf16[40,1024]{1,0:T(8,128)(2,1)S(1)} collective-permute-done((bf16[40,1024]{1,0:T(8,128)(2,1)S(1)}, bf16[40,1024]{1,0:T(8,128)(2,1)S(1)}, u32[]{:S(2)}, u32[]{:S(2)}) %collective-permute-start.14) | collective-permute-done | bytes 81952 | tf_op jit(solution)/shard_map/ppermute | solution.py:63
  41.6 0.0 collective-permute-done.15.refs_8_.refs_3_
  41.6 0.0 copy-start.5
  41.6 0.4 place.5
  42.1 0.1 collective-permute-start.16
  42.1 0.2 copy-done.5
  42.3 1.0 %collective-permute-done.16.refs_5_ = f32[128,128]{1,0:T(8,128)S(1)} collective-permute-done((f32[128,128]{1,0:T(8,128)S(1)}, f32[128,128]{1,0:T(8,128)S(1)}, u32[]{:S(2)}, u32[]{:S(2)}) %collective-permute-start.16) | collective-permute-done | bytes 65568 | tf_op jit(solution)/shard_map/ppermute | solution.py:403
  43.4 1.2 %norm.1 = bf16[128,4096]{1,0:T(8,128)(2,1)} custom-call(bf16[128,1024]{1,0:T(8,128)(2,1)S(1)} %get-tuple-element.47.refs_0_, bf16[128,1024]{1,0:T(8,128)(2,1)S(1)} %get-tuple-element.54.refs_1_, bf16[128,1024]{1,0:T(8,128)(2,1)S(1)} %get-tuple-element.65.refs_2_, bf16[128,1024]{1,0:T(8,128)(2,1)S(1)} %collective-permute-done.15.refs_8_.refs_3_, ...), custom_call_target="tpu_custom_call" | custom-call | flops 1 | bytes 1 | tf_op jit(solution)/shard_map/norm/pallas_call | solution.py:350
  (1 shorter events, 0.0 us)
Async XLA Ops:
  0.0 11.4 %collective-permute-start.4 = (bf16[128,1024]{1,0:T(8,128)(2,1)}, bf16[128,1024]{1,0:T(8,128)(2,1)S(1)}, u32[]{:S(2)}, u32[]{:S(2)}) collective-permute-start(bf16[128,1024]{1,0:T(8,128)(2,1)} %bitcast.8), channel_id=1, source_target_pairs={{0,8},{8,24},{24,16},{16,0},{1,9},{9,25},{25,17},{17,1},{2,10},{10... | collective-permute-start | bytes 786440 | tf_op jit(solution)/shard_map/ppermute | solution.py:378
  3.0 3.7 %copy-start.2 = (bf16[128,1,1,1024]{3,0,2,1:T(8,128)(2,1)S(1)}, bf16[128,1,1,1024]{3,0,2,1:T(8,128)(2,1)}, u32[]{:S(2)}) copy-start(bf16[128,1,1,1024]{3,0,2,1:T(8,128)(2,1)} %param.8) | copy-start | bytes 786436
  4.0 13.0 %collective-permute-start = (bf16[128,1024]{1,0:T(8,128)(2,1)S(1)}, bf16[128,1024]{1,0:T(8,128)(2,1)S(1)}, u32[]{:S(2)}, u32[]{:S(2)}) collective-permute-start(bf16[128,1024]{1,0:T(8,128)(2,1)S(1)} %dynamic-slice_bitcast_fusion), channel_id=1, source_target_pairs={{0,8},{8,24},{24,16},{16,0},{1,9},{9,25},{25,17},{17,1},{2,10},{10... | collective-permute-start | bytes 786440 | tf_op jit(solution)/shard_map/ppermute | solution.py:379
  6.7 15.9 %collective-permute-start.5 = (bf16[128,1024]{1,0:T(8,128)(2,1)S(1)}, bf16[128,1024]{1,0:T(8,128)(2,1)S(1)}, u32[]{:S(2)}, u32[]{:S(2)}) collective-permute-start(bf16[128,1024]{1,0:T(8,128)(2,1)S(1)} %bitcast.11), channel_id=1, source_target_pairs={{0,8},{8,24},{24,16},{16,0},{1,9},{9,25},{25,17},{17,1},{2,10},{10... | collective-permute-start | bytes 786440 | tf_op jit(solution)/shard_map/ppermute | solution.py:378
  11.4 18.7 %collective-permute-start.9 = (bf16[128,1024]{1,0:T(8,128)(2,1)S(1)}, bf16[128,1024]{1,0:T(8,128)(2,1)S(1)}, u32[]{:S(2)}, u32[]{:S(2)}) collective-permute-start(bf16[128,1024]{1,0:T(8,128)(2,1)S(1)} %collective-permute-done.4.k_ref), channel_id=1, source_target_pairs={{0,8},{8,24},{24,16},{16,0},{1,9},{9,25},{25,17},{17,1},{2,10},{10... | collective-permute-start | bytes 786440 | tf_op jit(solution)/shard_map/ppermute | solution.py:391
  12.6 1.2 %copy-start = (bf16[1,128,4096]{2,1,0:T(8,128)(2,1)S(1)}, bf16[1,128,4096]{2,1,0:T(8,128)(2,1)}, u32[]{:S(2)}) copy-start(bf16[1,128,4096]{2,1,0:T(8,128)(2,1)} %param.6) | copy-start | bytes 3145732
  13.9 0.7 %copy-start.3 = (s32[4,4]{1,0:T(4,128)S(1)}, s32[4,4]{1,0:T(4,128)}, u32[]{:S(2)}) copy-start(s32[4,4]{1,0:T(4,128)} %counts.1) | copy-start | bytes 196
  13.9 0.7 %copy-start.4 = (s32[1,6]{1,0:T(1,128)S(1)}, s32[1,6]{1,0:T(1,128)}, u32[]{:S(2)}) copy-start(s32[1,6]{1,0:T(1,128)} %docs.1) | copy-start | bytes 76
  13.9 1.4 %copy-start.1 = (bf16[128,1,1,1024]{3,0,2,1:T(8,128)(2,1)S(1)}, bf16[128,1,1,1024]{3,0,2,1:T(8,128)(2,1)}, u32[]{:S(2)}) copy-start(bf16[128,1,1,1024]{3,0,2,1:T(8,128)(2,1)} %param.7) | copy-start | bytes 786436
  17.7 7.3 %collective-permute-start.1 = (bf16[40,2048]{1,0:T(8,128)(2,1)S(1)}, bf16[40,2048]{1,0:T(8,128)(2,1)S(1)}, u32[]{:S(2)}, u32[]{:S(2)}) collective-permute-start(bf16[40,2048]{1,0:T(8,128)(2,1)S(1)} %get-tuple-element.40), channel_id=1, source_target_pairs={{0,6},{2,4},{4,2},{6,0},{1,7},{3,5},{5,3},{7,1},{8,14},{10,12},{12... | collective-permute-start | bytes 491528 | tf_op jit(solution)/shard_map/ppermute | solution.py:63
  20.6 7.5 %collective-permute-start.2 = (bf16[40,2048]{1,0:T(8,128)(2,1)S(1)}, bf16[40,2048]{1,0:T(8,128)(2,1)S(1)}, u32[]{:S(2)}, u32[]{:S(2)}) collective-permute-start(bf16[40,2048]{1,0:T(8,128)(2,1)S(1)} %get-tuple-element.41), channel_id=1, source_target_pairs={{0,2},{2,0},{4,6},{6,4},{1,3},{3,1},{5,7},{7,5},{8,10},{10,8},{12,... | collective-permute-start | bytes 491528 | tf_op jit(solution)/shard_map/ppermute | solution.py:63
  21.2 7.7 %collective-permute-start.3 = (bf16[40,2048]{1,0:T(8,128)(2,1)S(1)}, bf16[40,2048]{1,0:T(8,128)(2,1)S(1)}, u32[]{:S(2)}, u32[]{:S(2)}) collective-permute-start(bf16[40,2048]{1,0:T(8,128)(2,1)S(1)} %get-tuple-element.42), channel_id=1, source_target_pairs={{0,4},{2,6},{4,0},{6,2},{1,5},{3,7},{5,1},{7,3},{8,12},{10,14},{12... | collective-permute-start | bytes 491528 | tf_op jit(solution)/shard_map/ppermute | solution.py:63
  22.6 12.2 %collective-permute-start.10 = (bf16[128,1024]{1,0:T(8,128)(2,1)S(1)}, bf16[128,1024]{1,0:T(8,128)(2,1)S(1)}, u32[]{:S(2)}, u32[]{:S(2)}) collective-permute-start(bf16[128,1024]{1,0:T(8,128)(2,1)S(1)} %collective-permute-done.5.v_ref), channel_id=1, source_target_pairs={{0,8},{8,24},{24,16},{16,0},{1,9},{9,25},{25,17},{17,1},{2,10},{10... | collective-permute-start | bytes 786440 | tf_op jit(solution)/shard_map/ppermute | solution.py:391
  25.8 5.4 %collective-permute-start.6 = (bf16[40,1024]{1,0:T(8,128)(2,1)S(1)}, bf16[40,1024]{1,0:T(8,128)(2,1)S(1)}, u32[]{:S(2)}, u32[]{:S(2)}) collective-permute-start(bf16[40,1024]{1,0:T(8,128)(2,1)S(1)} %get-tuple-element.50), channel_id=1, source_target_pairs={{0,6},{2,4},{4,2},{6,0},{1,7},{3,5},{5,3},{7,1},{8,14},{10,12},{12... | collective-permute-start | bytes 245768 | tf_op jit(solution)/shard_map/ppermute | solution.py:63
  28.1 4.4 %collective-permute-start.7 = (bf16[40,1024]{1,0:T(8,128)(2,1)S(1)}, bf16[40,1024]{1,0:T(8,128)(2,1)S(1)}, u32[]{:S(2)}, u32[]{:S(2)}) collective-permute-start(bf16[40,1024]{1,0:T(8,128)(2,1)S(1)} %get-tuple-element.51), channel_id=1, source_target_pairs={{0,2},{2,0},{4,6},{6,4},{1,3},{3,1},{5,7},{7,5},{8,10},{10,8},{12,... | collective-permute-start | bytes 245768 | tf_op jit(solution)/shard_map/ppermute | solution.py:63
  28.9 4.4 %collective-permute-start.8 = (bf16[40,1024]{1,0:T(8,128)(2,1)S(1)}, bf16[40,1024]{1,0:T(8,128)(2,1)S(1)}, u32[]{:S(2)}, u32[]{:S(2)}) collective-permute-start(bf16[40,1024]{1,0:T(8,128)(2,1)S(1)} %get-tuple-element.52), channel_id=1, source_target_pairs={{0,4},{2,6},{4,0},{6,2},{1,5},{3,7},{5,1},{7,3},{8,12},{10,14},{12... | collective-permute-start | bytes 245768 | tf_op jit(solution)/shard_map/ppermute | solution.py:63
  30.4 2.9 %collective-permute-start.11 = (f32[8,128]{1,0:T(8,128)S(1)}, f32[8,128]{1,0:T(8,128)S(1)}, u32[]{:S(2)}, u32[]{:S(2)}) collective-permute-start(f32[8,128]{1,0:T(8,128)S(1)} %get-tuple-element.58.inverses), channel_id=1, source_target_pairs={{0,1},{1,0},{2,3},{3,2},{4,5},{5,4},{6,7},{7,6},{8,9},{9,8},{10,11... | collective-permute-start | bytes 12296 | tf_op jit(solution)/shard_map/ppermute | solution.py:394
  33.3 8.3 %collective-permute-start.15 = (bf16[128,1024]{1,0:T(8,128)(2,1)S(1)}, bf16[128,1024]{1,0:T(8,128)(2,1)S(1)}, u32[]{:S(2)}, u32[]{:S(2)}) collective-permute-start(bf16[128,1024]{1,0:T(8,128)(2,1)S(1)} %get-tuple-element.63.refs_0_), channel_id=1, source_target_pairs={{8,0},{24,8},{16,24},{0,16},{9,1},{25,9},{17,25},{1,17},{10,2},{26... | collective-permute-start | bytes 786440 | tf_op jit(solution)/shard_map/ppermute | solution.py:398
  35.3 5.4 %collective-permute-start.12 = (bf16[40,1024]{1,0:T(8,128)(2,1)S(1)}, bf16[40,1024]{1,0:T(8,128)(2,1)S(1)}, u32[]{:S(2)}, u32[]{:S(2)}) collective-permute-start(bf16[40,1024]{1,0:T(8,128)(2,1)S(1)} %get-tuple-element.60), channel_id=1, source_target_pairs={{0,6},{2,4},{4,2},{6,0},{1,7},{3,5},{5,3},{7,1},{8,14},{10,12},{12... | collective-permute-start | bytes 245768 | tf_op jit(solution)/shard_map/ppermute | solution.py:63
  36.7 4.4 %collective-permute-start.13 = (bf16[40,1024]{1,0:T(8,128)(2,1)S(1)}, bf16[40,1024]{1,0:T(8,128)(2,1)S(1)}, u32[]{:S(2)}, u32[]{:S(2)}) collective-permute-start(bf16[40,1024]{1,0:T(8,128)(2,1)S(1)} %get-tuple-element.61), channel_id=1, source_target_pairs={{0,2},{2,0},{4,6},{6,4},{1,3},{3,1},{5,7},{7,5},{8,10},{10,8},{12,... | collective-permute-start | bytes 245768 | tf_op jit(solution)/shard_map/ppermute | solution.py:63
  37.2 4.4 %collective-permute-start.14 = (bf16[40,1024]{1,0:T(8,128)(2,1)S(1)}, bf16[40,1024]{1,0:T(8,128)(2,1)S(1)}, u32[]{:S(2)}, u32[]{:S(2)}) collective-permute-start(bf16[40,1024]{1,0:T(8,128)(2,1)S(1)} %get-tuple-element.62), channel_id=1, source_target_pairs={{0,4},{2,6},{4,0},{6,2},{1,5},{3,7},{5,1},{7,3},{8,12},{10,14},{12... | collective-permute-start | bytes 245768 | tf_op jit(solution)/shard_map/ppermute | solution.py:63
  41.6 0.7 %copy-start.5 = (bf16[4096]{0:T(1024)(128)(2,1)S(1)}, bf16[4096]{0:T(1024)(128)(2,1)}, u32[]{:S(2)}) copy-start(bf16[4096]{0:T(1024)(128)(2,1)} %param.11) | copy-start | bytes 24580
  42.1 1.3 %collective-permute-start.16 = (f32[128,128]{1,0:T(8,128)S(1)}, f32[128,128]{1,0:T(8,128)S(1)}, u32[]{:S(2)}, u32[]{:S(2)}) collective-permute-start(f32[128,128]{1,0:T(8,128)S(1)} %get-tuple-element.66.refs_4_), channel_id=1, source_target_pairs={{0,1},{1,0},{2,3},{3,2},{4,5},{5,4},{6,7},{7,6},{8,9},{9,8},{10,11... | collective-permute-start | bytes 196616 | tf_op jit(solution)/shard_map/ppermute | solution.py:403

commit v9 on v7

--- a/solution.py
+++ b/solution.py
@@ -180,22 +180,22 @@
         out[...] = picked[part * plan.rows : (part + 1) * plan.rows].astype(jnp.bfloat16)
 
 
-def heads_kernel(plan, q_ref, k_ref, v_ref, bias, _, attn):
+def heads_kernel(plan, q_ref, k_ref, v_ref, bias, attn):
     weights = all_weights(plan, q_ref, k_ref, bias)
     for cols, (weight, inverse) in zip(head_columns(plan), weights, strict=True):
         attn[cols, :] = weighted(v_ref, cols, weight, inverse)
 
 
-def heads(plan, query, k, v, bias, after):
+def heads(plan, query, k, v, bias):
     return pl.pallas_call(
         functools.partial(heads_kernel, plan),
         out_shape=jax.ShapeDtypeStruct((plan.block, plan.seq), jnp.bfloat16),
-        in_specs=[VMEM] * 4 + [ANY],
+        in_specs=[VMEM] * 4,
         out_specs=VMEM,
         compiler_params=PARAMS,
         cost_estimate=COST,
         name="heads",
-    )(query, k, v, bias, after)
+    )(query, k, v, bias)
 
 
 def attend_kernel(plan, bases, q_ref, k_ref, v_ref, bias, send, *refs):
@@ -209,29 +209,28 @@
     pick_rows(plan, send, attn, outs)
 
 
-def attend(plan, query, k, v, bias, send, bases=(), after=()):
+def attend(plan, query, k, v, bias, send, bases=()):
     width = (len(bases) + 1) * plan.block
     return pl.pallas_call(
         functools.partial(attend_kernel, plan, len(bases)),
         out_shape=[jax.ShapeDtypeStruct((plan.rows, width), jnp.bfloat16)] * plan.parts,
-        in_specs=[VMEM] * (5 + len(bases)) + [ANY] * len(after),
+        in_specs=[VMEM] * (5 + len(bases)),
         out_specs=[VMEM] * plan.parts,
         scratch_shapes=[pltpu.VMEM((width, plan.seq), jnp.bfloat16)],
         compiler_params=PARAMS,
         cost_estimate=COST,
         name="attend",
-    )(query, k, v, bias, send, *bases, *after)
-
-
-def weigh_kernel(plan, q_ref, k_ref, bias, *refs):
-    weights, inverses = refs[-2:]
+    )(query, k, v, bias, send, *bases)
+
+
+def weigh_kernel(plan, q_ref, k_ref, bias, _, weights, inverses):
     found = all_weights(plan, q_ref, k_ref, bias)
     for h, (cols, (weight, inverse)) in enumerate(zip(head_columns(plan), found, strict=True)):
         weights[cols, :] = weight
         inverses[h : h + 1, :] = inverse
 
 
-def weigh(plan, query, k, bias, after=()):
+def weigh(plan, query, k, bias, after):
     count = plan.block // HEAD_DIM
     return pl.pallas_call(
         functools.partial(weigh_kernel, plan),
@@ -239,32 +238,32 @@
             jax.ShapeDtypeStruct((plan.block, plan.seq), jnp.bfloat16),
             jax.ShapeDtypeStruct((count, plan.seq), jnp.float32),
         ],
-        in_specs=[VMEM] * 3 + [ANY] * len(after),
+        in_specs=[VMEM] * 3 + [ANY],
         out_specs=[VMEM] * 2,
         compiler_params=PARAMS,
         cost_estimate=COST,
         name="weigh",
-    )(query, k, bias, *after)
-
-
-def finish_kernel(plan, weights, inverses, v_ref, send, *refs):
+    )(query, k, bias, after)
+
+
+def finish_kernel(plan, weights, inverses, v_ref, send, _, *refs):
     outs, attn = refs[:-1], refs[-1]
     for h, cols in enumerate(head_columns(plan)):
         attn[cols, :] = weighted(v_ref, cols, weights[cols, :], inverses[h : h + 1, :])
     pick_rows(plan, send, attn, outs)
 
 
-def finish(plan, weights, inverses, v, send):
+def finish(plan, weights, inverses, v, send, after):
     return pl.pallas_call(
         functools.partial(finish_kernel, plan),
         out_shape=[jax.ShapeDtypeStruct((plan.rows, plan.block), jnp.bfloat16)] * plan.parts,
-        in_specs=[VMEM] * 4,
+        in_specs=[VMEM] * 4 + [ANY],
         out_specs=[VMEM] * plan.parts,
         scratch_shapes=[pltpu.VMEM((plan.block, plan.seq), jnp.bfloat16)],
         compiler_params=PARAMS,
         cost_estimate=COST,
         name="finish",
-    )(weights, inverses, v, send)
+    )(weights, inverses, v, send, after)
 
 
 def squares_of(ref):
@@ -366,7 +365,7 @@
     query = queries[0]
     seq, local_width = query.shape
     plan = Plan(mesh, seq, local_width)
-    n, block, half = plan.pipe, plan.block, plan.block // 2
+    n, block = plan.pipe, plan.block
     forward, backward = plan.ring, [(b, a) for a, b in plan.ring]
     keys, values = cache_keys.reshape(seq, block), cache_values.reshape(seq, block)
     gain = out_gain.astype(jnp.float32).reshape(1, local_width)
@@ -377,22 +376,24 @@
     bias, send, places = tables(plan, doc_lengths, row_counts)
     k, v = lax.ppermute(keys, "pipe", forward), lax.ppermute(values, "pipe", forward)
     lent = lax.ppermute(ahead, "pipe", forward)
-    own = heads(plan, asked[0], keys, values, bias, after=bias)
+    own = heads(plan, asked[0], keys, values, bias)
     arrived = plan.regroup(attend(plan, lent, keys, values, bias, send, bases=(own,)))
     mine, borrowed, total = place(plan, arrived, places, (block, block), summed=1)
     pieces = [(mine, 0, 0)]
     for t in range(1, n - 2):
         sent = attend(plan, asked[t], k, v, bias, send)
+        *sent, _ = lax.optimization_barrier((*sent, arrived[1 % len(arrived)]))
         got = plan.regroup(sent)
         placed, total = place(plan, got, places, (block,), sums=(total,))
         pieces.append((placed, t, 0))
-        if t == 1:
-            v, *_ = lax.optimization_barrier((v, *arrived))
         k, v = lax.ppermute(k, "pipe", forward), lax.ppermute(v, "pipe", forward)
-    weights = weigh(plan, asked[n - 2], k, bias, after=())
-    borrowed, *_ = lax.optimization_barrier((borrowed, *weights, v, *got))
+    weights, inverses = weigh(plan, asked[n - 2], k, bias, borrowed)
+    met = inverses
+    if plan.tensor == 2:
+        met = lax.ppermute(inverses, "tensor", [(0, 1), (1, 0)])
+    borrowed, *_ = lax.optimization_barrier((borrowed, met, *got))
     returned = lax.ppermute(borrowed, "pipe", backward)
-    got = plan.regroup(finish(plan, *weights, v, send))
+    got = plan.regroup(finish(plan, weights, inverses, v, send, met))
     placed, total = place(plan, got, places, (block,), blocks=(returned,), sums=(total,))
     pieces += [(placed, n - 2, 0), (returned, n - 1, 0)]
     if plan.tensor == 2:

time: 46.8 us -> 44.7 us (0.955)
  waiting for transfers between devices: 16.1 us -> 13.7 us
    ppermute x1, waiting for transfers between devices: 4.46 us -> 1.31 us  [body(): lax.ppermute(values, 'pipe', forward)]
    ppermute x1, waiting for transfers between devices: 1.31 us -> 4.24 us  [body(): lax.ppermute(keys, 'pipe', forward)]
    ppermute x2, waiting for transfers between devices: 0.97 us -> 0.01 us  [body(): k, v = (lax.ppermute(k, 'pipe', forward), lax.ppermute(v, 'pipe', forward))]
    ppermute x1, waiting for transfers between devices: 1.97 us -> 1.22 us  [body(): lent = lax.ppermute(ahead, 'pipe', forward)]
    ppermute x9, starting transfers between devices: 10.7 us -> 11.4 us  [regroup(): lax.ppermute(part, 'dp', [(g, g ^ step) for g in range(self.groups)])]
    ppermute x1, starting transfers between devices: 1.74 us -> 1.24 us  [body(): returned = lax.ppermute(borrowed, 'pipe', backward)]
    ppermute x9, waiting for transfers between devices: 6.39 us -> 5.91 us  [regroup(): lax.ppermute(part, 'dp', [(g, g ^ step) for g in range(self.groups)])]
  transfers between devices with their start and end apart: 16 -> 17, of which waited for: 11 -> 11; matrix products, arithmetic and copies ran while one was open for 0% -> 2% of each run, Pallas kernels for 10% -> 11%
where the time goes in v9:
time: 44.7 us; the launch traced here: 44.5 us
  starting transfers between devices  21.3 us (48%)
  waiting for transfers between devices  13.7 us (31%)
  Pallas kernels  6.28 us (14%)
  local copies, waits for them, and re-layouts  3.02 us (7%)
    ppermute x9, starting transfers between devices, regroup(): lax.ppermute(part, 'dp', [(g, g ^ step) for g in range(self.groups)])  11.4 us
    ppermute x9, waiting for transfers between devices, regroup(): lax.ppermute(part, 'dp', [(g, g ^ step) for g in range(self.groups)])  5.91 us
    ppermute x1, waiting for transfers between devices, body(): lax.ppermute(keys, 'pipe', forward)  4.24 us
    ppermute x1, starting transfers between devices, body(): lax.ppermute(keys, 'pipe', forward)  3.02 us
    ppermute x1, starting transfers between devices, body(): lent = lax.ppermute(ahead, 'pipe', forward)  2.64 us
    ppermute x2, starting transfers between devices, body(): k, v = (lax.ppermute(k, 'pipe', forward), lax.ppermute(v, 'pipe', forward))  2.42 us
    unnamed x12, local copies, waits for them, and re-layouts  2.01 us
    pallas_call x3, Pallas kernels, place(): pl.pallas_call(functools.partial(place_kernel, plan, widths, summed, len(...  1.5 us
  transfers between devices with their start and end apart: 17, of which 11 were waited for; matrix products, arithmetic and copies ran while one was open for 2% of the time, Pallas kernels for 11%

profile of v9, /device:TPU:0, one launch (start us, length us, event | category | flops | bytes accessed | tf_op | source)
XLA Modules:
  0.0 44.5 jit_solution(17960420573232702936)
XLA Ops:
  0.0 3.0 %collective-permute-start.4 = (bf16[128,1024]{1,0:T(8,128)(2,1)}, bf16[128,1024]{1,0:T(8,128)(2,1)S(1)}, u32[]{:S(2)}, u32[]{:S(2)}) collective-permute-start(bf16[128,1024]{1,0:T(8,128)(2,1)} %bitcast.8), channel_id=1, source_target_pairs={{0,8},{8,24},{24,16},{16,0},{1,9},{9,25},{25,17},{17,1},{2,10},{10... | collective-permute-start | bytes 786440 | tf_op jit(solution)/shard_map/ppermute | solution.py:377
  3.0 0.0 copy-start.2
  3.0 1.0 %dynamic-slice_bitcast_fusion = bf16[128,1024]{1,0:T(8,128)(2,1)S(1)} fusion(bf16[1,128,4096]{2,1,0:T(8,128)(2,1)} %param.6, s32[]{:T(128)S(6)} %select_n.16), kind=kLoop, calls=%fused_computation | loop fusion | bytes 524292 | tf_op jit(solution)/shard_map/dynamic_slice | solution.py:374
  4.0 2.6 %collective-permute-start = (bf16[128,1024]{1,0:T(8,128)(2,1)S(1)}, bf16[128,1024]{1,0:T(8,128)(2,1)S(1)}, u32[]{:S(2)}, u32[]{:S(2)}) collective-permute-start(bf16[128,1024]{1,0:T(8,128)(2,1)S(1)} %dynamic-slice_bitcast_fusion), channel_id=1, source_target_pairs={{0,8},{8,24},{24,16},{16,0},{1,9},{9,25},{25,17},{17,1},{2,10},{10... | collective-permute-start | bytes 786440 | tf_op jit(solution)/shard_map/ppermute | solution.py:378
  6.7 0.0 copy-done.2
  6.7 0.4 %collective-permute-start.5 = (bf16[128,1024]{1,0:T(8,128)(2,1)S(1)}, bf16[128,1024]{1,0:T(8,128)(2,1)S(1)}, u32[]{:S(2)}, u32[]{:S(2)}) collective-permute-start(bf16[128,1024]{1,0:T(8,128)(2,1)S(1)} %bitcast.11), channel_id=1, source_target_pairs={{0,8},{8,24},{24,16},{16,0},{1,9},{9,25},{25,17},{17,1},{2,10},{10... | collective-permute-start | bytes 786440 | tf_op jit(solution)/shard_map/ppermute | solution.py:377
  7.1 4.2 %collective-permute-done.4.k_ref = bf16[128,1024]{1,0:T(8,128)(2,1)S(1)} collective-permute-done((bf16[128,1024]{1,0:T(8,128)(2,1)}, bf16[128,1024]{1,0:T(8,128)(2,1)S(1)}, u32[]{:S(2)}, u32[]{:S(2)}) %collective-permute-start.4) | collective-permute-done | bytes 262176 | tf_op jit(solution)/shard_map/ppermute | solution.py:377
  11.4 1.3 %collective-permute-start.9 = (bf16[128,1024]{1,0:T(8,128)(2,1)S(1)}, bf16[128,1024]{1,0:T(8,128)(2,1)S(1)}, u32[]{:S(2)}, u32[]{:S(2)}) collective-permute-start(bf16[128,1024]{1,0:T(8,128)(2,1)S(1)} %collective-permute-done.4.k_ref), channel_id=1, source_target_pairs={{0,8},{8,24},{24,16},{16,0},{1,9},{9,25},{25,17},{17,1},{2,10},{10... | collective-permute-start | bytes 786440 | tf_op jit(solution)/shard_map/ppermute | solution.py:389
  12.6 0.0 copy-start
  12.6 1.2 %copy-done = bf16[1,128,4096]{2,1,0:T(8,128)(2,1)S(1)} copy-done((bf16[1,128,4096]{2,1,0:T(8,128)(2,1)S(1)}, bf16[1,128,4096]{2,1,0:T(8,128)(2,1)}, u32[]{:S(2)}) %copy-start) | copy-done | bytes 1048600
  13.9 0.0 copy-start.3
  13.9 0.0 copy-start.4
  13.9 0.0 copy-start.1
  13.9 0.1 split.1
  14.0 0.6 %copy-done.3 = s32[4,4]{1,0:T(4,128)S(1)} copy-done((s32[4,4]{1,0:T(4,128)S(1)}, s32[4,4]{1,0:T(4,128)}, u32[]{:S(2)}) %copy-start.3) | copy-done | bytes 88
  14.5 0.0 copy-done.4
  14.6 0.7 %tables.1 = (f32[128,128]{1,0:T(8,128)S(1)}, bf16[160,128]{1,0:T(8,128)(2,1)S(1)}, bf16[128,40]{1,0:T(8,128)(2,1)S(1)}, bf16[128,40]{1,0:T(8,128)(2,1)S(1)}, bf1...) custom-call(s32[1,6]{1,0:T(1,128)S(1)} %copy-done.4, s32[4,4]{1,0:T(4,128)S(1)} %copy-done.3), custom_call_target="tpu_custom_call" | custom-call | flops 1 | bytes 1 | tf_op jit(solution)/shard_map/tables/pallas_call | solution.py:136
  15.2 0.0 copy-done.1
  15.2 0.5 %heads.1.refs_0_ = bf16[1024,128]{1,0:T(8,128)(2,1)S(1)} custom-call(bf16[128,1024]{1,0:T(8,128)(2,1)S(1)} %get-tuple-element.42.q_ref, bf16[128,1024]{1,0:T(8,128)(2,1)S(1)} %bitcast.9, bf16[128,1024]{1,0:T(8,128)(2,1)S(1)} %bitcast.12, f32[128,128]{1,0:T(8,128)S(1)} %get-tuple-element.40.bias), custom_call_target="tpu_custom_call" | custom-call | flops 1 | bytes 1 | tf_op jit(solution)/shard_map/heads/pallas_call | solution.py:190
  15.8 1.2 %collective-permute-done.q_ref = bf16[128,1024]{1,0:T(8,128)(2,1)S(1)} collective-permute-done((bf16[128,1024]{1,0:T(8,128)(2,1)S(1)}, bf16[128,1024]{1,0:T(8,128)(2,1)S(1)}, u32[]{:S(2)}, u32[]{:S(2)}) %collective-permute-start) | collective-permute-done | bytes 262176 | tf_op jit(solution)/shard_map/ppermute | solution.py:378
  17.0 0.7 %attend.2 = (bf16[40,2048]{1,0:T(8,128)(2,1)S(1)}, bf16[40,2048]{1,0:T(8,128)(2,1)S(1)}, bf16[40,2048]{1,0:T(8,128)(2,1)S(1)}, bf16[40,2048]{1,0:T(8,128)(2,1)S(1)}) custom-call(bf16[128,1024]{1,0:T(8,128)(2,1)S(1)} %collective-permute-done.q_ref, bf16[128,1024]{1,0:T(8,128)(2,1)S(1)} %bitcast.10, bf16[128,1024]{1,0:T(8,128)(2,1)S(1)} %bitcast.13, ...), custom_call_target="tpu_custom_call" | custom-call | flops 1 | bytes 1 | tf_op jit(solution)/shard_map/attend/pallas_call | solution.py:214
  17.7 2.9 %collective-permute-start.1 = (bf16[40,2048]{1,0:T(8,128)(2,1)S(1)}, bf16[40,2048]{1,0:T(8,128)(2,1)S(1)}, u32[]{:S(2)}, u32[]{:S(2)}) collective-permute-start(bf16[40,2048]{1,0:T(8,128)(2,1)S(1)} %get-tuple-element.44), channel_id=1, source_target_pairs={{0,6},{2,4},{4,2},{6,0},{1,7},{3,5},{5,3},{7,1},{8,14},{10,12},{12... | collective-permute-start | bytes 491528 | tf_op jit(solution)/shard_map/ppermute | solution.py:63
  20.6 0.5 %collective-permute-start.2 = (bf16[40,2048]{1,0:T(8,128)(2,1)S(1)}, bf16[40,2048]{1,0:T(8,128)(2,1)S(1)}, u32[]{:S(2)}, u32[]{:S(2)}) collective-permute-start(bf16[40,2048]{1,0:T(8,128)(2,1)S(1)} %get-tuple-element.45), channel_id=1, source_target_pairs={{0,2},{2,0},{4,6},{6,4},{1,3},{3,1},{5,7},{7,5},{8,10},{10,8},{12,... | collective-permute-start | bytes 491528 | tf_op jit(solution)/shard_map/ppermute | solution.py:63
  21.2 0.1 collective-permute-start.3
  21.3 1.3 %collective-permute-done.5.v_ref = bf16[128,1024]{1,0:T(8,128)(2,1)S(1)} collective-permute-done((bf16[128,1024]{1,0:T(8,128)(2,1)S(1)}, bf16[128,1024]{1,0:T(8,128)(2,1)S(1)}, u32[]{:S(2)}, u32[]{:S(2)}) %collective-permute-start.5) | collective-permute-done | bytes 262176 | tf_op jit(solution)/shard_map/ppermute | solution.py:377
  22.6 1.2 %collective-permute-start.10 = (bf16[128,1024]{1,0:T(8,128)(2,1)S(1)}, bf16[128,1024]{1,0:T(8,128)(2,1)S(1)}, u32[]{:S(2)}, u32[]{:S(2)}) collective-permute-start(bf16[128,1024]{1,0:T(8,128)(2,1)S(1)} %collective-permute-done.5.v_ref), channel_id=1, source_target_pairs={{0,8},{8,24},{24,16},{16,0},{1,9},{9,25},{25,17},{17,1},{2,10},{10... | collective-permute-start | bytes 786440 | tf_op jit(solution)/shard_map/ppermute | solution.py:389
  23.8 0.7 %attend.3 = (bf16[40,1024]{1,0:T(8,128)(2,1)S(1)}, bf16[40,1024]{1,0:T(8,128)(2,1)S(1)}, bf16[40,1024]{1,0:T(8,128)(2,1)S(1)}, bf16[40,1024]{1,0:T(8,128)(2,1)S(1)}) custom-call(bf16[128,1024]{1,0:T(8,128)(2,1)S(1)} %get-tuple-element.52.q_ref, bf16[128,1024]{1,0:T(8,128)(2,1)S(1)} %collective-permute-done.4.k_ref, ...), custom_call_target="tpu_custom_call" | custom-call | flops 1 | bytes 1 | tf_op jit(solution)/shard_map/attend/pallas_call | solution.py:214
  24.5 0.5 %collective-permute-done.1.refs_1_ = bf16[40,2048]{1,0:T(8,128)(2,1)S(1)} collective-permute-done((bf16[40,2048]{1,0:T(8,128)(2,1)S(1)}, bf16[40,2048]{1,0:T(8,128)(2,1)S(1)}, u32[]{:S(2)}, u32[]{:S(2)}) %collective-permute-start.1) | collective-permute-done | bytes 163872 | tf_op jit(solution)/shard_map/ppermute | solution.py:63
  25.0 2.3 %collective-permute-start.6 = (bf16[40,1024]{1,0:T(8,128)(2,1)S(1)}, bf16[40,1024]{1,0:T(8,128)(2,1)S(1)}, u32[]{:S(2)}, u32[]{:S(2)}) collective-permute-start(bf16[40,1024]{1,0:T(8,128)(2,1)S(1)} %get-tuple-element.58), channel_id=1, source_target_pairs={{0,6},{2,4},{4,2},{6,0},{1,7},{3,5},{5,3},{7,1},{8,14},{10,12},{12... | collective-permute-start | bytes 245768 | tf_op jit(solution)/shard_map/ppermute | solution.py:63
  27.3 0.1 collective-permute-done.2.refs_2_
  27.4 1.5 %collective-permute-start.7 = (bf16[40,1024]{1,0:T(8,128)(2,1)S(1)}, bf16[40,1024]{1,0:T(8,128)(2,1)S(1)}, u32[]{:S(2)}, u32[]{:S(2)}) collective-permute-start(bf16[40,1024]{1,0:T(8,128)(2,1)S(1)} %get-tuple-element.59), channel_id=1, source_target_pairs={{0,2},{2,0},{4,6},{6,4},{1,3},{3,1},{5,7},{7,5},{8,10},{10,8},{12,... | collective-permute-start | bytes 245768 | tf_op jit(solution)/shard_map/ppermute | solution.py:63
  28.9 0.0 collective-permute-done.3.refs_3_
  28.9 0.5 %collective-permute-start.8 = (bf16[40,1024]{1,0:T(8,128)(2,1)S(1)}, bf16[40,1024]{1,0:T(8,128)(2,1)S(1)}, u32[]{:S(2)}, u32[]{:S(2)}) collective-permute-start(bf16[40,1024]{1,0:T(8,128)(2,1)S(1)} %get-tuple-element.60), channel_id=1, source_target_pairs={{0,4},{2,6},{4,0},{6,2},{1,5},{3,7},{5,1},{7,3},{8,12},{10,14},{12... | collective-permute-start | bytes 245768 | tf_op jit(solution)/shard_map/ppermute | solution.py:63
  29.4 0.7 %place.3 = (bf16[128,1024]{1,0:T(8,128)(2,1)S(1)}, bf16[128,1024]{1,0:T(8,128)(2,1)S(1)}, f32[128,128]{1,0:T(8,128)S(1)}) custom-call(bf16[40,2048]{1,0:T(8,128)(2,1)S(1)} %get-tuple-element.43.refs_0_, bf16[40,2048]{1,0:T(8,128)(2,1)S(1)} %collective-permute-done.1.refs_1_, bf16[40,2048]{1,0:T(8,128)(2,1)S(1)} %collective-permute-done.2.refs_2_, ...), custom_call_target="tpu_custom_call" | custom-call | flops 1 | bytes 1 | tf_op jit(solution)/shard_map/place/pallas_call | solution.py:308
  30.1 0.0 collective-permute-done.9.k_ref
  30.1 0.4 weigh.1
  30.5 0.1 collective-permute-start.11
  30.6 0.0 collective-permute-done.6.refs_1_
  30.6 1.3 %collective-permute-done.7.refs_2_ = bf16[40,1024]{1,0:T(8,128)(2,1)S(1)} collective-permute-done((bf16[40,1024]{1,0:T(8,128)(2,1)S(1)}, bf16[40,1024]{1,0:T(8,128)(2,1)S(1)}, u32[]{:S(2)}, u32[]{:S(2)}) %collective-permute-start.7) | collective-permute-done | bytes 81952 | tf_op jit(solution)/shard_map/ppermute | solution.py:63
  31.8 1.5 %collective-permute-done.8.refs_3_ = bf16[40,1024]{1,0:T(8,128)(2,1)S(1)} collective-permute-done((bf16[40,1024]{1,0:T(8,128)(2,1)S(1)}, bf16[40,1024]{1,0:T(8,128)(2,1)S(1)}, u32[]{:S(2)}, u32[]{:S(2)}) %collective-permute-start.8) | collective-permute-done | bytes 81952 | tf_op jit(solution)/shard_map/ppermute | solution.py:63
  33.3 0.0 collective-permute-done.11._
  33.3 1.2 %collective-permute-start.15 = (bf16[128,1024]{1,0:T(8,128)(2,1)S(1)}, bf16[128,1024]{1,0:T(8,128)(2,1)S(1)}, u32[]{:S(2)}, u32[]{:S(2)}) collective-permute-start(bf16[128,1024]{1,0:T(8,128)(2,1)S(1)} %get-tuple-element.71._), channel_id=1, source_target_pairs={{8,0},{24,8},{16,24},{0,16},{9,1},{25,9},{17,25},{1,17},{10,2},{26... | collective-permute-start | bytes 786440 | tf_op jit(solution)/shard_map/ppermute | solution.py:395
  34.6 0.0 collective-permute-done.10.v_ref
  34.6 0.5 %finish.1 = (bf16[40,1024]{1,0:T(8,128)(2,1)S(1)}, bf16[40,1024]{1,0:T(8,128)(2,1)S(1)}, bf16[40,1024]{1,0:T(8,128)(2,1)S(1)}, bf16[40,1024]{1,0:T(8,128)(2,1)S(1)}) custom-call(bf16[1024,128]{1,0:T(8,128)(2,1)S(1)} %get-tuple-element.65.weights, f32[8,128]{1,0:T(8,128)S(1)} %get-tuple-element.66.inverses, ...), custom_call_target="tpu_custom_call" | custom-call | flops 1 | bytes 1 | tf_op jit(solution)/shard_map/finish/pallas_call | solution.py:257
  35.1 1.1 %collective-permute-start.12 = (bf16[40,1024]{1,0:T(8,128)(2,1)S(1)}, bf16[40,1024]{1,0:T(8,128)(2,1)S(1)}, u32[]{:S(2)}, u32[]{:S(2)}) collective-permute-start(bf16[40,1024]{1,0:T(8,128)(2,1)S(1)} %get-tuple-element.68), channel_id=1, source_target_pairs={{0,6},{2,4},{4,2},{6,0},{1,7},{3,5},{5,3},{7,1},{8,14},{10,12},{12... | collective-permute-start | bytes 245768 | tf_op jit(solution)/shard_map/ppermute | solution.py:63
  36.1 1.0 %collective-permute-start.13 = (bf16[40,1024]{1,0:T(8,128)(2,1)S(1)}, bf16[40,1024]{1,0:T(8,128)(2,1)S(1)}, u32[]{:S(2)}, u32[]{:S(2)}) collective-permute-start(bf16[40,1024]{1,0:T(8,128)(2,1)S(1)} %get-tuple-element.69), channel_id=1, source_target_pairs={{0,2},{2,0},{4,6},{6,4},{1,3},{3,1},{5,7},{7,5},{8,10},{10,8},{12,... | collective-permute-start | bytes 245768 | tf_op jit(solution)/shard_map/ppermute | solution.py:63
  37.1 1.5 %collective-permute-start.14 = (bf16[40,1024]{1,0:T(8,128)(2,1)S(1)}, bf16[40,1024]{1,0:T(8,128)(2,1)S(1)}, u32[]{:S(2)}, u32[]{:S(2)}) collective-permute-start(bf16[40,1024]{1,0:T(8,128)(2,1)S(1)} %get-tuple-element.70), channel_id=1, source_target_pairs={{0,4},{2,6},{4,0},{6,2},{1,5},{3,7},{5,1},{7,3},{8,12},{10,14},{12... | collective-permute-start | bytes 245768 | tf_op jit(solution)/shard_map/ppermute | solution.py:63
  38.6 0.4 place.4
  39.0 1.4 %collective-permute-done.12.refs_1_ = bf16[40,1024]{1,0:T(8,128)(2,1)S(1)} collective-permute-done((bf16[40,1024]{1,0:T(8,128)(2,1)S(1)}, bf16[40,1024]{1,0:T(8,128)(2,1)S(1)}, u32[]{:S(2)}, u32[]{:S(2)}) %collective-permute-start.12) | collective-permute-done | bytes 81952 | tf_op jit(solution)/shard_map/ppermute | solution.py:63
  40.5 0.1 collective-permute-done.13.refs_2_
  40.6 1.0 %collective-permute-done.14.refs_3_ = bf16[40,1024]{1,0:T(8,128)(2,1)S(1)} collective-permute-done((bf16[40,1024]{1,0:T(8,128)(2,1)S(1)}, bf16[40,1024]{1,0:T(8,128)(2,1)S(1)}, u32[]{:S(2)}, u32[]{:S(2)}) %collective-permute-start.14) | collective-permute-done | bytes 81952 | tf_op jit(solution)/shard_map/ppermute | solution.py:63
  41.5 0.0 collective-permute-done.15.refs_8_.refs_3_
  41.5 0.0 copy-start.5
  41.5 0.4 place.5
  42.0 0.1 collective-permute-start.16
  42.0 0.2 copy-done.5
  42.2 1.0 %collective-permute-done.16.refs_5_ = f32[128,128]{1,0:T(8,128)S(1)} collective-permute-done((f32[128,128]{1,0:T(8,128)S(1)}, f32[128,128]{1,0:T(8,128)S(1)}, u32[]{:S(2)}, u32[]{:S(2)}) %collective-permute-start.16) | collective-permute-done | bytes 65568 | tf_op jit(solution)/shard_map/ppermute | solution.py:400
  43.3 1.2 %norm.1 = bf16[128,4096]{1,0:T(8,128)(2,1)} custom-call(bf16[128,1024]{1,0:T(8,128)(2,1)S(1)} %get-tuple-element.51.refs_0_, bf16[128,1024]{1,0:T(8,128)(2,1)S(1)} %get-tuple-element.62.refs_1_, bf16[128,1024]{1,0:T(8,128)(2,1)S(1)} %get-tuple-element.73.refs_2_, bf16[128,1024]{1,0:T(8,128)(2,1)S(1)} %collective-permute-done.15.refs_8_.refs_3_, ...), custom_call_target="tpu_custom_call" | custom-call | flops 1 | bytes 1 | tf_op jit(solution)/shard_map/norm/pallas_call | solution.py:349
  (1 shorter events, 0.0 us)
Async XLA Ops:
  0.0 11.4 %collective-permute-start.4 = (bf16[128,1024]{1,0:T(8,128)(2,1)}, bf16[128,1024]{1,0:T(8,128)(2,1)S(1)}, u32[]{:S(2)}, u32[]{:S(2)}) collective-permute-start(bf16[128,1024]{1,0:T(8,128)(2,1)} %bitcast.8), channel_id=1, source_target_pairs={{0,8},{8,24},{24,16},{16,0},{1,9},{9,25},{25,17},{17,1},{2,10},{10... | collective-permute-start | bytes 786440 | tf_op jit(solution)/shard_map/ppermute | solution.py:377
  3.0 3.7 %copy-start.2 = (bf16[128,1,1,1024]{3,0,2,1:T(8,128)(2,1)S(1)}, bf16[128,1,1,1024]{3,0,2,1:T(8,128)(2,1)}, u32[]{:S(2)}) copy-start(bf16[128,1,1,1024]{3,0,2,1:T(8,128)(2,1)} %param.8) | copy-start | bytes 786436
  4.0 13.0 %collective-permute-start = (bf16[128,1024]{1,0:T(8,128)(2,1)S(1)}, bf16[128,1024]{1,0:T(8,128)(2,1)S(1)}, u32[]{:S(2)}, u32[]{:S(2)}) collective-permute-start(bf16[128,1024]{1,0:T(8,128)(2,1)S(1)} %dynamic-slice_bitcast_fusion), channel_id=1, source_target_pairs={{0,8},{8,24},{24,16},{16,0},{1,9},{9,25},{25,17},{17,1},{2,10},{10... | collective-permute-start | bytes 786440 | tf_op jit(solution)/shard_map/ppermute | solution.py:378
  6.7 15.9 %collective-permute-start.5 = (bf16[128,1024]{1,0:T(8,128)(2,1)S(1)}, bf16[128,1024]{1,0:T(8,128)(2,1)S(1)}, u32[]{:S(2)}, u32[]{:S(2)}) collective-permute-start(bf16[128,1024]{1,0:T(8,128)(2,1)S(1)} %bitcast.11), channel_id=1, source_target_pairs={{0,8},{8,24},{24,16},{16,0},{1,9},{9,25},{25,17},{17,1},{2,10},{10... | collective-permute-start | bytes 786440 | tf_op jit(solution)/shard_map/ppermute | solution.py:377
  11.4 18.7 %collective-permute-start.9 = (bf16[128,1024]{1,0:T(8,128)(2,1)S(1)}, bf16[128,1024]{1,0:T(8,128)(2,1)S(1)}, u32[]{:S(2)}, u32[]{:S(2)}) collective-permute-start(bf16[128,1024]{1,0:T(8,128)(2,1)S(1)} %collective-permute-done.4.k_ref), channel_id=1, source_target_pairs={{0,8},{8,24},{24,16},{16,0},{1,9},{9,25},{25,17},{17,1},{2,10},{10... | collective-permute-start | bytes 786440 | tf_op jit(solution)/shard_map/ppermute | solution.py:389
  12.6 1.2 %copy-start = (bf16[1,128,4096]{2,1,0:T(8,128)(2,1)S(1)}, bf16[1,128,4096]{2,1,0:T(8,128)(2,1)}, u32[]{:S(2)}) copy-start(bf16[1,128,4096]{2,1,0:T(8,128)(2,1)} %param.6) | copy-start | bytes 3145732
  13.9 0.7 %copy-start.3 = (s32[4,4]{1,0:T(4,128)S(1)}, s32[4,4]{1,0:T(4,128)}, u32[]{:S(2)}) copy-start(s32[4,4]{1,0:T(4,128)} %counts.1) | copy-start | bytes 196
  13.9 0.7 %copy-start.4 = (s32[1,6]{1,0:T(1,128)S(1)}, s32[1,6]{1,0:T(1,128)}, u32[]{:S(2)}) copy-start(s32[1,6]{1,0:T(1,128)} %docs.1) | copy-start | bytes 76
  13.9 1.4 %copy-start.1 = (bf16[128,1,1,1024]{3,0,2,1:T(8,128)(2,1)S(1)}, bf16[128,1,1,1024]{3,0,2,1:T(8,128)(2,1)}, u32[]{:S(2)}) copy-start(bf16[128,1,1,1024]{3,0,2,1:T(8,128)(2,1)} %param.7) | copy-start | bytes 786436
  17.7 7.3 %collective-permute-start.1 = (bf16[40,2048]{1,0:T(8,128)(2,1)S(1)}, bf16[40,2048]{1,0:T(8,128)(2,1)S(1)}, u32[]{:S(2)}, u32[]{:S(2)}) collective-permute-start(bf16[40,2048]{1,0:T(8,128)(2,1)S(1)} %get-tuple-element.44), channel_id=1, source_target_pairs={{0,6},{2,4},{4,2},{6,0},{1,7},{3,5},{5,3},{7,1},{8,14},{10,12},{12... | collective-permute-start | bytes 491528 | tf_op jit(solution)/shard_map/ppermute | solution.py:63
  20.6 6.8 %collective-permute-start.2 = (bf16[40,2048]{1,0:T(8,128)(2,1)S(1)}, bf16[40,2048]{1,0:T(8,128)(2,1)S(1)}, u32[]{:S(2)}, u32[]{:S(2)}) collective-permute-start(bf16[40,2048]{1,0:T(8,128)(2,1)S(1)} %get-tuple-element.45), channel_id=1, source_target_pairs={{0,2},{2,0},{4,6},{6,4},{1,3},{3,1},{5,7},{7,5},{8,10},{10,8},{12,... | collective-permute-start | bytes 491528 | tf_op jit(solution)/shard_map/ppermute | solution.py:63
  21.2 7.7 %collective-permute-start.3 = (bf16[40,2048]{1,0:T(8,128)(2,1)S(1)}, bf16[40,2048]{1,0:T(8,128)(2,1)S(1)}, u32[]{:S(2)}, u32[]{:S(2)}) collective-permute-start(bf16[40,2048]{1,0:T(8,128)(2,1)S(1)} %get-tuple-element.46), channel_id=1, source_target_pairs={{0,4},{2,6},{4,0},{6,2},{1,5},{3,7},{5,1},{7,3},{8,12},{10,14},{12... | collective-permute-start | bytes 491528 | tf_op jit(solution)/shard_map/ppermute | solution.py:63
  22.6 12.0 %collective-permute-start.10 = (bf16[128,1024]{1,0:T(8,128)(2,1)S(1)}, bf16[128,1024]{1,0:T(8,128)(2,1)S(1)}, u32[]{:S(2)}, u32[]{:S(2)}) collective-permute-start(bf16[128,1024]{1,0:T(8,128)(2,1)S(1)} %collective-permute-done.5.v_ref), channel_id=1, source_target_pairs={{0,8},{8,24},{24,16},{16,0},{1,9},{9,25},{25,17},{17,1},{2,10},{10... | collective-permute-start | bytes 786440 | tf_op jit(solution)/shard_map/ppermute | solution.py:389
  25.0 5.5 %collective-permute-start.6 = (bf16[40,1024]{1,0:T(8,128)(2,1)S(1)}, bf16[40,1024]{1,0:T(8,128)(2,1)S(1)}, u32[]{:S(2)}, u32[]{:S(2)}) collective-permute-start(bf16[40,1024]{1,0:T(8,128)(2,1)S(1)} %get-tuple-element.58), channel_id=1, source_target_pairs={{0,6},{2,4},{4,2},{6,0},{1,7},{3,5},{5,3},{7,1},{8,14},{10,12},{12... | collective-permute-start | bytes 245768 | tf_op jit(solution)/shard_map/ppermute | solution.py:63
  27.4 4.4 %collective-permute-start.7 = (bf16[40,1024]{1,0:T(8,128)(2,1)S(1)}, bf16[40,1024]{1,0:T(8,128)(2,1)S(1)}, u32[]{:S(2)}, u32[]{:S(2)}) collective-permute-start(bf16[40,1024]{1,0:T(8,128)(2,1)S(1)} %get-tuple-element.59), channel_id=1, source_target_pairs={{0,2},{2,0},{4,6},{6,4},{1,3},{3,1},{5,7},{7,5},{8,10},{10,8},{12,... | collective-permute-start | bytes 245768 | tf_op jit(solution)/shard_map/ppermute | solution.py:63
  28.9 4.4 %collective-permute-start.8 = (bf16[40,1024]{1,0:T(8,128)(2,1)S(1)}, bf16[40,1024]{1,0:T(8,128)(2,1)S(1)}, u32[]{:S(2)}, u32[]{:S(2)}) collective-permute-start(bf16[40,1024]{1,0:T(8,128)(2,1)S(1)} %get-tuple-element.60), channel_id=1, source_target_pairs={{0,4},{2,6},{4,0},{6,2},{1,5},{3,7},{5,1},{7,3},{8,12},{10,14},{12... | collective-permute-start | bytes 245768 | tf_op jit(solution)/shard_map/ppermute | solution.py:63
  30.5 2.9 %collective-permute-start.11 = (f32[8,128]{1,0:T(8,128)S(1)}, f32[8,128]{1,0:T(8,128)S(1)}, u32[]{:S(2)}, u32[]{:S(2)}) collective-permute-start(f32[8,128]{1,0:T(8,128)S(1)} %get-tuple-element.66.inverses), channel_id=1, source_target_pairs={{0,1},{1,0},{2,3},{3,2},{4,5},{5,4},{6,7},{7,6},{8,9},{9,8},{10,11... | collective-permute-start | bytes 12296 | tf_op jit(solution)/shard_map/ppermute | solution.py:393
  33.3 8.2 %collective-permute-start.15 = (bf16[128,1024]{1,0:T(8,128)(2,1)S(1)}, bf16[128,1024]{1,0:T(8,128)(2,1)S(1)}, u32[]{:S(2)}, u32[]{:S(2)}) collective-permute-start(bf16[128,1024]{1,0:T(8,128)(2,1)S(1)} %get-tuple-element.71._), channel_id=1, source_target_pairs={{8,0},{24,8},{16,24},{0,16},{9,1},{25,9},{17,25},{1,17},{10,2},{26... | collective-permute-start | bytes 786440 | tf_op jit(solution)/shard_map/ppermute | solution.py:395
  35.1 5.4 %collective-permute-start.12 = (bf16[40,1024]{1,0:T(8,128)(2,1)S(1)}, bf16[40,1024]{1,0:T(8,128)(2,1)S(1)}, u32[]{:S(2)}, u32[]{:S(2)}) collective-permute-start(bf16[40,1024]{1,0:T(8,128)(2,1)S(1)} %get-tuple-element.68), channel_id=1, source_target_pairs={{0,6},{2,4},{4,2},{6,0},{1,7},{3,5},{5,3},{7,1},{8,14},{10,12},{12... | collective-permute-start | bytes 245768 | tf_op jit(solution)/shard_map/ppermute | solution.py:63
  36.1 4.4 %collective-permute-start.13 = (bf16[40,1024]{1,0:T(8,128)(2,1)S(1)}, bf16[40,1024]{1,0:T(8,128)(2,1)S(1)}, u32[]{:S(2)}, u32[]{:S(2)}) collective-permute-start(bf16[40,1024]{1,0:T(8,128)(2,1)S(1)} %get-tuple-element.69), channel_id=1, source_target_pairs={{0,2},{2,0},{4,6},{6,4},{1,3},{3,1},{5,7},{7,5},{8,10},{10,8},{12,... | collective-permute-start | bytes 245768 | tf_op jit(solution)/shard_map/ppermute | solution.py:63
  37.1 4.4 %collective-permute-start.14 = (bf16[40,1024]{1,0:T(8,128)(2,1)S(1)}, bf16[40,1024]{1,0:T(8,128)(2,1)S(1)}, u32[]{:S(2)}, u32[]{:S(2)}) collective-permute-start(bf16[40,1024]{1,0:T(8,128)(2,1)S(1)} %get-tuple-element.70), channel_id=1, source_target_pairs={{0,4},{2,6},{4,0},{6,2},{1,5},{3,7},{5,1},{7,3},{8,12},{10,14},{12... | collective-permute-start | bytes 245768 | tf_op jit(solution)/shard_map/ppermute | solution.py:63
  41.5 0.7 %copy-start.5 = (bf16[4096]{0:T(1024)(128)(2,1)S(1)}, bf16[4096]{0:T(1024)(128)(2,1)}, u32[]{:S(2)}) copy-start(bf16[4096]{0:T(1024)(128)(2,1)} %param.11) | copy-start | bytes 24580
  42.0 1.3 %collective-permute-start.16 = (f32[128,128]{1,0:T(8,128)S(1)}, f32[128,128]{1,0:T(8,128)S(1)}, u32[]{:S(2)}, u32[]{:S(2)}) collective-permute-start(f32[128,128]{1,0:T(8,128)S(1)} %get-tuple-element.74.refs_4_), channel_id=1, source_target_pairs={{0,1},{1,0},{2,3},{3,2},{4,5},{5,4},{6,7},{7,6},{8,9},{9,8},{10,11... | collective-permute-start | bytes 196616 | tf_op jit(solution)/shard_map/ppermute | solution.py:400

commit v10 on v9

--- a/solution.py
+++ b/solution.py
@@ -223,10 +223,11 @@
     )(query, k, v, bias, send, *bases)
 
 
-def weigh_kernel(plan, q_ref, k_ref, bias, _, weights, inverses):
+def weigh_kernel(plan, q_ref, k_ref, bias, _, weights, spread, inverses):
     found = all_weights(plan, q_ref, k_ref, bias)
     for h, (cols, (weight, inverse)) in enumerate(zip(head_columns(plan), found, strict=True)):
-        weights[cols, :] = weight
+        weights[:, cols] = weight.T
+        spread[:, cols] = jnp.broadcast_to(inverse, (HEAD_DIM, plan.seq)).T
         inverses[h : h + 1, :] = inverse
 
 
@@ -235,35 +236,39 @@
     return pl.pallas_call(
         functools.partial(weigh_kernel, plan),
         out_shape=[
-            jax.ShapeDtypeStruct((plan.block, plan.seq), jnp.bfloat16),
+            jax.ShapeDtypeStruct((plan.seq, plan.block), jnp.bfloat16),
+            jax.ShapeDtypeStruct((plan.seq, plan.block), jnp.float32),
             jax.ShapeDtypeStruct((count, plan.seq), jnp.float32),
         ],
         in_specs=[VMEM] * 3 + [ANY],
-        out_specs=[VMEM] * 2,
+        out_specs=[VMEM] * 3,
         compiler_params=PARAMS,
         cost_estimate=COST,
         name="weigh",
     )(query, k, bias, after)
 
 
-def finish_kernel(plan, weights, inverses, v_ref, send, _, *refs):
+def finish_kernel(plan, weights, spread, v_ref, send, _, *refs):
     outs, attn = refs[:-1], refs[-1]
-    for h, cols in enumerate(head_columns(plan)):
-        attn[cols, :] = weighted(v_ref, cols, weights[cols, :], inverses[h : h + 1, :])
-    pick_rows(plan, send, attn, outs)
-
-
-def finish(plan, weights, inverses, v, send, after):
+    for cols in head_columns(plan):
+        accum = jnp.dot(weights[:, cols], v_ref[:, cols], preferred_element_type=jnp.float32)
+        attn[:, cols] = (accum * spread[:, cols]).astype(jnp.bfloat16)
+    picked = jnp.dot(send[...], attn[...], preferred_element_type=jnp.float32)
+    for part, out in enumerate(outs):
+        out[...] = picked[part * plan.rows : (part + 1) * plan.rows].astype(jnp.bfloat16)
+
+
+def finish(plan, weights, spread, v, send, after):
     return pl.pallas_call(
         functools.partial(finish_kernel, plan),
         out_shape=[jax.ShapeDtypeStruct((plan.rows, plan.block), jnp.bfloat16)] * plan.parts,
         in_specs=[VMEM] * 4 + [ANY],
         out_specs=[VMEM] * plan.parts,
-        scratch_shapes=[pltpu.VMEM((plan.block, plan.seq), jnp.bfloat16)],
+        scratch_shapes=[pltpu.VMEM((plan.seq, plan.block), jnp.bfloat16)],
         compiler_params=PARAMS,
         cost_estimate=COST,
         name="finish",
-    )(weights, inverses, v, send, after)
+    )(weights, spread, v, send, after)
 
 
 def squares_of(ref):
@@ -387,13 +392,13 @@
         placed, total = place(plan, got, places, (block,), sums=(total,))
         pieces.append((placed, t, 0))
         k, v = lax.ppermute(k, "pipe", forward), lax.ppermute(v, "pipe", forward)
-    weights, inverses = weigh(plan, asked[n - 2], k, bias, borrowed)
+    weights, spread, inverses = weigh(plan, asked[n - 2], k, bias, borrowed)
     met = inverses
     if plan.tensor == 2:
         met = lax.ppermute(inverses, "tensor", [(0, 1), (1, 0)])
     borrowed, *_ = lax.optimization_barrier((borrowed, met, *got))
     returned = lax.ppermute(borrowed, "pipe", backward)
-    got = plan.regroup(finish(plan, weights, inverses, v, send, met))
+    got = plan.regroup(finish(plan, weights, spread, v, send, met))
     placed, total = place(plan, got, places, (block,), blocks=(returned,), sums=(total,))
     pieces += [(placed, n - 2, 0), (returned, n - 1, 0)]
     if plan.tensor == 2:

time: 44.7 us -> 44.6 us (level)
  no operation moved by 1% of the time
where the time goes in v10:
time: 44.6 us; the launch traced here: 44.4 us
  starting transfers between devices  21.3 us (48%)
  waiting for transfers between devices  13.6 us (30%)
  Pallas kernels  6.4 us (14%)
  local copies, waits for them, and re-layouts  3.02 us (7%)
    ppermute x9, starting transfers between devices, regroup(): lax.ppermute(part, 'dp', [(g, g ^ step) for g in range(self.groups)])  11.4 us
    ppermute x9, waiting for transfers between devices, regroup(): lax.ppermute(part, 'dp', [(g, g ^ step) for g in range(self.groups)])  5.73 us
    ppermute x1, waiting for transfers between devices, body(): lax.ppermute(keys, 'pipe', forward)  4.24 us
    ppermute x1, starting transfers between devices, body(): lax.ppermute(keys, 'pipe', forward)  3.02 us
    ppermute x1, starting transfers between devices, body(): lent = lax.ppermute(ahead, 'pipe', forward)  2.64 us
    ppermute x2, starting transfers between devices, body(): k, v = (lax.ppermute(k, 'pipe', forward), lax.ppermute(v, 'pipe', forward))  2.42 us
    unnamed x12, local copies, waits for them, and re-layouts  2.01 us
    pallas_call x3, Pallas kernels, place(): pl.pallas_call(functools.partial(place_kernel, plan, widths, summed, len(...  1.5 us
  transfers between devices with their start and end apart: 17, of which 11 were waited for; matrix products, arithmetic and copies ran while one was open for 2% of the time, Pallas kernels for 11%

profile of v10, /device:TPU:0, one launch (start us, length us, event | category | flops | bytes accessed | tf_op | source)
XLA Modules:
  0.0 44.4 jit_solution(2226294985996763505)
XLA Ops:
  0.0 3.0 %collective-permute-start.4 = (bf16[128,1024]{1,0:T(8,128)(2,1)}, bf16[128,1024]{1,0:T(8,128)(2,1)S(1)}, u32[]{:S(2)}, u32[]{:S(2)}) collective-permute-start(bf16[128,1024]{1,0:T(8,128)(2,1)} %bitcast.8), channel_id=1, source_target_pairs={{0,8},{8,24},{24,16},{16,0},{1,9},{9,25},{25,17},{17,1},{2,10},{10... | collective-permute-start | bytes 786440 | tf_op jit(solution)/shard_map/ppermute | solution.py:382
  3.0 0.0 copy-start.2
  3.0 1.0 %dynamic-slice_bitcast_fusion = bf16[128,1024]{1,0:T(8,128)(2,1)S(1)} fusion(bf16[1,128,4096]{2,1,0:T(8,128)(2,1)} %param.6, s32[]{:T(128)S(6)} %select_n.16), kind=kLoop, calls=%fused_computation | loop fusion | bytes 524292 | tf_op jit(solution)/shard_map/dynamic_slice | solution.py:379
  4.0 2.6 %collective-permute-start = (bf16[128,1024]{1,0:T(8,128)(2,1)S(1)}, bf16[128,1024]{1,0:T(8,128)(2,1)S(1)}, u32[]{:S(2)}, u32[]{:S(2)}) collective-permute-start(bf16[128,1024]{1,0:T(8,128)(2,1)S(1)} %dynamic-slice_bitcast_fusion), channel_id=1, source_target_pairs={{0,8},{8,24},{24,16},{16,0},{1,9},{9,25},{25,17},{17,1},{2,10},{10... | collective-permute-start | bytes 786440 | tf_op jit(solution)/shard_map/ppermute | solution.py:383
  6.7 0.0 copy-done.2
  6.7 0.4 %collective-permute-start.5 = (bf16[128,1024]{1,0:T(8,128)(2,1)S(1)}, bf16[128,1024]{1,0:T(8,128)(2,1)S(1)}, u32[]{:S(2)}, u32[]{:S(2)}) collective-permute-start(bf16[128,1024]{1,0:T(8,128)(2,1)S(1)} %bitcast.11), channel_id=1, source_target_pairs={{0,8},{8,24},{24,16},{16,0},{1,9},{9,25},{25,17},{17,1},{2,10},{10... | collective-permute-start | bytes 786440 | tf_op jit(solution)/shard_map/ppermute | solution.py:382
  7.1 4.2 %collective-permute-done.4.k_ref = bf16[128,1024]{1,0:T(8,128)(2,1)S(1)} collective-permute-done((bf16[128,1024]{1,0:T(8,128)(2,1)}, bf16[128,1024]{1,0:T(8,128)(2,1)S(1)}, u32[]{:S(2)}, u32[]{:S(2)}) %collective-permute-start.4) | collective-permute-done | bytes 262176 | tf_op jit(solution)/shard_map/ppermute | solution.py:382
  11.4 1.3 %collective-permute-start.9 = (bf16[128,1024]{1,0:T(8,128)(2,1)S(1)}, bf16[128,1024]{1,0:T(8,128)(2,1)S(1)}, u32[]{:S(2)}, u32[]{:S(2)}) collective-permute-start(bf16[128,1024]{1,0:T(8,128)(2,1)S(1)} %collective-permute-done.4.k_ref), channel_id=1, source_target_pairs={{0,8},{8,24},{24,16},{16,0},{1,9},{9,25},{25,17},{17,1},{2,10},{10... | collective-permute-start | bytes 786440 | tf_op jit(solution)/shard_map/ppermute | solution.py:394
  12.6 0.0 copy-start
  12.6 1.2 %copy-done = bf16[1,128,4096]{2,1,0:T(8,128)(2,1)S(1)} copy-done((bf16[1,128,4096]{2,1,0:T(8,128)(2,1)S(1)}, bf16[1,128,4096]{2,1,0:T(8,128)(2,1)}, u32[]{:S(2)}) %copy-start) | copy-done | bytes 1048600
  13.9 0.0 copy-start.3
  13.9 0.0 copy-start.4
  13.9 0.0 copy-start.1
  13.9 0.1 split.1
  14.0 0.6 %copy-done.3 = s32[4,4]{1,0:T(4,128)S(1)} copy-done((s32[4,4]{1,0:T(4,128)S(1)}, s32[4,4]{1,0:T(4,128)}, u32[]{:S(2)}) %copy-start.3) | copy-done | bytes 88
  14.5 0.0 copy-done.4
  14.6 0.7 %tables.1 = (f32[128,128]{1,0:T(8,128)S(1)}, bf16[160,128]{1,0:T(8,128)(2,1)S(1)}, bf16[128,40]{1,0:T(8,128)(2,1)S(1)}, bf16[128,40]{1,0:T(8,128)(2,1)S(1)}, bf1...) custom-call(s32[1,6]{1,0:T(1,128)S(1)} %copy-done.4, s32[4,4]{1,0:T(4,128)S(1)} %copy-done.3), custom_call_target="tpu_custom_call" | custom-call | flops 1 | bytes 1 | tf_op jit(solution)/shard_map/tables/pallas_call | solution.py:136
  15.2 0.0 copy-done.1
  15.2 0.5 %heads.1.refs_0_ = bf16[1024,128]{1,0:T(8,128)(2,1)S(1)} custom-call(bf16[128,1024]{1,0:T(8,128)(2,1)S(1)} %get-tuple-element.43.q_ref, bf16[128,1024]{1,0:T(8,128)(2,1)S(1)} %bitcast.9, bf16[128,1024]{1,0:T(8,128)(2,1)S(1)} %bitcast.12, f32[128,128]{1,0:T(8,128)S(1)} %get-tuple-element.41.bias), custom_call_target="tpu_custom_call" | custom-call | flops 1 | bytes 1 | tf_op jit(solution)/shard_map/heads/pallas_call | solution.py:190
  15.8 1.2 %collective-permute-done.q_ref = bf16[128,1024]{1,0:T(8,128)(2,1)S(1)} collective-permute-done((bf16[128,1024]{1,0:T(8,128)(2,1)S(1)}, bf16[128,1024]{1,0:T(8,128)(2,1)S(1)}, u32[]{:S(2)}, u32[]{:S(2)}) %collective-permute-start) | collective-permute-done | bytes 262176 | tf_op jit(solution)/shard_map/ppermute | solution.py:383
  17.0 0.7 %attend.2 = (bf16[40,2048]{1,0:T(8,128)(2,1)S(1)}, bf16[40,2048]{1,0:T(8,128)(2,1)S(1)}, bf16[40,2048]{1,0:T(8,128)(2,1)S(1)}, bf16[40,2048]{1,0:T(8,128)(2,1)S(1)}) custom-call(bf16[128,1024]{1,0:T(8,128)(2,1)S(1)} %collective-permute-done.q_ref, bf16[128,1024]{1,0:T(8,128)(2,1)S(1)} %bitcast.10, bf16[128,1024]{1,0:T(8,128)(2,1)S(1)} %bitcast.13, ...), custom_call_target="tpu_custom_call" | custom-call | flops 1 | bytes 1 | tf_op jit(solution)/shard_map/attend/pallas_call | solution.py:214
  17.7 2.9 %collective-permute-start.1 = (bf16[40,2048]{1,0:T(8,128)(2,1)S(1)}, bf16[40,2048]{1,0:T(8,128)(2,1)S(1)}, u32[]{:S(2)}, u32[]{:S(2)}) collective-permute-start(bf16[40,2048]{1,0:T(8,128)(2,1)S(1)} %get-tuple-element.45), channel_id=1, source_target_pairs={{0,6},{2,4},{4,2},{6,0},{1,7},{3,5},{5,3},{7,1},{8,14},{10,12},{12... | collective-permute-start | bytes 491528 | tf_op jit(solution)/shard_map/ppermute | solution.py:63
  20.6 0.5 %collective-permute-start.2 = (bf16[40,2048]{1,0:T(8,128)(2,1)S(1)}, bf16[40,2048]{1,0:T(8,128)(2,1)S(1)}, u32[]{:S(2)}, u32[]{:S(2)}) collective-permute-start(bf16[40,2048]{1,0:T(8,128)(2,1)S(1)} %get-tuple-element.46), channel_id=1, source_target_pairs={{0,2},{2,0},{4,6},{6,4},{1,3},{3,1},{5,7},{7,5},{8,10},{10,8},{12,... | collective-permute-start | bytes 491528 | tf_op jit(solution)/shard_map/ppermute | solution.py:63
  21.2 0.1 collective-permute-start.3
  21.3 1.3 %collective-permute-done.5.v_ref = bf16[128,1024]{1,0:T(8,128)(2,1)S(1)} collective-permute-done((bf16[128,1024]{1,0:T(8,128)(2,1)S(1)}, bf16[128,1024]{1,0:T(8,128)(2,1)S(1)}, u32[]{:S(2)}, u32[]{:S(2)}) %collective-permute-start.5) | collective-permute-done | bytes 262176 | tf_op jit(solution)/shard_map/ppermute | solution.py:382
  22.6 1.2 %collective-permute-start.10 = (bf16[128,1024]{1,0:T(8,128)(2,1)S(1)}, bf16[128,1024]{1,0:T(8,128)(2,1)S(1)}, u32[]{:S(2)}, u32[]{:S(2)}) collective-permute-start(bf16[128,1024]{1,0:T(8,128)(2,1)S(1)} %collective-permute-done.5.v_ref), channel_id=1, source_target_pairs={{0,8},{8,24},{24,16},{16,0},{1,9},{9,25},{25,17},{17,1},{2,10},{10... | collective-permute-start | bytes 786440 | tf_op jit(solution)/shard_map/ppermute | solution.py:394
  23.8 0.7 %attend.3 = (bf16[40,1024]{1,0:T(8,128)(2,1)S(1)}, bf16[40,1024]{1,0:T(8,128)(2,1)S(1)}, bf16[40,1024]{1,0:T(8,128)(2,1)S(1)}, bf16[40,1024]{1,0:T(8,128)(2,1)S(1)}) custom-call(bf16[128,1024]{1,0:T(8,128)(2,1)S(1)} %get-tuple-element.53.q_ref, bf16[128,1024]{1,0:T(8,128)(2,1)S(1)} %collective-permute-done.4.k_ref, ...), custom_call_target="tpu_custom_call" | custom-call | flops 1 | bytes 1 | tf_op jit(solution)/shard_map/attend/pallas_call | solution.py:214
  24.5 0.5 %collective-permute-done.1.refs_1_ = bf16[40,2048]{1,0:T(8,128)(2,1)S(1)} collective-permute-done((bf16[40,2048]{1,0:T(8,128)(2,1)S(1)}, bf16[40,2048]{1,0:T(8,128)(2,1)S(1)}, u32[]{:S(2)}, u32[]{:S(2)}) %collective-permute-start.1) | collective-permute-done | bytes 163872 | tf_op jit(solution)/shard_map/ppermute | solution.py:63
  25.0 2.3 %collective-permute-start.6 = (bf16[40,1024]{1,0:T(8,128)(2,1)S(1)}, bf16[40,1024]{1,0:T(8,128)(2,1)S(1)}, u32[]{:S(2)}, u32[]{:S(2)}) collective-permute-start(bf16[40,1024]{1,0:T(8,128)(2,1)S(1)} %get-tuple-element.59), channel_id=1, source_target_pairs={{0,6},{2,4},{4,2},{6,0},{1,7},{3,5},{5,3},{7,1},{8,14},{10,12},{12... | collective-permute-start | bytes 245768 | tf_op jit(solution)/shard_map/ppermute | solution.py:63
  27.3 0.1 collective-permute-done.2.refs_2_
  27.4 1.5 %collective-permute-start.7 = (bf16[40,1024]{1,0:T(8,128)(2,1)S(1)}, bf16[40,1024]{1,0:T(8,128)(2,1)S(1)}, u32[]{:S(2)}, u32[]{:S(2)}) collective-permute-start(bf16[40,1024]{1,0:T(8,128)(2,1)S(1)} %get-tuple-element.60), channel_id=1, source_target_pairs={{0,2},{2,0},{4,6},{6,4},{1,3},{3,1},{5,7},{7,5},{8,10},{10,8},{12,... | collective-permute-start | bytes 245768 | tf_op jit(solution)/shard_map/ppermute | solution.py:63
  28.9 0.0 collective-permute-done.3.refs_3_
  28.9 0.5 %collective-permute-start.8 = (bf16[40,1024]{1,0:T(8,128)(2,1)S(1)}, bf16[40,1024]{1,0:T(8,128)(2,1)S(1)}, u32[]{:S(2)}, u32[]{:S(2)}) collective-permute-start(bf16[40,1024]{1,0:T(8,128)(2,1)S(1)} %get-tuple-element.61), channel_id=1, source_target_pairs={{0,4},{2,6},{4,0},{6,2},{1,5},{3,7},{5,1},{7,3},{8,12},{10,14},{12... | collective-permute-start | bytes 245768 | tf_op jit(solution)/shard_map/ppermute | solution.py:63
  29.4 0.7 %place.3 = (bf16[128,1024]{1,0:T(8,128)(2,1)S(1)}, bf16[128,1024]{1,0:T(8,128)(2,1)S(1)}, f32[128,128]{1,0:T(8,128)S(1)}) custom-call(bf16[40,2048]{1,0:T(8,128)(2,1)S(1)} %get-tuple-element.44.refs_0_, bf16[40,2048]{1,0:T(8,128)(2,1)S(1)} %collective-permute-done.1.refs_1_, bf16[40,2048]{1,0:T(8,128)(2,1)S(1)} %collective-permute-done.2.refs_2_, ...), custom_call_target="tpu_custom_call" | custom-call | flops 1 | bytes 1 | tf_op jit(solution)/shard_map/place/pallas_call | solution.py:313
  30.1 0.0 collective-permute-done.9.k_ref
  30.1 0.6 %weigh.1 = (bf16[128,1024]{1,0:T(8,128)(2,1)S(1)}, f32[128,1024]{1,0:T(8,128)S(1)}, f32[8,128]{1,0:T(8,128)S(1)}) custom-call(bf16[128,1024]{1,0:T(8,128)(2,1)S(1)} %get-tuple-element.64.q_ref, bf16[128,1024]{1,0:T(8,128)(2,1)S(1)} %collective-permute-done.9.k_ref, f32[128,128]{1,0:T(8,128)S(1)} %get-tuple-element.41.bias, ...), custom_call_target="tpu_custom_call" | custom-call | flops 1 | bytes 1 | tf_op jit(solution)/shard_map/weigh/pallas_call | solution.py:236
  30.7 0.1 collective-permute-start.11
  30.7 0.0 collective-permute-done.6.refs_1_
  30.7 1.1 %collective-permute-done.7.refs_2_ = bf16[40,1024]{1,0:T(8,128)(2,1)S(1)} collective-permute-done((bf16[40,1024]{1,0:T(8,128)(2,1)S(1)}, bf16[40,1024]{1,0:T(8,128)(2,1)S(1)}, u32[]{:S(2)}, u32[]{:S(2)}) %collective-permute-start.7) | collective-permute-done | bytes 81952 | tf_op jit(solution)/shard_map/ppermute | solution.py:63
  31.8 1.5 %collective-permute-done.8.refs_3_ = bf16[40,1024]{1,0:T(8,128)(2,1)S(1)} collective-permute-done((bf16[40,1024]{1,0:T(8,128)(2,1)S(1)}, bf16[40,1024]{1,0:T(8,128)(2,1)S(1)}, u32[]{:S(2)}, u32[]{:S(2)}) %collective-permute-start.8) | collective-permute-done | bytes 81952 | tf_op jit(solution)/shard_map/ppermute | solution.py:63
  33.3 0.0 collective-permute-done.11._
  33.3 1.2 %collective-permute-start.15 = (bf16[128,1024]{1,0:T(8,128)(2,1)S(1)}, bf16[128,1024]{1,0:T(8,128)(2,1)S(1)}, u32[]{:S(2)}, u32[]{:S(2)}) collective-permute-start(bf16[128,1024]{1,0:T(8,128)(2,1)S(1)} %get-tuple-element.73._), channel_id=1, source_target_pairs={{8,0},{24,8},{16,24},{0,16},{9,1},{25,9},{17,25},{1,17},{10,2},{26... | collective-permute-start | bytes 786440 | tf_op jit(solution)/shard_map/ppermute | solution.py:400
  34.6 0.0 collective-permute-done.10.v_ref
  34.6 0.4 finish.1
  35.0 1.1 %collective-permute-start.12 = (bf16[40,1024]{1,0:T(8,128)(2,1)S(1)}, bf16[40,1024]{1,0:T(8,128)(2,1)S(1)}, u32[]{:S(2)}, u32[]{:S(2)}) collective-permute-start(bf16[40,1024]{1,0:T(8,128)(2,1)S(1)} %get-tuple-element.70), channel_id=1, source_target_pairs={{0,6},{2,4},{4,2},{6,0},{1,7},{3,5},{5,3},{7,1},{8,14},{10,12},{12... | collective-permute-start | bytes 245768 | tf_op jit(solution)/shard_map/ppermute | solution.py:63
  36.1 1.0 %collective-permute-start.13 = (bf16[40,1024]{1,0:T(8,128)(2,1)S(1)}, bf16[40,1024]{1,0:T(8,128)(2,1)S(1)}, u32[]{:S(2)}, u32[]{:S(2)}) collective-permute-start(bf16[40,1024]{1,0:T(8,128)(2,1)S(1)} %get-tuple-element.71), channel_id=1, source_target_pairs={{0,2},{2,0},{4,6},{6,4},{1,3},{3,1},{5,7},{7,5},{8,10},{10,8},{12,... | collective-permute-start | bytes 245768 | tf_op jit(solution)/shard_map/ppermute | solution.py:63
  37.0 1.5 %collective-permute-start.14 = (bf16[40,1024]{1,0:T(8,128)(2,1)S(1)}, bf16[40,1024]{1,0:T(8,128)(2,1)S(1)}, u32[]{:S(2)}, u32[]{:S(2)}) collective-permute-start(bf16[40,1024]{1,0:T(8,128)(2,1)S(1)} %get-tuple-element.72), channel_id=1, source_target_pairs={{0,4},{2,6},{4,0},{6,2},{1,5},{3,7},{5,1},{7,3},{8,12},{10,14},{12... | collective-permute-start | bytes 245768 | tf_op jit(solution)/shard_map/ppermute | solution.py:63
  38.5 0.4 place.4
  39.0 1.4 %collective-permute-done.12.refs_1_ = bf16[40,1024]{1,0:T(8,128)(2,1)S(1)} collective-permute-done((bf16[40,1024]{1,0:T(8,128)(2,1)S(1)}, bf16[40,1024]{1,0:T(8,128)(2,1)S(1)}, u32[]{:S(2)}, u32[]{:S(2)}) %collective-permute-start.12) | collective-permute-done | bytes 81952 | tf_op jit(solution)/shard_map/ppermute | solution.py:63
  40.4 0.1 collective-permute-done.13.refs_2_
  40.5 0.9 %collective-permute-done.14.refs_3_ = bf16[40,1024]{1,0:T(8,128)(2,1)S(1)} collective-permute-done((bf16[40,1024]{1,0:T(8,128)(2,1)S(1)}, bf16[40,1024]{1,0:T(8,128)(2,1)S(1)}, u32[]{:S(2)}, u32[]{:S(2)}) %collective-permute-start.14) | collective-permute-done | bytes 81952 | tf_op jit(solution)/shard_map/ppermute | solution.py:63
  41.5 0.0 collective-permute-done.15.refs_8_.refs_3_
  41.5 0.0 copy-start.5
  41.5 0.4 place.5
  41.9 0.1 collective-permute-start.16
  42.0 0.2 copy-done.5
  42.2 1.0 %collective-permute-done.16.refs_5_ = f32[128,128]{1,0:T(8,128)S(1)} collective-permute-done((f32[128,128]{1,0:T(8,128)S(1)}, f32[128,128]{1,0:T(8,128)S(1)}, u32[]{:S(2)}, u32[]{:S(2)}) %collective-permute-start.16) | collective-permute-done | bytes 65568 | tf_op jit(solution)/shard_map/ppermute | solution.py:405
  43.2 1.2 %norm.1 = bf16[128,4096]{1,0:T(8,128)(2,1)} custom-call(bf16[128,1024]{1,0:T(8,128)(2,1)S(1)} %get-tuple-element.52.refs_0_, bf16[128,1024]{1,0:T(8,128)(2,1)S(1)} %get-tuple-element.63.refs_1_, bf16[128,1024]{1,0:T(8,128)(2,1)S(1)} %get-tuple-element.75.refs_2_, bf16[128,1024]{1,0:T(8,128)(2,1)S(1)} %collective-permute-done.15.refs_8_.refs_3_, ...), custom_call_target="tpu_custom_call" | custom-call | flops 1 | bytes 1 | tf_op jit(solution)/shard_map/norm/pallas_call | solution.py:354
  (1 shorter events, 0.0 us)
Async XLA Ops:
  0.0 11.4 %collective-permute-start.4 = (bf16[128,1024]{1,0:T(8,128)(2,1)}, bf16[128,1024]{1,0:T(8,128)(2,1)S(1)}, u32[]{:S(2)}, u32[]{:S(2)}) collective-permute-start(bf16[128,1024]{1,0:T(8,128)(2,1)} %bitcast.8), channel_id=1, source_target_pairs={{0,8},{8,24},{24,16},{16,0},{1,9},{9,25},{25,17},{17,1},{2,10},{10... | collective-permute-start | bytes 786440 | tf_op jit(solution)/shard_map/ppermute | solution.py:382
  3.0 3.7 %copy-start.2 = (bf16[128,1,1,1024]{3,0,2,1:T(8,128)(2,1)S(1)}, bf16[128,1,1,1024]{3,0,2,1:T(8,128)(2,1)}, u32[]{:S(2)}) copy-start(bf16[128,1,1,1024]{3,0,2,1:T(8,128)(2,1)} %param.8) | copy-start | bytes 786436
  4.0 13.0 %collective-permute-start = (bf16[128,1024]{1,0:T(8,128)(2,1)S(1)}, bf16[128,1024]{1,0:T(8,128)(2,1)S(1)}, u32[]{:S(2)}, u32[]{:S(2)}) collective-permute-start(bf16[128,1024]{1,0:T(8,128)(2,1)S(1)} %dynamic-slice_bitcast_fusion), channel_id=1, source_target_pairs={{0,8},{8,24},{24,16},{16,0},{1,9},{9,25},{25,17},{17,1},{2,10},{10... | collective-permute-start | bytes 786440 | tf_op jit(solution)/shard_map/ppermute | solution.py:383
  6.7 15.9 %collective-permute-start.5 = (bf16[128,1024]{1,0:T(8,128)(2,1)S(1)}, bf16[128,1024]{1,0:T(8,128)(2,1)S(1)}, u32[]{:S(2)}, u32[]{:S(2)}) collective-permute-start(bf16[128,1024]{1,0:T(8,128)(2,1)S(1)} %bitcast.11), channel_id=1, source_target_pairs={{0,8},{8,24},{24,16},{16,0},{1,9},{9,25},{25,17},{17,1},{2,10},{10... | collective-permute-start | bytes 786440 | tf_op jit(solution)/shard_map/ppermute | solution.py:382
  11.4 18.7 %collective-permute-start.9 = (bf16[128,1024]{1,0:T(8,128)(2,1)S(1)}, bf16[128,1024]{1,0:T(8,128)(2,1)S(1)}, u32[]{:S(2)}, u32[]{:S(2)}) collective-permute-start(bf16[128,1024]{1,0:T(8,128)(2,1)S(1)} %collective-permute-done.4.k_ref), channel_id=1, source_target_pairs={{0,8},{8,24},{24,16},{16,0},{1,9},{9,25},{25,17},{17,1},{2,10},{10... | collective-permute-start | bytes 786440 | tf_op jit(solution)/shard_map/ppermute | solution.py:394
  12.6 1.2 %copy-start = (bf16[1,128,4096]{2,1,0:T(8,128)(2,1)S(1)}, bf16[1,128,4096]{2,1,0:T(8,128)(2,1)}, u32[]{:S(2)}) copy-start(bf16[1,128,4096]{2,1,0:T(8,128)(2,1)} %param.6) | copy-start | bytes 3145732
  13.9 0.7 %copy-start.3 = (s32[4,4]{1,0:T(4,128)S(1)}, s32[4,4]{1,0:T(4,128)}, u32[]{:S(2)}) copy-start(s32[4,4]{1,0:T(4,128)} %counts.1) | copy-start | bytes 196
  13.9 0.7 %copy-start.4 = (s32[1,6]{1,0:T(1,128)S(1)}, s32[1,6]{1,0:T(1,128)}, u32[]{:S(2)}) copy-start(s32[1,6]{1,0:T(1,128)} %docs.1) | copy-start | bytes 76
  13.9 1.4 %copy-start.1 = (bf16[128,1,1,1024]{3,0,2,1:T(8,128)(2,1)S(1)}, bf16[128,1,1,1024]{3,0,2,1:T(8,128)(2,1)}, u32[]{:S(2)}) copy-start(bf16[128,1,1,1024]{3,0,2,1:T(8,128)(2,1)} %param.7) | copy-start | bytes 786436
  17.7 7.3 %collective-permute-start.1 = (bf16[40,2048]{1,0:T(8,128)(2,1)S(1)}, bf16[40,2048]{1,0:T(8,128)(2,1)S(1)}, u32[]{:S(2)}, u32[]{:S(2)}) collective-permute-start(bf16[40,2048]{1,0:T(8,128)(2,1)S(1)} %get-tuple-element.45), channel_id=1, source_target_pairs={{0,6},{2,4},{4,2},{6,0},{1,7},{3,5},{5,3},{7,1},{8,14},{10,12},{12... | collective-permute-start | bytes 491528 | tf_op jit(solution)/shard_map/ppermute | solution.py:63
  20.6 6.8 %collective-permute-start.2 = (bf16[40,2048]{1,0:T(8,128)(2,1)S(1)}, bf16[40,2048]{1,0:T(8,128)(2,1)S(1)}, u32[]{:S(2)}, u32[]{:S(2)}) collective-permute-start(bf16[40,2048]{1,0:T(8,128)(2,1)S(1)} %get-tuple-element.46), channel_id=1, source_target_pairs={{0,2},{2,0},{4,6},{6,4},{1,3},{3,1},{5,7},{7,5},{8,10},{10,8},{12,... | collective-permute-start | bytes 491528 | tf_op jit(solution)/shard_map/ppermute | solution.py:63
  21.2 7.7 %collective-permute-start.3 = (bf16[40,2048]{1,0:T(8,128)(2,1)S(1)}, bf16[40,2048]{1,0:T(8,128)(2,1)S(1)}, u32[]{:S(2)}, u32[]{:S(2)}) collective-permute-start(bf16[40,2048]{1,0:T(8,128)(2,1)S(1)} %get-tuple-element.47), channel_id=1, source_target_pairs={{0,4},{2,6},{4,0},{6,2},{1,5},{3,7},{5,1},{7,3},{8,12},{10,14},{12... | collective-permute-start | bytes 491528 | tf_op jit(solution)/shard_map/ppermute | solution.py:63
  22.6 12.0 %collective-permute-start.10 = (bf16[128,1024]{1,0:T(8,128)(2,1)S(1)}, bf16[128,1024]{1,0:T(8,128)(2,1)S(1)}, u32[]{:S(2)}, u32[]{:S(2)}) collective-permute-start(bf16[128,1024]{1,0:T(8,128)(2,1)S(1)} %collective-permute-done.5.v_ref), channel_id=1, source_target_pairs={{0,8},{8,24},{24,16},{16,0},{1,9},{9,25},{25,17},{17,1},{2,10},{10... | collective-permute-start | bytes 786440 | tf_op jit(solution)/shard_map/ppermute | solution.py:394
  25.0 5.7 %collective-permute-start.6 = (bf16[40,1024]{1,0:T(8,128)(2,1)S(1)}, bf16[40,1024]{1,0:T(8,128)(2,1)S(1)}, u32[]{:S(2)}, u32[]{:S(2)}) collective-permute-start(bf16[40,1024]{1,0:T(8,128)(2,1)S(1)} %get-tuple-element.59), channel_id=1, source_target_pairs={{0,6},{2,4},{4,2},{6,0},{1,7},{3,5},{5,3},{7,1},{8,14},{10,12},{12... | collective-permute-start | bytes 245768 | tf_op jit(solution)/shard_map/ppermute | solution.py:63
  27.4 4.4 %collective-permute-start.7 = (bf16[40,1024]{1,0:T(8,128)(2,1)S(1)}, bf16[40,1024]{1,0:T(8,128)(2,1)S(1)}, u32[]{:S(2)}, u32[]{:S(2)}) collective-permute-start(bf16[40,1024]{1,0:T(8,128)(2,1)S(1)} %get-tuple-element.60), channel_id=1, source_target_pairs={{0,2},{2,0},{4,6},{6,4},{1,3},{3,1},{5,7},{7,5},{8,10},{10,8},{12,... | collective-permute-start | bytes 245768 | tf_op jit(solution)/shard_map/ppermute | solution.py:63
  28.9 4.4 %collective-permute-start.8 = (bf16[40,1024]{1,0:T(8,128)(2,1)S(1)}, bf16[40,1024]{1,0:T(8,128)(2,1)S(1)}, u32[]{:S(2)}, u32[]{:S(2)}) collective-permute-start(bf16[40,1024]{1,0:T(8,128)(2,1)S(1)} %get-tuple-element.61), channel_id=1, source_target_pairs={{0,4},{2,6},{4,0},{6,2},{1,5},{3,7},{5,1},{7,3},{8,12},{10,14},{12... | collective-permute-start | bytes 245768 | tf_op jit(solution)/shard_map/ppermute | solution.py:63
  30.7 2.7 %collective-permute-start.11 = (f32[8,128]{1,0:T(8,128)S(1)}, f32[8,128]{1,0:T(8,128)S(1)}, u32[]{:S(2)}, u32[]{:S(2)}) collective-permute-start(f32[8,128]{1,0:T(8,128)S(1)} %get-tuple-element.68), channel_id=1, source_target_pairs={{0,1},{1,0},{2,3},{3,2},{4,5},{5,4},{6,7},{7,6},{8,9},{9,8},{10,11... | collective-permute-start | bytes 12296 | tf_op jit(solution)/shard_map/ppermute | solution.py:398
  33.3 8.1 %collective-permute-start.15 = (bf16[128,1024]{1,0:T(8,128)(2,1)S(1)}, bf16[128,1024]{1,0:T(8,128)(2,1)S(1)}, u32[]{:S(2)}, u32[]{:S(2)}) collective-permute-start(bf16[128,1024]{1,0:T(8,128)(2,1)S(1)} %get-tuple-element.73._), channel_id=1, source_target_pairs={{8,0},{24,8},{16,24},{0,16},{9,1},{25,9},{17,25},{1,17},{10,2},{26... | collective-permute-start | bytes 786440 | tf_op jit(solution)/shard_map/ppermute | solution.py:400
  35.0 5.4 %collective-permute-start.12 = (bf16[40,1024]{1,0:T(8,128)(2,1)S(1)}, bf16[40,1024]{1,0:T(8,128)(2,1)S(1)}, u32[]{:S(2)}, u32[]{:S(2)}) collective-permute-start(bf16[40,1024]{1,0:T(8,128)(2,1)S(1)} %get-tuple-element.70), channel_id=1, source_target_pairs={{0,6},{2,4},{4,2},{6,0},{1,7},{3,5},{5,3},{7,1},{8,14},{10,12},{12... | collective-permute-start | bytes 245768 | tf_op jit(solution)/shard_map/ppermute | solution.py:63
  36.1 4.5 %collective-permute-start.13 = (bf16[40,1024]{1,0:T(8,128)(2,1)S(1)}, bf16[40,1024]{1,0:T(8,128)(2,1)S(1)}, u32[]{:S(2)}, u32[]{:S(2)}) collective-permute-start(bf16[40,1024]{1,0:T(8,128)(2,1)S(1)} %get-tuple-element.71), channel_id=1, source_target_pairs={{0,2},{2,0},{4,6},{6,4},{1,3},{3,1},{5,7},{7,5},{8,10},{10,8},{12,... | collective-permute-start | bytes 245768 | tf_op jit(solution)/shard_map/ppermute | solution.py:63
  37.0 4.4 %collective-permute-start.14 = (bf16[40,1024]{1,0:T(8,128)(2,1)S(1)}, bf16[40,1024]{1,0:T(8,128)(2,1)S(1)}, u32[]{:S(2)}, u32[]{:S(2)}) collective-permute-start(bf16[40,1024]{1,0:T(8,128)(2,1)S(1)} %get-tuple-element.72), channel_id=1, source_target_pairs={{0,4},{2,6},{4,0},{6,2},{1,5},{3,7},{5,1},{7,3},{8,12},{10,14},{12... | collective-permute-start | bytes 245768 | tf_op jit(solution)/shard_map/ppermute | solution.py:63
  41.5 0.7 %copy-start.5 = (bf16[4096]{0:T(1024)(128)(2,1)S(1)}, bf16[4096]{0:T(1024)(128)(2,1)}, u32[]{:S(2)}) copy-start(bf16[4096]{0:T(1024)(128)(2,1)} %param.11) | copy-start | bytes 24580
  41.9 1.3 %collective-permute-start.16 = (f32[128,128]{1,0:T(8,128)S(1)}, f32[128,128]{1,0:T(8,128)S(1)}, u32[]{:S(2)}, u32[]{:S(2)}) collective-permute-start(f32[128,128]{1,0:T(8,128)S(1)} %get-tuple-element.76.refs_4_), channel_id=1, source_target_pairs={{0,1},{1,0},{2,3},{3,2},{4,5},{5,4},{6,7},{7,6},{8,9},{9,8},{10,11... | collective-permute-start | bytes 196616 | tf_op jit(solution)/shard_map/ppermute | solution.py:405

commit v11 on v10

--- a/solution.py
+++ b/solution.py
@@ -387,11 +387,12 @@
     pieces = [(mine, 0, 0)]
     for t in range(1, n - 2):
         sent = attend(plan, asked[t], k, v, bias, send)
+        v_out, _ = lax.optimization_barrier((v, sent[0]))
         *sent, _ = lax.optimization_barrier((*sent, arrived[1 % len(arrived)]))
         got = plan.regroup(sent)
         placed, total = place(plan, got, places, (block,), sums=(total,))
         pieces.append((placed, t, 0))
-        k, v = lax.ppermute(k, "pipe", forward), lax.ppermute(v, "pipe", forward)
+        k, v = lax.ppermute(k, "pipe", forward), lax.ppermute(v_out, "pipe", forward)
     weights, spread, inverses = weigh(plan, asked[n - 2], k, bias, borrowed)
     met = inverses
     if plan.tensor == 2:

time: 44.6 us -> 44.6 us (level)
  no operation moved by 1% of the time
where the time goes in v11:
time: 44.6 us; the launch traced here: 44.4 us
  starting transfers between devices  21.3 us (48%)
  waiting for transfers between devices  13.5 us (30%)
  Pallas kernels  6.39 us (14%)
  local copies, waits for them, and re-layouts  3.03 us (7%)
    ppermute x9, starting transfers between devices, regroup(): lax.ppermute(part, 'dp', [(g, g ^ step) for g in range(self.groups)])  11.4 us
    ppermute x9, waiting for transfers between devices, regroup(): lax.ppermute(part, 'dp', [(g, g ^ step) for g in range(self.groups)])  5.69 us
    ppermute x1, waiting for transfers between devices, body(): lax.ppermute(keys, 'pipe', forward)  4.24 us
    ppermute x1, starting transfers between devices, body(): lax.ppermute(keys, 'pipe', forward)  3.02 us
    ppermute x1, starting transfers between devices, body(): lent = lax.ppermute(ahead, 'pipe', forward)  2.64 us
    unnamed x12, local copies, waits for them, and re-layouts  2.02 us
    pallas_call x3, Pallas kernels, place(): pl.pallas_call(functools.partial(place_kernel, plan, widths, summed, len(...  1.49 us
    pallas_call x2, Pallas kernels, attend(): pl.pallas_call(functools.partial(attend_kernel, plan, len(bases)), out_sh...  1.47 us
  transfers between devices with their start and end apart: 17, of which 11 were waited for; matrix products, arithmetic and copies ran while one was open for 2% of the time, Pallas kernels for 11%

profile of v11, /device:TPU:0, one launch (start us, length us, event | category | flops | bytes accessed | tf_op | source)
XLA Modules:
  0.0 44.4 jit_solution(13459409194915754069)
XLA Ops:
  0.0 3.0 %collective-permute-start.4 = (bf16[128,1024]{1,0:T(8,128)(2,1)}, bf16[128,1024]{1,0:T(8,128)(2,1)S(1)}, u32[]{:S(2)}, u32[]{:S(2)}) collective-permute-start(bf16[128,1024]{1,0:T(8,128)(2,1)} %bitcast.8), channel_id=1, source_target_pairs={{0,8},{8,24},{24,16},{16,0},{1,9},{9,25},{25,17},{17,1},{2,10},{10... | collective-permute-start | bytes 786440 | tf_op jit(solution)/shard_map/ppermute | solution.py:382
  3.0 0.0 copy-start.2
  3.0 1.0 %dynamic-slice_bitcast_fusion = bf16[128,1024]{1,0:T(8,128)(2,1)S(1)} fusion(bf16[1,128,4096]{2,1,0:T(8,128)(2,1)} %param.6, s32[]{:T(128)S(6)} %select_n.16), kind=kLoop, calls=%fused_computation | loop fusion | bytes 524292 | tf_op jit(solution)/shard_map/dynamic_slice | solution.py:379
  4.0 2.6 %collective-permute-start = (bf16[128,1024]{1,0:T(8,128)(2,1)S(1)}, bf16[128,1024]{1,0:T(8,128)(2,1)S(1)}, u32[]{:S(2)}, u32[]{:S(2)}) collective-permute-start(bf16[128,1024]{1,0:T(8,128)(2,1)S(1)} %dynamic-slice_bitcast_fusion), channel_id=1, source_target_pairs={{0,8},{8,24},{24,16},{16,0},{1,9},{9,25},{25,17},{17,1},{2,10},{10... | collective-permute-start | bytes 786440 | tf_op jit(solution)/shard_map/ppermute | solution.py:383
  6.7 0.0 copy-done.2
  6.7 0.4 %collective-permute-start.5 = (bf16[128,1024]{1,0:T(8,128)(2,1)S(1)}, bf16[128,1024]{1,0:T(8,128)(2,1)S(1)}, u32[]{:S(2)}, u32[]{:S(2)}) collective-permute-start(bf16[128,1024]{1,0:T(8,128)(2,1)S(1)} %bitcast.11), channel_id=1, source_target_pairs={{0,8},{8,24},{24,16},{16,0},{1,9},{9,25},{25,17},{17,1},{2,10},{10... | collective-permute-start | bytes 786440 | tf_op jit(solution)/shard_map/ppermute | solution.py:382
  7.1 4.2 %collective-permute-done.4.k_ref = bf16[128,1024]{1,0:T(8,128)(2,1)S(1)} collective-permute-done((bf16[128,1024]{1,0:T(8,128)(2,1)}, bf16[128,1024]{1,0:T(8,128)(2,1)S(1)}, u32[]{:S(2)}, u32[]{:S(2)}) %collective-permute-start.4) | collective-permute-done | bytes 262176 | tf_op jit(solution)/shard_map/ppermute | solution.py:382
  11.4 1.3 %collective-permute-start.9 = (bf16[128,1024]{1,0:T(8,128)(2,1)S(1)}, bf16[128,1024]{1,0:T(8,128)(2,1)S(1)}, u32[]{:S(2)}, u32[]{:S(2)}) collective-permute-start(bf16[128,1024]{1,0:T(8,128)(2,1)S(1)} %collective-permute-done.4.k_ref), channel_id=1, source_target_pairs={{0,8},{8,24},{24,16},{16,0},{1,9},{9,25},{25,17},{17,1},{2,10},{10... | collective-permute-start | bytes 786440 | tf_op jit(solution)/shard_map/ppermute | solution.py:395
  12.6 0.0 copy-start
  12.6 1.2 %copy-done = bf16[1,128,4096]{2,1,0:T(8,128)(2,1)S(1)} copy-done((bf16[1,128,4096]{2,1,0:T(8,128)(2,1)S(1)}, bf16[1,128,4096]{2,1,0:T(8,128)(2,1)}, u32[]{:S(2)}) %copy-start) | copy-done | bytes 1048600
  13.9 0.0 copy-start.3
  13.9 0.0 copy-start.4
  13.9 0.0 copy-start.1
  13.9 0.1 split.1
  14.0 0.6 %copy-done.3 = s32[4,4]{1,0:T(4,128)S(1)} copy-done((s32[4,4]{1,0:T(4,128)S(1)}, s32[4,4]{1,0:T(4,128)}, u32[]{:S(2)}) %copy-start.3) | copy-done | bytes 88
  14.5 0.0 copy-done.4
  14.6 0.7 %tables.1 = (f32[128,128]{1,0:T(8,128)S(1)}, bf16[160,128]{1,0:T(8,128)(2,1)S(1)}, bf16[128,40]{1,0:T(8,128)(2,1)S(1)}, bf16[128,40]{1,0:T(8,128)(2,1)S(1)}, bf1...) custom-call(s32[1,6]{1,0:T(1,128)S(1)} %copy-done.4, s32[4,4]{1,0:T(4,128)S(1)} %copy-done.3), custom_call_target="tpu_custom_call" | custom-call | flops 1 | bytes 1 | tf_op jit(solution)/shard_map/tables/pallas_call | solution.py:136
  15.2 0.0 copy-done.1
  15.2 0.5 %heads.1.refs_0_ = bf16[1024,128]{1,0:T(8,128)(2,1)S(1)} custom-call(bf16[128,1024]{1,0:T(8,128)(2,1)S(1)} %get-tuple-element.44.q_ref, bf16[128,1024]{1,0:T(8,128)(2,1)S(1)} %bitcast.9, bf16[128,1024]{1,0:T(8,128)(2,1)S(1)} %bitcast.12, f32[128,128]{1,0:T(8,128)S(1)} %get-tuple-element.42.bias), custom_call_target="tpu_custom_call" | custom-call | flops 1 | bytes 1 | tf_op jit(solution)/shard_map/heads/pallas_call | solution.py:190
  15.8 1.2 %collective-permute-done.q_ref = bf16[128,1024]{1,0:T(8,128)(2,1)S(1)} collective-permute-done((bf16[128,1024]{1,0:T(8,128)(2,1)S(1)}, bf16[128,1024]{1,0:T(8,128)(2,1)S(1)}, u32[]{:S(2)}, u32[]{:S(2)}) %collective-permute-start) | collective-permute-done | bytes 262176 | tf_op jit(solution)/shard_map/ppermute | solution.py:383
  17.0 0.7 %attend.2 = (bf16[40,2048]{1,0:T(8,128)(2,1)S(1)}, bf16[40,2048]{1,0:T(8,128)(2,1)S(1)}, bf16[40,2048]{1,0:T(8,128)(2,1)S(1)}, bf16[40,2048]{1,0:T(8,128)(2,1)S(1)}) custom-call(bf16[128,1024]{1,0:T(8,128)(2,1)S(1)} %collective-permute-done.q_ref, bf16[128,1024]{1,0:T(8,128)(2,1)S(1)} %bitcast.10, bf16[128,1024]{1,0:T(8,128)(2,1)S(1)} %bitcast.13, ...), custom_call_target="tpu_custom_call" | custom-call | flops 1 | bytes 1 | tf_op jit(solution)/shard_map/attend/pallas_call | solution.py:214
  17.7 2.9 %collective-permute-start.1 = (bf16[40,2048]{1,0:T(8,128)(2,1)S(1)}, bf16[40,2048]{1,0:T(8,128)(2,1)S(1)}, u32[]{:S(2)}, u32[]{:S(2)}) collective-permute-start(bf16[40,2048]{1,0:T(8,128)(2,1)S(1)} %get-tuple-element.46), channel_id=1, source_target_pairs={{0,6},{2,4},{4,2},{6,0},{1,7},{3,5},{5,3},{7,1},{8,14},{10,12},{12... | collective-permute-start | bytes 491528 | tf_op jit(solution)/shard_map/ppermute | solution.py:63
  20.6 0.5 %collective-permute-start.2 = (bf16[40,2048]{1,0:T(8,128)(2,1)S(1)}, bf16[40,2048]{1,0:T(8,128)(2,1)S(1)}, u32[]{:S(2)}, u32[]{:S(2)}) collective-permute-start(bf16[40,2048]{1,0:T(8,128)(2,1)S(1)} %get-tuple-element.47), channel_id=1, source_target_pairs={{0,2},{2,0},{4,6},{6,4},{1,3},{3,1},{5,7},{7,5},{8,10},{10,8},{12,... | collective-permute-start | bytes 491528 | tf_op jit(solution)/shard_map/ppermute | solution.py:63
  21.2 0.1 collective-permute-start.3
  21.3 1.3 %collective-permute-done.5.v_ref = bf16[128,1024]{1,0:T(8,128)(2,1)S(1)} collective-permute-done((bf16[128,1024]{1,0:T(8,128)(2,1)S(1)}, bf16[128,1024]{1,0:T(8,128)(2,1)S(1)}, u32[]{:S(2)}, u32[]{:S(2)}) %collective-permute-start.5) | collective-permute-done | bytes 262176 | tf_op jit(solution)/shard_map/ppermute | solution.py:382
  22.6 0.7 %attend.3 = (bf16[40,1024]{1,0:T(8,128)(2,1)S(1)}, bf16[40,1024]{1,0:T(8,128)(2,1)S(1)}, bf16[40,1024]{1,0:T(8,128)(2,1)S(1)}, bf16[40,1024]{1,0:T(8,128)(2,1)S(1)}) custom-call(bf16[128,1024]{1,0:T(8,128)(2,1)S(1)} %get-tuple-element.54.q_ref, bf16[128,1024]{1,0:T(8,128)(2,1)S(1)} %collective-permute-done.4.k_ref, ...), custom_call_target="tpu_custom_call" | custom-call | flops 1 | bytes 1 | tf_op jit(solution)/shard_map/attend/pallas_call | solution.py:214
  23.4 1.2 %collective-permute-start.10 = (bf16[128,1024]{1,0:T(8,128)(2,1)S(1)}, bf16[128,1024]{1,0:T(8,128)(2,1)S(1)}, u32[]{:S(2)}, u32[]{:S(2)}) collective-permute-start(bf16[128,1024]{1,0:T(8,128)(2,1)S(1)} %collective-permute-done.5.v_ref), channel_id=1, source_target_pairs={{0,8},{8,24},{24,16},{16,0},{1,9},{9,25},{25,17},{17,1},{2,10},{10... | collective-permute-start | bytes 786440 | tf_op jit(solution)/shard_map/ppermute | solution.py:395
  24.6 0.5 %collective-permute-done.1.refs_1_ = bf16[40,2048]{1,0:T(8,128)(2,1)S(1)} collective-permute-done((bf16[40,2048]{1,0:T(8,128)(2,1)S(1)}, bf16[40,2048]{1,0:T(8,128)(2,1)S(1)}, u32[]{:S(2)}, u32[]{:S(2)}) %collective-permute-start.1) | collective-permute-done | bytes 163872 | tf_op jit(solution)/shard_map/ppermute | solution.py:63
  25.0 2.3 %collective-permute-start.6 = (bf16[40,1024]{1,0:T(8,128)(2,1)S(1)}, bf16[40,1024]{1,0:T(8,128)(2,1)S(1)}, u32[]{:S(2)}, u32[]{:S(2)}) collective-permute-start(bf16[40,1024]{1,0:T(8,128)(2,1)S(1)} %get-tuple-element.60), channel_id=1, source_target_pairs={{0,6},{2,4},{4,2},{6,0},{1,7},{3,5},{5,3},{7,1},{8,14},{10,12},{12... | collective-permute-start | bytes 245768 | tf_op jit(solution)/shard_map/ppermute | solution.py:63
  27.3 0.1 collective-permute-done.2.refs_2_
  27.4 1.5 %collective-permute-start.7 = (bf16[40,1024]{1,0:T(8,128)(2,1)S(1)}, bf16[40,1024]{1,0:T(8,128)(2,1)S(1)}, u32[]{:S(2)}, u32[]{:S(2)}) collective-permute-start(bf16[40,1024]{1,0:T(8,128)(2,1)S(1)} %get-tuple-element.61), channel_id=1, source_target_pairs={{0,2},{2,0},{4,6},{6,4},{1,3},{3,1},{5,7},{7,5},{8,10},{10,8},{12,... | collective-permute-start | bytes 245768 | tf_op jit(solution)/shard_map/ppermute | solution.py:63
  28.9 0.0 collective-permute-done.3.refs_3_
  28.9 0.5 %collective-permute-start.8 = (bf16[40,1024]{1,0:T(8,128)(2,1)S(1)}, bf16[40,1024]{1,0:T(8,128)(2,1)S(1)}, u32[]{:S(2)}, u32[]{:S(2)}) collective-permute-start(bf16[40,1024]{1,0:T(8,128)(2,1)S(1)} %get-tuple-element.62), channel_id=1, source_target_pairs={{0,4},{2,6},{4,0},{6,2},{1,5},{3,7},{5,1},{7,3},{8,12},{10,14},{12... | collective-permute-start | bytes 245768 | tf_op jit(solution)/shard_map/ppermute | solution.py:63
  29.4 0.7 %place.3 = (bf16[128,1024]{1,0:T(8,128)(2,1)S(1)}, bf16[128,1024]{1,0:T(8,128)(2,1)S(1)}, f32[128,128]{1,0:T(8,128)S(1)}) custom-call(bf16[40,2048]{1,0:T(8,128)(2,1)S(1)} %get-tuple-element.45.refs_0_, bf16[40,2048]{1,0:T(8,128)(2,1)S(1)} %collective-permute-done.1.refs_1_, bf16[40,2048]{1,0:T(8,128)(2,1)S(1)} %collective-permute-done.2.refs_2_, ...), custom_call_target="tpu_custom_call" | custom-call | flops 1 | bytes 1 | tf_op jit(solution)/shard_map/place/pallas_call | solution.py:313
  30.1 0.0 collective-permute-done.9.k_ref
  30.1 0.6 %weigh.1 = (bf16[128,1024]{1,0:T(8,128)(2,1)S(1)}, f32[128,1024]{1,0:T(8,128)S(1)}, f32[8,128]{1,0:T(8,128)S(1)}) custom-call(bf16[128,1024]{1,0:T(8,128)(2,1)S(1)} %get-tuple-element.65.q_ref, bf16[128,1024]{1,0:T(8,128)(2,1)S(1)} %collective-permute-done.9.k_ref, f32[128,128]{1,0:T(8,128)S(1)} %get-tuple-element.42.bias, ...), custom_call_target="tpu_custom_call" | custom-call | flops 1 | bytes 1 | tf_op jit(solution)/shard_map/weigh/pallas_call | solution.py:236
  30.7 0.1 collective-permute-start.11
  30.8 0.0 collective-permute-done.6.refs_1_
  30.8 1.1 %collective-permute-done.7.refs_2_ = bf16[40,1024]{1,0:T(8,128)(2,1)S(1)} collective-permute-done((bf16[40,1024]{1,0:T(8,128)(2,1)S(1)}, bf16[40,1024]{1,0:T(8,128)(2,1)S(1)}, u32[]{:S(2)}, u32[]{:S(2)}) %collective-permute-start.7) | collective-permute-done | bytes 81952 | tf_op jit(solution)/shard_map/ppermute | solution.py:63
  31.9 1.5 %collective-permute-done.8.refs_3_ = bf16[40,1024]{1,0:T(8,128)(2,1)S(1)} collective-permute-done((bf16[40,1024]{1,0:T(8,128)(2,1)S(1)}, bf16[40,1024]{1,0:T(8,128)(2,1)S(1)}, u32[]{:S(2)}, u32[]{:S(2)}) %collective-permute-start.8) | collective-permute-done | bytes 81952 | tf_op jit(solution)/shard_map/ppermute | solution.py:63
  33.4 0.0 collective-permute-done.11._
  33.4 1.2 %collective-permute-start.15 = (bf16[128,1024]{1,0:T(8,128)(2,1)S(1)}, bf16[128,1024]{1,0:T(8,128)(2,1)S(1)}, u32[]{:S(2)}, u32[]{:S(2)}) collective-permute-start(bf16[128,1024]{1,0:T(8,128)(2,1)S(1)} %get-tuple-element.75._), channel_id=1, source_target_pairs={{8,0},{24,8},{16,24},{0,16},{9,1},{25,9},{17,25},{1,17},{10,2},{26... | collective-permute-start | bytes 786440 | tf_op jit(solution)/shard_map/ppermute | solution.py:401
  34.6 0.0 collective-permute-done.10.v_ref
  34.6 0.4 finish.1
  35.0 1.5 %collective-permute-start.12 = (bf16[40,1024]{1,0:T(8,128)(2,1)S(1)}, bf16[40,1024]{1,0:T(8,128)(2,1)S(1)}, u32[]{:S(2)}, u32[]{:S(2)}) collective-permute-start(bf16[40,1024]{1,0:T(8,128)(2,1)S(1)} %get-tuple-element.72), channel_id=1, source_target_pairs={{0,6},{2,4},{4,2},{6,0},{1,7},{3,5},{5,3},{7,1},{8,14},{10,12},{12... | collective-permute-start | bytes 245768 | tf_op jit(solution)/shard_map/ppermute | solution.py:63
  36.5 0.5 %collective-permute-start.13 = (bf16[40,1024]{1,0:T(8,128)(2,1)S(1)}, bf16[40,1024]{1,0:T(8,128)(2,1)S(1)}, u32[]{:S(2)}, u32[]{:S(2)}) collective-permute-start(bf16[40,1024]{1,0:T(8,128)(2,1)S(1)} %get-tuple-element.73), channel_id=1, source_target_pairs={{0,2},{2,0},{4,6},{6,4},{1,3},{3,1},{5,7},{7,5},{8,10},{10,8},{12,... | collective-permute-start | bytes 245768 | tf_op jit(solution)/shard_map/ppermute | solution.py:63
  37.0 1.5 %collective-permute-start.14 = (bf16[40,1024]{1,0:T(8,128)(2,1)S(1)}, bf16[40,1024]{1,0:T(8,128)(2,1)S(1)}, u32[]{:S(2)}, u32[]{:S(2)}) collective-permute-start(bf16[40,1024]{1,0:T(8,128)(2,1)S(1)} %get-tuple-element.74), channel_id=1, source_target_pairs={{0,4},{2,6},{4,0},{6,2},{1,5},{3,7},{5,1},{7,3},{8,12},{10,14},{12... | collective-permute-start | bytes 245768 | tf_op jit(solution)/shard_map/ppermute | solution.py:63
  38.6 0.4 place.4
  39.0 1.4 %collective-permute-done.12.refs_1_ = bf16[40,1024]{1,0:T(8,128)(2,1)S(1)} collective-permute-done((bf16[40,1024]{1,0:T(8,128)(2,1)S(1)}, bf16[40,1024]{1,0:T(8,128)(2,1)S(1)}, u32[]{:S(2)}, u32[]{:S(2)}) %collective-permute-start.12) | collective-permute-done | bytes 81952 | tf_op jit(solution)/shard_map/ppermute | solution.py:63
  40.4 0.6 %collective-permute-done.13.refs_2_ = bf16[40,1024]{1,0:T(8,128)(2,1)S(1)} collective-permute-done((bf16[40,1024]{1,0:T(8,128)(2,1)S(1)}, bf16[40,1024]{1,0:T(8,128)(2,1)S(1)}, u32[]{:S(2)}, u32[]{:S(2)}) %collective-permute-start.13) | collective-permute-done | bytes 81952 | tf_op jit(solution)/shard_map/ppermute | solution.py:63
  41.0 0.5 %collective-permute-done.14.refs_3_ = bf16[40,1024]{1,0:T(8,128)(2,1)S(1)} collective-permute-done((bf16[40,1024]{1,0:T(8,128)(2,1)S(1)}, bf16[40,1024]{1,0:T(8,128)(2,1)S(1)}, u32[]{:S(2)}, u32[]{:S(2)}) %collective-permute-start.14) | collective-permute-done | bytes 81952 | tf_op jit(solution)/shard_map/ppermute | solution.py:63
  41.5 0.0 collective-permute-done.15.refs_8_.refs_3_
  41.5 0.0 copy-start.5
  41.5 0.4 place.5
  41.9 0.1 collective-permute-start.16
  42.0 0.2 copy-done.5
  42.2 1.0 %collective-permute-done.16.refs_5_ = f32[128,128]{1,0:T(8,128)S(1)} collective-permute-done((f32[128,128]{1,0:T(8,128)S(1)}, f32[128,128]{1,0:T(8,128)S(1)}, u32[]{:S(2)}, u32[]{:S(2)}) %collective-permute-start.16) | collective-permute-done | bytes 65568 | tf_op jit(solution)/shard_map/ppermute | solution.py:406
  43.2 1.2 %norm.1 = bf16[128,4096]{1,0:T(8,128)(2,1)} custom-call(bf16[128,1024]{1,0:T(8,128)(2,1)S(1)} %get-tuple-element.53.refs_0_, bf16[128,1024]{1,0:T(8,128)(2,1)S(1)} %get-tuple-element.64.refs_1_, bf16[128,1024]{1,0:T(8,128)(2,1)S(1)} %get-tuple-element.77.refs_2_, bf16[128,1024]{1,0:T(8,128)(2,1)S(1)} %collective-permute-done.15.refs_8_.refs_3_, ...), custom_call_target="tpu_custom_call" | custom-call | flops 1 | bytes 1 | tf_op jit(solution)/shard_map/norm/pallas_call | solution.py:354
  (1 shorter events, 0.0 us)
Async XLA Ops:
  0.0 11.4 %collective-permute-start.4 = (bf16[128,1024]{1,0:T(8,128)(2,1)}, bf16[128,1024]{1,0:T(8,128)(2,1)S(1)}, u32[]{:S(2)}, u32[]{:S(2)}) collective-permute-start(bf16[128,1024]{1,0:T(8,128)(2,1)} %bitcast.8), channel_id=1, source_target_pairs={{0,8},{8,24},{24,16},{16,0},{1,9},{9,25},{25,17},{17,1},{2,10},{10... | collective-permute-start | bytes 786440 | tf_op jit(solution)/shard_map/ppermute | solution.py:382
  3.0 3.7 %copy-start.2 = (bf16[128,1,1,1024]{3,0,2,1:T(8,128)(2,1)S(1)}, bf16[128,1,1,1024]{3,0,2,1:T(8,128)(2,1)}, u32[]{:S(2)}) copy-start(bf16[128,1,1,1024]{3,0,2,1:T(8,128)(2,1)} %param.8) | copy-start | bytes 786436
  4.0 13.0 %collective-permute-start = (bf16[128,1024]{1,0:T(8,128)(2,1)S(1)}, bf16[128,1024]{1,0:T(8,128)(2,1)S(1)}, u32[]{:S(2)}, u32[]{:S(2)}) collective-permute-start(bf16[128,1024]{1,0:T(8,128)(2,1)S(1)} %dynamic-slice_bitcast_fusion), channel_id=1, source_target_pairs={{0,8},{8,24},{24,16},{16,0},{1,9},{9,25},{25,17},{17,1},{2,10},{10... | collective-permute-start | bytes 786440 | tf_op jit(solution)/shard_map/ppermute | solution.py:383
  6.7 15.9 %collective-permute-start.5 = (bf16[128,1024]{1,0:T(8,128)(2,1)S(1)}, bf16[128,1024]{1,0:T(8,128)(2,1)S(1)}, u32[]{:S(2)}, u32[]{:S(2)}) collective-permute-start(bf16[128,1024]{1,0:T(8,128)(2,1)S(1)} %bitcast.11), channel_id=1, source_target_pairs={{0,8},{8,24},{24,16},{16,0},{1,9},{9,25},{25,17},{17,1},{2,10},{10... | collective-permute-start | bytes 786440 | tf_op jit(solution)/shard_map/ppermute | solution.py:382
  11.4 18.7 %collective-permute-start.9 = (bf16[128,1024]{1,0:T(8,128)(2,1)S(1)}, bf16[128,1024]{1,0:T(8,128)(2,1)S(1)}, u32[]{:S(2)}, u32[]{:S(2)}) collective-permute-start(bf16[128,1024]{1,0:T(8,128)(2,1)S(1)} %collective-permute-done.4.k_ref), channel_id=1, source_target_pairs={{0,8},{8,24},{24,16},{16,0},{1,9},{9,25},{25,17},{17,1},{2,10},{10... | collective-permute-start | bytes 786440 | tf_op jit(solution)/shard_map/ppermute | solution.py:395
  12.6 1.2 %copy-start = (bf16[1,128,4096]{2,1,0:T(8,128)(2,1)S(1)}, bf16[1,128,4096]{2,1,0:T(8,128)(2,1)}, u32[]{:S(2)}) copy-start(bf16[1,128,4096]{2,1,0:T(8,128)(2,1)} %param.6) | copy-start | bytes 3145732
  13.9 0.7 %copy-start.3 = (s32[4,4]{1,0:T(4,128)S(1)}, s32[4,4]{1,0:T(4,128)}, u32[]{:S(2)}) copy-start(s32[4,4]{1,0:T(4,128)} %counts.1) | copy-start | bytes 196
  13.9 0.7 %copy-start.4 = (s32[1,6]{1,0:T(1,128)S(1)}, s32[1,6]{1,0:T(1,128)}, u32[]{:S(2)}) copy-start(s32[1,6]{1,0:T(1,128)} %docs.1) | copy-start | bytes 76
  13.9 1.4 %copy-start.1 = (bf16[128,1,1,1024]{3,0,2,1:T(8,128)(2,1)S(1)}, bf16[128,1,1,1024]{3,0,2,1:T(8,128)(2,1)}, u32[]{:S(2)}) copy-start(bf16[128,1,1,1024]{3,0,2,1:T(8,128)(2,1)} %param.7) | copy-start | bytes 786436
  17.7 7.3 %collective-permute-start.1 = (bf16[40,2048]{1,0:T(8,128)(2,1)S(1)}, bf16[40,2048]{1,0:T(8,128)(2,1)S(1)}, u32[]{:S(2)}, u32[]{:S(2)}) collective-permute-start(bf16[40,2048]{1,0:T(8,128)(2,1)S(1)} %get-tuple-element.46), channel_id=1, source_target_pairs={{0,6},{2,4},{4,2},{6,0},{1,7},{3,5},{5,3},{7,1},{8,14},{10,12},{12... | collective-permute-start | bytes 491528 | tf_op jit(solution)/shard_map/ppermute | solution.py:63
  20.6 6.8 %collective-permute-start.2 = (bf16[40,2048]{1,0:T(8,128)(2,1)S(1)}, bf16[40,2048]{1,0:T(8,128)(2,1)S(1)}, u32[]{:S(2)}, u32[]{:S(2)}) collective-permute-start(bf16[40,2048]{1,0:T(8,128)(2,1)S(1)} %get-tuple-element.47), channel_id=1, source_target_pairs={{0,2},{2,0},{4,6},{6,4},{1,3},{3,1},{5,7},{7,5},{8,10},{10,8},{12,... | collective-permute-start | bytes 491528 | tf_op jit(solution)/shard_map/ppermute | solution.py:63
  21.2 7.7 %collective-permute-start.3 = (bf16[40,2048]{1,0:T(8,128)(2,1)S(1)}, bf16[40,2048]{1,0:T(8,128)(2,1)S(1)}, u32[]{:S(2)}, u32[]{:S(2)}) collective-permute-start(bf16[40,2048]{1,0:T(8,128)(2,1)S(1)} %get-tuple-element.48), channel_id=1, source_target_pairs={{0,4},{2,6},{4,0},{6,2},{1,5},{3,7},{5,1},{7,3},{8,12},{10,14},{12... | collective-permute-start | bytes 491528 | tf_op jit(solution)/shard_map/ppermute | solution.py:63
  23.4 11.2 %collective-permute-start.10 = (bf16[128,1024]{1,0:T(8,128)(2,1)S(1)}, bf16[128,1024]{1,0:T(8,128)(2,1)S(1)}, u32[]{:S(2)}, u32[]{:S(2)}) collective-permute-start(bf16[128,1024]{1,0:T(8,128)(2,1)S(1)} %collective-permute-done.5.v_ref), channel_id=1, source_target_pairs={{0,8},{8,24},{24,16},{16,0},{1,9},{9,25},{25,17},{17,1},{2,10},{10... | collective-permute-start | bytes 786440 | tf_op jit(solution)/shard_map/ppermute | solution.py:395
  25.0 5.7 %collective-permute-start.6 = (bf16[40,1024]{1,0:T(8,128)(2,1)S(1)}, bf16[40,1024]{1,0:T(8,128)(2,1)S(1)}, u32[]{:S(2)}, u32[]{:S(2)}) collective-permute-start(bf16[40,1024]{1,0:T(8,128)(2,1)S(1)} %get-tuple-element.60), channel_id=1, source_target_pairs={{0,6},{2,4},{4,2},{6,0},{1,7},{3,5},{5,3},{7,1},{8,14},{10,12},{12... | collective-permute-start | bytes 245768 | tf_op jit(solution)/shard_map/ppermute | solution.py:63
  27.4 4.4 %collective-permute-start.7 = (bf16[40,1024]{1,0:T(8,128)(2,1)S(1)}, bf16[40,1024]{1,0:T(8,128)(2,1)S(1)}, u32[]{:S(2)}, u32[]{:S(2)}) collective-permute-start(bf16[40,1024]{1,0:T(8,128)(2,1)S(1)} %get-tuple-element.61), channel_id=1, source_target_pairs={{0,2},{2,0},{4,6},{6,4},{1,3},{3,1},{5,7},{7,5},{8,10},{10,8},{12,... | collective-permute-start | bytes 245768 | tf_op jit(solution)/shard_map/ppermute | solution.py:63
  28.9 4.4 %collective-permute-start.8 = (bf16[40,1024]{1,0:T(8,128)(2,1)S(1)}, bf16[40,1024]{1,0:T(8,128)(2,1)S(1)}, u32[]{:S(2)}, u32[]{:S(2)}) collective-permute-start(bf16[40,1024]{1,0:T(8,128)(2,1)S(1)} %get-tuple-element.62), channel_id=1, source_target_pairs={{0,4},{2,6},{4,0},{6,2},{1,5},{3,7},{5,1},{7,3},{8,12},{10,14},{12... | collective-permute-start | bytes 245768 | tf_op jit(solution)/shard_map/ppermute | solution.py:63
  30.7 2.7 %collective-permute-start.11 = (f32[8,128]{1,0:T(8,128)S(1)}, f32[8,128]{1,0:T(8,128)S(1)}, u32[]{:S(2)}, u32[]{:S(2)}) collective-permute-start(f32[8,128]{1,0:T(8,128)S(1)} %get-tuple-element.70), channel_id=1, source_target_pairs={{0,1},{1,0},{2,3},{3,2},{4,5},{5,4},{6,7},{7,6},{8,9},{9,8},{10,11... | collective-permute-start | bytes 12296 | tf_op jit(solution)/shard_map/ppermute | solution.py:399
  33.4 8.1 %collective-permute-start.15 = (bf16[128,1024]{1,0:T(8,128)(2,1)S(1)}, bf16[128,1024]{1,0:T(8,128)(2,1)S(1)}, u32[]{:S(2)}, u32[]{:S(2)}) collective-permute-start(bf16[128,1024]{1,0:T(8,128)(2,1)S(1)} %get-tuple-element.75._), channel_id=1, source_target_pairs={{8,0},{24,8},{16,24},{0,16},{9,1},{25,9},{17,25},{1,17},{10,2},{26... | collective-permute-start | bytes 786440 | tf_op jit(solution)/shard_map/ppermute | solution.py:401
  35.0 5.4 %collective-permute-start.12 = (bf16[40,1024]{1,0:T(8,128)(2,1)S(1)}, bf16[40,1024]{1,0:T(8,128)(2,1)S(1)}, u32[]{:S(2)}, u32[]{:S(2)}) collective-permute-start(bf16[40,1024]{1,0:T(8,128)(2,1)S(1)} %get-tuple-element.72), channel_id=1, source_target_pairs={{0,6},{2,4},{4,2},{6,0},{1,7},{3,5},{5,3},{7,1},{8,14},{10,12},{12... | collective-permute-start | bytes 245768 | tf_op jit(solution)/shard_map/ppermute | solution.py:63
  36.5 4.4 %collective-permute-start.13 = (bf16[40,1024]{1,0:T(8,128)(2,1)S(1)}, bf16[40,1024]{1,0:T(8,128)(2,1)S(1)}, u32[]{:S(2)}, u32[]{:S(2)}) collective-permute-start(bf16[40,1024]{1,0:T(8,128)(2,1)S(1)} %get-tuple-element.73), channel_id=1, source_target_pairs={{0,2},{2,0},{4,6},{6,4},{1,3},{3,1},{5,7},{7,5},{8,10},{10,8},{12,... | collective-permute-start | bytes 245768 | tf_op jit(solution)/shard_map/ppermute | solution.py:63
  37.0 4.4 %collective-permute-start.14 = (bf16[40,1024]{1,0:T(8,128)(2,1)S(1)}, bf16[40,1024]{1,0:T(8,128)(2,1)S(1)}, u32[]{:S(2)}, u32[]{:S(2)}) collective-permute-start(bf16[40,1024]{1,0:T(8,128)(2,1)S(1)} %get-tuple-element.74), channel_id=1, source_target_pairs={{0,4},{2,6},{4,0},{6,2},{1,5},{3,7},{5,1},{7,3},{8,12},{10,14},{12... | collective-permute-start | bytes 245768 | tf_op jit(solution)/shard_map/ppermute | solution.py:63
  41.5 0.7 %copy-start.5 = (bf16[4096]{0:T(1024)(128)(2,1)S(1)}, bf16[4096]{0:T(1024)(128)(2,1)}, u32[]{:S(2)}) copy-start(bf16[4096]{0:T(1024)(128)(2,1)} %param.11) | copy-start | bytes 24580
  41.9 1.3 %collective-permute-start.16 = (f32[128,128]{1,0:T(8,128)S(1)}, f32[128,128]{1,0:T(8,128)S(1)}, u32[]{:S(2)}, u32[]{:S(2)}) collective-permute-start(f32[128,128]{1,0:T(8,128)S(1)} %get-tuple-element.78.refs_4_), channel_id=1, source_target_pairs={{0,1},{1,0},{2,3},{3,2},{4,5},{5,4},{6,7},{7,6},{8,9},{9,8},{10,11... | collective-permute-start | bytes 196616 | tf_op jit(solution)/shard_map/ppermute | solution.py:406

commit v12 on v11

--- a/solution.py
+++ b/solution.py
@@ -321,6 +321,33 @@
     )(*args)
 
 
+def sums_kernel(plan, *refs):
+    parts = plan.parts
+    got, matrices, (block, earlier, out) = refs[:parts], refs[parts : 2 * parts], refs[2 * parts :]
+    total = squares_of(block) + earlier[...]
+    for matrix, ref in zip(matrices, got, strict=True):
+        total = total + jnp.dot(
+            matrix[...].astype(jnp.float32),
+            squares_of(ref),
+            preferred_element_type=jnp.float32,
+            precision=lax.Precision.HIGHEST,
+        )
+    out[...] = total
+
+
+def sums_of(plan, got, matrices, block, earlier):
+    args = (*got, *matrices, block, earlier)
+    return pl.pallas_call(
+        functools.partial(sums_kernel, plan),
+        out_shape=jax.ShapeDtypeStruct((plan.seq, HEAD_DIM), jnp.float32),
+        in_specs=[VMEM] * len(args),
+        out_specs=VMEM,
+        compiler_params=PARAMS,
+        cost_estimate=COST,
+        name="sums",
+    )(*args)
+
+
 def norm_kernel(plan, spots, sums, *refs):
     count = len(spots)
     pieces, refs = refs[:count], refs[count:]
@@ -400,7 +427,8 @@
     borrowed, *_ = lax.optimization_barrier((borrowed, met, *got))
     returned = lax.ppermute(borrowed, "pipe", backward)
     got = plan.regroup(finish(plan, weights, spread, v, send, met))
-    placed, total = place(plan, got, places, (block,), blocks=(returned,), sums=(total,))
+    total = sums_of(plan, got, places, returned, total)
+    (placed,) = place(plan, got, places, (block,), summed=0)
     pieces += [(placed, n - 2, 0), (returned, n - 1, 0)]
     if plan.tensor == 2:
         sums = (total, lax.ppermute(total, "tensor", [(0, 1), (1, 0)]))

time: 44.6 us -> 44.6 us (level)
  transfers between devices with their start and end apart: 17 -> 17, of which waited for: 11 -> 11; matrix products, arithmetic and copies ran while one was open for 2% -> 2% of each run, Pallas kernels for 11% -> 12%
where the time goes in v12:
time: 44.6 us; the launch traced here: 44.4 us
  starting transfers between devices  21.3 us (48%)
  waiting for transfers between devices  13.1 us (29%)
  Pallas kernels  6.75 us (15%)
  local copies, waits for them, and re-layouts  3.06 us (7%)
    ppermute x9, starting transfers between devices, regroup(): lax.ppermute(part, 'dp', [(g, g ^ step) for g in range(self.groups)])  11.4 us
    ppermute x9, waiting for transfers between devices, regroup(): lax.ppermute(part, 'dp', [(g, g ^ step) for g in range(self.groups)])  5.69 us
    ppermute x1, waiting for transfers between devices, body(): lax.ppermute(keys, 'pipe', forward)  4.24 us
    ppermute x1, starting transfers between devices, body(): lax.ppermute(keys, 'pipe', forward)  3.02 us
    ppermute x1, starting transfers between devices, body(): lent = lax.ppermute(ahead, 'pipe', forward)  2.64 us
    unnamed x12, local copies, waits for them, and re-layouts  2.05 us
    pallas_call x3, Pallas kernels, place(): pl.pallas_call(functools.partial(place_kernel, plan, widths, summed, len(...  1.48 us
    pallas_call x2, Pallas kernels, attend(): pl.pallas_call(functools.partial(attend_kernel, plan, len(bases)), out_sh...  1.47 us
  transfers between devices with their start and end apart: 17, of which 11 were waited for; matrix products, arithmetic and copies ran while one was open for 2% of the time, Pallas kernels for 12%

profile of v12, /device:TPU:0, one launch (start us, length us, event | category | flops | bytes accessed | tf_op | source)
XLA Modules:
  0.0 44.4 jit_solution(12928333146307781739)
XLA Ops:
  0.0 3.0 %collective-permute-start.4 = (bf16[128,1024]{1,0:T(8,128)(2,1)}, bf16[128,1024]{1,0:T(8,128)(2,1)S(1)}, u32[]{:S(2)}, u32[]{:S(2)}) collective-permute-start(bf16[128,1024]{1,0:T(8,128)(2,1)} %bitcast.8), channel_id=1, source_target_pairs={{0,8},{8,24},{24,16},{16,0},{1,9},{9,25},{25,17},{17,1},{2,10},{10... | collective-permute-start | bytes 786440 | tf_op jit(solution)/shard_map/ppermute | solution.py:409
  3.0 0.0 copy-start.2
  3.0 1.0 %dynamic-slice_bitcast_fusion = bf16[128,1024]{1,0:T(8,128)(2,1)S(1)} fusion(bf16[1,128,4096]{2,1,0:T(8,128)(2,1)} %param.6, s32[]{:T(128)S(6)} %select_n.16), kind=kLoop, calls=%fused_computation | loop fusion | bytes 524292 | tf_op jit(solution)/shard_map/dynamic_slice | solution.py:406
  4.0 2.6 %collective-permute-start = (bf16[128,1024]{1,0:T(8,128)(2,1)S(1)}, bf16[128,1024]{1,0:T(8,128)(2,1)S(1)}, u32[]{:S(2)}, u32[]{:S(2)}) collective-permute-start(bf16[128,1024]{1,0:T(8,128)(2,1)S(1)} %dynamic-slice_bitcast_fusion), channel_id=1, source_target_pairs={{0,8},{8,24},{24,16},{16,0},{1,9},{9,25},{25,17},{17,1},{2,10},{10... | collective-permute-start | bytes 786440 | tf_op jit(solution)/shard_map/ppermute | solution.py:410
  6.7 0.0 copy-done.2
  6.7 0.4 %collective-permute-start.5 = (bf16[128,1024]{1,0:T(8,128)(2,1)S(1)}, bf16[128,1024]{1,0:T(8,128)(2,1)S(1)}, u32[]{:S(2)}, u32[]{:S(2)}) collective-permute-start(bf16[128,1024]{1,0:T(8,128)(2,1)S(1)} %bitcast.11), channel_id=1, source_target_pairs={{0,8},{8,24},{24,16},{16,0},{1,9},{9,25},{25,17},{17,1},{2,10},{10... | collective-permute-start | bytes 786440 | tf_op jit(solution)/shard_map/ppermute | solution.py:409
  7.1 4.2 %collective-permute-done.4.k_ref = bf16[128,1024]{1,0:T(8,128)(2,1)S(1)} collective-permute-done((bf16[128,1024]{1,0:T(8,128)(2,1)}, bf16[128,1024]{1,0:T(8,128)(2,1)S(1)}, u32[]{:S(2)}, u32[]{:S(2)}) %collective-permute-start.4) | collective-permute-done | bytes 262176 | tf_op jit(solution)/shard_map/ppermute | solution.py:409
  11.4 1.3 %collective-permute-start.9 = (bf16[128,1024]{1,0:T(8,128)(2,1)S(1)}, bf16[128,1024]{1,0:T(8,128)(2,1)S(1)}, u32[]{:S(2)}, u32[]{:S(2)}) collective-permute-start(bf16[128,1024]{1,0:T(8,128)(2,1)S(1)} %collective-permute-done.4.k_ref), channel_id=1, source_target_pairs={{0,8},{8,24},{24,16},{16,0},{1,9},{9,25},{25,17},{17,1},{2,10},{10... | collective-permute-start | bytes 786440 | tf_op jit(solution)/shard_map/ppermute | solution.py:422
  12.6 0.0 copy-start
  12.6 1.2 %copy-done = bf16[1,128,4096]{2,1,0:T(8,128)(2,1)S(1)} copy-done((bf16[1,128,4096]{2,1,0:T(8,128)(2,1)S(1)}, bf16[1,128,4096]{2,1,0:T(8,128)(2,1)}, u32[]{:S(2)}) %copy-start) | copy-done | bytes 1048600
  13.9 0.0 copy-start.3
  13.9 0.0 copy-start.4
  13.9 0.0 copy-start.1
  13.9 0.1 split.1
  14.0 0.6 %copy-done.3 = s32[4,4]{1,0:T(4,128)S(1)} copy-done((s32[4,4]{1,0:T(4,128)S(1)}, s32[4,4]{1,0:T(4,128)}, u32[]{:S(2)}) %copy-start.3) | copy-done | bytes 88
  14.5 0.0 copy-done.4
  14.6 0.7 %tables.1 = (f32[128,128]{1,0:T(8,128)S(1)}, bf16[160,128]{1,0:T(8,128)(2,1)S(1)}, bf16[128,40]{1,0:T(8,128)(2,1)S(1)}, bf16[128,40]{1,0:T(8,128)(2,1)S(1)}, bf1...) custom-call(s32[1,6]{1,0:T(1,128)S(1)} %copy-done.4, s32[4,4]{1,0:T(4,128)S(1)} %copy-done.3), custom_call_target="tpu_custom_call" | custom-call | flops 1 | bytes 1 | tf_op jit(solution)/shard_map/tables/pallas_call | solution.py:136
  15.2 0.0 copy-done.1
  15.2 0.5 %heads.1.refs_0_ = bf16[1024,128]{1,0:T(8,128)(2,1)S(1)} custom-call(bf16[128,1024]{1,0:T(8,128)(2,1)S(1)} %get-tuple-element.42.q_ref, bf16[128,1024]{1,0:T(8,128)(2,1)S(1)} %bitcast.9, bf16[128,1024]{1,0:T(8,128)(2,1)S(1)} %bitcast.12, f32[128,128]{1,0:T(8,128)S(1)} %get-tuple-element.40.bias), custom_call_target="tpu_custom_call" | custom-call | flops 1 | bytes 1 | tf_op jit(solution)/shard_map/heads/pallas_call | solution.py:190
  15.8 1.2 %collective-permute-done.q_ref = bf16[128,1024]{1,0:T(8,128)(2,1)S(1)} collective-permute-done((bf16[128,1024]{1,0:T(8,128)(2,1)S(1)}, bf16[128,1024]{1,0:T(8,128)(2,1)S(1)}, u32[]{:S(2)}, u32[]{:S(2)}) %collective-permute-start) | collective-permute-done | bytes 262176 | tf_op jit(solution)/shard_map/ppermute | solution.py:410
  17.0 0.7 %attend.2 = (bf16[40,2048]{1,0:T(8,128)(2,1)S(1)}, bf16[40,2048]{1,0:T(8,128)(2,1)S(1)}, bf16[40,2048]{1,0:T(8,128)(2,1)S(1)}, bf16[40,2048]{1,0:T(8,128)(2,1)S(1)}) custom-call(bf16[128,1024]{1,0:T(8,128)(2,1)S(1)} %collective-permute-done.q_ref, bf16[128,1024]{1,0:T(8,128)(2,1)S(1)} %bitcast.10, bf16[128,1024]{1,0:T(8,128)(2,1)S(1)} %bitcast.13, ...), custom_call_target="tpu_custom_call" | custom-call | flops 1 | bytes 1 | tf_op jit(solution)/shard_map/attend/pallas_call | solution.py:214
  17.7 2.9 %collective-permute-start.1 = (bf16[40,2048]{1,0:T(8,128)(2,1)S(1)}, bf16[40,2048]{1,0:T(8,128)(2,1)S(1)}, u32[]{:S(2)}, u32[]{:S(2)}) collective-permute-start(bf16[40,2048]{1,0:T(8,128)(2,1)S(1)} %get-tuple-element.44), channel_id=1, source_target_pairs={{0,6},{2,4},{4,2},{6,0},{1,7},{3,5},{5,3},{7,1},{8,14},{10,12},{12... | collective-permute-start | bytes 491528 | tf_op jit(solution)/shard_map/ppermute | solution.py:63
  20.6 0.5 %collective-permute-start.2 = (bf16[40,2048]{1,0:T(8,128)(2,1)S(1)}, bf16[40,2048]{1,0:T(8,128)(2,1)S(1)}, u32[]{:S(2)}, u32[]{:S(2)}) collective-permute-start(bf16[40,2048]{1,0:T(8,128)(2,1)S(1)} %get-tuple-element.45), channel_id=1, source_target_pairs={{0,2},{2,0},{4,6},{6,4},{1,3},{3,1},{5,7},{7,5},{8,10},{10,8},{12,... | collective-permute-start | bytes 491528 | tf_op jit(solution)/shard_map/ppermute | solution.py:63
  21.2 0.1 collective-permute-start.3
  21.3 1.3 %collective-permute-done.5.v_ref = bf16[128,1024]{1,0:T(8,128)(2,1)S(1)} collective-permute-done((bf16[128,1024]{1,0:T(8,128)(2,1)S(1)}, bf16[128,1024]{1,0:T(8,128)(2,1)S(1)}, u32[]{:S(2)}, u32[]{:S(2)}) %collective-permute-start.5) | collective-permute-done | bytes 262176 | tf_op jit(solution)/shard_map/ppermute | solution.py:409
  22.6 0.7 %attend.3 = (bf16[40,1024]{1,0:T(8,128)(2,1)S(1)}, bf16[40,1024]{1,0:T(8,128)(2,1)S(1)}, bf16[40,1024]{1,0:T(8,128)(2,1)S(1)}, bf16[40,1024]{1,0:T(8,128)(2,1)S(1)}) custom-call(bf16[128,1024]{1,0:T(8,128)(2,1)S(1)} %get-tuple-element.52.q_ref, bf16[128,1024]{1,0:T(8,128)(2,1)S(1)} %collective-permute-done.4.k_ref, ...), custom_call_target="tpu_custom_call" | custom-call | flops 1 | bytes 1 | tf_op jit(solution)/shard_map/attend/pallas_call | solution.py:214
  23.4 1.2 %collective-permute-start.10 = (bf16[128,1024]{1,0:T(8,128)(2,1)S(1)}, bf16[128,1024]{1,0:T(8,128)(2,1)S(1)}, u32[]{:S(2)}, u32[]{:S(2)}) collective-permute-start(bf16[128,1024]{1,0:T(8,128)(2,1)S(1)} %collective-permute-done.5.v_ref), channel_id=1, source_target_pairs={{0,8},{8,24},{24,16},{16,0},{1,9},{9,25},{25,17},{17,1},{2,10},{10... | collective-permute-start | bytes 786440 | tf_op jit(solution)/shard_map/ppermute | solution.py:422
  24.6 0.5 %collective-permute-done.1.refs_1_ = bf16[40,2048]{1,0:T(8,128)(2,1)S(1)} collective-permute-done((bf16[40,2048]{1,0:T(8,128)(2,1)S(1)}, bf16[40,2048]{1,0:T(8,128)(2,1)S(1)}, u32[]{:S(2)}, u32[]{:S(2)}) %collective-permute-start.1) | collective-permute-done | bytes 163872 | tf_op jit(solution)/shard_map/ppermute | solution.py:63
  25.0 2.3 %collective-permute-start.6 = (bf16[40,1024]{1,0:T(8,128)(2,1)S(1)}, bf16[40,1024]{1,0:T(8,128)(2,1)S(1)}, u32[]{:S(2)}, u32[]{:S(2)}) collective-permute-start(bf16[40,1024]{1,0:T(8,128)(2,1)S(1)} %get-tuple-element.58), channel_id=1, source_target_pairs={{0,6},{2,4},{4,2},{6,0},{1,7},{3,5},{5,3},{7,1},{8,14},{10,12},{12... | collective-permute-start | bytes 245768 | tf_op jit(solution)/shard_map/ppermute | solution.py:63
  27.3 0.1 collective-permute-done.2.refs_2_
  27.4 1.5 %collective-permute-start.7 = (bf16[40,1024]{1,0:T(8,128)(2,1)S(1)}, bf16[40,1024]{1,0:T(8,128)(2,1)S(1)}, u32[]{:S(2)}, u32[]{:S(2)}) collective-permute-start(bf16[40,1024]{1,0:T(8,128)(2,1)S(1)} %get-tuple-element.59), channel_id=1, source_target_pairs={{0,2},{2,0},{4,6},{6,4},{1,3},{3,1},{5,7},{7,5},{8,10},{10,8},{12,... | collective-permute-start | bytes 245768 | tf_op jit(solution)/shard_map/ppermute | solution.py:63
  28.9 0.0 collective-permute-done.3.refs_3_
  28.9 0.5 %collective-permute-start.8 = (bf16[40,1024]{1,0:T(8,128)(2,1)S(1)}, bf16[40,1024]{1,0:T(8,128)(2,1)S(1)}, u32[]{:S(2)}, u32[]{:S(2)}) collective-permute-start(bf16[40,1024]{1,0:T(8,128)(2,1)S(1)} %get-tuple-element.60), channel_id=1, source_target_pairs={{0,4},{2,6},{4,0},{6,2},{1,5},{3,7},{5,1},{7,3},{8,12},{10,14},{12... | collective-permute-start | bytes 245768 | tf_op jit(solution)/shard_map/ppermute | solution.py:63
  29.4 0.7 %place.3 = (bf16[128,1024]{1,0:T(8,128)(2,1)S(1)}, bf16[128,1024]{1,0:T(8,128)(2,1)S(1)}, f32[128,128]{1,0:T(8,128)S(1)}) custom-call(bf16[40,2048]{1,0:T(8,128)(2,1)S(1)} %get-tuple-element.43.refs_0_, bf16[40,2048]{1,0:T(8,128)(2,1)S(1)} %collective-permute-done.1.refs_1_, bf16[40,2048]{1,0:T(8,128)(2,1)S(1)} %collective-permute-done.2.refs_2_, ...), custom_call_target="tpu_custom_call" | custom-call | flops 1 | bytes 1 | tf_op jit(solution)/shard_map/place/pallas_call | solution.py:313
  30.1 0.0 collective-permute-done.9.k_ref
  30.1 0.6 %weigh.1 = (bf16[128,1024]{1,0:T(8,128)(2,1)S(1)}, f32[128,1024]{1,0:T(8,128)S(1)}, f32[8,128]{1,0:T(8,128)S(1)}) custom-call(bf16[128,1024]{1,0:T(8,128)(2,1)S(1)} %get-tuple-element.63.q_ref, bf16[128,1024]{1,0:T(8,128)(2,1)S(1)} %collective-permute-done.9.k_ref, f32[128,128]{1,0:T(8,128)S(1)} %get-tuple-element.40.bias, ...), custom_call_target="tpu_custom_call" | custom-call | flops 1 | bytes 1 | tf_op jit(solution)/shard_map/weigh/pallas_call | solution.py:236
  30.7 0.1 collective-permute-start.11
  30.8 0.0 collective-permute-done.6.refs_1_
  30.8 1.1 %collective-permute-done.7.refs_2_ = bf16[40,1024]{1,0:T(8,128)(2,1)S(1)} collective-permute-done((bf16[40,1024]{1,0:T(8,128)(2,1)S(1)}, bf16[40,1024]{1,0:T(8,128)(2,1)S(1)}, u32[]{:S(2)}, u32[]{:S(2)}) %collective-permute-start.7) | collective-permute-done | bytes 81952 | tf_op jit(solution)/shard_map/ppermute | solution.py:63
  31.9 1.5 %collective-permute-done.8.refs_3_ = bf16[40,1024]{1,0:T(8,128)(2,1)S(1)} collective-permute-done((bf16[40,1024]{1,0:T(8,128)(2,1)S(1)}, bf16[40,1024]{1,0:T(8,128)(2,1)S(1)}, u32[]{:S(2)}, u32[]{:S(2)}) %collective-permute-start.8) | collective-permute-done | bytes 81952 | tf_op jit(solution)/shard_map/ppermute | solution.py:63
  33.4 0.0 collective-permute-done.11._
  33.4 1.2 %collective-permute-start.15 = (bf16[128,1024]{1,0:T(8,128)(2,1)S(1)}, bf16[128,1024]{1,0:T(8,128)(2,1)S(1)}, u32[]{:S(2)}, u32[]{:S(2)}) collective-permute-start(bf16[128,1024]{1,0:T(8,128)(2,1)S(1)} %get-tuple-element.73._), channel_id=1, source_target_pairs={{8,0},{24,8},{16,24},{0,16},{9,1},{25,9},{17,25},{1,17},{10,2},{26... | collective-permute-start | bytes 786440 | tf_op jit(solution)/shard_map/ppermute | solution.py:428
  34.6 0.0 collective-permute-done.10.v_ref
  34.6 0.4 finish.1
  35.0 1.5 %collective-permute-start.12 = (bf16[40,1024]{1,0:T(8,128)(2,1)S(1)}, bf16[40,1024]{1,0:T(8,128)(2,1)S(1)}, u32[]{:S(2)}, u32[]{:S(2)}) collective-permute-start(bf16[40,1024]{1,0:T(8,128)(2,1)S(1)} %get-tuple-element.70), channel_id=1, source_target_pairs={{0,6},{2,4},{4,2},{6,0},{1,7},{3,5},{5,3},{7,1},{8,14},{10,12},{12... | collective-permute-start | bytes 245768 | tf_op jit(solution)/shard_map/ppermute | solution.py:63
  36.6 0.5 %collective-permute-start.13 = (bf16[40,1024]{1,0:T(8,128)(2,1)S(1)}, bf16[40,1024]{1,0:T(8,128)(2,1)S(1)}, u32[]{:S(2)}, u32[]{:S(2)}) collective-permute-start(bf16[40,1024]{1,0:T(8,128)(2,1)S(1)} %get-tuple-element.71), channel_id=1, source_target_pairs={{0,2},{2,0},{4,6},{6,4},{1,3},{3,1},{5,7},{7,5},{8,10},{10,8},{12,... | collective-permute-start | bytes 245768 | tf_op jit(solution)/shard_map/ppermute | solution.py:63
  37.0 1.5 %collective-permute-start.14 = (bf16[40,1024]{1,0:T(8,128)(2,1)S(1)}, bf16[40,1024]{1,0:T(8,128)(2,1)S(1)}, u32[]{:S(2)}, u32[]{:S(2)}) collective-permute-start(bf16[40,1024]{1,0:T(8,128)(2,1)S(1)} %get-tuple-element.72), channel_id=1, source_target_pairs={{0,4},{2,6},{4,0},{6,2},{1,5},{3,7},{5,1},{7,3},{8,12},{10,14},{12... | collective-permute-start | bytes 245768 | tf_op jit(solution)/shard_map/ppermute | solution.py:63
  38.6 0.4 place.4
  39.0 1.4 %collective-permute-done.12.refs_1_ = bf16[40,1024]{1,0:T(8,128)(2,1)S(1)} collective-permute-done((bf16[40,1024]{1,0:T(8,128)(2,1)S(1)}, bf16[40,1024]{1,0:T(8,128)(2,1)S(1)}, u32[]{:S(2)}, u32[]{:S(2)}) %collective-permute-start.12) | collective-permute-done | bytes 81952 | tf_op jit(solution)/shard_map/ppermute | solution.py:63
  40.4 0.6 %collective-permute-done.13.refs_2_ = bf16[40,1024]{1,0:T(8,128)(2,1)S(1)} collective-permute-done((bf16[40,1024]{1,0:T(8,128)(2,1)S(1)}, bf16[40,1024]{1,0:T(8,128)(2,1)S(1)}, u32[]{:S(2)}, u32[]{:S(2)}) %collective-permute-start.13) | collective-permute-done | bytes 81952 | tf_op jit(solution)/shard_map/ppermute | solution.py:63
  41.0 0.5 %collective-permute-done.14.refs_3_ = bf16[40,1024]{1,0:T(8,128)(2,1)S(1)} collective-permute-done((bf16[40,1024]{1,0:T(8,128)(2,1)S(1)}, bf16[40,1024]{1,0:T(8,128)(2,1)S(1)}, u32[]{:S(2)}, u32[]{:S(2)}) %collective-permute-start.14) | collective-permute-done | bytes 81952 | tf_op jit(solution)/shard_map/ppermute | solution.py:63
  41.5 0.0 collective-permute-done.15.refs_8_.refs_3_
  41.5 0.0 copy-start.5
  41.5 0.4 sums.1.refs_4_
  41.9 0.1 collective-permute-start.16
  42.0 0.2 copy-done.5
  42.2 0.4 place.5.refs_2_
  42.6 0.6 %collective-permute-done.16.refs_5_ = f32[128,128]{1,0:T(8,128)S(1)} collective-permute-done((f32[128,128]{1,0:T(8,128)S(1)}, f32[128,128]{1,0:T(8,128)S(1)}, u32[]{:S(2)}, u32[]{:S(2)}) %collective-permute-start.16) | collective-permute-done | bytes 65568 | tf_op jit(solution)/shard_map/ppermute | solution.py:434
  43.2 1.2 %norm.1 = bf16[128,4096]{1,0:T(8,128)(2,1)} custom-call(bf16[128,1024]{1,0:T(8,128)(2,1)S(1)} %get-tuple-element.51.refs_0_, bf16[128,1024]{1,0:T(8,128)(2,1)S(1)} %get-tuple-element.62.refs_1_, bf16[128,1024]{1,0:T(8,128)(2,1)S(1)} %place.5.refs_2_, bf16[128,1024]{1,0:T(8,128)(2,1)S(1)} %collective-permute-done.15.refs_8_.refs_3_, ...), custom_call_target="tpu_custom_call" | custom-call | flops 1 | bytes 1 | tf_op jit(solution)/shard_map/norm/pallas_call | solution.py:381
  (1 shorter events, 0.0 us)
Async XLA Ops:
  0.0 11.4 %collective-permute-start.4 = (bf16[128,1024]{1,0:T(8,128)(2,1)}, bf16[128,1024]{1,0:T(8,128)(2,1)S(1)}, u32[]{:S(2)}, u32[]{:S(2)}) collective-permute-start(bf16[128,1024]{1,0:T(8,128)(2,1)} %bitcast.8), channel_id=1, source_target_pairs={{0,8},{8,24},{24,16},{16,0},{1,9},{9,25},{25,17},{17,1},{2,10},{10... | collective-permute-start | bytes 786440 | tf_op jit(solution)/shard_map/ppermute | solution.py:409
  3.0 3.7 %copy-start.2 = (bf16[128,1,1,1024]{3,0,2,1:T(8,128)(2,1)S(1)}, bf16[128,1,1,1024]{3,0,2,1:T(8,128)(2,1)}, u32[]{:S(2)}) copy-start(bf16[128,1,1,1024]{3,0,2,1:T(8,128)(2,1)} %param.8) | copy-start | bytes 786436
  4.0 13.0 %collective-permute-start = (bf16[128,1024]{1,0:T(8,128)(2,1)S(1)}, bf16[128,1024]{1,0:T(8,128)(2,1)S(1)}, u32[]{:S(2)}, u32[]{:S(2)}) collective-permute-start(bf16[128,1024]{1,0:T(8,128)(2,1)S(1)} %dynamic-slice_bitcast_fusion), channel_id=1, source_target_pairs={{0,8},{8,24},{24,16},{16,0},{1,9},{9,25},{25,17},{17,1},{2,10},{10... | collective-permute-start | bytes 786440 | tf_op jit(solution)/shard_map/ppermute | solution.py:410
  6.7 15.9 %collective-permute-start.5 = (bf16[128,1024]{1,0:T(8,128)(2,1)S(1)}, bf16[128,1024]{1,0:T(8,128)(2,1)S(1)}, u32[]{:S(2)}, u32[]{:S(2)}) collective-permute-start(bf16[128,1024]{1,0:T(8,128)(2,1)S(1)} %bitcast.11), channel_id=1, source_target_pairs={{0,8},{8,24},{24,16},{16,0},{1,9},{9,25},{25,17},{17,1},{2,10},{10... | collective-permute-start | bytes 786440 | tf_op jit(solution)/shard_map/ppermute | solution.py:409
  11.4 18.7 %collective-permute-start.9 = (bf16[128,1024]{1,0:T(8,128)(2,1)S(1)}, bf16[128,1024]{1,0:T(8,128)(2,1)S(1)}, u32[]{:S(2)}, u32[]{:S(2)}) collective-permute-start(bf16[128,1024]{1,0:T(8,128)(2,1)S(1)} %collective-permute-done.4.k_ref), channel_id=1, source_target_pairs={{0,8},{8,24},{24,16},{16,0},{1,9},{9,25},{25,17},{17,1},{2,10},{10... | collective-permute-start | bytes 786440 | tf_op jit(solution)/shard_map/ppermute | solution.py:422
  12.6 1.2 %copy-start = (bf16[1,128,4096]{2,1,0:T(8,128)(2,1)S(1)}, bf16[1,128,4096]{2,1,0:T(8,128)(2,1)}, u32[]{:S(2)}) copy-start(bf16[1,128,4096]{2,1,0:T(8,128)(2,1)} %param.6) | copy-start | bytes 3145732
  13.9 0.7 %copy-start.3 = (s32[4,4]{1,0:T(4,128)S(1)}, s32[4,4]{1,0:T(4,128)}, u32[]{:S(2)}) copy-start(s32[4,4]{1,0:T(4,128)} %counts.1) | copy-start | bytes 196
  13.9 0.7 %copy-start.4 = (s32[1,6]{1,0:T(1,128)S(1)}, s32[1,6]{1,0:T(1,128)}, u32[]{:S(2)}) copy-start(s32[1,6]{1,0:T(1,128)} %docs.1) | copy-start | bytes 76
  13.9 1.4 %copy-start.1 = (bf16[128,1,1,1024]{3,0,2,1:T(8,128)(2,1)S(1)}, bf16[128,1,1,1024]{3,0,2,1:T(8,128)(2,1)}, u32[]{:S(2)}) copy-start(bf16[128,1,1,1024]{3,0,2,1:T(8,128)(2,1)} %param.7) | copy-start | bytes 786436
  17.7 7.3 %collective-permute-start.1 = (bf16[40,2048]{1,0:T(8,128)(2,1)S(1)}, bf16[40,2048]{1,0:T(8,128)(2,1)S(1)}, u32[]{:S(2)}, u32[]{:S(2)}) collective-permute-start(bf16[40,2048]{1,0:T(8,128)(2,1)S(1)} %get-tuple-element.44), channel_id=1, source_target_pairs={{0,6},{2,4},{4,2},{6,0},{1,7},{3,5},{5,3},{7,1},{8,14},{10,12},{12... | collective-permute-start | bytes 491528 | tf_op jit(solution)/shard_map/ppermute | solution.py:63
  20.6 6.8 %collective-permute-start.2 = (bf16[40,2048]{1,0:T(8,128)(2,1)S(1)}, bf16[40,2048]{1,0:T(8,128)(2,1)S(1)}, u32[]{:S(2)}, u32[]{:S(2)}) collective-permute-start(bf16[40,2048]{1,0:T(8,128)(2,1)S(1)} %get-tuple-element.45), channel_id=1, source_target_pairs={{0,2},{2,0},{4,6},{6,4},{1,3},{3,1},{5,7},{7,5},{8,10},{10,8},{12,... | collective-permute-start | bytes 491528 | tf_op jit(solution)/shard_map/ppermute | solution.py:63
  21.2 7.7 %collective-permute-start.3 = (bf16[40,2048]{1,0:T(8,128)(2,1)S(1)}, bf16[40,2048]{1,0:T(8,128)(2,1)S(1)}, u32[]{:S(2)}, u32[]{:S(2)}) collective-permute-start(bf16[40,2048]{1,0:T(8,128)(2,1)S(1)} %get-tuple-element.46), channel_id=1, source_target_pairs={{0,4},{2,6},{4,0},{6,2},{1,5},{3,7},{5,1},{7,3},{8,12},{10,14},{12... | collective-permute-start | bytes 491528 | tf_op jit(solution)/shard_map/ppermute | solution.py:63
  23.4 11.2 %collective-permute-start.10 = (bf16[128,1024]{1,0:T(8,128)(2,1)S(1)}, bf16[128,1024]{1,0:T(8,128)(2,1)S(1)}, u32[]{:S(2)}, u32[]{:S(2)}) collective-permute-start(bf16[128,1024]{1,0:T(8,128)(2,1)S(1)} %collective-permute-done.5.v_ref), channel_id=1, source_target_pairs={{0,8},{8,24},{24,16},{16,0},{1,9},{9,25},{25,17},{17,1},{2,10},{10... | collective-permute-start | bytes 786440 | tf_op jit(solution)/shard_map/ppermute | solution.py:422
  25.0 5.7 %collective-permute-start.6 = (bf16[40,1024]{1,0:T(8,128)(2,1)S(1)}, bf16[40,1024]{1,0:T(8,128)(2,1)S(1)}, u32[]{:S(2)}, u32[]{:S(2)}) collective-permute-start(bf16[40,1024]{1,0:T(8,128)(2,1)S(1)} %get-tuple-element.58), channel_id=1, source_target_pairs={{0,6},{2,4},{4,2},{6,0},{1,7},{3,5},{5,3},{7,1},{8,14},{10,12},{12... | collective-permute-start | bytes 245768 | tf_op jit(solution)/shard_map/ppermute | solution.py:63
  27.4 4.4 %collective-permute-start.7 = (bf16[40,1024]{1,0:T(8,128)(2,1)S(1)}, bf16[40,1024]{1,0:T(8,128)(2,1)S(1)}, u32[]{:S(2)}, u32[]{:S(2)}) collective-permute-start(bf16[40,1024]{1,0:T(8,128)(2,1)S(1)} %get-tuple-element.59), channel_id=1, source_target_pairs={{0,2},{2,0},{4,6},{6,4},{1,3},{3,1},{5,7},{7,5},{8,10},{10,8},{12,... | collective-permute-start | bytes 245768 | tf_op jit(solution)/shard_map/ppermute | solution.py:63
  28.9 4.4 %collective-permute-start.8 = (bf16[40,1024]{1,0:T(8,128)(2,1)S(1)}, bf16[40,1024]{1,0:T(8,128)(2,1)S(1)}, u32[]{:S(2)}, u32[]{:S(2)}) collective-permute-start(bf16[40,1024]{1,0:T(8,128)(2,1)S(1)} %get-tuple-element.60), channel_id=1, source_target_pairs={{0,4},{2,6},{4,0},{6,2},{1,5},{3,7},{5,1},{7,3},{8,12},{10,14},{12... | collective-permute-start | bytes 245768 | tf_op jit(solution)/shard_map/ppermute | solution.py:63
  30.7 2.7 %collective-permute-start.11 = (f32[8,128]{1,0:T(8,128)S(1)}, f32[8,128]{1,0:T(8,128)S(1)}, u32[]{:S(2)}, u32[]{:S(2)}) collective-permute-start(f32[8,128]{1,0:T(8,128)S(1)} %get-tuple-element.68), channel_id=1, source_target_pairs={{0,1},{1,0},{2,3},{3,2},{4,5},{5,4},{6,7},{7,6},{8,9},{9,8},{10,11... | collective-permute-start | bytes 12296 | tf_op jit(solution)/shard_map/ppermute | solution.py:426
  33.4 8.1 %collective-permute-start.15 = (bf16[128,1024]{1,0:T(8,128)(2,1)S(1)}, bf16[128,1024]{1,0:T(8,128)(2,1)S(1)}, u32[]{:S(2)}, u32[]{:S(2)}) collective-permute-start(bf16[128,1024]{1,0:T(8,128)(2,1)S(1)} %get-tuple-element.73._), channel_id=1, source_target_pairs={{8,0},{24,8},{16,24},{0,16},{9,1},{25,9},{17,25},{1,17},{10,2},{26... | collective-permute-start | bytes 786440 | tf_op jit(solution)/shard_map/ppermute | solution.py:428
  35.0 5.4 %collective-permute-start.12 = (bf16[40,1024]{1,0:T(8,128)(2,1)S(1)}, bf16[40,1024]{1,0:T(8,128)(2,1)S(1)}, u32[]{:S(2)}, u32[]{:S(2)}) collective-permute-start(bf16[40,1024]{1,0:T(8,128)(2,1)S(1)} %get-tuple-element.70), channel_id=1, source_target_pairs={{0,6},{2,4},{4,2},{6,0},{1,7},{3,5},{5,3},{7,1},{8,14},{10,12},{12... | collective-permute-start | bytes 245768 | tf_op jit(solution)/shard_map/ppermute | solution.py:63
  36.6 4.4 %collective-permute-start.13 = (bf16[40,1024]{1,0:T(8,128)(2,1)S(1)}, bf16[40,1024]{1,0:T(8,128)(2,1)S(1)}, u32[]{:S(2)}, u32[]{:S(2)}) collective-permute-start(bf16[40,1024]{1,0:T(8,128)(2,1)S(1)} %get-tuple-element.71), channel_id=1, source_target_pairs={{0,2},{2,0},{4,6},{6,4},{1,3},{3,1},{5,7},{7,5},{8,10},{10,8},{12,... | collective-permute-start | bytes 245768 | tf_op jit(solution)/shard_map/ppermute | solution.py:63
  37.0 4.4 %collective-permute-start.14 = (bf16[40,1024]{1,0:T(8,128)(2,1)S(1)}, bf16[40,1024]{1,0:T(8,128)(2,1)S(1)}, u32[]{:S(2)}, u32[]{:S(2)}) collective-permute-start(bf16[40,1024]{1,0:T(8,128)(2,1)S(1)} %get-tuple-element.72), channel_id=1, source_target_pairs={{0,4},{2,6},{4,0},{6,2},{1,5},{3,7},{5,1},{7,3},{8,12},{10,14},{12... | collective-permute-start | bytes 245768 | tf_op jit(solution)/shard_map/ppermute | solution.py:63
  41.5 0.7 %copy-start.5 = (bf16[4096]{0:T(1024)(128)(2,1)S(1)}, bf16[4096]{0:T(1024)(128)(2,1)}, u32[]{:S(2)}) copy-start(bf16[4096]{0:T(1024)(128)(2,1)} %param.11) | copy-start | bytes 24580
  41.9 1.3 %collective-permute-start.16 = (f32[128,128]{1,0:T(8,128)S(1)}, f32[128,128]{1,0:T(8,128)S(1)}, u32[]{:S(2)}, u32[]{:S(2)}) collective-permute-start(f32[128,128]{1,0:T(8,128)S(1)} %sums.1.refs_4_), channel_id=1, source_target_pairs={{0,1},{1,0},{2,3},{3,2},{4,5},{5,4},{6,7},{7,6},{8,9},{9,8},{10,11... | collective-permute-start | bytes 196616 | tf_op jit(solution)/shard_map/ppermute | solution.py:434
